TPU v7x, 32 devices: a whole 2x2x4 slice. The times are simulated.
32 devices in a mesh: parts: 2 (over y), map: 16 (over z, x, core).
Axes of the slice: x: 2, y: 2, z: 4, core: 2. Of those that a mesh axis runs over, the one named last changes fastest.
Arguments:
- crust_velocity: float32 [6, 128, 32, 32], P('parts', 'map'), parts along dimension 0, may hold values from -6 to 6
- crust_stress: float32 [12, 128, 32, 32], P('parts', 'map'), parts along dimension 0, may hold values from -6 to 6
- ocean_state: float32 [8, 32, 32, 128], P('parts', 'map'), parts along dimension 0, may hold values from -6 to 6
- zones: int32 [128, 64, 32], P('map', 'parts'), parts along dimension 1, may hold values from 0 to 7
- materials: float32 [3, 8], replicated, may hold values from 0.4 to 1.2
- slip_rate: float32 [128, 64], P('map', 'parts'), parts along dimension 1, may hold values from -6 to 6
- bathymetry: int32 [32, 256], P('map', 'parts'), parts along dimension 1, may hold values from 1 to 32
Outputs:
- new_velocity: float32 [6, 128, 32, 32], P('parts', 'map'), parts along dimension 0
- new_stress: float32 [12, 128, 32, 32], P('parts', 'map'), parts along dimension 0
- new_ocean: float32 [8, 32, 32, 128], P('parts', 'map'), parts along dimension 0
There are 2 independent parts, one for each index of `parts`. A program takes and returns all parts, laid end to end along the dimension named above; an argument that names none is the same for every part. Nothing has to cross between parts.
All inputs are finite; a program needn't handle non-finite values.
Results may differ from a plain program's by a relative error of at most 0.0001.
Values sent between devices are 32-bit elements; how exact they have to be, the bound alone decides.
No kernel may reach another device: no remote copies, remote signals or barrier semaphores. Data moves between devices by JAX's collectives and lax.ppermute only.
A program may use at most 64 MiB of HBM per device.

v0:
```python
import jax
import jax.numpy as jnp
from jax import lax
from jax.sharding import PartitionSpec as P

STEPS = 4
ZONES = 8


DT = 0.25
KBULK = 2.25
GRAV = 0.1


def with_halo(block, sides, width):
    for axis, dim in sides:
        count = lax.axis_size(axis)
        forward = [(i, i + 1) for i in range(count - 1)]
        backward = [(target, source) for source, target in forward]
        low = lax.ppermute(
            lax.slice_in_dim(block, block.shape[dim] - width, None, axis=dim), axis, forward
        )
        high = lax.ppermute(lax.slice_in_dim(block, 0, width, axis=dim), axis, backward)
        block = jnp.concatenate([low, block, high], axis=dim)
    return block


def central(field, axis):
    count = field.shape[axis]
    widths = [(0, 0)] * field.ndim
    widths[axis] = (1, 1)
    padded = jnp.pad(field, widths)
    return (
        lax.slice_in_dim(padded, 2, count + 2, axis=axis)
        - lax.slice_in_dim(padded, 0, count, axis=axis)
    ) * 0.5


def crust_x(field):
    extended = with_halo(field, (("map", 1),), 1)
    count = field.shape[1]
    return (extended[:, 2 : count + 2] - extended[:, 0:count]) * 0.5


def strip_y(field):
    extended = with_halo(field, (("map", 0),), 1)
    count = field.shape[0]
    return (extended[2 : count + 2] - extended[0:count]) * 0.5


def depth_diff(field, top):
    above = jnp.concatenate([top[:, None, :], field[:, :-1, :]], axis=1)
    below = jnp.concatenate([field[:, 1:, :], jnp.zeros_like(field[:, :1, :])], axis=1)
    return (below - above) * 0.5


def crust_step(velocity, stress, mats, fault, load):
    buoy, lamb, shear = (mats[0], mats[1], mats[2])
    sxx, syy, szz, sxy, sxz, syz = (
        stress[0],
        stress[1],
        stress[2],
        stress[3],
        stress[4],
        stress[5],
    )
    zero = jnp.zeros_like(load)
    grads = crust_x(jnp.stack([sxx, sxy, sxz]))
    acc_x = grads[0] + central(sxy, 2) + depth_diff(sxz, zero)
    acc_y = grads[1] + central(syy, 2) + depth_diff(syz, zero)
    acc_z = grads[2] + central(syz, 2) + depth_diff(szz, -load)
    vel_x = velocity[0] + DT * buoy * acc_x
    vel_y = velocity[1] + DT * buoy * acc_y
    vel_z = velocity[2] + DT * buoy * acc_z
    slopes = crust_x(jnp.stack([vel_x, vel_y, vel_z]))
    exx = slopes[0]
    eyy = central(vel_y, 2)
    ezz = depth_diff(vel_z, vel_z[:, 0, :])
    exy = 0.5 * (central(vel_x, 2) + slopes[1])
    exz = 0.5 * (depth_diff(vel_x, vel_x[:, 0, :]) + slopes[2])
    eyz = 0.5 * (depth_diff(vel_y, vel_y[:, 0, :]) + central(vel_z, 2))
    trace = exx + eyy + ezz
    new_stress = jnp.stack(
        [
            sxx + DT * (lamb * trace + 2.0 * shear * exx),
            syy + DT * (lamb * trace + 2.0 * shear * eyy),
            szz + DT * (lamb * trace + 2.0 * shear * ezz),
            sxy + DT * 2.0 * shear * exy,
            sxz + DT * 2.0 * shear * exz + DT * fault,
            syz + DT * 2.0 * shear * eyz,
        ]
    )
    return (jnp.stack([vel_x, vel_y, vel_z]), new_stress)


def next_layer(field):
    return jnp.concatenate([field[:, 1:, :], jnp.zeros_like(field[:, :1, :])], axis=1)


def ocean_step(fields, water, bottom, floor, xdiff, ydiff):
    press, flow_x, flow_y, flow_w = fields
    p_up = jnp.concatenate([-press[:, :1, :], press[:, :-1, :]], axis=1)
    p_down = next_layer(press) + bottom * press
    flow_x = water * (flow_x - DT * xdiff(press))
    flow_y = water * (flow_y - DT * ydiff(press))
    flow_w = water * (flow_w - DT * ((p_down - p_up) * 0.5 + GRAV * press))
    w_up = jnp.concatenate([flow_w[:, :1, :], flow_w[:, :-1, :]], axis=1)
    w_down = next_layer(flow_w) + bottom * floor[:, None, :]
    diverge = xdiff(flow_x) + ydiff(flow_y) + (w_down - w_up) * 0.5
    press = water * (press - DT * KBULK * diverge)
    return (press, flow_x, flow_y, flow_w)


def on_device(crust_velocity, crust_stress, ocean_state, zones, materials, slip_rate, bathymetry):
    onehot = (zones[None] == jnp.arange(ZONES, dtype=jnp.int32)[:, None, None, None]).astype(
        jnp.float32
    )
    mats = jnp.einsum("cz,zabk->cabk", materials, onehot, precision=lax.Precision.HIGHEST)
    depth_cells = crust_velocity.shape[2]
    layer = (jnp.arange(depth_cells, dtype=jnp.int32) == depth_cells // 2).astype(jnp.float32)
    fault = slip_rate[:, None, :] * layer[None, :, None]
    layers = ocean_state.shape[2]
    depth_idx = jnp.arange(layers, dtype=jnp.int32)
    water = (depth_idx[None, :, None] < bathymetry[:, None, :]).astype(jnp.float32)
    velocity, stress = (crust_velocity, crust_stress)
    bottom = water - next_layer(water)
    fields = tuple((water * ocean_state[i] for i in range(4)))
    for step in range(STEPS):
        floor = lax.all_to_all(
            velocity[2][:, 0, :], "map", split_axis=1, concat_axis=0, tiled=True
        ).T
        fields = ocean_step(fields, water, bottom, floor, lambda f: central(f, 2), strip_y)
        strip_load = jnp.sum(bottom * fields[0], axis=1)
        load = lax.all_to_all(strip_load.T, "map", split_axis=0, concat_axis=1, tiled=True)
        velocity, stress = crust_step(velocity, stress, mats, fault, load)
    ocean_out = jnp.stack(fields)
    return (velocity, stress, ocean_out)


def solution(mesh):
    return jax.shard_map(
        on_device,
        mesh=mesh,
        in_specs=(
            P("parts", "map", None, None),
            P("parts", "map", None, None),
            P("parts", "map", None, None),
            P("map", "parts", None),
            P(),
            P("map", "parts"),
            P("map", "parts"),
        ),
        out_specs=(
            P("parts", "map", None, None),
            P("parts", "map", None, None),
            P("parts", "map", None, None),
        ),
        check_vma=False,
    )
```

profile of v0, /device:TPU:0, one launch (start us, length us, event | category | flops | bytes accessed | tf_op | source)
XLA Modules:
  0.0 208.9 jit_solution(1538869870880392524)
XLA Ops:
  7.4 7.9 %all-to-all-start = ((f32[8,16,2]{0,2,1:T(2,128)}), f32[8,16,2]{0,2,1:T(2,128)S(1)}, u32[]{:S(2)}, u32[]{:S(2)}) async-start(f32[8,16,2]{0,2,1:T(2,128)} %bitcast.23), calls=%async_computation | async-start | bytes 32768 | tf_op jit(solution)/shard_map/all_to_all | solution.py:129
  18.1 3.0 %collective-permute-start.1 = (f32[3,1,32,32]{3,2,1,0:T(8,128)S(1)}, f32[3,1,32,32]{3,2,1,0:T(8,128)S(1)}, u32[]{:S(2)}, u32[]{:S(2)}) collective-permute-start(f32[3,1,32,32]{3,2,1,0:T(8,128)S(1)} %get-tuple-element.67), channel_id=1, source_target_pairs={{0,1},{1,2},{2,3},{3,4},{4,5},{5,6},{6,7},{7,8},{8,9},{9,10},{10,1... | collective-permute-start | bytes 36872 | tf_op jit(solution)/shard_map/ppermute | solution.py:20
  26.5 4.2 %collective-permute-start.5 = (f32[1,32,128]{2,1,0:T(8,128)S(1)}, f32[1,32,128]{2,1,0:T(8,128)S(1)}, u32[]{:S(2)}, u32[]{:S(2)}) collective-permute-start(f32[1,32,128]{2,1,0:T(8,128)S(1)} %get-tuple-element.153), channel_id=1, source_target_pairs={{0,1},{1,2},{2,3},{3,4},{4,5},{5,6},{6,7},{7,8},{8,9},{9,10},{10,1... | collective-permute-start | bytes 49160 | tf_op jit(solution)/shard_map/ppermute | solution.py:20
  33.5 10.0 %all-to-all-start.1 = ((f32[16,8,2]{1,2,0:T(2,128)}), f32[16,8,2]{1,2,0:T(2,128)S(1)}, u32[]{:S(2)}, u32[]{:S(2)}) async-start(f32[16,8,2]{1,2,0:T(2,128)} %copy.36), calls=%async_computation.1 | async-start | bytes 32768 | tf_op jit(solution)/shard_map/all_to_all | solution.py:134
  45.4 3.6 %collective-permute-start.11 = (f32[1,32,128]{2,1,0:T(8,128)}, f32[1,32,128]{2,1,0:T(8,128)}, u32[]{:S(2)}, u32[]{:S(2)}) collective-permute-start(f32[1,32,128]{2,1,0:T(8,128)} %get-tuple-element.147), channel_id=1, source_target_pairs={{0,1},{1,2},{2,3},{3,4},{4,5},{5,6},{6,7},{7,8},{8,9},{9,10},{10,1... | collective-permute-start | bytes 49160 | tf_op jit(solution)/shard_map/ppermute | solution.py:20
  52.2 5.4 %all-to-all-start.2 = ((f32[8,16,2]{0,2,1:T(2,128)}), f32[8,16,2]{0,2,1:T(2,128)S(1)}, u32[]{:S(2)}, u32[]{:S(2)}) async-start(f32[8,16,2]{0,2,1:T(2,128)} %bitcast.44), calls=%async_computation.2 | async-start | bytes 32768 | tf_op jit(solution)/shard_map/all_to_all | solution.py:129
  58.9 3.0 %collective-permute-start.7 = (f32[3,1,32,32]{3,2,1,0:T(8,128)S(1)}, f32[3,1,32,32]{3,2,1,0:T(8,128)S(1)}, u32[]{:S(2)}, u32[]{:S(2)}) collective-permute-start(f32[3,1,32,32]{3,2,1,0:T(8,128)S(1)} %get-tuple-element.65), channel_id=1, source_target_pairs={{0,1},{1,2},{2,3},{3,4},{4,5},{5,6},{6,7},{7,8},{8,9},{9,10},{10,1... | collective-permute-start | bytes 36872 | tf_op jit(solution)/shard_map/ppermute | solution.py:20
  69.2 3.0 %collective-permute-start.9 = (f32[3,1,32,32]{3,2,1,0:T(8,128)S(1)}, f32[3,1,32,32]{3,2,1,0:T(8,128)S(1)}, u32[]{:S(2)}, u32[]{:S(2)}) collective-permute-start(f32[3,1,32,32]{3,2,1,0:T(8,128)S(1)} %get-tuple-element.63), channel_id=1, source_target_pairs={{0,1},{1,2},{2,3},{3,4},{4,5},{5,6},{6,7},{7,8},{8,9},{9,10},{10,1... | collective-permute-start | bytes 36872 | tf_op jit(solution)/shard_map/ppermute | solution.py:20
  75.1 4.4 %collective-permute-start.13 = (f32[1,32,128]{2,1,0:T(8,128)S(1)}, f32[1,32,128]{2,1,0:T(8,128)S(1)}, u32[]{:S(2)}, u32[]{:S(2)}) collective-permute-start(f32[1,32,128]{2,1,0:T(8,128)S(1)} %get-tuple-element.145), channel_id=1, source_target_pairs={{0,1},{1,2},{2,3},{3,4},{4,5},{5,6},{6,7},{7,8},{8,9},{9,10},{10,1... | collective-permute-start | bytes 49160 | tf_op jit(solution)/shard_map/ppermute | solution.py:20
  83.0 10.9 %all-to-all-start.3 = ((f32[16,8,2]{1,2,0:T(2,128)}), f32[16,8,2]{1,2,0:T(2,128)S(1)}, u32[]{:S(2)}, u32[]{:S(2)}) async-start(f32[16,8,2]{1,2,0:T(2,128)} %copy.41), calls=%async_computation.3 | async-start | bytes 32768 | tf_op jit(solution)/shard_map/all_to_all | solution.py:134
  95.8 3.6 %collective-permute-start.19 = (f32[1,32,128]{2,1,0:T(8,128)}, f32[1,32,128]{2,1,0:T(8,128)}, u32[]{:S(2)}, u32[]{:S(2)}) collective-permute-start(f32[1,32,128]{2,1,0:T(8,128)} %get-tuple-element.139), channel_id=1, source_target_pairs={{0,1},{1,2},{2,3},{3,4},{4,5},{5,6},{6,7},{7,8},{8,9},{9,10},{10,1... | collective-permute-start | bytes 49160 | tf_op jit(solution)/shard_map/ppermute | solution.py:20
  103.5 5.4 %all-to-all-start.4 = ((f32[8,16,2]{0,2,1:T(2,128)}), f32[8,16,2]{0,2,1:T(2,128)S(1)}, u32[]{:S(2)}, u32[]{:S(2)}) async-start(f32[8,16,2]{0,2,1:T(2,128)} %bitcast.62), calls=%async_computation.4 | async-start | bytes 32768 | tf_op jit(solution)/shard_map/all_to_all | solution.py:129
  111.6 3.7 %collective-permute-start.15 = (f32[3,1,32,32]{3,2,1,0:T(8,128)}, f32[3,1,32,32]{3,2,1,0:T(8,128)}, u32[]{:S(2)}, u32[]{:S(2)}) collective-permute-start(f32[3,1,32,32]{3,2,1,0:T(8,128)} %get-tuple-element.61), channel_id=1, source_target_pairs={{0,1},{1,2},{2,3},{3,4},{4,5},{5,6},{6,7},{7,8},{8,9},{9,10},{10,1... | collective-permute-start | bytes 36872 | tf_op jit(solution)/shard_map/ppermute | solution.py:20
  120.6 3.6 %collective-permute-start.17 = (f32[3,1,32,32]{3,2,1,0:T(8,128)S(1)}, f32[3,1,32,32]{3,2,1,0:T(8,128)S(1)}, u32[]{:S(2)}, u32[]{:S(2)}) collective-permute-start(f32[3,1,32,32]{3,2,1,0:T(8,128)S(1)} %get-tuple-element.58), channel_id=1, source_target_pairs={{0,1},{1,2},{2,3},{3,4},{4,5},{5,6},{6,7},{7,8},{8,9},{9,10},{10,1... | collective-permute-start | bytes 36872 | tf_op jit(solution)/shard_map/ppermute | solution.py:20
  127.1 4.8 %collective-permute-start.21 = (f32[1,32,128]{2,1,0:T(8,128)S(1)}, f32[1,32,128]{2,1,0:T(8,128)S(1)}, u32[]{:S(2)}, u32[]{:S(2)}) collective-permute-start(f32[1,32,128]{2,1,0:T(8,128)S(1)} %get-tuple-element.137), channel_id=1, source_target_pairs={{0,1},{1,2},{2,3},{3,4},{4,5},{5,6},{6,7},{7,8},{8,9},{9,10},{10,1... | collective-permute-start | bytes 49160 | tf_op jit(solution)/shard_map/ppermute | solution.py:20
  135.4 10.9 %all-to-all-start.5 = ((f32[16,8,2]{1,2,0:T(2,128)}), f32[16,8,2]{1,2,0:T(2,128)S(1)}, u32[]{:S(2)}, u32[]{:S(2)}) async-start(f32[16,8,2]{1,2,0:T(2,128)} %copy.45), calls=%async_computation.5 | async-start | bytes 32768 | tf_op jit(solution)/shard_map/all_to_all | solution.py:134
  148.2 3.6 %collective-permute-start.27 = (f32[1,32,128]{2,1,0:T(8,128)}, f32[1,32,128]{2,1,0:T(8,128)}, u32[]{:S(2)}, u32[]{:S(2)}) collective-permute-start(f32[1,32,128]{2,1,0:T(8,128)} %get-tuple-element.131), channel_id=1, source_target_pairs={{0,1},{1,2},{2,3},{3,4},{4,5},{5,6},{6,7},{7,8},{8,9},{9,10},{10,1... | collective-permute-start | bytes 49160 | tf_op jit(solution)/shard_map/ppermute | solution.py:20
  154.0 5.4 %all-to-all-start.6 = ((f32[8,16,2]{0,2,1:T(2,128)}), f32[8,16,2]{0,2,1:T(2,128)S(1)}, u32[]{:S(2)}, u32[]{:S(2)}) async-start(f32[8,16,2]{0,2,1:T(2,128)} %bitcast.80), calls=%async_computation.6 | async-start | bytes 32768 | tf_op jit(solution)/shard_map/all_to_all | solution.py:129
  160.8 3.0 %collective-permute-start.23 = (f32[3,1,32,32]{3,2,1,0:T(8,128)S(1)}, f32[3,1,32,32]{3,2,1,0:T(8,128)S(1)}, u32[]{:S(2)}, u32[]{:S(2)}) collective-permute-start(f32[3,1,32,32]{3,2,1,0:T(8,128)S(1)} %get-tuple-element.56), channel_id=1, source_target_pairs={{0,1},{1,2},{2,3},{3,4},{4,5},{5,6},{6,7},{7,8},{8,9},{9,10},{10,1... | collective-permute-start | bytes 36872 | tf_op jit(solution)/shard_map/ppermute | solution.py:20
  170.6 3.0 %collective-permute-start.25 = (f32[3,1,32,32]{3,2,1,0:T(8,128)S(1)}, f32[3,1,32,32]{3,2,1,0:T(8,128)S(1)}, u32[]{:S(2)}, u32[]{:S(2)}) collective-permute-start(f32[3,1,32,32]{3,2,1,0:T(8,128)S(1)} %get-tuple-element.53), channel_id=1, source_target_pairs={{0,1},{1,2},{2,3},{3,4},{4,5},{5,6},{6,7},{7,8},{8,9},{9,10},{10,1... | collective-permute-start | bytes 36872 | tf_op jit(solution)/shard_map/ppermute | solution.py:20
  176.5 4.4 %collective-permute-start.29 = (f32[1,32,128]{2,1,0:T(8,128)S(1)}, f32[1,32,128]{2,1,0:T(8,128)S(1)}, u32[]{:S(2)}, u32[]{:S(2)}) collective-permute-start(f32[1,32,128]{2,1,0:T(8,128)S(1)} %get-tuple-element.129), channel_id=1, source_target_pairs={{0,1},{1,2},{2,3},{3,4},{4,5},{5,6},{6,7},{7,8},{8,9},{9,10},{10,1... | collective-permute-start | bytes 49160 | tf_op jit(solution)/shard_map/ppermute | solution.py:20
  183.2 10.9 %all-to-all-start.7 = ((f32[16,8,2]{1,2,0:T(2,128)}), f32[16,8,2]{1,2,0:T(2,128)S(1)}, u32[]{:S(2)}, u32[]{:S(2)}) async-start(f32[16,8,2]{1,2,0:T(2,128)} %copy.49), calls=%async_computation.7 | async-start | bytes 32768 | tf_op jit(solution)/shard_map/all_to_all | solution.py:134
  194.8 5.8 %all-to-all-done.7 = f32[16,8,2]{1,2,0:T(2,128)S(1)} async-done(((f32[16,8,2]{1,2,0:T(2,128)}), f32[16,8,2]{1,2,0:T(2,128)S(1)}, u32[]{:S(2)}, u32[]{:S(2)}) %all-to-all-start.7) | async-done | bytes 1056 | tf_op jit(solution)/shard_map/all_to_all | solution.py:134
  203.3 3.0 %collective-permute-start.31 = (f32[3,1,32,32]{3,2,1,0:T(8,128)S(1)}, f32[3,1,32,32]{3,2,1,0:T(8,128)S(1)}, u32[]{:S(2)}, u32[]{:S(2)}) collective-permute-start(f32[3,1,32,32]{3,2,1,0:T(8,128)S(1)} %get-tuple-element.51), channel_id=1, source_target_pairs={{0,1},{1,2},{2,3},{3,4},{4,5},{5,6},{6,7},{7,8},{8,9},{9,10},{10,1... | collective-permute-start | bytes 36872 | tf_op jit(solution)/shard_map/ppermute | solution.py:20
  (284 shorter events, 80.1 us)
Async XLA Ops:
  1.4 22.7 %collective-permute-start.2 = (f32[1,32,128]{2,1,0:T(8,128)S(1)}, f32[1,32,128]{2,1,0:T(8,128)S(1)}, u32[]{:S(2)}, u32[]{:S(2)}) collective-permute-start(f32[1,32,128]{2,1,0:T(8,128)S(1)} %get-tuple-element.154), channel_id=1, source_target_pairs={{1,0},{2,1},{3,2},{4,3},{5,4},{6,5},{7,6},{8,7},{9,8},{10,9},{11,1... | collective-permute-start | bytes 49160 | tf_op jit(solution)/shard_map/ppermute | solution.py:23
  2.7 21.4 %collective-permute-start.3 = (f32[1,32,128]{2,1,0:T(8,128)S(1)}, f32[1,32,128]{2,1,0:T(8,128)S(1)}, u32[]{:S(2)}, u32[]{:S(2)}) collective-permute-start(f32[1,32,128]{2,1,0:T(8,128)S(1)} %get-tuple-element.155), channel_id=1, source_target_pairs={{0,1},{1,2},{2,3},{3,4},{4,5},{5,6},{6,7},{7,8},{8,9},{9,10},{10,1... | collective-permute-start | bytes 49160 | tf_op jit(solution)/shard_map/ppermute | solution.py:20
  7.4 16.5 %all-to-all-start = ((f32[8,16,2]{0,2,1:T(2,128)}), f32[8,16,2]{0,2,1:T(2,128)S(1)}, u32[]{:S(2)}, u32[]{:S(2)}) async-start(f32[8,16,2]{0,2,1:T(2,128)} %bitcast.23), calls=%async_computation | async-start | bytes 32768 | tf_op jit(solution)/shard_map/all_to_all | solution.py:129
  16.8 7.2 %collective-permute-start = (f32[3,1,32,32]{3,2,1,0:T(8,128)S(1)}, f32[3,1,32,32]{3,2,1,0:T(8,128)S(1)}, u32[]{:S(2)}, u32[]{:S(2)}) collective-permute-start(f32[3,1,32,32]{3,2,1,0:T(8,128)S(1)} %get-tuple-element.66), channel_id=1, source_target_pairs={{1,0},{2,1},{3,2},{4,3},{5,4},{6,5},{7,6},{8,7},{9,8},{10,9},{11,1... | collective-permute-start | bytes 36872 | tf_op jit(solution)/shard_map/ppermute | solution.py:23
  33.5 16.5 %all-to-all-start.1 = ((f32[16,8,2]{1,2,0:T(2,128)}), f32[16,8,2]{1,2,0:T(2,128)S(1)}, u32[]{:S(2)}, u32[]{:S(2)}) async-start(f32[16,8,2]{1,2,0:T(2,128)} %copy.36), calls=%async_computation.1 | async-start | bytes 32768 | tf_op jit(solution)/shard_map/all_to_all | solution.py:134
  44.1 28.2 %collective-permute-start.10 = (f32[1,32,128]{2,1,0:T(8,128)}, f32[1,32,128]{2,1,0:T(8,128)}, u32[]{:S(2)}, u32[]{:S(2)}) collective-permute-start(f32[1,32,128]{2,1,0:T(8,128)} %get-tuple-element.146), channel_id=1, source_target_pairs={{1,0},{2,1},{3,2},{4,3},{5,4},{6,5},{7,6},{8,7},{9,8},{10,9},{11,1... | collective-permute-start | bytes 49160 | tf_op jit(solution)/shard_map/ppermute | solution.py:23
  45.4 26.9 %collective-permute-start.11 = (f32[1,32,128]{2,1,0:T(8,128)}, f32[1,32,128]{2,1,0:T(8,128)}, u32[]{:S(2)}, u32[]{:S(2)}) collective-permute-start(f32[1,32,128]{2,1,0:T(8,128)} %get-tuple-element.147), channel_id=1, source_target_pairs={{0,1},{1,2},{2,3},{3,4},{4,5},{5,6},{6,7},{7,8},{8,9},{9,10},{10,1... | collective-permute-start | bytes 49160 | tf_op jit(solution)/shard_map/ppermute | solution.py:20
  52.2 11.9 %all-to-all-start.2 = ((f32[8,16,2]{0,2,1:T(2,128)}), f32[8,16,2]{0,2,1:T(2,128)S(1)}, u32[]{:S(2)}, u32[]{:S(2)}) async-start(f32[8,16,2]{0,2,1:T(2,128)} %bitcast.44), calls=%async_computation.2 | async-start | bytes 32768 | tf_op jit(solution)/shard_map/all_to_all | solution.py:129
  67.8 11.7 %collective-permute-start.8 = (f32[3,1,32,32]{3,2,1,0:T(8,128)S(1)}, f32[3,1,32,32]{3,2,1,0:T(8,128)S(1)}, u32[]{:S(2)}, u32[]{:S(2)}) collective-permute-start(f32[3,1,32,32]{3,2,1,0:T(8,128)S(1)} %get-tuple-element.62), channel_id=1, source_target_pairs={{1,0},{2,1},{3,2},{4,3},{5,4},{6,5},{7,6},{8,7},{9,8},{10,9},{11,1... | collective-permute-start | bytes 36872 | tf_op jit(solution)/shard_map/ppermute | solution.py:23
  69.2 10.3 %collective-permute-start.9 = (f32[3,1,32,32]{3,2,1,0:T(8,128)S(1)}, f32[3,1,32,32]{3,2,1,0:T(8,128)S(1)}, u32[]{:S(2)}, u32[]{:S(2)}) collective-permute-start(f32[3,1,32,32]{3,2,1,0:T(8,128)S(1)} %get-tuple-element.63), channel_id=1, source_target_pairs={{0,1},{1,2},{2,3},{3,4},{4,5},{5,6},{6,7},{7,8},{8,9},{9,10},{10,1... | collective-permute-start | bytes 36872 | tf_op jit(solution)/shard_map/ppermute | solution.py:20
  83.0 17.4 %all-to-all-start.3 = ((f32[16,8,2]{1,2,0:T(2,128)}), f32[16,8,2]{1,2,0:T(2,128)S(1)}, u32[]{:S(2)}, u32[]{:S(2)}) async-start(f32[16,8,2]{1,2,0:T(2,128)} %copy.41), calls=%async_computation.3 | async-start | bytes 32768 | tf_op jit(solution)/shard_map/all_to_all | solution.py:134
  94.5 29.7 %collective-permute-start.18 = (f32[1,32,128]{2,1,0:T(8,128)}, f32[1,32,128]{2,1,0:T(8,128)}, u32[]{:S(2)}, u32[]{:S(2)}) collective-permute-start(f32[1,32,128]{2,1,0:T(8,128)} %get-tuple-element.138), channel_id=1, source_target_pairs={{1,0},{2,1},{3,2},{4,3},{5,4},{6,5},{7,6},{8,7},{9,8},{10,9},{11,1... | collective-permute-start | bytes 49160 | tf_op jit(solution)/shard_map/ppermute | solution.py:23
  95.8 28.4 %collective-permute-start.19 = (f32[1,32,128]{2,1,0:T(8,128)}, f32[1,32,128]{2,1,0:T(8,128)}, u32[]{:S(2)}, u32[]{:S(2)}) collective-permute-start(f32[1,32,128]{2,1,0:T(8,128)} %get-tuple-element.139), channel_id=1, source_target_pairs={{0,1},{1,2},{2,3},{3,4},{4,5},{5,6},{6,7},{7,8},{8,9},{9,10},{10,1... | collective-permute-start | bytes 49160 | tf_op jit(solution)/shard_map/ppermute | solution.py:20
  103.5 12.6 %all-to-all-start.4 = ((f32[8,16,2]{0,2,1:T(2,128)}), f32[8,16,2]{0,2,1:T(2,128)S(1)}, u32[]{:S(2)}, u32[]{:S(2)}) async-start(f32[8,16,2]{0,2,1:T(2,128)} %bitcast.62), calls=%async_computation.4 | async-start | bytes 32768 | tf_op jit(solution)/shard_map/all_to_all | solution.py:129
  119.3 12.6 %collective-permute-start.16 = (f32[3,1,32,32]{3,2,1,0:T(8,128)S(1)}, f32[3,1,32,32]{3,2,1,0:T(8,128)S(1)}, u32[]{:S(2)}, u32[]{:S(2)}) collective-permute-start(f32[3,1,32,32]{3,2,1,0:T(8,128)S(1)} %get-tuple-element.57), channel_id=1, source_target_pairs={{1,0},{2,1},{3,2},{4,3},{5,4},{6,5},{7,6},{8,7},{9,8},{10,9},{11,1... | collective-permute-start | bytes 36872 | tf_op jit(solution)/shard_map/ppermute | solution.py:23
  120.6 11.3 %collective-permute-start.17 = (f32[3,1,32,32]{3,2,1,0:T(8,128)S(1)}, f32[3,1,32,32]{3,2,1,0:T(8,128)S(1)}, u32[]{:S(2)}, u32[]{:S(2)}) collective-permute-start(f32[3,1,32,32]{3,2,1,0:T(8,128)S(1)} %get-tuple-element.58), channel_id=1, source_target_pairs={{0,1},{1,2},{2,3},{3,4},{4,5},{5,6},{6,7},{7,8},{8,9},{9,10},{10,1... | collective-permute-start | bytes 36872 | tf_op jit(solution)/shard_map/ppermute | solution.py:20
  135.4 17.4 %all-to-all-start.5 = ((f32[16,8,2]{1,2,0:T(2,128)}), f32[16,8,2]{1,2,0:T(2,128)S(1)}, u32[]{:S(2)}, u32[]{:S(2)}) async-start(f32[16,8,2]{1,2,0:T(2,128)} %copy.45), calls=%async_computation.5 | async-start | bytes 32768 | tf_op jit(solution)/shard_map/all_to_all | solution.py:134
  146.9 26.8 %collective-permute-start.26 = (f32[1,32,128]{2,1,0:T(8,128)}, f32[1,32,128]{2,1,0:T(8,128)}, u32[]{:S(2)}, u32[]{:S(2)}) collective-permute-start(f32[1,32,128]{2,1,0:T(8,128)} %get-tuple-element.130), channel_id=1, source_target_pairs={{1,0},{2,1},{3,2},{4,3},{5,4},{6,5},{7,6},{8,7},{9,8},{10,9},{11,1... | collective-permute-start | bytes 49160 | tf_op jit(solution)/shard_map/ppermute | solution.py:23
  148.2 25.5 %collective-permute-start.27 = (f32[1,32,128]{2,1,0:T(8,128)}, f32[1,32,128]{2,1,0:T(8,128)}, u32[]{:S(2)}, u32[]{:S(2)}) collective-permute-start(f32[1,32,128]{2,1,0:T(8,128)} %get-tuple-element.131), channel_id=1, source_target_pairs={{0,1},{1,2},{2,3},{3,4},{4,5},{5,6},{6,7},{7,8},{8,9},{9,10},{10,1... | collective-permute-start | bytes 49160 | tf_op jit(solution)/shard_map/ppermute | solution.py:20
  154.0 11.9 %all-to-all-start.6 = ((f32[8,16,2]{0,2,1:T(2,128)}), f32[8,16,2]{0,2,1:T(2,128)S(1)}, u32[]{:S(2)}, u32[]{:S(2)}) async-start(f32[8,16,2]{0,2,1:T(2,128)} %bitcast.80), calls=%async_computation.6 | async-start | bytes 32768 | tf_op jit(solution)/shard_map/all_to_all | solution.py:129
  159.5 7.1 %collective-permute-start.22 = (f32[3,1,32,32]{3,2,1,0:T(8,128)S(1)}, f32[3,1,32,32]{3,2,1,0:T(8,128)S(1)}, u32[]{:S(2)}, u32[]{:S(2)}) collective-permute-start(f32[3,1,32,32]{3,2,1,0:T(8,128)S(1)} %get-tuple-element.55), channel_id=1, source_target_pairs={{1,0},{2,1},{3,2},{4,3},{5,4},{6,5},{7,6},{8,7},{9,8},{10,9},{11,1... | collective-permute-start | bytes 36872 | tf_op jit(solution)/shard_map/ppermute | solution.py:23
  169.2 11.7 %collective-permute-start.24 = (f32[3,1,32,32]{3,2,1,0:T(8,128)S(1)}, f32[3,1,32,32]{3,2,1,0:T(8,128)S(1)}, u32[]{:S(2)}, u32[]{:S(2)}) collective-permute-start(f32[3,1,32,32]{3,2,1,0:T(8,128)S(1)} %get-tuple-element.52), channel_id=1, source_target_pairs={{1,0},{2,1},{3,2},{4,3},{5,4},{6,5},{7,6},{8,7},{9,8},{10,9},{11,1... | collective-permute-start | bytes 36872 | tf_op jit(solution)/shard_map/ppermute | solution.py:23
  170.6 10.3 %collective-permute-start.25 = (f32[3,1,32,32]{3,2,1,0:T(8,128)S(1)}, f32[3,1,32,32]{3,2,1,0:T(8,128)S(1)}, u32[]{:S(2)}, u32[]{:S(2)}) collective-permute-start(f32[3,1,32,32]{3,2,1,0:T(8,128)S(1)} %get-tuple-element.53), channel_id=1, source_target_pairs={{0,1},{1,2},{2,3},{3,4},{4,5},{5,6},{6,7},{7,8},{8,9},{9,10},{10,1... | collective-permute-start | bytes 36872 | tf_op jit(solution)/shard_map/ppermute | solution.py:20
  183.2 17.4 %all-to-all-start.7 = ((f32[16,8,2]{1,2,0:T(2,128)}), f32[16,8,2]{1,2,0:T(2,128)S(1)}, u32[]{:S(2)}, u32[]{:S(2)}) async-start(f32[16,8,2]{1,2,0:T(2,128)} %copy.49), calls=%async_computation.7 | async-start | bytes 32768 | tf_op jit(solution)/shard_map/all_to_all | solution.py:134
  (58 other events, 342.0 us)
where the time goes:
time: 213 us; the launch traced here: 209 us
  starting transfers between devices  145 us (68%)
  local copies, waits for them, and re-layouts  30.4 us (14%)
  other arithmetic  16.2 us (8%)
  waiting for transfers between devices  14.6 us (7%)
    ppermute x16, starting transfers between devices, with_halo(): lax.ppermute(lax.slice_in_dim(block, block.shape[dim] - width, None, axis...  57.2 us
    all_to_all x4, starting transfers between devices, on_device(): lax.all_to_all(strip_load.T, 'map', split_axis=0, concat_axis=1, tiled=True)  42.8 us
    all_to_all x4, starting transfers between devices, on_device(): lax.all_to_all(velocity[2][:, 0, :], 'map', split_axis=1, concat_axis=0,...  24.2 us
    ppermute x16, starting transfers between devices, with_halo(): lax.ppermute(lax.slice_in_dim(block, 0, width, axis=dim), axis, backward)  21 us
    all_to_all x4, waiting for transfers between devices, on_device(): lax.all_to_all(strip_load.T, 'map', split_axis=0, concat_axis=1, tiled=True)  8.86 us
    slice x23, local copies, waits for them, and re-layouts, depth_diff(): field[:, 1:, :]  8.61 us
    unnamed x84, local copies, waits for them, and re-layouts  7.88 us
    add x4, other arithmetic, crust_step(): vel_x = velocity[0] + DT * buoy * acc_x  4.44 us
  transfers between devices with their start and end apart: 40, of which 10 were waited for; matrix products, arithmetic and copies ran while one was open for 13% of the time, Pallas kernels for 0%

commit v1 on v0

v1 whole, which is shorter than its diff:
```python
import functools

import jax
import jax.numpy as jnp
from jax import lax
from jax.experimental import pallas as pl
from jax.experimental.pallas import tpu as pltpu
from jax.sharding import PartitionSpec as P

STEPS = 4
ZONES = 8
DT = 0.25
KBULK = 2.25
GRAV = 0.1
HALO = 2 * STEPS
LANES = 128
F32 = jnp.float32


class Plan:
    def __init__(self, devices, cells, depth, ny, strips):
        self.n = devices
        self.cells = cells
        self.depth = depth
        self.ny = ny
        self.strips = strips
        self.chunks = max(1, LANES // ny)
        self.sub = depth // self.chunks
        self.lanes = self.chunks * ny
        self.width = cells + 2 * HALO
        self.own_groups = cells // self.chunks
        self.halo_groups = HALO // self.chunks
        self.groups = self.width // self.chunks
        self.lead = self.chunks * strips
        self.rows = self.lead * (self.groups + 1)
        self.back_rows = self.lead * self.own_groups
        self.nx = devices * cells
        self.unrolled = self.sub * self.lanes <= 1024


BATHY_LANE = 64


def place(pieces, wanted, block):
    out = None
    for i, piece in enumerate(pieces):
        shift = (i - wanted[i]) * block % piece.shape[-1]
        moved = pltpu.roll(piece, shift, piece.ndim - 1) if shift else piece
        if out is None:
            out = moved
        else:
            lane = lax.broadcasted_iota(jnp.int32, moved.shape, moved.ndim - 1)
            out = jnp.where(lane >= i * block, moved, out)
    return out


def pack_kernel(
    plan, vel, stress, zones, slip, ocean, bathy, crust, message, turned, grouped, extra
):
    cells, sub, chunks, ny, n = plan.cells, plan.sub, plan.chunks, plan.ny, plan.n
    strips = plan.strips
    block = 4 * sub
    grouped[...] = jnp.zeros_like(grouped)
    for yl in range(strips):
        stacked = jnp.concatenate(
            [ocean[f, yl, kc * sub : (kc + 1) * sub, :] for kc in range(chunks) for f in range(4)],
            axis=0,
        )
        turned[yl] = stacked.T
        by_x = [turned[yl, pl.ds(i, plan.nx // chunks, stride=chunks), :] for i in range(chunks)]
        for kc in range(chunks):
            grouped[kc * strips + yl, pl.ds(plan.halo_groups, plan.nx // chunks), :] = place(
                by_x, [kc] * chunks, block
            )
    count = n - 2
    lane = lax.broadcasted_iota(jnp.int32, (n, LANES), 1)
    row = lax.broadcasted_iota(jnp.int32, (n, LANES), 0)
    for yl in range(strips):
        depths = bathy[yl : yl + 1, :].astype(F32)
        wide = lax.broadcasted_iota(jnp.int32, depths.shape, 1)
        for d in range(n):
            first = d * cells - HALO - 1
            moved = pltpu.roll(depths, (BATHY_LANE - first) % plan.nx, 1)
            at = wide - BATHY_LANE + first
            moved = jnp.where((at >= 0) & (at < plan.nx), moved, 0.0)
            extra[yl, d : d + 1, :] = moved[:, :LANES]
        left = jnp.zeros((n, LANES), F32)
        edges_low = turned[yl, pl.ds(2 * cells - HALO - 1, count, stride=cells), :]
        edges_high = turned[yl, pl.ds(cells + HALO, count, stride=cells), :]
        low = jnp.concatenate([jnp.zeros((2, LANES), F32), edges_low], axis=0)
        high = jnp.concatenate([edges_high, jnp.zeros((2, LANES), F32)], axis=0)
        for kc in range(chunks):
            low_moved = pltpu.roll(low, (-kc * block) % LANES, 1) if kc else low
            high_moved = pltpu.roll(high, (sub - kc * block) % LANES, 1)
            rest = jnp.where(lane < sub, low_moved, extra[yl])
            rest = jnp.where((lane >= sub) & (lane < 2 * sub), high_moved, rest)
            at = (kc * strips + yl) * (plan.groups + 1) + plan.groups
            message[pl.ds(at, n, stride=plan.rows), :] = rest
    for d in range(n):
        for q in range(plan.lead):
            start = d * plan.rows + q * (plan.groups + 1)
            message[start : start + plan.groups, :] = grouped[
                q, d * plan.own_groups : d * plan.own_groups + plan.groups, :
            ]
    def packed(ref, f, x):
        parts = [ref[f, x, kc * sub : (kc + 1) * sub, :] for kc in range(chunks)]
        return jnp.concatenate(parts, axis=-1) if chunks > 1 else parts[0]

    for f in range(3):
        for x in range(cells):
            crust[f * cells + x] = packed(vel, f, x)
    for f in range(6):
        for x in range(cells):
            crust[(3 + f) * cells + x] = packed(stress, f, x)
    for x in range(cells):
        parts = [zones[x, kc * sub : (kc + 1) * sub, :] for kc in range(chunks)]
        plane = jnp.concatenate(parts, axis=-1) if chunks > 1 else parts[0]
        crust[9 * cells + x] = (plane + 1).astype(F32)
    fault_chunk = (plan.depth // 2) // sub
    pieces = [
        slip[...] if kc == fault_chunk else jnp.zeros((cells, ny), F32) for kc in range(chunks)
    ]
    fault = jnp.concatenate(pieces, axis=-1) if chunks > 1 else pieces[0]
    if sub > cells:
        fault = jnp.concatenate([fault, jnp.zeros((sub - cells, plan.lanes), F32)], axis=0)
    crust[10 * cells] = fault


class Shifts:
    def __init__(self, plan):
        self.plan = plan
        shape = (plan.sub, plan.lanes)
        self.row = lax.broadcasted_iota(jnp.int32, shape, 0)
        self.lane = lax.broadcasted_iota(jnp.int32, shape, 1)
        self.y = lax.rem(self.lane, plan.ny)
        self.first_row = self.row == 0
        self.last_row = self.row == plan.sub - 1
        self.top = self.first_row & (self.lane < plan.ny)
        self.floor_cell = self.last_row & (self.lane >= plan.lanes - plan.ny)
        self.not_low_y = jnp.where(self.y == 0, 0.0, 1.0).astype(F32)
        self.not_high_y = jnp.where(self.y == plan.ny - 1, 0.0, 1.0).astype(F32)
        self.depth = (
            lax.div(self.lane, plan.ny) * plan.sub + self.row
        ).astype(F32)

    def dy(self, f):
        lanes = self.plan.lanes
        return pltpu.roll(f, lanes - 1, 1) * self.not_high_y - pltpu.roll(f, 1, 1) * self.not_low_y

    def below(self, f):
        plan = self.plan
        moved = pltpu.roll(f, plan.sub - 1, 0)
        if plan.chunks > 1:
            moved = jnp.where(self.last_row, pltpu.roll(moved, plan.lanes - plan.ny, 1), moved)
        return jnp.where(self.floor_cell, 0.0, moved)

    def above(self, f, top):
        plan = self.plan
        moved = pltpu.roll(f, 1, 0)
        if plan.chunks > 1:
            moved = jnp.where(self.first_row, pltpu.roll(moved, plan.ny, 1), moved)
        return jnp.where(self.top, top, moved)

    def over_chunks(self, f):
        shift = self.plan.ny
        while shift < self.plan.lanes:
            f = f + pltpu.roll(f, shift, 1)
            shift *= 2
        return f


def steps_kernel(
    plan, mats, own, low, high, arrived, vel_out, stress_out, message,
    crust, oc, water, bottom, buoy, lamb, shear, gather, depths,
):
    cells, sub, chunks, n, strips = plan.cells, plan.sub, plan.chunks, plan.n, plan.strips
    width = plan.width
    sh = Shifts(plan)
    half = 0.5 * DT

    def planes(start, stop, body):
        if plan.unrolled:
            for j in range(start, stop):
                body(j)
        else:
            def run(j, carry):
                body(j)
                return carry

            lax.fori_loop(start, stop, run, 0)

    def turn(group):
        for kc in range(chunks):
            for yl in range(strips):
                at = (kc * strips + yl) * (plan.groups + 1) + group
                gather[pl.ds(kc * plan.ny + yl, n, stride=strips), :] = arrived[
                    pl.ds(at, n, stride=plan.rows), :
                ]
        return gather[...].T

    rest = turn(plan.groups)
    oc[0, 0] = rest[:sub]
    oc[0, width + 1] = rest[sub : 2 * sub]
    depths[...] = rest[BATHY_LANE : BATHY_LANE + depths.shape[0]]
    for group in range(plan.groups):
        turned = turn(group)
        for i in range(chunks):
            for f in range(4):
                at = (i * 4 + f) * sub
                oc[f, 1 + group * chunks + i] = turned[at : at + sub]

    def mask(j):
        deep = jnp.broadcast_to(depths[pl.ds(j, 1), :], (sub, plan.lanes))
        wet = jnp.where(sh.depth < deep, 1.0, 0.0).astype(F32)
        water[j] = wet
        bottom[j] = jnp.where(sh.depth == deep - 1.0, 1.0, 0.0).astype(F32)
        oc[0, j] = oc[0, j] * wet

    def mask_flow(j):
        for f in range(1, 4):
            oc[f, j] = oc[f, j] * water[j]

    planes(0, width + 2, mask)
    planes(1, width + 1, mask_flow)

    for part, ref in enumerate((low, own, high)):
        def bring(x, part=part, ref=ref):
            j = part * cells + x
            for f in range(9):
                crust[f, j] = ref[f * cells + x]
            zone = ref[9 * cells + x]
            values = [jnp.zeros_like(zone) for _ in range(3)]
            for z in range(ZONES):
                here = zone == float(z + 1)
                values = [jnp.where(here, mats[c, z], values[c]) for c in range(3)]
            buoy[j] = values[0] * half
            lamb[j] = values[1] * half
            shear[j] = values[2] * half
            slip = jnp.broadcast_to(ref[10 * cells, pl.ds(x, 1), :], (sub, plan.lanes))
            crust[9, j] = jnp.where(sh.row == (plan.depth // 2) % sub, DT * slip, 0.0)

        planes(0, cells, bring)

    VX, VY, VZ, SXX, SYY, SZZ, SXY, SXZ, SYZ, FAULT = range(10)

    for t in range(STEPS):
        def flow(j):
            p = oc[0, j + 1]
            wet = water[j + 1]
            oc[1, j + 1] = wet * (oc[1, j + 1] - half * (oc[0, j + 2] - oc[0, j]))
            oc[2, j + 1] = wet * (oc[2, j + 1] - half * sh.dy(p))
            rise = sh.below(p) + bottom[j + 1] * p - sh.above(p, -p)
            oc[3, j + 1] = wet * (oc[3, j + 1] - (half * rise + (DT * GRAV) * p))

        def press(j):
            w = oc[3, j + 1]
            floor = jnp.where(sh.top, crust[VZ, j], 0.0)[0:1]
            floor = jnp.broadcast_to(sh.over_chunks(floor), (sub, plan.lanes))
            rise = sh.below(w) + bottom[j + 1] * floor - sh.above(w, w)
            spread = oc[1, j + 2] - oc[1, j] + sh.dy(oc[2, j + 1]) + rise
            oc[0, j + 1] = water[j + 1] * (oc[0, j + 1] - (half * KBULK) * spread)

        def move(j):
            load = jnp.sum(bottom[j + 1] * oc[0, j + 1], axis=0, keepdims=True)
            load = jnp.broadcast_to(sh.over_chunks(load), (sub, plan.lanes))
            b = buoy[j]
            syz, szz = crust[SYZ, j], crust[SZZ, j]
            sxy, sxz = crust[SXY, j], crust[SXZ, j]
            ax = crust[SXX, j + 1] - crust[SXX, j - 1] + sh.dy(sxy) + sh.below(sxz) - sh.above(sxz, 0.0)
            ay = crust[SXY, j + 1] - crust[SXY, j - 1] + sh.dy(crust[SYY, j]) + sh.below(syz) - sh.above(syz, 0.0)
            az = crust[SXZ, j + 1] - crust[SXZ, j - 1] + sh.dy(syz) + sh.below(szz) - sh.above(szz, -load)
            crust[VX, j] = crust[VX, j] + b * ax
            crust[VY, j] = crust[VY, j] + b * ay
            crust[VZ, j] = crust[VZ, j] + b * az

        def strain(j):
            vx, vy, vz = crust[VX, j], crust[VY, j], crust[VZ, j]
            exx = crust[VX, j + 1] - crust[VX, j - 1]
            eyy = sh.dy(vy)
            ezz = sh.below(vz) - sh.above(vz, vz)
            mu = shear[j]
            mu2 = mu + mu
            common = lamb[j] * (exx + eyy + ezz)
            crust[SXX, j] = crust[SXX, j] + (common + mu2 * exx)
            crust[SYY, j] = crust[SYY, j] + (common + mu2 * eyy)
            crust[SZZ, j] = crust[SZZ, j] + (common + mu2 * ezz)
            exy = sh.dy(vx) + crust[VY, j + 1] - crust[VY, j - 1]
            exz = sh.below(vx) - sh.above(vx, vx) + crust[VZ, j + 1] - crust[VZ, j - 1]
            eyz = sh.below(vy) - sh.above(vy, vy) + sh.dy(vz)
            crust[SXY, j] = crust[SXY, j] + mu * exy
            crust[SXZ, j] = crust[SXZ, j] + (mu * exz + crust[FAULT, j])
            crust[SYZ, j] = crust[SYZ, j] + mu * eyz

        planes(2 * t, width - 2 * t, flow)
        planes(2 * t + 1, width - 2 * t - 1, press)
        planes(2 * t + 1, width - 2 * t - 1, move)
        planes(2 * t + 2, width - 2 * t - 2, strain)

    def put(x):
        j = HALO + x
        for f in range(9):
            plane = crust[f, j]
            out, at = (vel_out, f) if f < 3 else (stress_out, f - 3)
            for kc in range(chunks):
                out[at, x, kc * sub : (kc + 1) * sub, :] = plane[:, kc * plan.ny : (kc + 1) * plan.ny]

    planes(0, cells, put)
    for group in range(plan.own_groups):
        stacked = jnp.concatenate(
            [
                oc[f, 1 + HALO + group * chunks + i]
                for i in range(chunks)
                for f in range(4)
            ],
            axis=0,
        )
        gather[...] = stacked.T
        for kc in range(chunks):
            for yl in range(strips):
                at = group * plan.lead + kc * strips + yl
                message[pl.ds(at, n, stride=plan.back_rows), :] = gather[
                    pl.ds(kc * plan.ny + yl, n, stride=strips), :
                ]


def unpack_kernel(plan, arrived, ocean, turned):
    sub, chunks = plan.sub, plan.chunks
    block = 4 * sub
    for yl in range(plan.strips):
        by_chunk = [
            arrived[pl.ds(kc * plan.strips + yl, plan.nx // chunks, stride=plan.lead), :]
            for kc in range(chunks)
        ]
        for i in range(chunks):
            turned[pl.ds(i, plan.nx // chunks, stride=chunks), :] = place(
                by_chunk, [i] * chunks, block
            )
        whole = turned[...].T
        for kc in range(chunks):
            for f in range(4):
                at = (kc * 4 + f) * sub
                ocean[f, yl, kc * sub : (kc + 1) * sub, :] = whole[at : at + sub]


def on_device(plan, velocity, stress, ocean, zones, materials, slip, bathy):
    n, cells, sub, lanes = plan.n, plan.cells, plan.sub, plan.lanes
    width = plan.width
    vmem = pl.BlockSpec(memory_space=pltpu.VMEM)
    smem = pl.BlockSpec(memory_space=pltpu.SMEM)
    params = pltpu.CompilerParams(vmem_limit_bytes=56 * 1024 * 1024)
    count = 10 * cells + 1
    crust, message = pl.pallas_call(
        functools.partial(pack_kernel, plan),
        out_shape=(
            jax.ShapeDtypeStruct((count, sub, lanes), F32),
            jax.ShapeDtypeStruct((n * plan.rows, LANES), F32),
        ),
        in_specs=[vmem] * 6,
        out_specs=(vmem, vmem),
        scratch_shapes=[
            pltpu.VMEM((plan.strips, plan.nx, LANES), F32),
            pltpu.VMEM(
                (plan.lead, plan.nx // plan.chunks + 2 * plan.halo_groups, LANES), F32
            ),
            pltpu.VMEM((plan.strips, n, LANES), F32),
        ],
        compiler_params=params,
        name="pack",
    )(velocity, stress, zones, slip, ocean, bathy)
    arrived = lax.all_to_all(
        message.reshape(n, plan.rows, LANES), "map", split_axis=0, concat_axis=0, tiled=True
    ).reshape(n * plan.rows, LANES)
    low = lax.ppermute(crust, "map", [(i, i + 1) for i in range(n - 1)])
    high = lax.ppermute(crust, "map", [(i + 1, i) for i in range(n - 1)])
    out = pl.pallas_call(
        functools.partial(steps_kernel, plan),
        out_shape=(
            jax.ShapeDtypeStruct(velocity.shape, F32),
            jax.ShapeDtypeStruct(stress.shape, F32),
            jax.ShapeDtypeStruct((n * plan.back_rows, LANES), F32),
        ),
        in_specs=[smem] + [vmem] * 4,
        out_specs=(vmem, vmem, vmem),
        scratch_shapes=[
            pltpu.VMEM((10, width, sub, lanes), F32),
            pltpu.VMEM((4, width + 2, sub, lanes), F32),
            pltpu.VMEM((width + 2, sub, lanes), F32),
            pltpu.VMEM((width + 2, sub, lanes), F32),
            pltpu.VMEM((width, sub, lanes), F32),
            pltpu.VMEM((width, sub, lanes), F32),
            pltpu.VMEM((width, sub, lanes), F32),
            pltpu.VMEM((lanes, LANES), F32),
            pltpu.VMEM((32, lanes), F32),
        ],
        compiler_params=params,
        name="substeps",
    )(materials, crust, low, high, arrived)
    new_velocity, new_stress, back = out
    returned = lax.all_to_all(
        back.reshape(n, plan.back_rows, LANES), "map", split_axis=0, concat_axis=0, tiled=True
    ).reshape(n * plan.back_rows, LANES)
    new_ocean = pl.pallas_call(
        functools.partial(unpack_kernel, plan),
        out_shape=jax.ShapeDtypeStruct(ocean.shape, F32),
        in_specs=[vmem],
        out_specs=vmem,
        scratch_shapes=[pltpu.VMEM((plan.nx, LANES), F32)],
        compiler_params=params,
        name="unpack",
    )(returned)
    return new_velocity, new_stress, new_ocean


def solution(mesh):
    n = mesh.shape["map"]

    def body(velocity, stress, ocean, zones, materials, slip, bathy):
        _, cells, depth, ny = velocity.shape
        plan = Plan(n, cells, depth, ny, ocean.shape[1])
        return on_device(plan, velocity, stress, ocean, zones, materials, slip, bathy)

    return jax.shard_map(
        body,
        mesh=mesh,
        in_specs=(
            P("parts", "map", None, None),
            P("parts", "map", None, None),
            P("parts", "map", None, None),
            P("map", "parts", None),
            P(),
            P("map", "parts"),
            P("map", "parts"),
        ),
        out_specs=(
            P("parts", "map", None, None),
            P("parts", "map", None, None),
            P("parts", "map", None, None),
        ),
        check_vma=False,
    )
```

time: 213 us -> 49 us (0.23); the launches traced: 209 us -> 48.6 us
  starting transfers between devices: 145 us -> 11.8 us
  local copies, waits for them, and re-layouts: 30.4 us -> 0.77 us
  other arithmetic: 16.2 us -> 0 us
  blocking collectives: 0 us -> 16.1 us
  Pallas kernels: 0 us -> 10.3 us
  waiting for transfers between devices: 14.6 us -> 8.86 us
    ppermute x32 -> x2, starting transfers between devices: 78.2 us -> 4.34 us  [the longest x1 3.05 us: on_device(): low = lax.ppermute(crust, 'map', [(i, i + 1) for i in range(n - 1)])]
    all_to_all x8 -> x1, starting transfers between devices: 66.9 us -> 7.49 us  [on_device(): lax.all_to_all(message.reshape(n, plan.rows, LANES), 'map', split_axis=0,...]
    all_to_all x0 -> x1, blocking collectives: none -> 16.1 us  [on_device(): lax.all_to_all(back.reshape(n, plan.back_rows, LANES), 'map', split_axis=...]
    slice x63 -> x0, local copies, waits for them, and re-layouts: 15.2 us -> none  [the longest x23 8.61 us: depth_diff(): field[:, 1:, :]]
    pallas_call x0 -> x3, Pallas kernels: none -> 10.3 us  [the longest x1 5.77 us: on_device(): pl.pallas_call(functools.partial(steps_kernel, plan), out_shape=(jax.Shap...]
    unnamed x84 -> x8, local copies, waits for them, and re-layouts: 7.88 us -> 0.77 us
    add x15 -> x0, other arithmetic: 6.19 us -> none  [the longest x4 4.44 us: crust_step(): vel_x = velocity[0] + DT * buoy * acc_x]
    mul x13 -> x0, other arithmetic: 5.33 us -> none  [the longest x4 2.56 us: ocean_step(): flow_x = water * (flow_x - DT * xdiff(press))]
  transfers between devices with their start and end apart: 40 -> 3, of which waited for: 10 -> 2; matrix products, arithmetic and copies ran while one was open for 13% -> 0% of each run, Pallas kernels for 0% -> 0%
where the time goes in v1:
time: 49 us; the launch traced here: 48.6 us
  blocking collectives  16.1 us (33%)
  starting transfers between devices  11.8 us (24%)
  Pallas kernels  10.3 us (21%)
  waiting for transfers between devices  8.86 us (18%)
  local copies, waits for them, and re-layouts  0.77 us (2%)
  between operations  0.69 us (1%)
    all_to_all x1, blocking collectives, on_device(): lax.all_to_all(back.reshape(n, plan.back_rows, LANES), 'map', split_axis=...  16.1 us
    all_to_all x1, waiting for transfers between devices, on_device(): lax.all_to_all(message.reshape(n, plan.rows, LANES), 'map', split_axis=0,...  7.66 us
    all_to_all x1, starting transfers between devices, on_device(): lax.all_to_all(message.reshape(n, plan.rows, LANES), 'map', split_axis=0,...  7.49 us
    pallas_call x1, Pallas kernels, on_device(): pl.pallas_call(functools.partial(steps_kernel, plan), out_shape=(jax.Shap...  5.77 us
    ppermute x1, starting transfers between devices, on_device(): low = lax.ppermute(crust, 'map', [(i, i + 1) for i in range(n - 1)])  3.05 us
    pallas_call x1, Pallas kernels, on_device(): pl.pallas_call(functools.partial(pack_kernel, plan), out_shape=(jax.Shape...  2.72 us
    pallas_call x1, Pallas kernels, on_device(): pl.pallas_call(functools.partial(unpack_kernel, plan), out_shape=jax.Shap...  1.85 us
    ppermute x1, starting transfers between devices, on_device(): high = lax.ppermute(crust, 'map', [(i + 1, i) for i in range(n - 1)])  1.29 us
  transfers between devices with their start and end apart: 3, of which 2 were waited for; matrix products, arithmetic and copies ran while one was open for 0% of the time, Pallas kernels for 0%

profile of v1, /device:TPU:0, one launch (start us, length us, event | category | flops | bytes accessed | tf_op | source)
XLA Modules:
  0.0 48.6 jit_solution(6590229915319629221)
XLA Ops:
  0.6 2.7 %pack.1 = (f32[81,8,128]{2,1,0:T(8,128)}, f32[896,128]{1,0:T(8,128)}) custom-call(f32[3,8,32,32]{3,2,1,0:T(8,128)} %vel.1, f32[6,8,32,32]{3,2,1,0:T(8,128)} %stress.1, s32[8,32,32]{2,1,0:T(8,128)} %zones.1, f32[8,32]{1,0:T(8,128)} %slip.1, f32[4,2,32,128]{3,2,1,0:T(8,128)} %ocean.1, s32[2,128]{1,0:T(2,128)} %bathy.1), custom_call_target="tpu_custom_call" | custom-call | tf_op jit(solution)/shard_map/pack/pallas_call | solution.py:352
  3.4 0.0 copy-start.1
  3.4 7.5 %all-to-all-start = ((f32[16,56,128]{2,1,0:T(8,128)}), f32[16,56,128]{2,1,0:T(8,128)S(1)}, u32[]{:S(2)}, u32[]{:S(2)}) async-start(f32[16,56,128]{2,1,0:T(8,128)} %bitcast.6), calls=%async_computation | async-start | bytes 917504 | tf_op jit(solution)/shard_map/all_to_all | solution.py:370
  10.9 0.0 copy-done.1
  10.9 1.3 %collective-permute-start.1 = (f32[81,8,128]{2,1,0:T(8,128)S(1)}, f32[81,8,128]{2,1,0:T(8,128)S(1)}, u32[]{:S(2)}, u32[]{:S(2)}) collective-permute-start(f32[81,8,128]{2,1,0:T(8,128)S(1)} %copy-done.1), channel_id=1, source_target_pairs={{1,0},{2,1},{3,2},{4,3},{5,4},{6,5},{7,6},{8,7},{9,8},{10,9},{11,1... | collective-permute-start | bytes 995336 | tf_op jit(solution)/shard_map/ppermute | solution.py:374
  12.2 3.1 %collective-permute-start = (f32[81,8,128]{2,1,0:T(8,128)S(1)}, f32[81,8,128]{2,1,0:T(8,128)S(1)}, u32[]{:S(2)}, u32[]{:S(2)}) collective-permute-start(f32[81,8,128]{2,1,0:T(8,128)S(1)} %copy-done.1), channel_id=1, source_target_pairs={{0,1},{1,2},{2,3},{3,4},{4,5},{5,6},{6,7},{7,8},{8,9},{9,10},{10,1... | collective-permute-start | bytes 995336 | tf_op jit(solution)/shard_map/ppermute | solution.py:373
  15.2 0.0 collective-permute-done.1.high
  15.2 0.0 copy-start.2
  15.2 1.2 %collective-permute-done.low = f32[81,8,128]{2,1,0:T(8,128)S(1)} collective-permute-done((f32[81,8,128]{2,1,0:T(8,128)S(1)}, f32[81,8,128]{2,1,0:T(8,128)S(1)}, u32[]{:S(2)}, u32[]{:S(2)}) %collective-permute-start) | collective-permute-done | bytes 331808 | tf_op jit(solution)/shard_map/ppermute | solution.py:373
  16.4 0.0 copy-start.3
  16.4 7.7 %all-to-all-done = f32[16,56,128]{2,1,0:T(8,128)S(1)} async-done(((f32[16,56,128]{2,1,0:T(8,128)}), f32[16,56,128]{2,1,0:T(8,128)S(1)}, u32[]{:S(2)}, u32[]{:S(2)}) %all-to-all-start) | async-done | bytes 458784 | tf_op jit(solution)/shard_map/all_to_all | solution.py:370
  24.1 0.0 copy-start
  24.1 0.0 copy-done.2
  24.1 0.0 copy-done.3
  24.1 0.8 %copy-done = f32[16,56,128]{2,1,0:T(8,128)} copy-done((f32[16,56,128]{2,1,0:T(8,128)}, f32[16,56,128]{2,1,0:T(8,128)S(1)}, u32[]{:S(2)}) %copy-start) | copy-done | bytes 458776
  24.9 5.8 %substeps.1 = (f32[3,8,32,32]{3,2,1,0:T(8,128)}, f32[6,8,32,32]{3,2,1,0:T(8,128)}, f32[256,128]{1,0:T(8,128)}) custom-call(f32[3,8]{1,0:T(4,128)} %mats.1, f32[81,8,128]{2,1,0:T(8,128)} %get-tuple-element.8.own, f32[81,8,128]{2,1,0:T(8,128)} %copy-done.3, f32[81,8,128]{2,1,0:T(8,128)} %copy-done.2, f32[896,128]{1,0:T(8,128)} %bitcast.4), custom_call_target="tpu_custom_call" | custom-call | tf_op jit(solution)/shard_map/substeps/pallas_call | solution.py:375
  30.6 16.1 %all_to_all.10 = f32[16,16,128]{2,1,0:T(8,128)} all-to-all(f32[16,16,128]{2,1,0:T(8,128)} %bitcast.7), channel_id=1, replica_groups=mesh['parts'=2,'map'=16] {'map'}, dimensions={0} | all-to-all | bytes 262144 | tf_op jit(solution)/shard_map/all_to_all | solution.py:399
  46.7 1.8 %unpack.1 = f32[4,2,32,128]{3,2,1,0:T(8,128)} custom-call(f32[256,128]{1,0:T(8,128)} %bitcast.5), custom_call_target="tpu_custom_call" | custom-call | tf_op jit(solution)/shard_map/unpack/pallas_call | solution.py:402
Async XLA Ops:
  3.4 7.5 %copy-start.1 = (f32[81,8,128]{2,1,0:T(8,128)S(1)}, f32[81,8,128]{2,1,0:T(8,128)}, u32[]{:S(2)}) copy-start(f32[81,8,128]{2,1,0:T(8,128)} %get-tuple-element.8.own) | copy-start | bytes 995332
  3.4 20.7 %all-to-all-start = ((f32[16,56,128]{2,1,0:T(8,128)}), f32[16,56,128]{2,1,0:T(8,128)S(1)}, u32[]{:S(2)}, u32[]{:S(2)}) async-start(f32[16,56,128]{2,1,0:T(8,128)} %bitcast.6), calls=%async_computation | async-start | bytes 917504 | tf_op jit(solution)/shard_map/all_to_all | solution.py:370
  10.9 4.4 %collective-permute-start.1 = (f32[81,8,128]{2,1,0:T(8,128)S(1)}, f32[81,8,128]{2,1,0:T(8,128)S(1)}, u32[]{:S(2)}, u32[]{:S(2)}) collective-permute-start(f32[81,8,128]{2,1,0:T(8,128)S(1)} %copy-done.1), channel_id=1, source_target_pairs={{1,0},{2,1},{3,2},{4,3},{5,4},{6,5},{7,6},{8,7},{9,8},{10,9},{11,1... | collective-permute-start | bytes 995336 | tf_op jit(solution)/shard_map/ppermute | solution.py:374
  12.2 4.3 %collective-permute-start = (f32[81,8,128]{2,1,0:T(8,128)S(1)}, f32[81,8,128]{2,1,0:T(8,128)S(1)}, u32[]{:S(2)}, u32[]{:S(2)}) collective-permute-start(f32[81,8,128]{2,1,0:T(8,128)S(1)} %copy-done.1), channel_id=1, source_target_pairs={{0,1},{1,2},{2,3},{3,4},{4,5},{5,6},{6,7},{7,8},{8,9},{9,10},{10,1... | collective-permute-start | bytes 995336 | tf_op jit(solution)/shard_map/ppermute | solution.py:373
  15.2 8.9 %copy-start.2 = (f32[81,8,128]{2,1,0:T(8,128)}, f32[81,8,128]{2,1,0:T(8,128)S(1)}, u32[]{:S(2)}) copy-start(f32[81,8,128]{2,1,0:T(8,128)S(1)} %collective-permute-done.1.high) | copy-start | bytes 995332
  16.4 7.7 %copy-start.3 = (f32[81,8,128]{2,1,0:T(8,128)}, f32[81,8,128]{2,1,0:T(8,128)S(1)}, u32[]{:S(2)}) copy-start(f32[81,8,128]{2,1,0:T(8,128)S(1)} %collective-permute-done.low) | copy-start | bytes 995332
  24.1 0.8 %copy-start = (f32[16,56,128]{2,1,0:T(8,128)}, f32[16,56,128]{2,1,0:T(8,128)S(1)}, u32[]{:S(2)}) copy-start(f32[16,56,128]{2,1,0:T(8,128)S(1)} %all-to-all-done) | copy-start | bytes 1376260

commit v2 on v1

--- a/solution.py
+++ b/solution.py
@@ -84,7 +84,6 @@
             at = wide - BATHY_LANE + first
             moved = jnp.where((at >= 0) & (at < plan.nx), moved, 0.0)
             extra[yl, d : d + 1, :] = moved[:, :LANES]
-        left = jnp.zeros((n, LANES), F32)
         edges_low = turned[yl, pl.ds(2 * cells - HALO - 1, count, stride=cells), :]
         edges_high = turned[yl, pl.ds(cells + HALO, count, stride=cells), :]
         low = jnp.concatenate([jnp.zeros((2, LANES), F32), edges_low], axis=0)
@@ -347,7 +346,7 @@
     width = plan.width
     vmem = pl.BlockSpec(memory_space=pltpu.VMEM)
     smem = pl.BlockSpec(memory_space=pltpu.SMEM)
-    params = pltpu.CompilerParams(vmem_limit_bytes=56 * 1024 * 1024)
+    params = pltpu.CompilerParams(vmem_limit_bytes=(16 if plan.unrolled else 56) * 1024 * 1024)
     count = 10 * cells + 1
     crust, message = pl.pallas_call(
         functools.partial(pack_kernel, plan),

time: 49 us -> 49.8 us (1.016)
  local copies, waits for them, and re-layouts: 0.77 us -> 5.3 us
  Pallas kernels: 10.3 us -> 7.14 us
  blocking collectives: 16.1 us -> 15.6 us
    unnamed x8 -> x14, local copies, waits for them, and re-layouts: 0.77 us -> 5.3 us
    pallas_call x1, Pallas kernels: 2.72 us -> 1.19 us  [on_device(): pl.pallas_call(functools.partial(pack_kernel, plan), out_shape=(jax.Shape...]
    pallas_call x1, Pallas kernels: 1.85 us -> 0.94 us  [on_device(): pl.pallas_call(functools.partial(unpack_kernel, plan), out_shape=jax.Shap...]
    pallas_call x1, Pallas kernels: 5.77 us -> 5.01 us  [on_device(): pl.pallas_call(functools.partial(steps_kernel, plan), out_shape=(jax.Shap...]
where the time goes in v2:
time: 49.8 us; the launch traced here: 49.3 us
  blocking collectives  15.6 us (31%)
  starting transfers between devices  11.7 us (23%)
  waiting for transfers between devices  8.87 us (18%)
  Pallas kernels  7.14 us (14%)
  local copies, waits for them, and re-layouts  5.3 us (11%)
  between operations  0.69 us (1%)
    all_to_all x1, blocking collectives, on_device(): lax.all_to_all(back.reshape(n, plan.back_rows, LANES), 'map', split_axis=...  15.6 us
    all_to_all x1, waiting for transfers between devices, on_device(): lax.all_to_all(message.reshape(n, plan.rows, LANES), 'map', split_axis=0,...  7.66 us
    all_to_all x1, starting transfers between devices, on_device(): lax.all_to_all(message.reshape(n, plan.rows, LANES), 'map', split_axis=0,...  7.36 us
    unnamed x14, local copies, waits for them, and re-layouts  5.3 us
    pallas_call x1, Pallas kernels, on_device(): pl.pallas_call(functools.partial(steps_kernel, plan), out_shape=(jax.Shap...  5.01 us
    ppermute x1, starting transfers between devices, on_device(): low = lax.ppermute(crust, 'map', [(i, i + 1) for i in range(n - 1)])  3.05 us
    ppermute x1, starting transfers between devices, on_device(): high = lax.ppermute(crust, 'map', [(i + 1, i) for i in range(n - 1)])  1.29 us
    ppermute x1, waiting for transfers between devices, on_device(): low = lax.ppermute(crust, 'map', [(i, i + 1) for i in range(n - 1)])  1.21 us
  transfers between devices with their start and end apart: 3, of which 2 were waited for; matrix products, arithmetic and copies ran while one was open for 0% of the time, Pallas kernels for 0%

profile of v2, /device:TPU:0, one launch (start us, length us, event | category | flops | bytes accessed | tf_op | source)
XLA Modules:
  0.0 49.3 jit_solution(14582497168077224635)
XLA Ops:
  0.6 0.0 copy-start
  0.6 1.1 %copy-done = f32[6,8,32,32]{3,2,1,0:T(8,128)S(1)} copy-done((f32[6,8,32,32]{3,2,1,0:T(8,128)S(1)}, f32[6,8,32,32]{3,2,1,0:T(8,128)}, u32[]{:S(2)}) %copy-start) | copy-done | bytes 196632
  1.8 0.0 copy-start.1
  1.8 1.0 %copy-done.1 = f32[3,8,32,32]{3,2,1,0:T(8,128)S(1)} copy-done((f32[3,8,32,32]{3,2,1,0:T(8,128)S(1)}, f32[3,8,32,32]{3,2,1,0:T(8,128)}, u32[]{:S(2)}) %copy-start.1) | copy-done | bytes 98328
  2.8 0.0 copy-start.2
  2.8 0.9 %copy-done.2 = s32[8,32,32]{2,1,0:T(8,128)S(1)} copy-done((s32[8,32,32]{2,1,0:T(8,128)S(1)}, s32[8,32,32]{2,1,0:T(8,128)}, u32[]{:S(2)}) %copy-start.2) | copy-done | bytes 32792
  3.7 0.0 copy-start.3
  3.7 0.9 %copy-done.3 = f32[4,2,32,128]{3,2,1,0:T(8,128)S(1)} copy-done((f32[4,2,32,128]{3,2,1,0:T(8,128)S(1)}, f32[4,2,32,128]{3,2,1,0:T(8,128)}, u32[]{:S(2)}) %copy-start.3) | copy-done | bytes 131096
  4.6 0.0 copy-start.4
  4.6 0.7 %copy-done.4 = f32[8,32]{1,0:T(8,128)S(1)} copy-done((f32[8,32]{1,0:T(8,128)S(1)}, f32[8,32]{1,0:T(8,128)}, u32[]{:S(2)}) %copy-start.4) | copy-done | bytes 1048
  5.3 0.0 copy-start.6
  5.3 0.7 %copy-done.6 = s32[2,128]{1,0:T(2,128)S(1)} copy-done((s32[2,128]{1,0:T(2,128)S(1)}, s32[2,128]{1,0:T(2,128)}, u32[]{:S(2)}) %copy-start.6) | copy-done | bytes 1048
  5.9 1.2 %pack.1 = (f32[81,8,128]{2,1,0:T(8,128)S(1)}, f32[896,128]{1,0:T(8,128)}) custom-call(f32[3,8,32,32]{3,2,1,0:T(8,128)S(1)} %copy-done.1, f32[6,8,32,32]{3,2,1,0:T(8,128)S(1)} %copy-done, s32[8,32,32]{2,1,0:T(8,128)S(1)} %copy-done.2, f32[8,32]{1,0:T(8,128)S(1)} %copy-done.4, f32[4,2,32,128]{3,2,1,0:T(8,128)S(1)} %copy-done.3, s32[2,128]{1,0:T(2,128)S(1)} %copy-done.6), custom_call_target="tpu_custom_call" | custom-call | tf_op jit(solution)/shard_map/pack/pallas_call | solution.py:351
  7.1 7.4 %all-to-all-start = ((f32[16,56,128]{2,1,0:T(8,128)}), f32[16,56,128]{2,1,0:T(8,128)S(1)}, u32[]{:S(2)}, u32[]{:S(2)}) async-start(f32[16,56,128]{2,1,0:T(8,128)} %bitcast), calls=%async_computation | async-start | bytes 917504 | tf_op jit(solution)/shard_map/all_to_all | solution.py:369
  14.5 0.0 copy-start.5
  14.5 1.3 %collective-permute-start.1 = (f32[81,8,128]{2,1,0:T(8,128)S(1)}, f32[81,8,128]{2,1,0:T(8,128)S(1)}, u32[]{:S(2)}, u32[]{:S(2)}) collective-permute-start(f32[81,8,128]{2,1,0:T(8,128)S(1)} %get-tuple-element.8.own), channel_id=1, source_target_pairs={{1,0},{2,1},{3,2},{4,3},{5,4},{6,5},{7,6},{8,7},{9,8},{10,9},{11,1... | collective-permute-start | bytes 995336 | tf_op jit(solution)/shard_map/ppermute | solution.py:373
  15.8 3.1 %collective-permute-start = (f32[81,8,128]{2,1,0:T(8,128)S(1)}, f32[81,8,128]{2,1,0:T(8,128)S(1)}, u32[]{:S(2)}, u32[]{:S(2)}) collective-permute-start(f32[81,8,128]{2,1,0:T(8,128)S(1)} %get-tuple-element.8.own), channel_id=1, source_target_pairs={{0,1},{1,2},{2,3},{3,4},{4,5},{5,6},{6,7},{7,8},{8,9},{9,10},{10,1... | collective-permute-start | bytes 995336 | tf_op jit(solution)/shard_map/ppermute | solution.py:372
  18.9 0.0 collective-permute-done.1.high
  18.9 1.2 %collective-permute-done.low = f32[81,8,128]{2,1,0:T(8,128)S(1)} collective-permute-done((f32[81,8,128]{2,1,0:T(8,128)S(1)}, f32[81,8,128]{2,1,0:T(8,128)S(1)}, u32[]{:S(2)}, u32[]{:S(2)}) %collective-permute-start) | collective-permute-done | bytes 331808 | tf_op jit(solution)/shard_map/ppermute | solution.py:372
  20.1 7.7 %all-to-all-done = f32[16,56,128]{2,1,0:T(8,128)S(1)} async-done(((f32[16,56,128]{2,1,0:T(8,128)}), f32[16,56,128]{2,1,0:T(8,128)S(1)}, u32[]{:S(2)}, u32[]{:S(2)}) %all-to-all-start) | async-done | bytes 458784 | tf_op jit(solution)/shard_map/all_to_all | solution.py:369
  27.7 0.0 copy-done.5
  27.7 5.0 %substeps.1 = (f32[3,8,32,32]{3,2,1,0:T(8,128)}, f32[6,8,32,32]{3,2,1,0:T(8,128)}, f32[256,128]{1,0:T(8,128)S(1)}) custom-call(f32[3,8]{1,0:T(4,128)S(1)} %copy-done.5, f32[81,8,128]{2,1,0:T(8,128)S(1)} %get-tuple-element.8.own, f32[81,8,128]{2,1,0:T(8,128)S(1)} %collective-permute-done.low, f32[81,8,128]{2,1,0:T(8,128)S(1)} %collective-permute-done.1.high, ...), custom_call_target="tpu_custom_call" | custom-call | tf_op jit(solution)/shard_map/substeps/pallas_call | solution.py:374
  32.8 15.6 %all_to_all.10 = f32[16,16,128]{2,1,0:T(8,128)S(1)} all-to-all(f32[16,16,128]{2,1,0:T(8,128)S(1)} %bitcast.6), channel_id=1, replica_groups=mesh['parts'=2,'map'=16] {'map'}, dimensions={0} | all-to-all | bytes 262144 | tf_op jit(solution)/shard_map/all_to_all | solution.py:398
  48.4 0.9 %unpack.1 = f32[4,2,32,128]{3,2,1,0:T(8,128)} custom-call(f32[256,128]{1,0:T(8,128)S(1)} %bitcast.5), custom_call_target="tpu_custom_call" | custom-call | tf_op jit(solution)/shard_map/unpack/pallas_call | solution.py:401
Async XLA Ops:
  0.6 1.1 %copy-start = (f32[6,8,32,32]{3,2,1,0:T(8,128)S(1)}, f32[6,8,32,32]{3,2,1,0:T(8,128)}, u32[]{:S(2)}) copy-start(f32[6,8,32,32]{3,2,1,0:T(8,128)} %stress.1) | copy-start | bytes 589828
  1.8 1.0 %copy-start.1 = (f32[3,8,32,32]{3,2,1,0:T(8,128)S(1)}, f32[3,8,32,32]{3,2,1,0:T(8,128)}, u32[]{:S(2)}) copy-start(f32[3,8,32,32]{3,2,1,0:T(8,128)} %vel.1) | copy-start | bytes 294916
  2.8 0.9 %copy-start.2 = (s32[8,32,32]{2,1,0:T(8,128)S(1)}, s32[8,32,32]{2,1,0:T(8,128)}, u32[]{:S(2)}) copy-start(s32[8,32,32]{2,1,0:T(8,128)} %zones.1) | copy-start | bytes 98308
  3.7 0.9 %copy-start.3 = (f32[4,2,32,128]{3,2,1,0:T(8,128)S(1)}, f32[4,2,32,128]{3,2,1,0:T(8,128)}, u32[]{:S(2)}) copy-start(f32[4,2,32,128]{3,2,1,0:T(8,128)} %ocean.1) | copy-start | bytes 393220
  4.6 0.7 %copy-start.4 = (f32[8,32]{1,0:T(8,128)S(1)}, f32[8,32]{1,0:T(8,128)}, u32[]{:S(2)}) copy-start(f32[8,32]{1,0:T(8,128)} %slip.1) | copy-start | bytes 3076
  5.3 0.7 %copy-start.6 = (s32[2,128]{1,0:T(2,128)S(1)}, s32[2,128]{1,0:T(2,128)}, u32[]{:S(2)}) copy-start(s32[2,128]{1,0:T(2,128)} %bathy.1) | copy-start | bytes 3076
  7.1 20.6 %all-to-all-start = ((f32[16,56,128]{2,1,0:T(8,128)}), f32[16,56,128]{2,1,0:T(8,128)S(1)}, u32[]{:S(2)}, u32[]{:S(2)}) async-start(f32[16,56,128]{2,1,0:T(8,128)} %bitcast), calls=%async_computation | async-start | bytes 917504 | tf_op jit(solution)/shard_map/all_to_all | solution.py:369
  14.5 13.3 %copy-start.5 = (f32[3,8]{1,0:T(4,128)S(1)}, f32[3,8]{1,0:T(4,128)}, u32[]{:S(2)}) copy-start(f32[3,8]{1,0:T(4,128)} %mats.1) | copy-start | bytes 292
  14.5 4.4 %collective-permute-start.1 = (f32[81,8,128]{2,1,0:T(8,128)S(1)}, f32[81,8,128]{2,1,0:T(8,128)S(1)}, u32[]{:S(2)}, u32[]{:S(2)}) collective-permute-start(f32[81,8,128]{2,1,0:T(8,128)S(1)} %get-tuple-element.8.own), channel_id=1, source_target_pairs={{1,0},{2,1},{3,2},{4,3},{5,4},{6,5},{7,6},{8,7},{9,8},{10,9},{11,1... | collective-permute-start | bytes 995336 | tf_op jit(solution)/shard_map/ppermute | solution.py:373
  15.8 4.3 %collective-permute-start = (f32[81,8,128]{2,1,0:T(8,128)S(1)}, f32[81,8,128]{2,1,0:T(8,128)S(1)}, u32[]{:S(2)}, u32[]{:S(2)}) collective-permute-start(f32[81,8,128]{2,1,0:T(8,128)S(1)} %get-tuple-element.8.own), channel_id=1, source_target_pairs={{0,1},{1,2},{2,3},{3,4},{4,5},{5,6},{6,7},{7,8},{8,9},{9,10},{10,1... | collective-permute-start | bytes 995336 | tf_op jit(solution)/shard_map/ppermute | solution.py:372

commit v3 on v2

v3 whole, which is shorter than its diff:
```python
import functools

import jax
import jax.numpy as jnp
from jax import lax
from jax.experimental import pallas as pl
from jax.experimental.pallas import tpu as pltpu
from jax.sharding import PartitionSpec as P

STEPS = 4
ZONES = 8
DT = 0.25
HALF = 0.5 * DT
KBULK = 2.25
GRAV = 0.1
HALO = 2 * STEPS
LANES = 128
F32 = jnp.float32
VX, VY, VZ = range(3)
SXX, SYY, SZZ, SXY, SXZ, SYZ = range(6)
BUOY, LAMB, SHEAR, FAULT, FLOOR = range(5)


class Plan:
    def __init__(self, devices, cells, depth, ny, strips):
        self.n = devices
        self.cells = cells
        self.depth = depth
        self.ny = ny
        self.strips = strips
        self.chunks = max(1, LANES // ny)
        self.sub = depth // self.chunks
        self.lanes = self.chunks * ny
        self.width = cells + 2 * HALO
        self.own_groups = cells // self.chunks
        self.halo_groups = HALO // self.chunks
        self.sent_groups = self.own_groups + self.halo_groups
        self.lead = self.chunks * strips
        self.rows = self.lead * self.sent_groups
        self.back_rows = self.lead * self.own_groups
        self.nx = devices * cells
        self.block = 4 * self.sub
        self.unrolled = self.sub * self.lanes <= 1024
        assert devices % 2 == 0 and cells == HALO and self.block * self.chunks == LANES

    def planes(self, start, stop, body):
        if self.unrolled:
            for j in range(start, stop):
                body(j)
        else:
            def run(j, carry):
                body(j)
                return carry

            lax.fori_loop(start, stop, run, 0)


def odd_device():
    return lax.rem(lax.axis_index("map"), 2)


def place(pieces, wanted, block):
    out = None
    for i, piece in enumerate(pieces):
        shift = (i - wanted[i]) * block % piece.shape[-1]
        moved = pltpu.roll(piece, shift, piece.ndim - 1) if shift else piece
        if out is None:
            out = moved
        else:
            lane = lax.broadcasted_iota(jnp.int32, moved.shape, moved.ndim - 1)
            out = jnp.where(lane >= i * block, moved, out)
    return out


def ocean_kernel(plan, ocean_ref, bathy_ref, message, ocean, bathy, turned, grouped, extra, sems):
    cells, sub, chunks, n, strips = plan.cells, plan.sub, plan.chunks, plan.n, plan.strips
    block, sent, rows = plan.block, plan.sent_groups, plan.rows
    copies = [
        pltpu.make_async_copy(ocean_ref, ocean, sems.at[0]),
        pltpu.make_async_copy(bathy_ref, bathy, sems.at[1]),
    ]
    for copy in copies:
        copy.start()
    for copy in copies:
        copy.wait()
    border = jnp.zeros((plan.lead, plan.halo_groups, LANES), F32)
    count = plan.nx // chunks
    grouped[:, : plan.halo_groups, :] = border
    grouped[:, plan.halo_groups + count :, :] = border
    for yl in range(strips):
        stacked = jnp.concatenate(
            [ocean[f, yl, kc * sub : (kc + 1) * sub, :] for kc in range(chunks) for f in range(4)],
            axis=0,
        )
        turned[yl] = stacked.T
        by_x = [turned[yl, pl.ds(i, count, stride=chunks), :] for i in range(chunks)]
        for kc in range(chunks):
            grouped[kc * strips + yl, pl.ds(plan.halo_groups, count), :] = place(
                by_x, [kc] * chunks, block
            )
    for d in range(n):
        start = d * plan.own_groups + (d % 2) * plan.halo_groups
        for q in range(plan.lead):
            message[d * rows + q * sent : d * rows + (q + 1) * sent, :] = grouped[
                q, start : start + sent, :
            ]
    depths = bathy[...].astype(F32)
    wide = lax.broadcasted_iota(jnp.int32, depths.shape, 1)
    for d in range(n):
        first = d * cells - HALO - 1
        moved = pltpu.roll(depths, -first % plan.nx, 1)
        moved = jnp.where((wide + first >= 0) & (wide + first < plan.nx), moved, 0.0)
        extra[d * strips : (d + 1) * strips, :] = moved[:, :LANES]
    pairs = n // 2
    lane = lax.broadcasted_iota(jnp.int32, (pairs, LANES), 1)
    blank = jnp.zeros((1, LANES), F32)
    for odd in range(2):
        slot = (odd * (chunks - 1) * 4 + 2) * sub
        group = odd * (sent - 1)
        for yl in range(strips):
            if odd:
                column = turned[yl, pl.ds(2 * cells + HALO, pairs - 1, stride=2 * cells), :]
                column = jnp.concatenate([column, blank], axis=0)
            else:
                column = turned[yl, pl.ds(2 * cells - HALO - 1, pairs - 1, stride=2 * cells), :]
                column = jnp.concatenate([blank, column], axis=0)
            deep = extra[pl.ds(odd * strips + yl, pairs, stride=2 * strips), :]
            for kc in range(chunks):
                at = odd * rows + (kc * strips + yl) * sent + group
                old = message[pl.ds(at, pairs, stride=2 * rows), :]
                edge = pltpu.roll(column, (slot - kc * block) % LANES, 1)
                floor = pltpu.roll(deep, (slot + sub - kc * sub) % LANES, 1)
                new = jnp.where((lane >= slot) & (lane < slot + sub), edge, old)
                new = jnp.where((lane >= slot + sub) & (lane < slot + 2 * sub), floor, new)
                message[pl.ds(at, pairs, stride=2 * rows), :] = new


def crust_kernel(
    plan, vel_ref, stress_ref, zones_ref, slip_ref, _, crust, vel, stress, zones, slip, sems
):
    cells, sub, chunks, ny = plan.cells, plan.sub, plan.chunks, plan.ny
    copies = [
        pltpu.make_async_copy(source, target, sems.at[i])
        for i, (source, target) in enumerate(
            ((vel_ref, vel), (stress_ref, stress), (zones_ref, zones), (slip_ref, slip))
        )
    ]
    for copy in copies:
        copy.start()

    def joined(ref, *at):
        parts = [ref[(*at, pl.ds(kc * sub, sub), slice(None))] for kc in range(chunks)]
        return jnp.concatenate(parts, axis=-1) if chunks > 1 else parts[0]

    copies[0].wait()
    for f in range(3):
        for x in range(cells):
            crust[f * cells + x] = joined(vel, f, x)
    copies[1].wait()
    for f in range(6):
        for x in range(cells):
            crust[(3 + f) * cells + x] = joined(stress, f, x)
    copies[2].wait()
    for x in range(cells):
        crust[9 * cells + x] = (joined(zones, x) + 1).astype(F32)
    copies[3].wait()
    fault_chunk = (plan.depth // 2) // sub
    pieces = [
        slip[...] if kc == fault_chunk else jnp.zeros((cells, ny), F32) for kc in range(chunks)
    ]
    fault = jnp.concatenate(pieces, axis=-1) if chunks > 1 else pieces[0]
    if sub > cells:
        fault = jnp.concatenate([fault, jnp.zeros((sub - cells, plan.lanes), F32)], axis=0)
    crust[10 * cells] = fault


class Shifts:
    def __init__(self, plan):
        self.plan = plan
        shape = (plan.sub, plan.lanes)
        self.row = lax.broadcasted_iota(jnp.int32, shape, 0)
        self.lane = lax.broadcasted_iota(jnp.int32, shape, 1)
        self.y = lax.rem(self.lane, plan.ny)
        self.first_row = self.row == 0
        self.last_row = self.row == plan.sub - 1
        self.top = self.first_row & (self.lane < plan.ny)
        self.floor_cell = self.last_row & (self.lane >= plan.lanes - plan.ny)
        self.not_low_y = jnp.where(self.y == 0, 0.0, 1.0).astype(F32)
        self.not_high_y = jnp.where(self.y == plan.ny - 1, 0.0, 1.0).astype(F32)
        self.depth = (
            lax.div(self.lane, plan.ny) * plan.sub + self.row
        ).astype(F32)

    def dy(self, f):
        lanes = self.plan.lanes
        return pltpu.roll(f, lanes - 1, 1) * self.not_high_y - pltpu.roll(f, 1, 1) * self.not_low_y

    def below(self, f):
        plan = self.plan
        moved = pltpu.roll(f, plan.sub - 1, 0)
        if plan.chunks > 1:
            moved = jnp.where(self.last_row, pltpu.roll(moved, plan.lanes - plan.ny, 1), moved)
        return jnp.where(self.floor_cell, 0.0, moved)

    def above(self, f, top):
        plan = self.plan
        moved = pltpu.roll(f, 1, 0)
        if plan.chunks > 1:
            moved = jnp.where(self.first_row, pltpu.roll(moved, plan.ny, 1), moved)
        return jnp.where(self.top, top, moved)

    def seafloor(self, vz):
        row = self.over_chunks(jnp.where(self.top, vz, 0.0)[0:1])
        return jnp.broadcast_to(row, vz.shape)

    def over_chunks(self, f):
        shift = self.plan.ny
        while shift < self.plan.lanes:
            f = f + pltpu.roll(f, shift, 1)
            shift *= 2
        return f


def acceleration(sh, stress, j):
    sxy, sxz = stress[SXY, j], stress[SXZ, j]
    syz, szz = stress[SYZ, j], stress[SZZ, j]
    ax = stress[SXX, j + 1] - stress[SXX, j - 1] + sh.dy(sxy) + sh.below(sxz) - sh.above(sxz, 0.0)
    ay = stress[SXY, j + 1] - stress[SXY, j - 1] + sh.dy(stress[SYY, j])
    ay = ay + sh.below(syz) - sh.above(syz, 0.0)
    az = stress[SXZ, j + 1] - stress[SXZ, j - 1] + sh.dy(syz) + sh.below(szz) - sh.above(szz, 0.0)
    return ax, ay, az


def strained(sh, vel, stress, mats, j):
    vx, vy, vz = vel[VX, j], vel[VY, j], vel[VZ, j]
    exx = vel[VX, j + 1] - vel[VX, j - 1]
    eyy = sh.dy(vy)
    ezz = sh.below(vz) - sh.above(vz, vz)
    mu = mats[SHEAR, j]
    mu2 = mu + mu
    common = mats[LAMB, j] * (exx + eyy + ezz)
    exy = sh.dy(vx) + vel[VY, j + 1] - vel[VY, j - 1]
    exz = sh.below(vx) - sh.above(vx, vx) + vel[VZ, j + 1] - vel[VZ, j - 1]
    eyz = sh.below(vy) - sh.above(vy, vy) + sh.dy(vz)
    return (
        stress[SXX, j] + (common + mu2 * exx),
        stress[SYY, j] + (common + mu2 * eyy),
        stress[SZZ, j] + (common + mu2 * ezz),
        stress[SXY, j] + mu * exy,
        stress[SXZ, j] + (mu * exz + mats[FAULT, j]),
        stress[SYZ, j] + mu * eyz,
    )


def begin_kernel(plan, table, own, mate, other, vel, stress, mats):
    cells, sub = plan.cells, plan.sub
    sh = Shifts(plan)
    odd = odd_device()
    starts = (HALO, (HALO + cells) * (1 - odd), (HALO + cells) * odd)
    for start, ref in zip(starts, (own, mate, other)):
        def bring(x, start=start, ref=ref):
            j = start + x
            for f in range(3):
                vel[f, j] = ref[f * cells + x]
            for f in range(6):
                stress[f, j] = ref[(3 + f) * cells + x]
            zone = ref[9 * cells + x]
            values = [jnp.zeros_like(zone) for _ in range(3)]
            for z in range(ZONES):
                here = zone == float(z + 1)
                values = [jnp.where(here, table[c, z], values[c]) for c in range(3)]
            for c in range(3):
                mats[c, j] = values[c] * HALF
            slip = jnp.broadcast_to(ref[10 * cells, pl.ds(x, 1), :], (sub, plan.lanes))
            mats[FAULT, j] = jnp.where(sh.row == (plan.depth // 2) % sub, DT * slip, 0.0)
            mats[FLOOR, j] = sh.seafloor(ref[VZ * cells + x])

        plan.planes(0, cells, bring)

    def move(j):
        b = mats[BUOY, j]
        for f, a in enumerate(acceleration(sh, stress, j)):
            vel[f, j] = vel[f, j] + b * a

    plan.planes(1, plan.width - 1, move)


def middle_kernel(
    plan, arrived, swapped, vel_in, stress_in, mats, vel, stress, loads, message,
    oc, water, bottom, gather, depths,
):
    sub, chunks, n, strips = plan.sub, plan.chunks, plan.n, plan.strips
    width, sent = plan.width, plan.sent_groups
    sh = Shifts(plan)
    odd = odd_device()

    def turn(ref, group):
        for kc in range(chunks):
            for yl in range(strips):
                at = (kc * strips + yl) * sent + group
                gather[pl.ds(kc * plan.ny + yl, n, stride=strips), :] = ref[
                    pl.ds(at, n, stride=plan.rows), :
                ]
        return gather[...].T

    def spread(turned, group):
        for i in range(chunks):
            for f in range(4):
                at = (i * 4 + f) * sub
                oc[f, 1 + group * chunks + i] = turned[at : at + sub]

    ends = []
    for group in range(sent):
        turned = turn(arrived, group)
        spread(turned, group + plan.halo_groups * odd)
        if group == 0:
            ends.append((turned[2 * sub : 3 * sub], turned[3 * sub : 4 * sub]))
        if group == sent - 1:
            ends.append((turned[LANES - 2 * sub : LANES - sub], turned[LANES - sub :]))
    for group in range(plan.halo_groups):
        spread(turn(swapped, group + plan.own_groups * odd), group + sent * (1 - odd))
    turned = turn(swapped, plan.own_groups - odd)
    is_odd = odd == 1
    oc[0, (width + 1) * odd] = jnp.where(is_odd, ends[1][0], ends[0][0])
    oc[0, (width + 1) * (1 - odd)] = jnp.where(
        is_odd, turned[LANES - 4 * sub : LANES - 3 * sub], turned[:sub]
    )
    deep = jnp.where(is_odd, ends[1][1], ends[0][1])
    for kc in range(chunks):
        mine = (sh.lane >= kc * plan.ny) & (sh.lane < (kc + 1) * plan.ny)
        depths[kc * sub : (kc + 1) * sub, :] = sh.over_chunks(jnp.where(mine, deep, 0.0))

    def mask(j):
        low = jnp.broadcast_to(depths[pl.ds(j, 1), :], (sub, plan.lanes))
        wet = jnp.where(sh.depth < low, 1.0, 0.0).astype(F32)
        water[j] = wet
        bottom[j] = jnp.where(sh.depth == low - 1.0, 1.0, 0.0).astype(F32)
        oc[0, j] = oc[0, j] * wet

    def mask_x(j):
        oc[1, j] = oc[1, j] * water[j]

    def mask_yw(j):
        oc[2, j] = oc[2, j] * water[j]
        oc[3, j] = oc[3, j] * water[j]

    plan.planes(0, width + 2, mask)
    plan.planes(1, width + 1, mask_x)
    plan.planes(2, width, mask_yw)

    for t in range(STEPS):
        first, last = 2 * t, width - 2 * t
        before = t == 0

        def flow_x(j):
            oc[1, j + 1] = water[j + 1] * (oc[1, j + 1] - HALF * (oc[0, j + 2] - oc[0, j]))

        def flow(j):
            p = oc[0, j + 1]
            wet = water[j + 1]
            oc[2, j + 1] = wet * (oc[2, j + 1] - HALF * sh.dy(p))
            rise = sh.below(p) + bottom[j + 1] * p - sh.above(p, -p)
            oc[3, j + 1] = wet * (oc[3, j + 1] - (HALF * rise + (DT * GRAV) * p))

        def press(j):
            w = oc[3, j + 1]
            floor = mats[FLOOR, j] if before else sh.seafloor(vel[VZ, j])
            rise = sh.below(w) + bottom[j + 1] * floor - sh.above(w, w)
            total = oc[1, j + 2] - oc[1, j] + sh.dy(oc[2, j + 1]) + rise
            oc[0, j + 1] = water[j + 1] * (oc[0, j + 1] - (HALF * KBULK) * total)

        def load(j):
            column = jnp.sum(bottom[j + 1] * oc[0, j + 1], axis=0, keepdims=True)
            column = jnp.broadcast_to(sh.over_chunks(column), (sub, plan.lanes))
            return jnp.where(sh.top, column, 0.0)

        plan.planes(first, last, flow_x)
        plan.planes(first + 1, last - 1, flow)
        plan.planes(first + 1, last - 1, press)
        if before:
            def add_load(j):
                for f in (VX, VY):
                    vel[f, j] = vel_in[f, j]
                vel[VZ, j] = vel_in[VZ, j] + mats[BUOY, j] * load(j)

            plan.planes(first + 1, last - 1, add_load)
        elif t < STEPS - 1:
            def move(j):
                ax, ay, az = acceleration(sh, stress, j)
                b = mats[BUOY, j]
                vel[VX, j] = vel[VX, j] + b * ax
                vel[VY, j] = vel[VY, j] + b * ay
                vel[VZ, j] = vel[VZ, j] + b * (az + load(j))

            plan.planes(first + 1, last - 1, move)
        else:
            def keep(j):
                loads[j] = load(j)

            plan.planes(first + 1, last - 1, keep)
        if t < STEPS - 2:
            def strain(j):
                source = stress_in if before else stress
                for f, value in enumerate(strained(sh, vel, source, mats, j)):
                    stress[f, j] = value

            plan.planes(first + 2, last - 2, strain)

    for group in range(plan.own_groups):
        stacked = jnp.concatenate(
            [
                oc[f, 1 + HALO + group * chunks + i]
                for i in range(chunks)
                for f in range(4)
            ],
            axis=0,
        )
        gather[...] = stacked.T
        for kc in range(chunks):
            for yl in range(strips):
                at = group * plan.lead + kc * strips + yl
                message[pl.ds(at, n, stride=plan.back_rows), :] = gather[
                    pl.ds(kc * plan.ny + yl, n, stride=strips), :
                ]


def end_kernel(plan, vel_in, stress_in, mats, loads, vel_out, stress_out, vel, stress):
    cells, sub, chunks, ny = plan.cells, plan.sub, plan.chunks, plan.ny
    sh = Shifts(plan)
    first, last = 2 * (STEPS - 1), plan.width - 2 * (STEPS - 1)

    def put(out, f, x, plane):
        for kc in range(chunks):
            out[f, x, kc * sub : (kc + 1) * sub, :] = plane[:, kc * ny : (kc + 1) * ny]

    def strain(j):
        for f, value in enumerate(strained(sh, vel_in, stress_in, mats, j)):
            stress[f, j] = value

    def move(j):
        ax, ay, az = acceleration(sh, stress, j)
        b = mats[BUOY, j]
        for f, a in enumerate((ax, ay, az + loads[j])):
            vel[f, j] = vel_in[f, j] + b * a

    def finish(x):
        for f in range(3):
            put(vel_out, f, x, vel[f, x + HALO])
        for f, value in enumerate(strained(sh, vel, stress, mats, x + HALO)):
            put(stress_out, f, x, value)

    plan.planes(first, last, strain)
    plan.planes(first + 1, last - 1, move)
    plan.planes(0, cells, finish)


def unpack_kernel(plan, arrived, ocean, turned):
    sub, chunks = plan.sub, plan.chunks
    block = 4 * sub
    for yl in range(plan.strips):
        by_chunk = [
            arrived[pl.ds(kc * plan.strips + yl, plan.nx // chunks, stride=plan.lead), :]
            for kc in range(chunks)
        ]
        for i in range(chunks):
            turned[pl.ds(i, plan.nx // chunks, stride=chunks), :] = place(
                by_chunk, [i] * chunks, block
            )
        whole = turned[...].T
        for kc in range(chunks):
            for f in range(4):
                at = (kc * 4 + f) * sub
                ocean[f, yl, kc * sub : (kc + 1) * sub, :] = whole[at : at + sub]


def on_device(plan, velocity, stress, ocean, zones, materials, slip, bathy):
    n, cells, sub, lanes, width = plan.n, plan.cells, plan.sub, plan.lanes, plan.width
    vmem = pl.BlockSpec(memory_space=pltpu.VMEM)
    smem = pl.BlockSpec(memory_space=pltpu.SMEM)
    hbm = pl.BlockSpec(memory_space=pltpu.HBM)

    def shape(*dims):
        return jax.ShapeDtypeStruct(dims, F32)

    def like(array):
        return pltpu.VMEM(array.shape, array.dtype)

    def call(kernel, name, out, ins, scratch, room=16, **rest):
        room = room if plan.unrolled else 56
        return pl.pallas_call(
            functools.partial(kernel, plan),
            out_shape=out,
            in_specs=ins,
            out_specs=jax.tree.map(lambda _: vmem, out),
            scratch_shapes=scratch,
            compiler_params=pltpu.CompilerParams(vmem_limit_bytes=room * 1024 * 1024),
            name=name,
            **rest,
        )

    def exchange(rows, count):
        whole = rows.reshape(n, count, LANES)
        moved = lax.all_to_all(whole, "map", split_axis=0, concat_axis=0, tiled=True)
        return moved.reshape(n * count, LANES)

    message = call(
        ocean_kernel,
        "ocean_rows",
        shape(n * plan.rows, LANES),
        [hbm] * 2,
        [
            like(ocean),
            like(bathy),
            pltpu.VMEM((plan.strips, plan.nx, LANES), F32),
            pltpu.VMEM(
                (plan.lead, plan.nx // plan.chunks + 2 * plan.halo_groups, LANES), F32
            ),
            pltpu.VMEM((n * plan.strips, LANES), F32),
            pltpu.SemaphoreType.DMA((2,)),
        ],
        room=56,
    )(ocean, bathy)
    arrived = exchange(message, plan.rows)
    crust = call(
        crust_kernel,
        "crust_planes",
        shape(10 * cells + 1, sub, lanes),
        [hbm] * 4 + [pl.BlockSpec(memory_space=pl.ANY)],
        [like(velocity), like(stress), like(zones), like(slip), pltpu.SemaphoreType.DMA((4,))],
        room=56,
    )(velocity, stress, zones, slip, message)
    mates = [(i, i ^ 1) for i in range(n)]
    others = [(i, i + 1) for i in range(1, n - 1, 2)]
    others += [(target, source) for source, target in others]
    other = lax.ppermute(crust, "map", others)
    mate = lax.ppermute(crust, "map", mates)
    vel, strs, mats = call(
        begin_kernel,
        "first_velocity",
        (shape(3, width, sub, lanes), shape(6, width, sub, lanes), shape(5, width, sub, lanes)),
        [smem] + [vmem] * 3,
        [],
    )(materials, crust, mate, other)
    swapped = lax.ppermute(arrived, "map", mates)
    vel, strs, loads, back = call(
        middle_kernel,
        "substeps",
        (
            shape(3, width, sub, lanes),
            shape(6, width, sub, lanes),
            shape(width, sub, lanes),
            shape(n * plan.back_rows, LANES),
        ),
        [vmem] * 5,
        [
            pltpu.VMEM((4, width + 2, sub, lanes), F32),
            pltpu.VMEM((width + 2, sub, lanes), F32),
            pltpu.VMEM((width + 2, sub, lanes), F32),
            pltpu.VMEM((lanes, LANES), F32),
            pltpu.VMEM((plan.depth, lanes), F32),
        ],
        input_output_aliases={2: 0, 3: 1},
    )(arrived, swapped, vel, strs, mats)
    returned = exchange(back, plan.back_rows)
    new_velocity, new_stress = call(
        end_kernel,
        "last_updates",
        (shape(*velocity.shape), shape(*stress.shape)),
        [vmem] * 4,
        [
            pltpu.VMEM((3, width, sub, lanes), F32),
            pltpu.VMEM((6, width, sub, lanes), F32),
        ],
    )(vel, strs, mats, loads)
    new_ocean = call(
        unpack_kernel,
        "ocean_strips",
        shape(*ocean.shape),
        [vmem],
        [pltpu.VMEM((plan.nx, LANES), F32)],
    )(returned)
    return new_velocity, new_stress, new_ocean


def solution(mesh):
    n = mesh.shape["map"]

    def body(velocity, stress, ocean, zones, materials, slip, bathy):
        _, cells, depth, ny = velocity.shape
        plan = Plan(n, cells, depth, ny, ocean.shape[1])
        return on_device(plan, velocity, stress, ocean, zones, materials, slip, bathy)

    return jax.shard_map(
        body,
        mesh=mesh,
        in_specs=(
            P("parts", "map", None, None),
            P("parts", "map", None, None),
            P("parts", "map", None, None),
            P("map", "parts", None),
            P(),
            P("map", "parts"),
            P("map", "parts"),
        ),
        out_specs=(
            P("parts", "map", None, None),
            P("parts", "map", None, None),
            P("parts", "map", None, None),
        ),
        check_vma=False,
    )
```

time: 49.8 us -> 44.7 us (0.90)
  blocking collectives: 15.6 us -> 0 us
  starting transfers between devices: 11.7 us -> 21 us
  Pallas kernels: 7.14 us -> 12.2 us
  local copies, waits for them, and re-layouts: 5.3 us -> 0.97 us
  waiting for transfers between devices: 8.87 us -> 9.46 us
    all_to_all x1 -> x0, blocking collectives: 15.6 us -> none  [on_device(): lax.all_to_all(back.reshape(n, plan.back_rows, LANES), 'map', split_axis=...]
    all_to_all x1 -> x2, starting transfers between devices: 7.36 us -> 17 us  [exchange(): lax.all_to_all(whole, 'map', split_axis=0, concat_axis=0, tiled=True)]
    pallas_call x3 -> x6, Pallas kernels: 7.14 us -> 12.2 us  [the longest x1 3.53 us: on_device(): call(middle_kernel, 'substeps', (shape(3, width, sub, lanes), shape(6, wi...]
    unnamed x14 -> x4, local copies, waits for them, and re-layouts: 5.3 us -> 0.97 us
    all_to_all x1 -> x2, waiting for transfers between devices: 7.66 us -> 9.45 us  [exchange(): lax.all_to_all(whole, 'map', split_axis=0, concat_axis=0, tiled=True)]
    ppermute x2 -> x3, waiting for transfers between devices: 1.22 us -> 0.01 us  [the longest x1 0.01 us: on_device(): swapped = lax.ppermute(arrived, 'map', mates)]
    ppermute x2 -> x3, starting transfers between devices: 4.34 us -> 4.01 us  [the longest x1 3.33 us: on_device(): mate = lax.ppermute(crust, 'map', mates)]
  transfers between devices with their start and end apart: 3 -> 5, of which waited for: 2 -> 2; matrix products, arithmetic and copies ran while one was open for 0% -> 0% of each run, Pallas kernels for 0% -> 13%
where the time goes in v3:
time: 44.7 us; the launch traced here: 44.3 us
  starting transfers between devices  21 us (47%)
  Pallas kernels  12.2 us (27%)
  waiting for transfers between devices  9.46 us (21%)
  local copies, waits for them, and re-layouts  0.97 us (2%)
  between operations  0.72 us (2%)
    all_to_all x2, starting transfers between devices, exchange(): lax.all_to_all(whole, 'map', split_axis=0, concat_axis=0, tiled=True)  17 us
    all_to_all x2, waiting for transfers between devices, exchange(): lax.all_to_all(whole, 'map', split_axis=0, concat_axis=0, tiled=True)  9.45 us
    pallas_call x1, Pallas kernels, on_device(): call(middle_kernel, 'substeps', (shape(3, width, sub, lanes), shape(6, wi...  3.53 us
    ppermute x1, starting transfers between devices, on_device(): mate = lax.ppermute(crust, 'map', mates)  3.33 us
    pallas_call x1, Pallas kernels, on_device(): call(crust_kernel, 'crust_planes', shape(10 * cells + 1, sub, lanes), [hb...  2.41 us
    pallas_call x1, Pallas kernels, on_device(): call(end_kernel, 'last_updates', (shape(*velocity.shape), shape(*stress.s...  2.1 us
    pallas_call x1, Pallas kernels, on_device(): call(ocean_kernel, 'ocean_rows', shape(n * plan.rows, LANES), [hbm] * 2,...  2.07 us
    pallas_call x1, Pallas kernels, on_device(): call(begin_kernel, 'first_velocity', (shape(3, width, sub, lanes), shape(...  1.1 us
  transfers between devices with their start and end apart: 5, of which 2 were waited for; matrix products, arithmetic and copies ran while one was open for 0% of the time, Pallas kernels for 13%

profile of v3, /device:TPU:0, one launch (start us, length us, event | category | flops | bytes accessed | tf_op | source)
XLA Modules:
  0.0 44.3 jit_solution(6560981210352415058)
XLA Ops:
  0.6 2.1 %ocean_rows.1._ = f32[512,128]{1,0:T(8,128)} custom-call(f32[4,2,32,128]{3,2,1,0:T(8,128)} %ocean_ref.1, s32[2,128]{1,0:T(2,128)} %bathy_ref.1), custom_call_target="tpu_custom_call" | custom-call | tf_op jit(solution)/shard_map/ocean_rows/pallas_call | solution.py:506
  2.7 7.4 %all-to-all-start = ((f32[16,32,128]{2,1,0:T(8,128)}), f32[16,32,128]{2,1,0:T(8,128)S(1)}, u32[]{:S(2)}, u32[]{:S(2)}) async-start(f32[16,32,128]{2,1,0:T(8,128)} %bitcast.7), calls=%async_computation | async-start | bytes 524288 | tf_op jit(solution)/shard_map/all_to_all | solution.py:503
  10.1 0.0 copy-start.1
  10.1 2.4 %crust_planes.1.own = f32[81,8,128]{2,1,0:T(8,128)} custom-call(f32[3,8,32,32]{3,2,1,0:T(8,128)} %vel_ref.1, f32[6,8,32,32]{3,2,1,0:T(8,128)} %stress_ref.1, s32[8,32,32]{2,1,0:T(8,128)} %zones_ref.1, f32[8,32]{1,0:T(8,128)} %slip_ref.1, f32[512,128]{1,0:T(8,128)} %ocean_rows.1._), custom_call_target="tpu_custom_call" | custom-call | tf_op jit(solution)/shard_map/crust_planes/pallas_call | solution.py:524
  12.5 0.7 %collective-permute-start.2 = (f32[81,8,128]{2,1,0:T(8,128)}, f32[81,8,128]{2,1,0:T(8,128)S(1)}, u32[]{:S(2)}, u32[]{:S(2)}) collective-permute-start(f32[81,8,128]{2,1,0:T(8,128)} %crust_planes.1.own), channel_id=1, source_target_pairs={{1,2},{3,4},{5,6},{7,8},{9,10},{11,12},{13,14},{2,1},{4,3},{6,5},{... | collective-permute-start | bytes 995336 | tf_op jit(solution)/shard_map/ppermute | solution.py:535
  13.2 3.3 %collective-permute-start.1 = (f32[81,8,128]{2,1,0:T(8,128)}, f32[81,8,128]{2,1,0:T(8,128)S(1)}, u32[]{:S(2)}, u32[]{:S(2)}) collective-permute-start(f32[81,8,128]{2,1,0:T(8,128)} %crust_planes.1.own), channel_id=1, source_target_pairs={{0,1},{1,0},{2,3},{3,2},{4,5},{5,4},{6,7},{7,6},{8,9},{9,8},{10,11... | collective-permute-start | bytes 995336 | tf_op jit(solution)/shard_map/ppermute | solution.py:536
  16.5 3.6 %all-to-all-done = f32[16,32,128]{2,1,0:T(8,128)S(1)} async-done(((f32[16,32,128]{2,1,0:T(8,128)}), f32[16,32,128]{2,1,0:T(8,128)S(1)}, u32[]{:S(2)}, u32[]{:S(2)}) %all-to-all-start) | async-done | bytes 262176 | tf_op jit(solution)/shard_map/all_to_all | solution.py:503
  20.1 0.0 collective-permute-start
  20.2 0.0 collective-permute-done.2.other
  20.2 0.0 collective-permute-done.1.mate
  20.2 0.0 copy-done.1
  20.2 0.0 copy-start
  20.2 1.0 %copy-done = f32[81,8,128]{2,1,0:T(8,128)S(1)} copy-done((f32[81,8,128]{2,1,0:T(8,128)S(1)}, f32[81,8,128]{2,1,0:T(8,128)}, u32[]{:S(2)}) %copy-start) | copy-done | bytes 331800
  21.1 1.1 %first_velocity.1 = (f32[3,24,8,128]{3,2,1,0:T(8,128)S(1)}, f32[6,24,8,128]{3,2,1,0:T(8,128)S(1)}, f32[5,24,8,128]{3,2,1,0:T(8,128)S(1)}) custom-call(f32[3,8]{1,0:T(4,128)S(1)} %copy-done.1, f32[81,8,128]{2,1,0:T(8,128)S(1)} %copy-done, f32[81,8,128]{2,1,0:T(8,128)S(1)} %collective-permute-done.1.mate, f32[81,8,128]{2,1,0:T(8,128)S(1)} %collective-permute-done.2.other), custom_call_target="tpu_custom_call" | custom-call | tf_op jit(solution)/shard_map/first_velocity/pallas_call | solution.py:537
  22.2 0.0 collective-permute-done.swapped
  22.3 3.5 %substeps.1 = (f32[3,24,8,128]{3,2,1,0:T(8,128)S(1)}, f32[6,24,8,128]{3,2,1,0:T(8,128)S(1)}, f32[24,8,128]{2,1,0:T(8,128)S(1)}, f32[256,128]{1,0:T(8,128)}) custom-call(f32[512,128]{1,0:T(8,128)S(1)} %bitcast.5, f32[512,128]{1,0:T(8,128)S(1)} %collective-permute-done.swapped, ...), custom_call_target="tpu_custom_call", output_to_operand_aliasing={{0}: (2, {}), {1}: (3, {})} | custom-call | tf_op jit(solution)/shard_map/substeps/pallas_call | solution.py:545
  25.8 9.7 %all-to-all-start.1 = ((f32[16,16,128]{2,1,0:T(8,128)}), f32[16,16,128]{2,1,0:T(8,128)S(1)}, u32[]{:S(2)}, u32[]{:S(2)}) async-start(f32[16,16,128]{2,1,0:T(8,128)} %bitcast.2), calls=%async_computation.1 | async-start | bytes 262144 | tf_op jit(solution)/shard_map/all_to_all | solution.py:503
  35.5 2.1 %last_updates.1 = (f32[3,8,32,32]{3,2,1,0:T(8,128)}, f32[6,8,32,32]{3,2,1,0:T(8,128)}) custom-call(f32[3,24,8,128]{3,2,1,0:T(8,128)S(1)} %get-tuple-element.15.vel_in, f32[6,24,8,128]{3,2,1,0:T(8,128)S(1)} %get-tuple-element.16.stress_in, f32[5,24,8,128]{3,2,1,0:T(8,128)S(1)} %get-tuple-element.14.mats, f32[24,8,128]{2,1,0:T(8,128)S(1)} %get-tuple-element.17.loads), custom_call_target="tpu_custom_call" | custom-call | tf_op jit(solution)/shard_map/last_updates/pallas_call | solution.py:565
  37.6 5.8 %all-to-all-done.1 = f32[16,16,128]{2,1,0:T(8,128)S(1)} async-done(((f32[16,16,128]{2,1,0:T(8,128)}), f32[16,16,128]{2,1,0:T(8,128)S(1)}, u32[]{:S(2)}, u32[]{:S(2)}) %all-to-all-start.1) | async-done | bytes 131104 | tf_op jit(solution)/shard_map/all_to_all | solution.py:503
  43.4 0.9 %ocean_strips.1 = f32[4,2,32,128]{3,2,1,0:T(8,128)} custom-call(f32[256,128]{1,0:T(8,128)S(1)} %bitcast.6), custom_call_target="tpu_custom_call" | custom-call | tf_op jit(solution)/shard_map/ocean_strips/pallas_call | solution.py:575
Async XLA Ops:
  2.7 17.4 %all-to-all-start = ((f32[16,32,128]{2,1,0:T(8,128)}), f32[16,32,128]{2,1,0:T(8,128)S(1)}, u32[]{:S(2)}, u32[]{:S(2)}) async-start(f32[16,32,128]{2,1,0:T(8,128)} %bitcast.7), calls=%async_computation | async-start | bytes 524288 | tf_op jit(solution)/shard_map/all_to_all | solution.py:503
  10.1 10.1 %copy-start.1 = (f32[3,8]{1,0:T(4,128)S(1)}, f32[3,8]{1,0:T(4,128)}, u32[]{:S(2)}) copy-start(f32[3,8]{1,0:T(4,128)} %table.1) | copy-start | bytes 292
  12.5 7.6 %collective-permute-start.2 = (f32[81,8,128]{2,1,0:T(8,128)}, f32[81,8,128]{2,1,0:T(8,128)S(1)}, u32[]{:S(2)}, u32[]{:S(2)}) collective-permute-start(f32[81,8,128]{2,1,0:T(8,128)} %crust_planes.1.own), channel_id=1, source_target_pairs={{1,2},{3,4},{5,6},{7,8},{9,10},{11,12},{13,14},{2,1},{4,3},{6,5},{... | collective-permute-start | bytes 995336 | tf_op jit(solution)/shard_map/ppermute | solution.py:535
  13.2 7.0 %collective-permute-start.1 = (f32[81,8,128]{2,1,0:T(8,128)}, f32[81,8,128]{2,1,0:T(8,128)S(1)}, u32[]{:S(2)}, u32[]{:S(2)}) collective-permute-start(f32[81,8,128]{2,1,0:T(8,128)} %crust_planes.1.own), channel_id=1, source_target_pairs={{0,1},{1,0},{2,3},{3,2},{4,5},{5,4},{6,7},{7,6},{8,9},{9,8},{10,11... | collective-permute-start | bytes 995336 | tf_op jit(solution)/shard_map/ppermute | solution.py:536
  20.1 2.1 %collective-permute-start = (f32[512,128]{1,0:T(8,128)S(1)}, f32[512,128]{1,0:T(8,128)S(1)}, u32[]{:S(2)}, u32[]{:S(2)}) collective-permute-start(f32[512,128]{1,0:T(8,128)S(1)} %bitcast.4), channel_id=1, source_target_pairs={{0,1},{1,0},{2,3},{3,2},{4,5},{5,4},{6,7},{7,6},{8,9},{9,8},{10,11... | collective-permute-start | bytes 786440 | tf_op jit(solution)/shard_map/ppermute | solution.py:544
  20.2 1.0 %copy-start = (f32[81,8,128]{2,1,0:T(8,128)S(1)}, f32[81,8,128]{2,1,0:T(8,128)}, u32[]{:S(2)}) copy-start(f32[81,8,128]{2,1,0:T(8,128)} %crust_planes.1.own) | copy-start | bytes 995332
  25.8 17.6 %all-to-all-start.1 = ((f32[16,16,128]{2,1,0:T(8,128)}), f32[16,16,128]{2,1,0:T(8,128)S(1)}, u32[]{:S(2)}, u32[]{:S(2)}) async-start(f32[16,16,128]{2,1,0:T(8,128)} %bitcast.2), calls=%async_computation.1 | async-start | bytes 262144 | tf_op jit(solution)/shard_map/all_to_all | solution.py:503

commit v4 on v3

--- a/solution.py
+++ b/solution.py
@@ -72,17 +72,9 @@
     return out
 
 
-def ocean_kernel(plan, ocean_ref, bathy_ref, message, ocean, bathy, turned, grouped, extra, sems):
+def ocean_kernel(plan, ocean, bathy, message, turned, grouped, extra):
     cells, sub, chunks, n, strips = plan.cells, plan.sub, plan.chunks, plan.n, plan.strips
     block, sent, rows = plan.block, plan.sent_groups, plan.rows
-    copies = [
-        pltpu.make_async_copy(ocean_ref, ocean, sems.at[0]),
-        pltpu.make_async_copy(bathy_ref, bathy, sems.at[1]),
-    ]
-    for copy in copies:
-        copy.start()
-    for copy in copies:
-        copy.wait()
     border = jnp.zeros((plan.lead, plan.halo_groups, LANES), F32)
     count = plan.nx // chunks
     grouped[:, : plan.halo_groups, :] = border
@@ -136,14 +128,21 @@
 
 
 def crust_kernel(
-    plan, vel_ref, stress_ref, zones_ref, slip_ref, _, crust, vel, stress, zones, slip, sems
+    plan, vel_ref, stress_ref, zones_ref, slip_ref, ocean_ref, bathy_ref,
+    crust, ocean, bathy, vel, stress, zones, slip, sems,
 ):
     cells, sub, chunks, ny = plan.cells, plan.sub, plan.chunks, plan.ny
+    pairs = (
+        (vel_ref, vel),
+        (stress_ref, stress),
+        (zones_ref, zones),
+        (slip_ref, slip),
+        (ocean_ref, ocean),
+        (bathy_ref, bathy),
+    )
     copies = [
         pltpu.make_async_copy(source, target, sems.at[i])
-        for i, (source, target) in enumerate(
-            ((vel_ref, vel), (stress_ref, stress), (zones_ref, zones), (slip_ref, slip))
-        )
+        for i, (source, target) in enumerate(pairs)
     ]
     for copy in copies:
         copy.start()
@@ -172,6 +171,8 @@
     if sub > cells:
         fault = jnp.concatenate([fault, jnp.zeros((sub - cells, plan.lanes), F32)], axis=0)
     crust[10 * cells] = fault
+    copies[4].wait()
+    copies[5].wait()
 
 
 class Shifts:
@@ -294,13 +295,18 @@
     sh = Shifts(plan)
     odd = odd_device()
 
-    def turn(ref, group):
-        for kc in range(chunks):
-            for yl in range(strips):
-                at = (kc * strips + yl) * sent + group
-                gather[pl.ds(kc * plan.ny + yl, n, stride=strips), :] = ref[
-                    pl.ds(at, n, stride=plan.rows), :
-                ]
+    half = n // 2
+    mate = 1 - odd
+
+    def turn(owner, group):
+        for core, ref in ((odd, arrived), (mate, swapped)):
+            for kc in range(chunks):
+                for yl in range(strips):
+                    at = owner * plan.rows + (kc * strips + yl) * sent + group
+                    to = kc * plan.ny + core * strips + yl
+                    gather[pl.ds(to, half, stride=2 * strips), :] = ref[
+                        pl.ds(at, half, stride=2 * plan.rows), :
+                    ]
         return gather[...].T
 
     def spread(turned, group):
@@ -311,18 +317,18 @@
 
     ends = []
     for group in range(sent):
-        turned = turn(arrived, group)
+        turned = turn(odd, group)
         spread(turned, group + plan.halo_groups * odd)
         if group == 0:
             ends.append((turned[2 * sub : 3 * sub], turned[3 * sub : 4 * sub]))
         if group == sent - 1:
             ends.append((turned[LANES - 2 * sub : LANES - sub], turned[LANES - sub :]))
     for group in range(plan.halo_groups):
-        spread(turn(swapped, group + plan.own_groups * odd), group + sent * (1 - odd))
-    turned = turn(swapped, plan.own_groups - odd)
+        spread(turn(mate, group + plan.own_groups * odd), group + sent * mate)
+    turned = turn(mate, plan.own_groups - odd)
     is_odd = odd == 1
     oc[0, (width + 1) * odd] = jnp.where(is_odd, ends[1][0], ends[0][0])
-    oc[0, (width + 1) * (1 - odd)] = jnp.where(
+    oc[0, (width + 1) * mate] = jnp.where(
         is_odd, turned[LANES - 4 * sub : LANES - 3 * sub], turned[:sub]
     )
     deep = jnp.where(is_odd, ends[1][1], ends[0][1])
@@ -483,6 +489,9 @@
         return jax.ShapeDtypeStruct(dims, F32)
 
     def like(array):
+        return jax.ShapeDtypeStruct(array.shape, array.dtype)
+
+    def held(array):
         return pltpu.VMEM(array.shape, array.dtype)
 
     def call(kernel, name, out, ins, scratch, room=16, **rest):
@@ -498,41 +507,41 @@
             **rest,
         )
 
-    def exchange(rows, count):
-        whole = rows.reshape(n, count, LANES)
-        moved = lax.all_to_all(whole, "map", split_axis=0, concat_axis=0, tiled=True)
-        return moved.reshape(n * count, LANES)
-
+    def pinned(array):
+        return pltpu.with_memory_space_constraint(array, pltpu.HBM)
+
+    mates = [(i, i ^ 1) for i in range(n)]
+    others = [(i, i + 1) for i in range(1, n - 1, 2)]
+    others += [(target, source) for source, target in others]
+    crust, ocean_near, bathy_near = call(
+        crust_kernel,
+        "crust_planes",
+        (shape(10 * cells + 1, sub, lanes), like(ocean), like(bathy)),
+        [hbm] * 6,
+        [held(velocity), held(stress), held(zones), held(slip), pltpu.SemaphoreType.DMA((6,))],
+    )(*(pinned(a) for a in (velocity, stress, zones, slip, ocean, bathy)))
+    other = lax.ppermute(crust, "map", others)
     message = call(
         ocean_kernel,
         "ocean_rows",
         shape(n * plan.rows, LANES),
-        [hbm] * 2,
+        [vmem] * 2,
         [
-            like(ocean),
-            like(bathy),
             pltpu.VMEM((plan.strips, plan.nx, LANES), F32),
             pltpu.VMEM(
                 (plan.lead, plan.nx // plan.chunks + 2 * plan.halo_groups, LANES), F32
             ),
             pltpu.VMEM((n * plan.strips, LANES), F32),
-            pltpu.SemaphoreType.DMA((2,)),
         ],
-        room=56,
-    )(ocean, bathy)
-    arrived = exchange(message, plan.rows)
-    crust = call(
-        crust_kernel,
-        "crust_planes",
-        shape(10 * cells + 1, sub, lanes),
-        [hbm] * 4 + [pl.BlockSpec(memory_space=pl.ANY)],
-        [like(velocity), like(stress), like(zones), like(slip), pltpu.SemaphoreType.DMA((4,))],
-        room=56,
-    )(velocity, stress, zones, slip, message)
-    mates = [(i, i ^ 1) for i in range(n)]
-    others = [(i, i + 1) for i in range(1, n - 1, 2)]
-    others += [(target, source) for source, target in others]
-    other = lax.ppermute(crust, "map", others)
+    )(ocean_near, bathy_near)
+    arrived = lax.all_to_all(
+        message.reshape(n // 2, 2 * plan.rows, LANES),
+        "map",
+        split_axis=0,
+        concat_axis=0,
+        axis_index_groups=[list(range(core, n, 2)) for core in range(2)],
+        tiled=True,
+    ).reshape(n * plan.rows, LANES)
     mate = lax.ppermute(crust, "map", mates)
     vel, strs, mats = call(
         begin_kernel,
@@ -540,6 +549,7 @@
         (shape(3, width, sub, lanes), shape(6, width, sub, lanes), shape(5, width, sub, lanes)),
         [smem] + [vmem] * 3,
         [],
+        cost_estimate=pl.CostEstimate(flops=0, bytes_accessed=20_000_000, transcendentals=0),
     )(materials, crust, mate, other)
     swapped = lax.ppermute(arrived, "map", mates)
     vel, strs, loads, back = call(
@@ -561,7 +571,9 @@
         ],
         input_output_aliases={2: 0, 3: 1},
     )(arrived, swapped, vel, strs, mats)
-    returned = exchange(back, plan.back_rows)
+    returned = lax.all_to_all(
+        back.reshape(n, plan.back_rows, LANES), "map", split_axis=0, concat_axis=0, tiled=True
+    ).reshape(n * plan.back_rows, LANES)
     new_velocity, new_stress = call(
         end_kernel,
         "last_updates",

time: 44.7 us -> 41.9 us (0.937)
  Pallas kernels: 12.2 us -> 10.5 us
  starting transfers between devices: 21 us -> 19.4 us
  waiting for transfers between devices: 9.46 us -> 11 us
  local copies, waits for them, and re-layouts: 0.97 us -> 0.01 us
    all_to_all x2, starting transfers between devices: 17 us -> 15.1 us  [the longest x1 7.89 us: on_device(): lax.all_to_all(back.reshape(n, plan.back_rows, LANES), 'map', split_axis=...]
    pallas_call x2, Pallas kernels: 4.48 us -> 2.85 us  [the longest x1 1.7 us: on_device(): call(crust_kernel, 'crust_planes', (shape(10 * cells + 1, sub, lanes), li...]
    all_to_all x2, waiting for transfers between devices: 9.45 us -> 10.6 us  [the longest x1 5.83 us: on_device(): lax.all_to_all(back.reshape(n, plan.back_rows, LANES), 'map', split_axis=...]
    unnamed x4 -> x2, local copies, waits for them, and re-layouts: 0.97 us -> 0.01 us
  transfers between devices with their start and end apart: 5 -> 5, of which waited for: 2 -> 3; matrix products, arithmetic and copies ran while one was open for 0% -> 0% of each run, Pallas kernels for 13% -> 8%
where the time goes in v4:
time: 41.9 us; the launch traced here: 41.6 us
  starting transfers between devices  19.4 us (46%)
  waiting for transfers between devices  11 us (26%)
  Pallas kernels  10.5 us (25%)
  between operations  0.68 us (2%)
    all_to_all x1, starting transfers between devices, on_device(): lax.all_to_all(back.reshape(n, plan.back_rows, LANES), 'map', split_axis=...  7.89 us
    all_to_all x1, starting transfers between devices, on_device(): lax.all_to_all(message.reshape(n // 2, 2 * plan.rows, LANES), 'map', spli...  7.25 us
    all_to_all x1, waiting for transfers between devices, on_device(): lax.all_to_all(back.reshape(n, plan.back_rows, LANES), 'map', split_axis=...  5.83 us
    all_to_all x1, waiting for transfers between devices, on_device(): lax.all_to_all(message.reshape(n // 2, 2 * plan.rows, LANES), 'map', spli...  4.79 us
    ppermute x1, starting transfers between devices, on_device(): mate = lax.ppermute(crust, 'map', mates)  3.54 us
    pallas_call x1, Pallas kernels, on_device(): call(middle_kernel, 'substeps', (shape(3, width, sub, lanes), shape(6, wi...  3.49 us
    pallas_call x1, Pallas kernels, on_device(): call(end_kernel, 'last_updates', (shape(*velocity.shape), shape(*stress.s...  2.1 us
    pallas_call x1, Pallas kernels, on_device(): call(crust_kernel, 'crust_planes', (shape(10 * cells + 1, sub, lanes), li...  1.7 us
  transfers between devices with their start and end apart: 5, of which 3 were waited for; matrix products, arithmetic and copies ran while one was open for 0% of the time, Pallas kernels for 8%

profile of v4, /device:TPU:0, one launch (start us, length us, event | category | flops | bytes accessed | tf_op | source)
XLA Modules:
  0.0 41.6 jit_solution(9859669580505432885)
XLA Ops:
  0.6 1.7 %crust_planes.1 = (f32[81,8,128]{2,1,0:T(8,128)S(1)}, f32[4,2,32,128]{3,2,1,0:T(8,128)S(1)}, s32[2,128]{1,0:T(2,128)S(1)}) custom-call(f32[3,8,32,32]{3,2,1,0:T(8,128)} %vel_ref.1, f32[6,8,32,32]{3,2,1,0:T(8,128)} %stress_ref.1, s32[8,32,32]{2,1,0:T(8,128)} %zones_ref.1, f32[8,32]{1,0:T(8,128)} %slip_ref.1, f32[4,2,32,128]{3,2,1,0:T(8,128)} %ocean_ref.1, ...), custom_call_target="tpu_custom_call" | custom-call | tf_op jit(solution)/shard_map/crust_planes/pallas_call | solution.py:516
  2.3 1.2 %ocean_rows.1 = f32[512,128]{1,0:T(8,128)} custom-call(f32[4,2,32,128]{3,2,1,0:T(8,128)S(1)} %get-tuple-element.15.ocean, s32[2,128]{1,0:T(2,128)S(1)} %get-tuple-element.16.bathy), custom_call_target="tpu_custom_call" | custom-call | tf_op jit(solution)/shard_map/ocean_rows/pallas_call | solution.py:524
  3.5 7.3 %all-to-all-start = ((f32[8,64,128]{2,1,0:T(8,128)}), f32[8,64,128]{2,1,0:T(8,128)S(1)}, u32[]{:S(2)}, u32[]{:S(2)}) async-start(f32[8,64,128]{2,1,0:T(8,128)} %bitcast), calls=%async_computation | async-start | bytes 524288 | tf_op jit(solution)/shard_map/all_to_all | solution.py:537
  10.7 0.0 copy-start
  10.7 0.7 %collective-permute-start.2 = (f32[81,8,128]{2,1,0:T(8,128)S(1)}, f32[81,8,128]{2,1,0:T(8,128)S(1)}, u32[]{:S(2)}, u32[]{:S(2)}) collective-permute-start(f32[81,8,128]{2,1,0:T(8,128)S(1)} %get-tuple-element.17.own), channel_id=1, source_target_pairs={{1,2},{3,4},{5,6},{7,8},{9,10},{11,12},{13,14},{2,1},{4,3},{6,5},{... | collective-permute-start | bytes 995336 | tf_op jit(solution)/shard_map/ppermute | solution.py:523
  11.4 3.5 %collective-permute-start.1 = (f32[81,8,128]{2,1,0:T(8,128)S(1)}, f32[81,8,128]{2,1,0:T(8,128)S(1)}, u32[]{:S(2)}, u32[]{:S(2)}) collective-permute-start(f32[81,8,128]{2,1,0:T(8,128)S(1)} %get-tuple-element.17.own), channel_id=1, source_target_pairs={{0,1},{1,0},{2,3},{3,2},{4,5},{5,4},{6,7},{7,6},{8,9},{9,8},{10,11... | collective-permute-start | bytes 995336 | tf_op jit(solution)/shard_map/ppermute | solution.py:545
  15.0 4.8 %all-to-all-done = f32[8,64,128]{2,1,0:T(8,128)S(1)} async-done(((f32[8,64,128]{2,1,0:T(8,128)}), f32[8,64,128]{2,1,0:T(8,128)S(1)}, u32[]{:S(2)}, u32[]{:S(2)}) %all-to-all-start) | async-done | bytes 262176 | tf_op jit(solution)/shard_map/all_to_all | solution.py:537
  19.8 0.0 collective-permute-start
  19.8 0.0 collective-permute-done.2.other
  19.8 0.0 collective-permute-done.1.mate
  19.8 0.0 copy-done
  19.8 1.1 %first_velocity.1 = (f32[3,24,8,128]{3,2,1,0:T(8,128)S(1)}, f32[6,24,8,128]{3,2,1,0:T(8,128)S(1)}, f32[5,24,8,128]{3,2,1,0:T(8,128)S(1)}) custom-call(f32[3,8]{1,0:T(4,128)S(1)} %copy-done, f32[81,8,128]{2,1,0:T(8,128)S(1)} %get-tuple-element.17.own, f32[81,8,128]{2,1,0:T(8,128)S(1)} %collective-permute-done.1.mate, ...), custom_call_target="tpu_custom_call" | custom-call | bytes 20000000 | tf_op jit(solution)/shard_map/first_velocity/pallas_call | solution.py:546
  20.9 0.4 collective-permute-done.swapped
  21.3 3.5 %substeps.1 = (f32[3,24,8,128]{3,2,1,0:T(8,128)S(1)}, f32[6,24,8,128]{3,2,1,0:T(8,128)S(1)}, f32[24,8,128]{2,1,0:T(8,128)S(1)}, f32[256,128]{1,0:T(8,128)}) custom-call(f32[512,128]{1,0:T(8,128)S(1)} %bitcast.5, f32[512,128]{1,0:T(8,128)S(1)} %collective-permute-done.swapped, ...), custom_call_target="tpu_custom_call", output_to_operand_aliasing={{0}: (2, {}), {1}: (3, {})} | custom-call | tf_op jit(solution)/shard_map/substeps/pallas_call | solution.py:555
  24.8 7.9 %all-to-all-start.1 = ((f32[16,16,128]{2,1,0:T(8,128)}), f32[16,16,128]{2,1,0:T(8,128)S(1)}, u32[]{:S(2)}, u32[]{:S(2)}) async-start(f32[16,16,128]{2,1,0:T(8,128)} %bitcast.2), calls=%async_computation.1 | async-start | bytes 262144 | tf_op jit(solution)/shard_map/all_to_all | solution.py:574
  32.7 2.1 %last_updates.1 = (f32[3,8,32,32]{3,2,1,0:T(8,128)}, f32[6,8,32,32]{3,2,1,0:T(8,128)}) custom-call(f32[3,24,8,128]{3,2,1,0:T(8,128)S(1)} %get-tuple-element.21.vel_in, f32[6,24,8,128]{3,2,1,0:T(8,128)S(1)} %get-tuple-element.22.stress_in, f32[5,24,8,128]{3,2,1,0:T(8,128)S(1)} %get-tuple-element.20.mats, f32[24,8,128]{2,1,0:T(8,128)S(1)} %get-tuple-element.23.loads), custom_call_target="tpu_custom_call" | custom-call | tf_op jit(solution)/shard_map/last_updates/pallas_call | solution.py:577
  34.8 5.8 %all-to-all-done.1 = f32[16,16,128]{2,1,0:T(8,128)S(1)} async-done(((f32[16,16,128]{2,1,0:T(8,128)}), f32[16,16,128]{2,1,0:T(8,128)S(1)}, u32[]{:S(2)}, u32[]{:S(2)}) %all-to-all-start.1) | async-done | bytes 131104 | tf_op jit(solution)/shard_map/all_to_all | solution.py:574
  40.6 0.9 %ocean_strips.1 = f32[4,2,32,128]{3,2,1,0:T(8,128)} custom-call(f32[256,128]{1,0:T(8,128)S(1)} %bitcast.6), custom_call_target="tpu_custom_call" | custom-call | tf_op jit(solution)/shard_map/ocean_strips/pallas_call | solution.py:587
Async XLA Ops:
  3.5 16.3 %all-to-all-start = ((f32[8,64,128]{2,1,0:T(8,128)}), f32[8,64,128]{2,1,0:T(8,128)S(1)}, u32[]{:S(2)}, u32[]{:S(2)}) async-start(f32[8,64,128]{2,1,0:T(8,128)} %bitcast), calls=%async_computation | async-start | bytes 524288 | tf_op jit(solution)/shard_map/all_to_all | solution.py:537
  10.7 9.0 %copy-start = (f32[3,8]{1,0:T(4,128)S(1)}, f32[3,8]{1,0:T(4,128)}, u32[]{:S(2)}) copy-start(f32[3,8]{1,0:T(4,128)} %table.1) | copy-start | bytes 292
  10.7 9.0 %collective-permute-start.2 = (f32[81,8,128]{2,1,0:T(8,128)S(1)}, f32[81,8,128]{2,1,0:T(8,128)S(1)}, u32[]{:S(2)}, u32[]{:S(2)}) collective-permute-start(f32[81,8,128]{2,1,0:T(8,128)S(1)} %get-tuple-element.17.own), channel_id=1, source_target_pairs={{1,2},{3,4},{5,6},{7,8},{9,10},{11,12},{13,14},{2,1},{4,3},{6,5},{... | collective-permute-start | bytes 995336 | tf_op jit(solution)/shard_map/ppermute | solution.py:523
  11.4 8.3 %collective-permute-start.1 = (f32[81,8,128]{2,1,0:T(8,128)S(1)}, f32[81,8,128]{2,1,0:T(8,128)S(1)}, u32[]{:S(2)}, u32[]{:S(2)}) collective-permute-start(f32[81,8,128]{2,1,0:T(8,128)S(1)} %get-tuple-element.17.own), channel_id=1, source_target_pairs={{0,1},{1,0},{2,3},{3,2},{4,5},{5,4},{6,7},{7,6},{8,9},{9,8},{10,11... | collective-permute-start | bytes 995336 | tf_op jit(solution)/shard_map/ppermute | solution.py:545
  19.8 1.5 %collective-permute-start = (f32[512,128]{1,0:T(8,128)S(1)}, f32[512,128]{1,0:T(8,128)S(1)}, u32[]{:S(2)}, u32[]{:S(2)}) collective-permute-start(f32[512,128]{1,0:T(8,128)S(1)} %bitcast.4), channel_id=1, source_target_pairs={{0,1},{1,0},{2,3},{3,2},{4,5},{5,4},{6,7},{7,6},{8,9},{9,8},{10,11... | collective-permute-start | bytes 786440 | tf_op jit(solution)/shard_map/ppermute | solution.py:554
  24.8 15.8 %all-to-all-start.1 = ((f32[16,16,128]{2,1,0:T(8,128)}), f32[16,16,128]{2,1,0:T(8,128)S(1)}, u32[]{:S(2)}, u32[]{:S(2)}) async-start(f32[16,16,128]{2,1,0:T(8,128)} %bitcast.2), calls=%async_computation.1 | async-start | bytes 262144 | tf_op jit(solution)/shard_map/all_to_all | solution.py:574

commit v5 on v4

--- a/solution.py
+++ b/solution.py
@@ -551,6 +551,7 @@
         [],
         cost_estimate=pl.CostEstimate(flops=0, bytes_accessed=20_000_000, transcendentals=0),
     )(materials, crust, mate, other)
+    arrived, vel = lax.optimization_barrier((arrived, vel))
     swapped = lax.ppermute(arrived, "map", mates)
     vel, strs, loads, back = call(
         middle_kernel,

time: 41.9 us -> 43.5 us (1.038)
  starting transfers between devices: 19.4 us -> 21.2 us
    ppermute x1, starting transfers between devices: 0.01 us -> 4.5 us  [on_device(): swapped = lax.ppermute(arrived, 'map', mates)]
    all_to_all x1, starting transfers between devices: 7.89 us -> 5.22 us  [on_device(): lax.all_to_all(back.reshape(n, plan.back_rows, LANES), 'map', split_axis=...]
    all_to_all x1, waiting for transfers between devices: 4.79 us -> 2.55 us  [on_device(): lax.all_to_all(message.reshape(n // 2, 2 * plan.rows, LANES), 'map', spli...]
    ppermute x1, waiting for transfers between devices: 0.01 us -> 1.26 us  [on_device(): mate = lax.ppermute(crust, 'map', mates)]
    ppermute x1, waiting for transfers between devices: 0.41 us -> 1.16 us  [on_device(): swapped = lax.ppermute(arrived, 'map', mates)]
  transfers between devices with their start and end apart: 5 -> 5, of which waited for: 3 -> 4; matrix products, arithmetic and copies ran while one was open for 0% -> 0% of each run, Pallas kernels for 8% -> 7%
where the time goes in v5:
time: 43.5 us; the launch traced here: 43.2 us
  starting transfers between devices  21.2 us (49%)
  waiting for transfers between devices  10.8 us (25%)
  Pallas kernels  10.5 us (24%)
  between operations  0.67 us (2%)
    all_to_all x1, starting transfers between devices, on_device(): lax.all_to_all(message.reshape(n // 2, 2 * plan.rows, LANES), 'map', spli...  7.38 us
    all_to_all x1, waiting for transfers between devices, on_device(): lax.all_to_all(back.reshape(n, plan.back_rows, LANES), 'map', split_axis=...  5.83 us
    all_to_all x1, starting transfers between devices, on_device(): lax.all_to_all(back.reshape(n, plan.back_rows, LANES), 'map', split_axis=...  5.22 us
    ppermute x1, starting transfers between devices, on_device(): swapped = lax.ppermute(arrived, 'map', mates)  4.5 us
    pallas_call x1, Pallas kernels, on_device(): call(middle_kernel, 'substeps', (shape(3, width, sub, lanes), shape(6, wi...  3.49 us
    ppermute x1, starting transfers between devices, on_device(): mate = lax.ppermute(crust, 'map', mates)  3.43 us
    all_to_all x1, waiting for transfers between devices, on_device(): lax.all_to_all(message.reshape(n // 2, 2 * plan.rows, LANES), 'map', spli...  2.55 us
    pallas_call x1, Pallas kernels, on_device(): call(end_kernel, 'last_updates', (shape(*velocity.shape), shape(*stress.s...  2.1 us
  transfers between devices with their start and end apart: 5, of which 4 were waited for; matrix products, arithmetic and copies ran while one was open for 0% of the time, Pallas kernels for 7%

profile of v5, /device:TPU:0, one launch (start us, length us, event | category | flops | bytes accessed | tf_op | source)
XLA Modules:
  0.0 43.2 jit_solution(8587070429087310158)
XLA Ops:
  0.6 1.7 %crust_planes.1 = (f32[81,8,128]{2,1,0:T(8,128)S(1)}, f32[4,2,32,128]{3,2,1,0:T(8,128)S(1)}, s32[2,128]{1,0:T(2,128)S(1)}) custom-call(f32[3,8,32,32]{3,2,1,0:T(8,128)} %vel_ref.1, f32[6,8,32,32]{3,2,1,0:T(8,128)} %stress_ref.1, s32[8,32,32]{2,1,0:T(8,128)} %zones_ref.1, f32[8,32]{1,0:T(8,128)} %slip_ref.1, f32[4,2,32,128]{3,2,1,0:T(8,128)} %ocean_ref.1, ...), custom_call_target="tpu_custom_call" | custom-call | tf_op jit(solution)/shard_map/crust_planes/pallas_call | solution.py:516
  2.3 1.2 %ocean_rows.1 = f32[512,128]{1,0:T(8,128)} custom-call(f32[4,2,32,128]{3,2,1,0:T(8,128)S(1)} %get-tuple-element.17.ocean, s32[2,128]{1,0:T(2,128)S(1)} %get-tuple-element.18.bathy), custom_call_target="tpu_custom_call" | custom-call | tf_op jit(solution)/shard_map/ocean_rows/pallas_call | solution.py:524
  3.5 0.0 copy-start
  3.5 7.4 %all-to-all-start = ((f32[8,64,128]{2,1,0:T(8,128)}), f32[8,64,128]{2,1,0:T(8,128)S(1)}, u32[]{:S(2)}, u32[]{:S(2)}) async-start(f32[8,64,128]{2,1,0:T(8,128)} %bitcast), calls=%async_computation | async-start | bytes 524288 | tf_op jit(solution)/shard_map/all_to_all | solution.py:537
  10.9 0.7 %collective-permute-start.1 = (f32[81,8,128]{2,1,0:T(8,128)S(1)}, f32[81,8,128]{2,1,0:T(8,128)S(1)}, u32[]{:S(2)}, u32[]{:S(2)}) collective-permute-start(f32[81,8,128]{2,1,0:T(8,128)S(1)} %get-tuple-element.19.own), channel_id=1, source_target_pairs={{1,2},{3,4},{5,6},{7,8},{9,10},{11,12},{13,14},{2,1},{4,3},{6,5},{... | collective-permute-start | bytes 995336 | tf_op jit(solution)/shard_map/ppermute | solution.py:523
  11.6 3.4 %collective-permute-start = (f32[81,8,128]{2,1,0:T(8,128)S(1)}, f32[81,8,128]{2,1,0:T(8,128)S(1)}, u32[]{:S(2)}, u32[]{:S(2)}) collective-permute-start(f32[81,8,128]{2,1,0:T(8,128)S(1)} %get-tuple-element.19.own), channel_id=1, source_target_pairs={{0,1},{1,0},{2,3},{3,2},{4,5},{5,4},{6,7},{7,6},{8,9},{9,8},{10,11... | collective-permute-start | bytes 995336 | tf_op jit(solution)/shard_map/ppermute | solution.py:545
  15.0 0.0 collective-permute-done.1.other
  15.0 1.3 %collective-permute-done.mate = f32[81,8,128]{2,1,0:T(8,128)S(1)} collective-permute-done((f32[81,8,128]{2,1,0:T(8,128)S(1)}, f32[81,8,128]{2,1,0:T(8,128)S(1)}, u32[]{:S(2)}, u32[]{:S(2)}) %collective-permute-start) | collective-permute-done | bytes 331808 | tf_op jit(solution)/shard_map/ppermute | solution.py:545
  16.2 0.0 copy-done
  16.2 1.1 %first_velocity.1 = (f32[3,24,8,128]{3,2,1,0:T(8,128)S(1)}, f32[6,24,8,128]{3,2,1,0:T(8,128)S(1)}, f32[5,24,8,128]{3,2,1,0:T(8,128)S(1)}) custom-call(f32[3,8]{1,0:T(4,128)S(1)} %copy-done, f32[81,8,128]{2,1,0:T(8,128)S(1)} %get-tuple-element.19.own, f32[81,8,128]{2,1,0:T(8,128)S(1)} %collective-permute-done.mate, f32[81,8,128]{2,1,0:T(8,128)S(1)} %collective-permute-done.1.other), custom_call_target="tpu_custom_call" | custom-call | bytes 20000000 | tf_op jit(solution)/shard_map/first_velocity/pallas_call | solution.py:546
  17.3 2.6 %all-to-all-done = f32[8,64,128]{2,1,0:T(8,128)S(1)} async-done(((f32[8,64,128]{2,1,0:T(8,128)}), f32[8,64,128]{2,1,0:T(8,128)S(1)}, u32[]{:S(2)}, u32[]{:S(2)}) %all-to-all-start) | async-done | bytes 262176 | tf_op jit(solution)/shard_map/all_to_all | solution.py:537
  19.9 4.5 %collective-permute-start.2 = (f32[512,128]{1,0:T(8,128)S(1)}, f32[512,128]{1,0:T(8,128)S(1)}, u32[]{:S(2)}, u32[]{:S(2)}) collective-permute-start(f32[512,128]{1,0:T(8,128)S(1)} %bitcast.4), channel_id=1, source_target_pairs={{0,1},{1,0},{2,3},{3,2},{4,5},{5,4},{6,7},{7,6},{8,9},{9,8},{10,11... | collective-permute-start | bytes 786440 | tf_op jit(solution)/shard_map/ppermute | solution.py:555
  24.4 1.2 %collective-permute-done.2.swapped = f32[512,128]{1,0:T(8,128)S(1)} collective-permute-done((f32[512,128]{1,0:T(8,128)S(1)}, f32[512,128]{1,0:T(8,128)S(1)}, u32[]{:S(2)}, u32[]{:S(2)}) %collective-permute-start.2) | collective-permute-done | bytes 262176 | tf_op jit(solution)/shard_map/ppermute | solution.py:555
  25.6 3.5 %substeps.1 = (f32[3,24,8,128]{3,2,1,0:T(8,128)S(1)}, f32[6,24,8,128]{3,2,1,0:T(8,128)S(1)}, f32[24,8,128]{2,1,0:T(8,128)S(1)}, f32[256,128]{1,0:T(8,128)}) custom-call(f32[512,128]{1,0:T(8,128)S(1)} %bitcast.5, f32[512,128]{1,0:T(8,128)S(1)} %collective-permute-done.2.swapped, ...), custom_call_target="tpu_custom_call", output_to_operand_aliasing={{0}: (2, {}), {1}: (3, {})} | custom-call | tf_op jit(solution)/shard_map/substeps/pallas_call | solution.py:556
  29.1 5.2 %all-to-all-start.1 = ((f32[16,16,128]{2,1,0:T(8,128)}), f32[16,16,128]{2,1,0:T(8,128)S(1)}, u32[]{:S(2)}, u32[]{:S(2)}) async-start(f32[16,16,128]{2,1,0:T(8,128)} %bitcast.2), calls=%async_computation.1 | async-start | bytes 262144 | tf_op jit(solution)/shard_map/all_to_all | solution.py:575
  34.3 2.1 %last_updates.1 = (f32[3,8,32,32]{3,2,1,0:T(8,128)}, f32[6,8,32,32]{3,2,1,0:T(8,128)}) custom-call(f32[3,24,8,128]{3,2,1,0:T(8,128)S(1)} %get-tuple-element.25.vel_in, f32[6,24,8,128]{3,2,1,0:T(8,128)S(1)} %get-tuple-element.26.stress_in, f32[5,24,8,128]{3,2,1,0:T(8,128)S(1)} %get-tuple-element.24.mats, f32[24,8,128]{2,1,0:T(8,128)S(1)} %get-tuple-element.27.loads), custom_call_target="tpu_custom_call" | custom-call | tf_op jit(solution)/shard_map/last_updates/pallas_call | solution.py:578
  36.4 5.8 %all-to-all-done.1 = f32[16,16,128]{2,1,0:T(8,128)S(1)} async-done(((f32[16,16,128]{2,1,0:T(8,128)}), f32[16,16,128]{2,1,0:T(8,128)S(1)}, u32[]{:S(2)}, u32[]{:S(2)}) %all-to-all-start.1) | async-done | bytes 131104 | tf_op jit(solution)/shard_map/all_to_all | solution.py:575
  42.2 0.9 %ocean_strips.1 = f32[4,2,32,128]{3,2,1,0:T(8,128)} custom-call(f32[256,128]{1,0:T(8,128)S(1)} %bitcast.6), custom_call_target="tpu_custom_call" | custom-call | tf_op jit(solution)/shard_map/ocean_strips/pallas_call | solution.py:588
Async XLA Ops:
  3.5 12.8 %copy-start = (f32[3,8]{1,0:T(4,128)S(1)}, f32[3,8]{1,0:T(4,128)}, u32[]{:S(2)}) copy-start(f32[3,8]{1,0:T(4,128)} %table.1) | copy-start | bytes 292
  3.5 16.4 %all-to-all-start = ((f32[8,64,128]{2,1,0:T(8,128)}), f32[8,64,128]{2,1,0:T(8,128)S(1)}, u32[]{:S(2)}, u32[]{:S(2)}) async-start(f32[8,64,128]{2,1,0:T(8,128)} %bitcast), calls=%async_computation | async-start | bytes 524288 | tf_op jit(solution)/shard_map/all_to_all | solution.py:537
  10.9 4.1 %collective-permute-start.1 = (f32[81,8,128]{2,1,0:T(8,128)S(1)}, f32[81,8,128]{2,1,0:T(8,128)S(1)}, u32[]{:S(2)}, u32[]{:S(2)}) collective-permute-start(f32[81,8,128]{2,1,0:T(8,128)S(1)} %get-tuple-element.19.own), channel_id=1, source_target_pairs={{1,2},{3,4},{5,6},{7,8},{9,10},{11,12},{13,14},{2,1},{4,3},{6,5},{... | collective-permute-start | bytes 995336 | tf_op jit(solution)/shard_map/ppermute | solution.py:523
  11.6 4.7 %collective-permute-start = (f32[81,8,128]{2,1,0:T(8,128)S(1)}, f32[81,8,128]{2,1,0:T(8,128)S(1)}, u32[]{:S(2)}, u32[]{:S(2)}) collective-permute-start(f32[81,8,128]{2,1,0:T(8,128)S(1)} %get-tuple-element.19.own), channel_id=1, source_target_pairs={{0,1},{1,0},{2,3},{3,2},{4,5},{5,4},{6,7},{7,6},{8,9},{9,8},{10,11... | collective-permute-start | bytes 995336 | tf_op jit(solution)/shard_map/ppermute | solution.py:545
  19.9 5.7 %collective-permute-start.2 = (f32[512,128]{1,0:T(8,128)S(1)}, f32[512,128]{1,0:T(8,128)S(1)}, u32[]{:S(2)}, u32[]{:S(2)}) collective-permute-start(f32[512,128]{1,0:T(8,128)S(1)} %bitcast.4), channel_id=1, source_target_pairs={{0,1},{1,0},{2,3},{3,2},{4,5},{5,4},{6,7},{7,6},{8,9},{9,8},{10,11... | collective-permute-start | bytes 786440 | tf_op jit(solution)/shard_map/ppermute | solution.py:555
  29.1 13.2 %all-to-all-start.1 = ((f32[16,16,128]{2,1,0:T(8,128)}), f32[16,16,128]{2,1,0:T(8,128)S(1)}, u32[]{:S(2)}, u32[]{:S(2)}) async-start(f32[16,16,128]{2,1,0:T(8,128)} %bitcast.2), calls=%async_computation.1 | async-start | bytes 262144 | tf_op jit(solution)/shard_map/all_to_all | solution.py:575

commit v6 on v5

--- a/solution.py
+++ b/solution.py
@@ -549,7 +549,9 @@
         (shape(3, width, sub, lanes), shape(6, width, sub, lanes), shape(5, width, sub, lanes)),
         [smem] + [vmem] * 3,
         [],
-        cost_estimate=pl.CostEstimate(flops=0, bytes_accessed=20_000_000, transcendentals=0),
+        cost_estimate=pl.CostEstimate(
+            flops=10**12, bytes_accessed=2 * 10**9, transcendentals=0
+        ),
     )(materials, crust, mate, other)
     arrived, vel = lax.optimization_barrier((arrived, vel))
     swapped = lax.ppermute(arrived, "map", mates)

time: 43.5 us -> 41.9 us (0.963)
  starting transfers between devices: 21.2 us -> 13.7 us
  waiting for transfers between devices: 10.8 us -> 15.7 us
  Pallas kernels: 10.5 us -> 11.4 us
    all_to_all x1, waiting for transfers between devices: 2.55 us -> 8.07 us  [on_device(): lax.all_to_all(message.reshape(n // 2, 2 * plan.rows, LANES), 'map', spli...]
    ppermute x1, starting transfers between devices: 4.5 us -> 0.01 us  [on_device(): swapped = lax.ppermute(arrived, 'map', mates)]
    all_to_all x1, starting transfers between devices: 7.38 us -> 5.01 us  [on_device(): lax.all_to_all(message.reshape(n // 2, 2 * plan.rows, LANES), 'map', spli...]
    all_to_all x1, starting transfers between devices: 5.22 us -> 3.69 us  [on_device(): lax.all_to_all(back.reshape(n, plan.back_rows, LANES), 'map', split_axis=...]
    ppermute x1, waiting for transfers between devices: 1.26 us -> 0.01 us  [on_device(): mate = lax.ppermute(crust, 'map', mates)]
    pallas_call x1, Pallas kernels: 3.49 us -> 4.44 us  [on_device(): call(middle_kernel, 'substeps', (shape(3, width, sub, lanes), shape(6, wi...]
    ppermute x1, starting transfers between devices: 3.43 us -> 4.35 us  [on_device(): mate = lax.ppermute(crust, 'map', mates)]
    ppermute x1, waiting for transfers between devices: 1.16 us -> 1.74 us  [on_device(): swapped = lax.ppermute(arrived, 'map', mates)]
  transfers between devices with their start and end apart: 5 -> 5, of which waited for: 4 -> 3; matrix products, arithmetic and copies ran while one was open for 0% -> 0% of each run, Pallas kernels for 7% -> 10%
where the time goes in v6:
time: 41.9 us; the launch traced here: 41.5 us
  waiting for transfers between devices  15.7 us (37%)
  starting transfers between devices  13.7 us (33%)
  Pallas kernels  11.4 us (27%)
  between operations  0.69 us (2%)
    all_to_all x1, waiting for transfers between devices, on_device(): lax.all_to_all(message.reshape(n // 2, 2 * plan.rows, LANES), 'map', spli...  8.07 us
    all_to_all x1, waiting for transfers between devices, on_device(): lax.all_to_all(back.reshape(n, plan.back_rows, LANES), 'map', split_axis=...  5.83 us
    all_to_all x1, starting transfers between devices, on_device(): lax.all_to_all(message.reshape(n // 2, 2 * plan.rows, LANES), 'map', spli...  5.01 us
    pallas_call x1, Pallas kernels, on_device(): call(middle_kernel, 'substeps', (shape(3, width, sub, lanes), shape(6, wi...  4.44 us
    ppermute x1, starting transfers between devices, on_device(): mate = lax.ppermute(crust, 'map', mates)  4.35 us
    all_to_all x1, starting transfers between devices, on_device(): lax.all_to_all(back.reshape(n, plan.back_rows, LANES), 'map', split_axis=...  3.69 us
    pallas_call x1, Pallas kernels, on_device(): call(end_kernel, 'last_updates', (shape(*velocity.shape), shape(*stress.s...  2.1 us
    ppermute x1, waiting for transfers between devices, on_device(): swapped = lax.ppermute(arrived, 'map', mates)  1.74 us
  transfers between devices with their start and end apart: 5, of which 3 were waited for; matrix products, arithmetic and copies ran while one was open for 0% of the time, Pallas kernels for 10%

profile of v6, /device:TPU:0, one launch (start us, length us, event | category | flops | bytes accessed | tf_op | source)
XLA Modules:
  0.0 41.5 jit_solution(7504325529193794508)
XLA Ops:
  0.6 1.7 %crust_planes.1 = (f32[81,8,128]{2,1,0:T(8,128)S(1)}, f32[4,2,32,128]{3,2,1,0:T(8,128)S(1)}, s32[2,128]{1,0:T(2,128)S(1)}) custom-call(f32[3,8,32,32]{3,2,1,0:T(8,128)} %vel_ref.1, f32[6,8,32,32]{3,2,1,0:T(8,128)} %stress_ref.1, s32[8,32,32]{2,1,0:T(8,128)} %zones_ref.1, f32[8,32]{1,0:T(8,128)} %slip_ref.1, f32[4,2,32,128]{3,2,1,0:T(8,128)} %ocean_ref.1, ...), custom_call_target="tpu_custom_call" | custom-call | tf_op jit(solution)/shard_map/crust_planes/pallas_call | solution.py:516
  2.3 0.7 %collective-permute-start.1 = (f32[81,8,128]{2,1,0:T(8,128)S(1)}, f32[81,8,128]{2,1,0:T(8,128)S(1)}, u32[]{:S(2)}, u32[]{:S(2)}) collective-permute-start(f32[81,8,128]{2,1,0:T(8,128)S(1)} %get-tuple-element.19.own), channel_id=1, source_target_pairs={{1,2},{3,4},{5,6},{7,8},{9,10},{11,12},{13,14},{2,1},{4,3},{6,5},{... | collective-permute-start | bytes 995336 | tf_op jit(solution)/shard_map/ppermute | solution.py:523
  3.0 4.3 %collective-permute-start = (f32[81,8,128]{2,1,0:T(8,128)S(1)}, f32[81,8,128]{2,1,0:T(8,128)S(1)}, u32[]{:S(2)}, u32[]{:S(2)}) collective-permute-start(f32[81,8,128]{2,1,0:T(8,128)S(1)} %get-tuple-element.19.own), channel_id=1, source_target_pairs={{0,1},{1,0},{2,3},{3,2},{4,5},{5,4},{6,7},{7,6},{8,9},{9,8},{10,11... | collective-permute-start | bytes 995336 | tf_op jit(solution)/shard_map/ppermute | solution.py:545
  7.4 1.1 %ocean_rows.1 = f32[512,128]{1,0:T(8,128)} custom-call(f32[4,2,32,128]{3,2,1,0:T(8,128)S(1)} %get-tuple-element.17.ocean, s32[2,128]{1,0:T(2,128)S(1)} %get-tuple-element.18.bathy), custom_call_target="tpu_custom_call" | custom-call | tf_op jit(solution)/shard_map/ocean_rows/pallas_call | solution.py:524
  8.5 0.0 copy-start
  8.5 5.0 %all-to-all-start = ((f32[8,64,128]{2,1,0:T(8,128)}), f32[8,64,128]{2,1,0:T(8,128)}, u32[]{:S(2)}, u32[]{:S(2)}) async-start(f32[8,64,128]{2,1,0:T(8,128)} %bitcast), calls=%async_computation | async-start | bytes 524288 | tf_op jit(solution)/shard_map/all_to_all | solution.py:537
  13.5 0.0 collective-permute-done.1.other
  13.5 0.0 collective-permute-done.mate
  13.6 0.0 copy-done
  13.6 1.1 %first_velocity.1 = (f32[3,24,8,128]{3,2,1,0:T(8,128)S(1)}, f32[6,24,8,128]{3,2,1,0:T(8,128)S(1)}, f32[5,24,8,128]{3,2,1,0:T(8,128)S(1)}) custom-call(f32[3,8]{1,0:T(4,128)S(1)} %copy-done, f32[81,8,128]{2,1,0:T(8,128)S(1)} %get-tuple-element.19.own, f32[81,8,128]{2,1,0:T(8,128)S(1)} %collective-permute-done.mate, f32[81,8,128]{2,1,0:T(8,128)S(1)} %collective-permute-done.1.other), custom_call_target="tpu_custom_call" | custom-call | flops 999999995904 | bytes 2000000000 | tf_op jit(solution)/shard_map/first_velocity/pallas_call | solution.py:546
  14.7 8.1 %all-to-all-done = f32[8,64,128]{2,1,0:T(8,128)} async-done(((f32[8,64,128]{2,1,0:T(8,128)}), f32[8,64,128]{2,1,0:T(8,128)}, u32[]{:S(2)}, u32[]{:S(2)}) %all-to-all-start) | async-done | bytes 262176 | tf_op jit(solution)/shard_map/all_to_all | solution.py:537
  22.7 0.0 collective-permute-start.2
  22.7 1.7 %collective-permute-done.2.swapped = f32[512,128]{1,0:T(8,128)S(1)} collective-permute-done((f32[512,128]{1,0:T(8,128)}, f32[512,128]{1,0:T(8,128)S(1)}, u32[]{:S(2)}, u32[]{:S(2)}) %collective-permute-start.2) | collective-permute-done | bytes 262176 | tf_op jit(solution)/shard_map/ppermute | solution.py:557
  24.5 4.4 %substeps.1 = (f32[3,24,8,128]{3,2,1,0:T(8,128)S(1)}, f32[6,24,8,128]{3,2,1,0:T(8,128)S(1)}, f32[24,8,128]{2,1,0:T(8,128)S(1)}, f32[256,128]{1,0:T(8,128)}) custom-call(f32[512,128]{1,0:T(8,128)} %bitcast.1.arrived, f32[512,128]{1,0:T(8,128)S(1)} %collective-permute-done.2.swapped, ...), custom_call_target="tpu_custom_call", output_to_operand_aliasing={{0}: (2, {}), {1}: (3, {})} | custom-call | tf_op jit(solution)/shard_map/substeps/pallas_call | solution.py:558
  28.9 3.7 %all-to-all-start.1 = ((f32[16,16,128]{2,1,0:T(8,128)}), f32[16,16,128]{2,1,0:T(8,128)S(1)}, u32[]{:S(2)}, u32[]{:S(2)}) async-start(f32[16,16,128]{2,1,0:T(8,128)} %bitcast.2), calls=%async_computation.1 | async-start | bytes 262144 | tf_op jit(solution)/shard_map/all_to_all | solution.py:577
  32.6 2.1 %last_updates.1 = (f32[3,8,32,32]{3,2,1,0:T(8,128)}, f32[6,8,32,32]{3,2,1,0:T(8,128)}) custom-call(f32[3,24,8,128]{3,2,1,0:T(8,128)S(1)} %get-tuple-element.25.vel_in, f32[6,24,8,128]{3,2,1,0:T(8,128)S(1)} %get-tuple-element.26.stress_in, f32[5,24,8,128]{3,2,1,0:T(8,128)S(1)} %get-tuple-element.24.mats, f32[24,8,128]{2,1,0:T(8,128)S(1)} %get-tuple-element.27.loads), custom_call_target="tpu_custom_call" | custom-call | tf_op jit(solution)/shard_map/last_updates/pallas_call | solution.py:580
  34.7 5.8 %all-to-all-done.1 = f32[16,16,128]{2,1,0:T(8,128)S(1)} async-done(((f32[16,16,128]{2,1,0:T(8,128)}), f32[16,16,128]{2,1,0:T(8,128)S(1)}, u32[]{:S(2)}, u32[]{:S(2)}) %all-to-all-start.1) | async-done | bytes 131104 | tf_op jit(solution)/shard_map/all_to_all | solution.py:577
  40.6 0.9 %ocean_strips.1 = f32[4,2,32,128]{3,2,1,0:T(8,128)} custom-call(f32[256,128]{1,0:T(8,128)S(1)} %bitcast.4), custom_call_target="tpu_custom_call" | custom-call | tf_op jit(solution)/shard_map/ocean_strips/pallas_call | solution.py:590
Async XLA Ops:
  2.3 11.2 %collective-permute-start.1 = (f32[81,8,128]{2,1,0:T(8,128)S(1)}, f32[81,8,128]{2,1,0:T(8,128)S(1)}, u32[]{:S(2)}, u32[]{:S(2)}) collective-permute-start(f32[81,8,128]{2,1,0:T(8,128)S(1)} %get-tuple-element.19.own), channel_id=1, source_target_pairs={{1,2},{3,4},{5,6},{7,8},{9,10},{11,12},{13,14},{2,1},{4,3},{6,5},{... | collective-permute-start | bytes 995336 | tf_op jit(solution)/shard_map/ppermute | solution.py:523
  3.0 10.5 %collective-permute-start = (f32[81,8,128]{2,1,0:T(8,128)S(1)}, f32[81,8,128]{2,1,0:T(8,128)S(1)}, u32[]{:S(2)}, u32[]{:S(2)}) collective-permute-start(f32[81,8,128]{2,1,0:T(8,128)S(1)} %get-tuple-element.19.own), channel_id=1, source_target_pairs={{0,1},{1,0},{2,3},{3,2},{4,5},{5,4},{6,7},{7,6},{8,9},{9,8},{10,11... | collective-permute-start | bytes 995336 | tf_op jit(solution)/shard_map/ppermute | solution.py:545
  8.5 5.0 %copy-start = (f32[3,8]{1,0:T(4,128)S(1)}, f32[3,8]{1,0:T(4,128)}, u32[]{:S(2)}) copy-start(f32[3,8]{1,0:T(4,128)} %table.1) | copy-start | bytes 292
  8.5 14.2 %all-to-all-start = ((f32[8,64,128]{2,1,0:T(8,128)}), f32[8,64,128]{2,1,0:T(8,128)}, u32[]{:S(2)}, u32[]{:S(2)}) async-start(f32[8,64,128]{2,1,0:T(8,128)} %bitcast), calls=%async_computation | async-start | bytes 524288 | tf_op jit(solution)/shard_map/all_to_all | solution.py:537
  22.7 1.7 %collective-permute-start.2 = (f32[512,128]{1,0:T(8,128)}, f32[512,128]{1,0:T(8,128)S(1)}, u32[]{:S(2)}, u32[]{:S(2)}) collective-permute-start(f32[512,128]{1,0:T(8,128)} %bitcast.1.arrived), channel_id=1, source_target_pairs={{0,1},{1,0},{2,3},{3,2},{4,5},{5,4},{6,7},{7,6},{8,9},{9,8},{10,11... | collective-permute-start | bytes 786440 | tf_op jit(solution)/shard_map/ppermute | solution.py:557
  28.9 11.6 %all-to-all-start.1 = ((f32[16,16,128]{2,1,0:T(8,128)}), f32[16,16,128]{2,1,0:T(8,128)S(1)}, u32[]{:S(2)}, u32[]{:S(2)}) async-start(f32[16,16,128]{2,1,0:T(8,128)} %bitcast.2), calls=%async_computation.1 | async-start | bytes 262144 | tf_op jit(solution)/shard_map/all_to_all | solution.py:577

commit v7 on v6

--- a/solution.py
+++ b/solution.py
@@ -253,28 +253,37 @@
     )
 
 
-def begin_kernel(plan, table, own, mate, other, vel, stress, mats):
+def begin_kernel(plan, table, own, mate, both, vel, stress, mats):
     cells, sub = plan.cells, plan.sub
     sh = Shifts(plan)
     odd = odd_device()
+    here = lax.axis_index("map")
+    inner = (here > 0) & (here < plan.n - 1)
     starts = (HALO, (HALO + cells) * (1 - odd), (HALO + cells) * odd)
-    for start, ref in zip(starts, (own, mate, other)):
-        def bring(x, start=start, ref=ref):
+    reads = (
+        lambda i: own[i],
+        lambda i: mate[i],
+        lambda i: jnp.where(inner, both[odd, i], 0.0),
+    )
+    for start, read in zip(starts, reads):
+        def bring(x, start=start, read=read):
             j = start + x
             for f in range(3):
-                vel[f, j] = ref[f * cells + x]
+                vel[f, j] = read(f * cells + x)
             for f in range(6):
-                stress[f, j] = ref[(3 + f) * cells + x]
-            zone = ref[9 * cells + x]
+                stress[f, j] = read((3 + f) * cells + x)
+            zone = read(9 * cells + x)
             values = [jnp.zeros_like(zone) for _ in range(3)]
             for z in range(ZONES):
                 here = zone == float(z + 1)
                 values = [jnp.where(here, table[c, z], values[c]) for c in range(3)]
             for c in range(3):
                 mats[c, j] = values[c] * HALF
-            slip = jnp.broadcast_to(ref[10 * cells, pl.ds(x, 1), :], (sub, plan.lanes))
+            slips = read(10 * cells)
+            slip = jnp.sum(jnp.where(sh.row == x, slips, 0.0), axis=0, keepdims=True)
+            slip = jnp.broadcast_to(slip, (sub, plan.lanes))
             mats[FAULT, j] = jnp.where(sh.row == (plan.depth // 2) % sub, DT * slip, 0.0)
-            mats[FLOOR, j] = sh.seafloor(ref[VZ * cells + x])
+            mats[FLOOR, j] = sh.seafloor(vel[VZ, j])
 
         plan.planes(0, cells, bring)
 
@@ -510,9 +519,11 @@
     def pinned(array):
         return pltpu.with_memory_space_constraint(array, pltpu.HBM)
 
+    def near(array):
+        return pltpu.with_memory_space_constraint(array, pltpu.VMEM) if plan.unrolled else array
+
     mates = [(i, i ^ 1) for i in range(n)]
-    others = [(i, i + 1) for i in range(1, n - 1, 2)]
-    others += [(target, source) for source, target in others]
+    pairs = [[0, n - 1]] + [[i, i + 1] for i in range(1, n - 1, 2)]
     crust, ocean_near, bathy_near = call(
         crust_kernel,
         "crust_planes",
@@ -520,7 +531,7 @@
         [hbm] * 6,
         [held(velocity), held(stress), held(zones), held(slip), pltpu.SemaphoreType.DMA((6,))],
     )(*(pinned(a) for a in (velocity, stress, zones, slip, ocean, bathy)))
-    other = lax.ppermute(crust, "map", others)
+    both = lax.all_gather(crust, "map", axis_index_groups=pairs)
     message = call(
         ocean_kernel,
         "ocean_rows",
@@ -534,6 +545,7 @@
             pltpu.VMEM((n * plan.strips, LANES), F32),
         ],
     )(ocean_near, bathy_near)
+    message, crust = lax.optimization_barrier((message, crust))
     arrived = lax.all_to_all(
         message.reshape(n // 2, 2 * plan.rows, LANES),
         "map",
@@ -550,9 +562,9 @@
         [smem] + [vmem] * 3,
         [],
         cost_estimate=pl.CostEstimate(
-            flops=10**12, bytes_accessed=2 * 10**9, transcendentals=0
+            flops=10**11, bytes_accessed=200 * 10**6, transcendentals=0
         ),
-    )(materials, crust, mate, other)
+    )(materials, crust, mate, both)
     arrived, vel = lax.optimization_barrier((arrived, vel))
     swapped = lax.ppermute(arrived, "map", mates)
     vel, strs, loads, back = call(
@@ -573,7 +585,7 @@
             pltpu.VMEM((plan.depth, lanes), F32),
         ],
         input_output_aliases={2: 0, 3: 1},
-    )(arrived, swapped, vel, strs, mats)
+    )(*(near(a) for a in (arrived, swapped, vel, strs, mats)))
     returned = lax.all_to_all(
         back.reshape(n, plan.back_rows, LANES), "map", split_axis=0, concat_axis=0, tiled=True
     ).reshape(n * plan.back_rows, LANES)

time: 41.9 us -> 43.9 us (1.048)
  blocking collectives: 0 us -> 13.5 us
  waiting for transfers between devices: 15.7 us -> 7.36 us
  starting transfers between devices: 13.7 us -> 11.5 us
  Pallas kernels: 11.4 us -> 10.5 us
    all_gather x0 -> x1, blocking collectives: none -> 13.5 us  [on_device(): both = lax.all_gather(crust, 'map', axis_index_groups=pairs)]
    all_to_all x1, waiting for transfers between devices: 8.07 us -> 0.01 us  [on_device(): lax.all_to_all(message.reshape(n // 2, 2 * plan.rows, LANES), 'map', spli...]
    ppermute x1, starting transfers between devices: 4.35 us -> 0.45 us  [on_device(): mate = lax.ppermute(crust, 'map', mates)]
    all_to_all x1, starting transfers between devices: 5.01 us -> 6.8 us  [on_device(): lax.all_to_all(message.reshape(n // 2, 2 * plan.rows, LANES), 'map', spli...]
    pallas_call x1, Pallas kernels: 4.44 us -> 3.49 us  [on_device(): call(middle_kernel, 'substeps', (shape(3, width, sub, lanes), shape(6, wi...]
    ppermute x1 -> x0, starting transfers between devices: 0.68 us -> none  [on_device(): other = lax.ppermute(crust, 'map', others)]
    all_to_all x1, starting transfers between devices: 3.69 us -> 4.21 us  [on_device(): lax.all_to_all(back.reshape(n, plan.back_rows, LANES), 'map', split_axis=...]
  transfers between devices with their start and end apart: 5 -> 4, of which waited for: 3 -> 2; matrix products, arithmetic and copies ran while one was open for 0% -> 0% of each run, Pallas kernels for 10% -> 7%
where the time goes in v7:
time: 43.9 us; the launch traced here: 43.6 us
  blocking collectives  13.5 us (31%)
  starting transfers between devices  11.5 us (26%)
  Pallas kernels  10.5 us (24%)
  waiting for transfers between devices  7.36 us (17%)
  between operations  0.68 us (2%)
    all_gather x1, blocking collectives, on_device(): both = lax.all_gather(crust, 'map', axis_index_groups=pairs)  13.5 us
    all_to_all x1, starting transfers between devices, on_device(): lax.all_to_all(message.reshape(n // 2, 2 * plan.rows, LANES), 'map', spli...  6.8 us
    all_to_all x1, waiting for transfers between devices, on_device(): lax.all_to_all(back.reshape(n, plan.back_rows, LANES), 'map', split_axis=...  5.83 us
    all_to_all x1, starting transfers between devices, on_device(): lax.all_to_all(back.reshape(n, plan.back_rows, LANES), 'map', split_axis=...  4.21 us
    pallas_call x1, Pallas kernels, on_device(): call(middle_kernel, 'substeps', (shape(3, width, sub, lanes), shape(6, wi...  3.49 us
    pallas_call x1, Pallas kernels, on_device(): call(end_kernel, 'last_updates', (shape(*velocity.shape), shape(*stress.s...  2.1 us
    pallas_call x1, Pallas kernels, on_device(): call(crust_kernel, 'crust_planes', (shape(10 * cells + 1, sub, lanes), li...  1.7 us
    ppermute x1, waiting for transfers between devices, on_device(): swapped = lax.ppermute(arrived, 'map', mates)  1.52 us
  transfers between devices with their start and end apart: 4, of which 2 were waited for; matrix products, arithmetic and copies ran while one was open for 0% of the time, Pallas kernels for 7%

profile of v7, /device:TPU:0, one launch (start us, length us, event | category | flops | bytes accessed | tf_op | source)
XLA Modules:
  0.0 43.6 jit_solution(12883837502296751184)
XLA Ops:
  0.6 1.7 %crust_planes.1 = (f32[81,8,128]{2,1,0:T(8,128)S(1)}, f32[4,2,32,128]{3,2,1,0:T(8,128)S(1)}, s32[2,128]{1,0:T(2,128)S(1)}) custom-call(f32[3,8,32,32]{3,2,1,0:T(8,128)} %vel_ref.1, f32[6,8,32,32]{3,2,1,0:T(8,128)} %stress_ref.1, s32[8,32,32]{2,1,0:T(8,128)} %zones_ref.1, f32[8,32]{1,0:T(8,128)} %slip_ref.1, f32[4,2,32,128]{3,2,1,0:T(8,128)} %ocean_ref.1, ...), custom_call_target="tpu_custom_call" | custom-call | tf_op jit(solution)/shard_map/crust_planes/pallas_call | solution.py:527
  2.3 1.2 %ocean_rows.1 = f32[512,128]{1,0:T(8,128)} custom-call(f32[4,2,32,128]{3,2,1,0:T(8,128)S(1)} %get-tuple-element.19.ocean, s32[2,128]{1,0:T(2,128)S(1)} %get-tuple-element.20.bathy), custom_call_target="tpu_custom_call" | custom-call | tf_op jit(solution)/shard_map/ocean_rows/pallas_call | solution.py:535
  3.5 0.5 %collective-permute-start = (f32[81,8,128]{2,1,0:T(8,128)S(1)}, f32[81,8,128]{2,1,0:T(8,128)S(1)}, u32[]{:S(2)}, u32[]{:S(2)}) collective-permute-start(f32[81,8,128]{2,1,0:T(8,128)S(1)} %get-tuple-element.23.own), channel_id=1, source_target_pairs={{0,1},{1,0},{2,3},{3,2},{4,5},{5,4},{6,7},{7,6},{8,9},{9,8},{10,11... | collective-permute-start | bytes 995336 | tf_op jit(solution)/shard_map/ppermute | solution.py:557
  3.9 6.8 %all-to-all-start = ((f32[8,64,128]{2,1,0:T(8,128)}), f32[8,64,128]{2,1,0:T(8,128)S(1)}, u32[]{:S(2)}, u32[]{:S(2)}) async-start(f32[8,64,128]{2,1,0:T(8,128)} %bitcast), calls=%async_computation | async-start | bytes 524288 | tf_op jit(solution)/shard_map/all_to_all | solution.py:549
  10.7 0.0 copy-start
  10.8 13.5 %all-gather = f32[162,8,128]{2,1,0:T(8,128)S(1)} all-gather(f32[81,8,128]{2,1,0:T(8,128)S(1)} %get-tuple-element.23.own), channel_id=2, replica_groups={{0,15},{1,2},{3,4},{5,6},{7,8},{9,10},{11,12},{13,14},{16,31},{17,18},{..., dimensions={0}, use_global_device_ids=true | all-gather | bytes 995328 | tf_op jit(solution)/shard_map/all_gather | solution.py:534
  24.2 0.0 collective-permute-done.mate
  24.2 0.0 copy-done
  24.2 1.1 %first_velocity.1 = (f32[3,24,8,128]{3,2,1,0:T(8,128)S(1)}, f32[6,24,8,128]{3,2,1,0:T(8,128)S(1)}, f32[5,24,8,128]{3,2,1,0:T(8,128)S(1)}) custom-call(f32[3,8]{1,0:T(4,128)S(1)} %copy-done, f32[81,8,128]{2,1,0:T(8,128)S(1)} %get-tuple-element.23.own, f32[81,8,128]{2,1,0:T(8,128)S(1)} %collective-permute-done.mate, f32[2,81,8,128]{3,2,1,0:T(8,128)S(1)} %bitcast.7), custom_call_target="tpu_custom_call" | custom-call | flops 99999997952 | bytes 200000000 | tf_op jit(solution)/shard_map/first_velocity/pallas_call | solution.py:558
  25.4 0.0 all-to-all-done
  25.4 0.1 collective-permute-start.1
  25.5 1.5 %collective-permute-done.1.swapped = f32[512,128]{1,0:T(8,128)S(1)} collective-permute-done((f32[512,128]{1,0:T(8,128)S(1)}, f32[512,128]{1,0:T(8,128)S(1)}, u32[]{:S(2)}, u32[]{:S(2)}) %collective-permute-start.1) | collective-permute-done | bytes 262176 | tf_op jit(solution)/shard_map/ppermute | solution.py:569
  27.0 3.5 %substeps.1 = (f32[3,24,8,128]{3,2,1,0:T(8,128)S(1)}, f32[6,24,8,128]{3,2,1,0:T(8,128)S(1)}, f32[24,8,128]{2,1,0:T(8,128)S(1)}, f32[256,128]{1,0:T(8,128)}) custom-call(f32[512,128]{1,0:T(8,128)S(1)} %bitcast.6, f32[512,128]{1,0:T(8,128)S(1)} %collective-permute-done.1.swapped, ...), custom_call_target="tpu_custom_call", output_to_operand_aliasing={{0}: (2, {}), {1}: (3, {})} | custom-call | tf_op jit(solution)/shard_map/substeps/pallas_call | solution.py:570
  30.5 4.2 %all-to-all-start.1 = ((f32[16,16,128]{2,1,0:T(8,128)}), f32[16,16,128]{2,1,0:T(8,128)S(1)}, u32[]{:S(2)}, u32[]{:S(2)}) async-start(f32[16,16,128]{2,1,0:T(8,128)} %bitcast.3), calls=%async_computation.1 | async-start | bytes 262144 | tf_op jit(solution)/shard_map/all_to_all | solution.py:589
  34.7 2.1 %last_updates.1 = (f32[3,8,32,32]{3,2,1,0:T(8,128)}, f32[6,8,32,32]{3,2,1,0:T(8,128)}) custom-call(f32[3,24,8,128]{3,2,1,0:T(8,128)S(1)} %get-tuple-element.29.vel_in, f32[6,24,8,128]{3,2,1,0:T(8,128)S(1)} %get-tuple-element.30.stress_in, f32[5,24,8,128]{3,2,1,0:T(8,128)S(1)} %get-tuple-element.28.mats, f32[24,8,128]{2,1,0:T(8,128)S(1)} %get-tuple-element.31.loads), custom_call_target="tpu_custom_call" | custom-call | tf_op jit(solution)/shard_map/last_updates/pallas_call | solution.py:592
  36.8 5.8 %all-to-all-done.1 = f32[16,16,128]{2,1,0:T(8,128)S(1)} async-done(((f32[16,16,128]{2,1,0:T(8,128)}), f32[16,16,128]{2,1,0:T(8,128)S(1)}, u32[]{:S(2)}, u32[]{:S(2)}) %all-to-all-start.1) | async-done | bytes 131104 | tf_op jit(solution)/shard_map/all_to_all | solution.py:589
  42.6 0.9 %ocean_strips.1 = f32[4,2,32,128]{3,2,1,0:T(8,128)} custom-call(f32[256,128]{1,0:T(8,128)S(1)} %bitcast.8), custom_call_target="tpu_custom_call" | custom-call | tf_op jit(solution)/shard_map/ocean_strips/pallas_call | solution.py:602
Async XLA Ops:
  3.5 20.8 %collective-permute-start = (f32[81,8,128]{2,1,0:T(8,128)S(1)}, f32[81,8,128]{2,1,0:T(8,128)S(1)}, u32[]{:S(2)}, u32[]{:S(2)}) collective-permute-start(f32[81,8,128]{2,1,0:T(8,128)S(1)} %get-tuple-element.23.own), channel_id=1, source_target_pairs={{0,1},{1,0},{2,3},{3,2},{4,5},{5,4},{6,7},{7,6},{8,9},{9,8},{10,11... | collective-permute-start | bytes 995336 | tf_op jit(solution)/shard_map/ppermute | solution.py:557
  3.9 21.4 %all-to-all-start = ((f32[8,64,128]{2,1,0:T(8,128)}), f32[8,64,128]{2,1,0:T(8,128)S(1)}, u32[]{:S(2)}, u32[]{:S(2)}) async-start(f32[8,64,128]{2,1,0:T(8,128)} %bitcast), calls=%async_computation | async-start | bytes 524288 | tf_op jit(solution)/shard_map/all_to_all | solution.py:549
  10.7 13.5 %copy-start = (f32[3,8]{1,0:T(4,128)S(1)}, f32[3,8]{1,0:T(4,128)}, u32[]{:S(2)}) copy-start(f32[3,8]{1,0:T(4,128)} %table.1) | copy-start | bytes 292
  25.4 1.6 %collective-permute-start.1 = (f32[512,128]{1,0:T(8,128)S(1)}, f32[512,128]{1,0:T(8,128)S(1)}, u32[]{:S(2)}, u32[]{:S(2)}) collective-permute-start(f32[512,128]{1,0:T(8,128)S(1)} %bitcast.5), channel_id=1, source_target_pairs={{0,1},{1,0},{2,3},{3,2},{4,5},{5,4},{6,7},{7,6},{8,9},{9,8},{10,11... | collective-permute-start | bytes 786440 | tf_op jit(solution)/shard_map/ppermute | solution.py:569
  30.5 12.2 %all-to-all-start.1 = ((f32[16,16,128]{2,1,0:T(8,128)}), f32[16,16,128]{2,1,0:T(8,128)S(1)}, u32[]{:S(2)}, u32[]{:S(2)}) async-start(f32[16,16,128]{2,1,0:T(8,128)} %bitcast.3), calls=%async_computation.1 | async-start | bytes 262144 | tf_op jit(solution)/shard_map/all_to_all | solution.py:589

commit v8 on v6

--- a/solution.py
+++ b/solution.py
@@ -72,9 +72,28 @@
     return out
 
 
-def ocean_kernel(plan, ocean, bathy, message, turned, grouped, extra):
-    cells, sub, chunks, n, strips = plan.cells, plan.sub, plan.chunks, plan.n, plan.strips
-    block, sent, rows = plan.block, plan.sent_groups, plan.rows
+def pack_kernel(
+    plan, vel_ref, stress_ref, zones_ref, slip_ref, ocean_ref, bathy_ref, crust, message,
+    vel, stress, zones, slip, ocean, bathy, turned, grouped, extra, sems,
+):
+    cells, sub, chunks, ny = plan.cells, plan.sub, plan.chunks, plan.ny
+    n, strips, block, sent, rows = plan.n, plan.strips, plan.block, plan.sent_groups, plan.rows
+    pairs = (
+        (ocean_ref, ocean),
+        (bathy_ref, bathy),
+        (vel_ref, vel),
+        (stress_ref, stress),
+        (zones_ref, zones),
+        (slip_ref, slip),
+    )
+    copies = [
+        pltpu.make_async_copy(source, target, sems.at[i])
+        for i, (source, target) in enumerate(pairs)
+    ]
+    for copy in copies:
+        copy.start()
+    copies[0].wait()
+    copies[1].wait()
     border = jnp.zeros((plan.lead, plan.halo_groups, LANES), F32)
     count = plan.nx // chunks
     grouped[:, : plan.halo_groups, :] = border
@@ -126,43 +145,22 @@
                 new = jnp.where((lane >= slot + sub) & (lane < slot + 2 * sub), floor, new)
                 message[pl.ds(at, pairs, stride=2 * rows), :] = new
 
-
-def crust_kernel(
-    plan, vel_ref, stress_ref, zones_ref, slip_ref, ocean_ref, bathy_ref,
-    crust, ocean, bathy, vel, stress, zones, slip, sems,
-):
-    cells, sub, chunks, ny = plan.cells, plan.sub, plan.chunks, plan.ny
-    pairs = (
-        (vel_ref, vel),
-        (stress_ref, stress),
-        (zones_ref, zones),
-        (slip_ref, slip),
-        (ocean_ref, ocean),
-        (bathy_ref, bathy),
-    )
-    copies = [
-        pltpu.make_async_copy(source, target, sems.at[i])
-        for i, (source, target) in enumerate(pairs)
-    ]
-    for copy in copies:
-        copy.start()
-
     def joined(ref, *at):
         parts = [ref[(*at, pl.ds(kc * sub, sub), slice(None))] for kc in range(chunks)]
         return jnp.concatenate(parts, axis=-1) if chunks > 1 else parts[0]
 
-    copies[0].wait()
+    copies[2].wait()
     for f in range(3):
         for x in range(cells):
             crust[f * cells + x] = joined(vel, f, x)
-    copies[1].wait()
+    copies[3].wait()
     for f in range(6):
         for x in range(cells):
             crust[(3 + f) * cells + x] = joined(stress, f, x)
-    copies[2].wait()
+    copies[4].wait()
     for x in range(cells):
         crust[9 * cells + x] = (joined(zones, x) + 1).astype(F32)
-    copies[3].wait()
+    copies[5].wait()
     fault_chunk = (plan.depth // 2) // sub
     pieces = [
         slip[...] if kc == fault_chunk else jnp.zeros((cells, ny), F32) for kc in range(chunks)
@@ -171,8 +169,6 @@
     if sub > cells:
         fault = jnp.concatenate([fault, jnp.zeros((sub - cells, plan.lanes), F32)], axis=0)
     crust[10 * cells] = fault
-    copies[4].wait()
-    copies[5].wait()
 
 
 class Shifts:
@@ -288,26 +284,25 @@
 
 def middle_kernel(
     plan, arrived, swapped, vel_in, stress_in, mats, vel, stress, loads, message,
-    oc, water, bottom, gather, depths,
+    oc, water, bottom, floors, gather, depths,
 ):
     sub, chunks, n, strips = plan.sub, plan.chunks, plan.n, plan.strips
     width, sent = plan.width, plan.sent_groups
     sh = Shifts(plan)
     odd = odd_device()
-
+    mate = 1 - odd
     half = n // 2
-    mate = 1 - odd
-
-    def turn(owner, group):
+
+    def turn(slot, owner, group):
         for core, ref in ((odd, arrived), (mate, swapped)):
             for kc in range(chunks):
                 for yl in range(strips):
                     at = owner * plan.rows + (kc * strips + yl) * sent + group
                     to = kc * plan.ny + core * strips + yl
-                    gather[pl.ds(to, half, stride=2 * strips), :] = ref[
+                    gather[slot, pl.ds(to, half, stride=2 * strips), :] = ref[
                         pl.ds(at, half, stride=2 * plan.rows), :
                     ]
-        return gather[...].T
+        return gather[slot].T
 
     def spread(turned, group):
         for i in range(chunks):
@@ -317,15 +312,17 @@
 
     ends = []
     for group in range(sent):
-        turned = turn(odd, group)
+        turned = turn(group, odd, group)
         spread(turned, group + plan.halo_groups * odd)
         if group == 0:
             ends.append((turned[2 * sub : 3 * sub], turned[3 * sub : 4 * sub]))
         if group == sent - 1:
             ends.append((turned[LANES - 2 * sub : LANES - sub], turned[LANES - sub :]))
     for group in range(plan.halo_groups):
-        spread(turn(mate, group + plan.own_groups * odd), group + sent * mate)
-    turned = turn(mate, plan.own_groups - odd)
+        spread(
+            turn(sent + group, mate, group + plan.own_groups * odd), group + sent * mate
+        )
+    turned = turn(sent + plan.halo_groups, mate, plan.own_groups - odd)
     is_odd = odd == 1
     oc[0, (width + 1) * odd] = jnp.where(is_odd, ends[1][0], ends[0][0])
     oc[0, (width + 1) * mate] = jnp.where(
@@ -354,63 +351,75 @@
     plan.planes(1, width + 1, mask_x)
     plan.planes(2, width, mask_yw)
 
-    for t in range(STEPS):
+    def flow_x(j):
+        oc[1, j + 1] = water[j + 1] * (oc[1, j + 1] - HALF * (oc[0, j + 2] - oc[0, j]))
+
+    def flow(j):
+        p = oc[0, j + 1]
+        wet = water[j + 1]
+        oc[2, j + 1] = wet * (oc[2, j + 1] - HALF * sh.dy(p))
+        rise = sh.below(p) + bottom[j + 1] * p - sh.above(p, -p)
+        oc[3, j + 1] = wet * (oc[3, j + 1] - (HALF * rise + (DT * GRAV) * p))
+
+    def press(j, floor):
+        w = oc[3, j + 1]
+        rise = sh.below(w) + bottom[j + 1] * floor - sh.above(w, w)
+        total = oc[1, j + 2] - oc[1, j] + sh.dy(oc[2, j + 1]) + rise
+        p = water[j + 1] * (oc[0, j + 1] - (HALF * KBULK) * total)
+        oc[0, j + 1] = p
+        column = jnp.sum(bottom[j + 1] * p, axis=0, keepdims=True)
+        column = jnp.broadcast_to(sh.over_chunks(column), (sub, plan.lanes))
+        loads[j] = jnp.where(sh.top, column, 0.0)
+
+    def first_load(j):
+        for f in (VX, VY):
+            vel[f, j] = vel_in[f, j]
+        vz = vel_in[VZ, j] + mats[BUOY, j] * loads[j]
+        vel[VZ, j] = vz
+        floors[j] = sh.seafloor(vz)
+
+    def move(j):
+        ax, ay, az = acceleration(sh, stress, j)
+        b = mats[BUOY, j]
+        vel[VX, j] = vel[VX, j] + b * ax
+        vel[VY, j] = vel[VY, j] + b * ay
+        vz = vel[VZ, j] + b * (az + loads[j])
+        vel[VZ, j] = vz
+        floors[j] = sh.seafloor(vz)
+
+    def strain(j, source):
+        for f, value in enumerate(strained(sh, vel, source, mats, j)):
+            stress[f, j] = value
+
+    plan.planes(0, width, flow_x)
+    plan.planes(1, width - 1, flow)
+    plan.planes(1, width - 1, lambda j: press(j, mats[FLOOR, j]))
+    for t in range(STEPS - 1):
         first, last = 2 * t, width - 2 * t
-        before = t == 0
-
-        def flow_x(j):
-            oc[1, j + 1] = water[j + 1] * (oc[1, j + 1] - HALF * (oc[0, j + 2] - oc[0, j]))
-
-        def flow(j):
-            p = oc[0, j + 1]
-            wet = water[j + 1]
-            oc[2, j + 1] = wet * (oc[2, j + 1] - HALF * sh.dy(p))
-            rise = sh.below(p) + bottom[j + 1] * p - sh.above(p, -p)
-            oc[3, j + 1] = wet * (oc[3, j + 1] - (HALF * rise + (DT * GRAV) * p))
-
-        def press(j):
-            w = oc[3, j + 1]
-            floor = mats[FLOOR, j] if before else sh.seafloor(vel[VZ, j])
-            rise = sh.below(w) + bottom[j + 1] * floor - sh.above(w, w)
-            total = oc[1, j + 2] - oc[1, j] + sh.dy(oc[2, j + 1]) + rise
-            oc[0, j + 1] = water[j + 1] * (oc[0, j + 1] - (HALF * KBULK) * total)
-
-        def load(j):
-            column = jnp.sum(bottom[j + 1] * oc[0, j + 1], axis=0, keepdims=True)
-            column = jnp.broadcast_to(sh.over_chunks(column), (sub, plan.lanes))
-            return jnp.where(sh.top, column, 0.0)
-
-        plan.planes(first, last, flow_x)
-        plan.planes(first + 1, last - 1, flow)
-        plan.planes(first + 1, last - 1, press)
-        if before:
-            def add_load(j):
-                for f in (VX, VY):
-                    vel[f, j] = vel_in[f, j]
-                vel[VZ, j] = vel_in[VZ, j] + mats[BUOY, j] * load(j)
-
-            plan.planes(first + 1, last - 1, add_load)
-        elif t < STEPS - 1:
-            def move(j):
-                ax, ay, az = acceleration(sh, stress, j)
-                b = mats[BUOY, j]
-                vel[VX, j] = vel[VX, j] + b * ax
-                vel[VY, j] = vel[VY, j] + b * ay
-                vel[VZ, j] = vel[VZ, j] + b * (az + load(j))
-
-            plan.planes(first + 1, last - 1, move)
-        else:
-            def keep(j):
-                loads[j] = load(j)
-
-            plan.planes(first + 1, last - 1, keep)
-        if t < STEPS - 2:
-            def strain(j):
-                source = stress_in if before else stress
-                for f, value in enumerate(strained(sh, vel, source, mats, j)):
-                    stress[f, j] = value
-
-            plan.planes(first + 2, last - 2, strain)
+
+        def velocity_and_flow(j, t=t, first=first, last=last):
+            if t == 0:
+                first_load(j)
+            else:
+                move(j)
+            if plan.unrolled and first + 2 <= j < last - 2:
+                flow_x(j)
+                if first + 3 <= j < last - 3:
+                    flow(j)
+
+        def stress_and_press(j, t=t, first=first, last=last):
+            if t < STEPS - 2:
+                strain(j, stress_in if t == 0 else stress)
+            if plan.unrolled and first + 3 <= j < last - 3:
+                press(j, floors[j])
+
+        plan.planes(first + 1, last - 1, velocity_and_flow)
+        if not plan.unrolled:
+            plan.planes(first + 2, last - 2, flow_x)
+            plan.planes(first + 3, last - 3, flow)
+        plan.planes(first + 2, last - 2, stress_and_press)
+        if not plan.unrolled:
+            plan.planes(first + 3, last - 3, lambda j: press(j, floors[j]))
 
     for group in range(plan.own_groups):
         stacked = jnp.concatenate(
@@ -421,12 +430,12 @@
             ],
             axis=0,
         )
-        gather[...] = stacked.T
+        gather[group] = stacked.T
         for kc in range(chunks):
             for yl in range(strips):
                 at = group * plan.lead + kc * strips + yl
                 message[pl.ds(at, n, stride=plan.back_rows), :] = gather[
-                    pl.ds(kc * plan.ny + yl, n, stride=strips), :
+                    group, pl.ds(kc * plan.ny + yl, n, stride=strips), :
                 ]
 
 
@@ -510,30 +519,28 @@
     def pinned(array):
         return pltpu.with_memory_space_constraint(array, pltpu.HBM)
 
+    def near(array):
+        return pltpu.with_memory_space_constraint(array, pltpu.VMEM) if plan.unrolled else array
+
     mates = [(i, i ^ 1) for i in range(n)]
     others = [(i, i + 1) for i in range(1, n - 1, 2)]
     others += [(target, source) for source, target in others]
-    crust, ocean_near, bathy_near = call(
-        crust_kernel,
-        "crust_planes",
-        (shape(10 * cells + 1, sub, lanes), like(ocean), like(bathy)),
+    crust, message = call(
+        pack_kernel,
+        "pack",
+        (shape(10 * cells + 1, sub, lanes), shape(n * plan.rows, LANES)),
         [hbm] * 6,
-        [held(velocity), held(stress), held(zones), held(slip), pltpu.SemaphoreType.DMA((6,))],
-    )(*(pinned(a) for a in (velocity, stress, zones, slip, ocean, bathy)))
-    other = lax.ppermute(crust, "map", others)
-    message = call(
-        ocean_kernel,
-        "ocean_rows",
-        shape(n * plan.rows, LANES),
-        [vmem] * 2,
-        [
+        [held(a) for a in (velocity, stress, zones, slip, ocean, bathy)]
+        + [
             pltpu.VMEM((plan.strips, plan.nx, LANES), F32),
             pltpu.VMEM(
                 (plan.lead, plan.nx // plan.chunks + 2 * plan.halo_groups, LANES), F32
             ),
             pltpu.VMEM((n * plan.strips, LANES), F32),
+            pltpu.SemaphoreType.DMA((6,)),
         ],
-    )(ocean_near, bathy_near)
+    )(*(pinned(a) for a in (velocity, stress, zones, slip, ocean, bathy)))
+    other = lax.ppermute(crust, "map", others)
     arrived = lax.all_to_all(
         message.reshape(n // 2, 2 * plan.rows, LANES),
         "map",
@@ -550,7 +557,7 @@
         [smem] + [vmem] * 3,
         [],
         cost_estimate=pl.CostEstimate(
-            flops=10**12, bytes_accessed=2 * 10**9, transcendentals=0
+            flops=10**11, bytes_accessed=200 * 10**6, transcendentals=0
         ),
     )(materials, crust, mate, other)
     arrived, vel = lax.optimization_barrier((arrived, vel))
@@ -569,11 +576,12 @@
             pltpu.VMEM((4, width + 2, sub, lanes), F32),
             pltpu.VMEM((width + 2, sub, lanes), F32),
             pltpu.VMEM((width + 2, sub, lanes), F32),
-            pltpu.VMEM((lanes, LANES), F32),
+            pltpu.VMEM((width, sub, lanes), F32),
+            pltpu.VMEM((plan.sent_groups + plan.halo_groups + 1, lanes, LANES), F32),
             pltpu.VMEM((plan.depth, lanes), F32),
         ],
         input_output_aliases={2: 0, 3: 1},
-    )(arrived, swapped, vel, strs, mats)
+    )(*(near(a) for a in (arrived, swapped, vel, strs, mats)))
     returned = lax.all_to_all(
         back.reshape(n, plan.back_rows, LANES), "map", split_axis=0, concat_axis=0, tiled=True
     ).reshape(n * plan.back_rows, LANES)

time: 41.9 us -> 45.2 us (1.079)
  Pallas kernels: 11.4 us -> 15.3 us
  waiting for transfers between devices: 15.7 us -> 15.2 us
    pallas_call x1, Pallas kernels: 4.44 us -> 8.54 us  [on_device(): call(middle_kernel, 'substeps', (shape(3, width, sub, lanes), shape(6, wi...]
    pallas_call x2 -> x1, Pallas kernels: 2.85 us -> 2.57 us  [on_device(): call(pack_kernel, 'pack', (shape(10 * cells + 1, sub, lanes), shape(n * p...]
  transfers between devices with their start and end apart: 5 -> 5, of which waited for: 3 -> 3; matrix products, arithmetic and copies ran while one was open for 0% -> 0% of each run, Pallas kernels for 10% -> 7%
where the time goes in v8:
time: 45.2 us; the launch traced here: 44.9 us
  Pallas kernels  15.3 us (34%)
  waiting for transfers between devices  15.2 us (34%)
  starting transfers between devices  13.7 us (30%)
  between operations  0.69 us (2%)
    pallas_call x1, Pallas kernels, on_device(): call(middle_kernel, 'substeps', (shape(3, width, sub, lanes), shape(6, wi...  8.54 us
    all_to_all x1, waiting for transfers between devices, on_device(): lax.all_to_all(message.reshape(n // 2, 2 * plan.rows, LANES), 'map', spli...  7.86 us
    all_to_all x1, waiting for transfers between devices, on_device(): lax.all_to_all(back.reshape(n, plan.back_rows, LANES), 'map', split_axis=...  5.83 us
    all_to_all x1, starting transfers between devices, on_device(): lax.all_to_all(message.reshape(n // 2, 2 * plan.rows, LANES), 'map', spli...  5.01 us
    ppermute x1, starting transfers between devices, on_device(): mate = lax.ppermute(crust, 'map', mates)  4.35 us
    all_to_all x1, starting transfers between devices, on_device(): lax.all_to_all(back.reshape(n, plan.back_rows, LANES), 'map', split_axis=...  3.69 us
    pallas_call x1, Pallas kernels, on_device(): call(pack_kernel, 'pack', (shape(10 * cells + 1, sub, lanes), shape(n * p...  2.57 us
    pallas_call x1, Pallas kernels, on_device(): call(end_kernel, 'last_updates', (shape(*velocity.shape), shape(*stress.s...  2.1 us
  transfers between devices with their start and end apart: 5, of which 3 were waited for; matrix products, arithmetic and copies ran while one was open for 0% of the time, Pallas kernels for 7%

profile of v8, /device:TPU:0, one launch (start us, length us, event | category | flops | bytes accessed | tf_op | source)
XLA Modules:
  0.0 44.9 jit_solution(14358196534613219656)
XLA Ops:
  0.6 2.6 %pack.1 = (f32[81,8,128]{2,1,0:T(8,128)S(1)}, f32[512,128]{1,0:T(8,128)}) custom-call(f32[3,8,32,32]{3,2,1,0:T(8,128)} %vel_ref.1, f32[6,8,32,32]{3,2,1,0:T(8,128)} %stress_ref.1, s32[8,32,32]{2,1,0:T(8,128)} %zones_ref.1, f32[8,32]{1,0:T(8,128)} %slip_ref.1, f32[4,2,32,128]{3,2,1,0:T(8,128)} %ocean_ref.1, s32[2,128]{1,0:T(2,128)} %bathy_ref.1), custom_call_target="tpu_custom_call" | custom-call | tf_op jit(solution)/shard_map/pack/pallas_call | solution.py:528
  3.2 0.7 %collective-permute-start.1 = (f32[81,8,128]{2,1,0:T(8,128)S(1)}, f32[81,8,128]{2,1,0:T(8,128)S(1)}, u32[]{:S(2)}, u32[]{:S(2)}) collective-permute-start(f32[81,8,128]{2,1,0:T(8,128)S(1)} %get-tuple-element.17.own), channel_id=1, source_target_pairs={{1,2},{3,4},{5,6},{7,8},{9,10},{11,12},{13,14},{2,1},{4,3},{6,5},{... | collective-permute-start | bytes 995336 | tf_op jit(solution)/shard_map/ppermute | solution.py:543
  3.9 4.3 %collective-permute-start = (f32[81,8,128]{2,1,0:T(8,128)S(1)}, f32[81,8,128]{2,1,0:T(8,128)S(1)}, u32[]{:S(2)}, u32[]{:S(2)}) collective-permute-start(f32[81,8,128]{2,1,0:T(8,128)S(1)} %get-tuple-element.17.own), channel_id=1, source_target_pairs={{0,1},{1,0},{2,3},{3,2},{4,5},{5,4},{6,7},{7,6},{8,9},{9,8},{10,11... | collective-permute-start | bytes 995336 | tf_op jit(solution)/shard_map/ppermute | solution.py:552
  8.2 0.0 copy-start
  8.2 5.0 %all-to-all-start = ((f32[8,64,128]{2,1,0:T(8,128)}), f32[8,64,128]{2,1,0:T(8,128)S(1)}, u32[]{:S(2)}, u32[]{:S(2)}) async-start(f32[8,64,128]{2,1,0:T(8,128)} %bitcast), calls=%async_computation | async-start | bytes 524288 | tf_op jit(solution)/shard_map/all_to_all | solution.py:544
  13.3 0.0 collective-permute-done.1.other
  13.3 0.0 collective-permute-done.mate
  13.3 0.0 copy-done
  13.3 1.1 %first_velocity.1 = (f32[3,24,8,128]{3,2,1,0:T(8,128)S(1)}, f32[6,24,8,128]{3,2,1,0:T(8,128)S(1)}, f32[5,24,8,128]{3,2,1,0:T(8,128)S(1)}) custom-call(f32[3,8]{1,0:T(4,128)S(1)} %copy-done, f32[81,8,128]{2,1,0:T(8,128)S(1)} %get-tuple-element.17.own, f32[81,8,128]{2,1,0:T(8,128)S(1)} %collective-permute-done.mate, f32[81,8,128]{2,1,0:T(8,128)S(1)} %collective-permute-done.1.other), custom_call_target="tpu_custom_call" | custom-call | flops 99999997952 | bytes 200000000 | tf_op jit(solution)/shard_map/first_velocity/pallas_call | solution.py:553
  14.4 7.9 %all-to-all-done = f32[8,64,128]{2,1,0:T(8,128)S(1)} async-done(((f32[8,64,128]{2,1,0:T(8,128)}), f32[8,64,128]{2,1,0:T(8,128)S(1)}, u32[]{:S(2)}, u32[]{:S(2)}) %all-to-all-start) | async-done | bytes 262176 | tf_op jit(solution)/shard_map/all_to_all | solution.py:544
  22.2 0.0 collective-permute-start.2
  22.2 1.5 %collective-permute-done.2.swapped = f32[512,128]{1,0:T(8,128)S(1)} collective-permute-done((f32[512,128]{1,0:T(8,128)S(1)}, f32[512,128]{1,0:T(8,128)S(1)}, u32[]{:S(2)}, u32[]{:S(2)}) %collective-permute-start.2) | collective-permute-done | bytes 262176 | tf_op jit(solution)/shard_map/ppermute | solution.py:564
  23.8 8.5 %substeps.1 = (f32[3,24,8,128]{3,2,1,0:T(8,128)S(1)}, f32[6,24,8,128]{3,2,1,0:T(8,128)S(1)}, f32[24,8,128]{2,1,0:T(8,128)S(1)}, f32[256,128]{1,0:T(8,128)}) custom-call(f32[512,128]{1,0:T(8,128)S(1)} %bitcast.5, f32[512,128]{1,0:T(8,128)S(1)} %collective-permute-done.2.swapped, ...), custom_call_target="tpu_custom_call", output_to_operand_aliasing={{0}: (2, {}), {1}: (3, {})} | custom-call | tf_op jit(solution)/shard_map/substeps/pallas_call | solution.py:565
  32.3 3.7 %all-to-all-start.1 = ((f32[16,16,128]{2,1,0:T(8,128)}), f32[16,16,128]{2,1,0:T(8,128)S(1)}, u32[]{:S(2)}, u32[]{:S(2)}) async-start(f32[16,16,128]{2,1,0:T(8,128)} %bitcast.2), calls=%async_computation.1 | async-start | bytes 262144 | tf_op jit(solution)/shard_map/all_to_all | solution.py:585
  36.0 2.1 %last_updates.1 = (f32[3,8,32,32]{3,2,1,0:T(8,128)}, f32[6,8,32,32]{3,2,1,0:T(8,128)}) custom-call(f32[3,24,8,128]{3,2,1,0:T(8,128)S(1)} %get-tuple-element.23.vel_in, f32[6,24,8,128]{3,2,1,0:T(8,128)S(1)} %get-tuple-element.24.stress_in, f32[5,24,8,128]{3,2,1,0:T(8,128)S(1)} %get-tuple-element.22.mats, f32[24,8,128]{2,1,0:T(8,128)S(1)} %get-tuple-element.25.loads), custom_call_target="tpu_custom_call" | custom-call | tf_op jit(solution)/shard_map/last_updates/pallas_call | solution.py:588
  38.1 5.8 %all-to-all-done.1 = f32[16,16,128]{2,1,0:T(8,128)S(1)} async-done(((f32[16,16,128]{2,1,0:T(8,128)}), f32[16,16,128]{2,1,0:T(8,128)S(1)}, u32[]{:S(2)}, u32[]{:S(2)}) %all-to-all-start.1) | async-done | bytes 131104 | tf_op jit(solution)/shard_map/all_to_all | solution.py:585
  44.0 0.9 %ocean_strips.1 = f32[4,2,32,128]{3,2,1,0:T(8,128)} custom-call(f32[256,128]{1,0:T(8,128)S(1)} %bitcast.6), custom_call_target="tpu_custom_call" | custom-call | tf_op jit(solution)/shard_map/ocean_strips/pallas_call | solution.py:598
Async XLA Ops:
  3.2 10.1 %collective-permute-start.1 = (f32[81,8,128]{2,1,0:T(8,128)S(1)}, f32[81,8,128]{2,1,0:T(8,128)S(1)}, u32[]{:S(2)}, u32[]{:S(2)}) collective-permute-start(f32[81,8,128]{2,1,0:T(8,128)S(1)} %get-tuple-element.17.own), channel_id=1, source_target_pairs={{1,2},{3,4},{5,6},{7,8},{9,10},{11,12},{13,14},{2,1},{4,3},{6,5},{... | collective-permute-start | bytes 995336 | tf_op jit(solution)/shard_map/ppermute | solution.py:543
  3.9 9.4 %collective-permute-start = (f32[81,8,128]{2,1,0:T(8,128)S(1)}, f32[81,8,128]{2,1,0:T(8,128)S(1)}, u32[]{:S(2)}, u32[]{:S(2)}) collective-permute-start(f32[81,8,128]{2,1,0:T(8,128)S(1)} %get-tuple-element.17.own), channel_id=1, source_target_pairs={{0,1},{1,0},{2,3},{3,2},{4,5},{5,4},{6,7},{7,6},{8,9},{9,8},{10,11... | collective-permute-start | bytes 995336 | tf_op jit(solution)/shard_map/ppermute | solution.py:552
  8.2 5.0 %copy-start = (f32[3,8]{1,0:T(4,128)S(1)}, f32[3,8]{1,0:T(4,128)}, u32[]{:S(2)}) copy-start(f32[3,8]{1,0:T(4,128)} %table.1) | copy-start | bytes 292
  8.2 14.0 %all-to-all-start = ((f32[8,64,128]{2,1,0:T(8,128)}), f32[8,64,128]{2,1,0:T(8,128)S(1)}, u32[]{:S(2)}, u32[]{:S(2)}) async-start(f32[8,64,128]{2,1,0:T(8,128)} %bitcast), calls=%async_computation | async-start | bytes 524288 | tf_op jit(solution)/shard_map/all_to_all | solution.py:544
  22.2 1.5 %collective-permute-start.2 = (f32[512,128]{1,0:T(8,128)S(1)}, f32[512,128]{1,0:T(8,128)S(1)}, u32[]{:S(2)}, u32[]{:S(2)}) collective-permute-start(f32[512,128]{1,0:T(8,128)S(1)} %bitcast.4), channel_id=1, source_target_pairs={{0,1},{1,0},{2,3},{3,2},{4,5},{5,4},{6,7},{7,6},{8,9},{9,8},{10,11... | collective-permute-start | bytes 786440 | tf_op jit(solution)/shard_map/ppermute | solution.py:564
  32.3 11.6 %all-to-all-start.1 = ((f32[16,16,128]{2,1,0:T(8,128)}), f32[16,16,128]{2,1,0:T(8,128)S(1)}, u32[]{:S(2)}, u32[]{:S(2)}) async-start(f32[16,16,128]{2,1,0:T(8,128)} %bitcast.2), calls=%async_computation.1 | async-start | bytes 262144 | tf_op jit(solution)/shard_map/all_to_all | solution.py:585

commit v9 on v8

--- a/solution.py
+++ b/solution.py
@@ -73,8 +73,8 @@
 
 
 def pack_kernel(
-    plan, vel_ref, stress_ref, zones_ref, slip_ref, ocean_ref, bathy_ref, crust, message,
-    vel, stress, zones, slip, ocean, bathy, turned, grouped, extra, sems,
+    plan, vel_ref, stress_ref, zones_ref, slip_ref, ocean_ref, bathy_ref, crust, message_out,
+    vel, stress, zones, slip, ocean, bathy, turned, grouped, extra, message, sems,
 ):
     cells, sub, chunks, ny = plan.cells, plan.sub, plan.chunks, plan.ny
     n, strips, block, sent, rows = plan.n, plan.strips, plan.block, plan.sent_groups, plan.rows
@@ -144,6 +144,7 @@
                 new = jnp.where((lane >= slot) & (lane < slot + sub), edge, old)
                 new = jnp.where((lane >= slot + sub) & (lane < slot + 2 * sub), floor, new)
                 message[pl.ds(at, pairs, stride=2 * rows), :] = new
+    message_out[...] = message[...]
 
     def joined(ref, *at):
         parts = [ref[(*at, pl.ds(kc * sub, sub), slice(None))] for kc in range(chunks)]
@@ -283,8 +284,8 @@
 
 
 def middle_kernel(
-    plan, arrived, swapped, vel_in, stress_in, mats, vel, stress, loads, message,
-    oc, water, bottom, floors, gather, depths,
+    plan, arrived, swapped, vel_in, stress_in, mats, vel_out, stress_out, loads_out, message,
+    vel, stress, loads, oc, water, bottom, floors, gather, rows, depths,
 ):
     sub, chunks, n, strips = plan.sub, plan.chunks, plan.n, plan.strips
     width, sent = plan.width, plan.sent_groups
@@ -292,6 +293,14 @@
     odd = odd_device()
     mate = 1 - odd
     half = n // 2
+
+    def bring(j):
+        for f in range(3):
+            vel[f, j] = vel_in[f, j]
+        for f in range(6):
+            stress[f, j] = stress_in[f, j]
+
+    plan.planes(0, width, bring)
 
     def turn(slot, owner, group):
         for core, ref in ((odd, arrived), (mate, swapped)):
@@ -372,9 +381,7 @@
         loads[j] = jnp.where(sh.top, column, 0.0)
 
     def first_load(j):
-        for f in (VX, VY):
-            vel[f, j] = vel_in[f, j]
-        vz = vel_in[VZ, j] + mats[BUOY, j] * loads[j]
+        vz = vel[VZ, j] + mats[BUOY, j] * loads[j]
         vel[VZ, j] = vz
         floors[j] = sh.seafloor(vz)
 
@@ -387,8 +394,8 @@
         vel[VZ, j] = vz
         floors[j] = sh.seafloor(vz)
 
-    def strain(j, source):
-        for f, value in enumerate(strained(sh, vel, source, mats, j)):
+    def strain(j):
+        for f, value in enumerate(strained(sh, vel, stress, mats, j)):
             stress[f, j] = value
 
     plan.planes(0, width, flow_x)
@@ -409,7 +416,7 @@
 
         def stress_and_press(j, t=t, first=first, last=last):
             if t < STEPS - 2:
-                strain(j, stress_in if t == 0 else stress)
+                strain(j)
             if plan.unrolled and first + 3 <= j < last - 3:
                 press(j, floors[j])
 
@@ -434,9 +441,20 @@
         for kc in range(chunks):
             for yl in range(strips):
                 at = group * plan.lead + kc * strips + yl
-                message[pl.ds(at, n, stride=plan.back_rows), :] = gather[
+                rows[pl.ds(at, n, stride=plan.back_rows), :] = gather[
                     group, pl.ds(kc * plan.ny + yl, n, stride=strips), :
                 ]
+    message[...] = rows[...]
+
+    def hand_on(j):
+        for f in range(3):
+            vel_out[f, j] = vel[f, j]
+        for f in range(6):
+            stress_out[f, j] = stress[f, j]
+        loads_out[j] = loads[j]
+
+    edge = 2 * STEPS - 3
+    plan.planes(edge, width - edge, hand_on)
 
 
 def end_kernel(plan, vel_in, stress_in, mats, loads, vel_out, stress_out, vel, stress):
@@ -537,6 +555,7 @@
                 (plan.lead, plan.nx // plan.chunks + 2 * plan.halo_groups, LANES), F32
             ),
             pltpu.VMEM((n * plan.strips, LANES), F32),
+            pltpu.VMEM((n * plan.rows, LANES), F32),
             pltpu.SemaphoreType.DMA((6,)),
         ],
     )(*(pinned(a) for a in (velocity, stress, zones, slip, ocean, bathy)))
@@ -573,14 +592,17 @@
         ),
         [vmem] * 5,
         [
+            pltpu.VMEM((3, width, sub, lanes), F32),
+            pltpu.VMEM((6, width, sub, lanes), F32),
+            pltpu.VMEM((width, sub, lanes), F32),
             pltpu.VMEM((4, width + 2, sub, lanes), F32),
             pltpu.VMEM((width + 2, sub, lanes), F32),
             pltpu.VMEM((width + 2, sub, lanes), F32),
             pltpu.VMEM((width, sub, lanes), F32),
             pltpu.VMEM((plan.sent_groups + plan.halo_groups + 1, lanes, LANES), F32),
+            pltpu.VMEM((n * plan.back_rows, LANES), F32),
             pltpu.VMEM((plan.depth, lanes), F32),
         ],
-        input_output_aliases={2: 0, 3: 1},
     )(*(near(a) for a in (arrived, swapped, vel, strs, mats)))
     returned = lax.all_to_all(
         back.reshape(n, plan.back_rows, LANES), "map", split_axis=0, concat_axis=0, tiled=True

time: 45.2 us -> 45.1 us (level)
  no operation moved by 1% of the time
where the time goes in v9:
time: 45.1 us; the launch traced here: 44.8 us
  waiting for transfers between devices  15.2 us (34%)
  Pallas kernels  15.1 us (33%)
  starting transfers between devices  13.7 us (30%)
  between operations  0.69 us (2%)
    pallas_call x1, Pallas kernels, on_device(): call(middle_kernel, 'substeps', (shape(3, width, sub, lanes), shape(6, wi...  8.41 us
    all_to_all x1, waiting for transfers between devices, on_device(): lax.all_to_all(message.reshape(n // 2, 2 * plan.rows, LANES), 'map', spli...  7.85 us
    all_to_all x1, waiting for transfers between devices, on_device(): lax.all_to_all(back.reshape(n, plan.back_rows, LANES), 'map', split_axis=...  5.83 us
    all_to_all x1, starting transfers between devices, on_device(): lax.all_to_all(message.reshape(n // 2, 2 * plan.rows, LANES), 'map', spli...  5.01 us
    ppermute x1, starting transfers between devices, on_device(): mate = lax.ppermute(crust, 'map', mates)  4.35 us
    all_to_all x1, starting transfers between devices, on_device(): lax.all_to_all(back.reshape(n, plan.back_rows, LANES), 'map', split_axis=...  3.69 us
    pallas_call x1, Pallas kernels, on_device(): call(pack_kernel, 'pack', (shape(10 * cells + 1, sub, lanes), shape(n * p...  2.6 us
    pallas_call x1, Pallas kernels, on_device(): call(end_kernel, 'last_updates', (shape(*velocity.shape), shape(*stress.s...  2.1 us
  transfers between devices with their start and end apart: 5, of which 3 were waited for; matrix products, arithmetic and copies ran while one was open for 0% of the time, Pallas kernels for 7%

profile of v9, /device:TPU:0, one launch (start us, length us, event | category | flops | bytes accessed | tf_op | source)
XLA Modules:
  0.0 44.8 jit_solution(12746879569577288085)
XLA Ops:
  0.6 2.6 %pack.1 = (f32[81,8,128]{2,1,0:T(8,128)S(1)}, f32[512,128]{1,0:T(8,128)}) custom-call(f32[3,8,32,32]{3,2,1,0:T(8,128)} %vel_ref.1, f32[6,8,32,32]{3,2,1,0:T(8,128)} %stress_ref.1, s32[8,32,32]{2,1,0:T(8,128)} %zones_ref.1, f32[8,32]{1,0:T(8,128)} %slip_ref.1, f32[4,2,32,128]{3,2,1,0:T(8,128)} %ocean_ref.1, s32[2,128]{1,0:T(2,128)} %bathy_ref.1), custom_call_target="tpu_custom_call" | custom-call | tf_op jit(solution)/shard_map/pack/pallas_call | solution.py:546
  3.2 0.7 %collective-permute-start.1 = (f32[81,8,128]{2,1,0:T(8,128)S(1)}, f32[81,8,128]{2,1,0:T(8,128)S(1)}, u32[]{:S(2)}, u32[]{:S(2)}) collective-permute-start(f32[81,8,128]{2,1,0:T(8,128)S(1)} %get-tuple-element.17.own), channel_id=1, source_target_pairs={{1,2},{3,4},{5,6},{7,8},{9,10},{11,12},{13,14},{2,1},{4,3},{6,5},{... | collective-permute-start | bytes 995336 | tf_op jit(solution)/shard_map/ppermute | solution.py:562
  3.9 4.3 %collective-permute-start = (f32[81,8,128]{2,1,0:T(8,128)S(1)}, f32[81,8,128]{2,1,0:T(8,128)S(1)}, u32[]{:S(2)}, u32[]{:S(2)}) collective-permute-start(f32[81,8,128]{2,1,0:T(8,128)S(1)} %get-tuple-element.17.own), channel_id=1, source_target_pairs={{0,1},{1,0},{2,3},{3,2},{4,5},{5,4},{6,7},{7,6},{8,9},{9,8},{10,11... | collective-permute-start | bytes 995336 | tf_op jit(solution)/shard_map/ppermute | solution.py:571
  8.3 0.0 copy-start
  8.3 5.0 %all-to-all-start = ((f32[8,64,128]{2,1,0:T(8,128)}), f32[8,64,128]{2,1,0:T(8,128)S(1)}, u32[]{:S(2)}, u32[]{:S(2)}) async-start(f32[8,64,128]{2,1,0:T(8,128)} %bitcast), calls=%async_computation | async-start | bytes 524288 | tf_op jit(solution)/shard_map/all_to_all | solution.py:563
  13.3 0.0 collective-permute-done.1.other
  13.3 0.0 collective-permute-done.mate
  13.3 0.0 copy-done
  13.3 1.1 %first_velocity.1 = (f32[3,24,8,128]{3,2,1,0:T(8,128)S(1)}, f32[6,24,8,128]{3,2,1,0:T(8,128)S(1)}, f32[5,24,8,128]{3,2,1,0:T(8,128)S(1)}) custom-call(f32[3,8]{1,0:T(4,128)S(1)} %copy-done, f32[81,8,128]{2,1,0:T(8,128)S(1)} %get-tuple-element.17.own, f32[81,8,128]{2,1,0:T(8,128)S(1)} %collective-permute-done.mate, f32[81,8,128]{2,1,0:T(8,128)S(1)} %collective-permute-done.1.other), custom_call_target="tpu_custom_call" | custom-call | flops 99999997952 | bytes 200000000 | tf_op jit(solution)/shard_map/first_velocity/pallas_call | solution.py:572
  14.4 7.9 %all-to-all-done = f32[8,64,128]{2,1,0:T(8,128)S(1)} async-done(((f32[8,64,128]{2,1,0:T(8,128)}), f32[8,64,128]{2,1,0:T(8,128)S(1)}, u32[]{:S(2)}, u32[]{:S(2)}) %all-to-all-start) | async-done | bytes 262176 | tf_op jit(solution)/shard_map/all_to_all | solution.py:563
  22.3 0.0 collective-permute-start.2
  22.3 1.5 %collective-permute-done.2.swapped = f32[512,128]{1,0:T(8,128)S(1)} collective-permute-done((f32[512,128]{1,0:T(8,128)S(1)}, f32[512,128]{1,0:T(8,128)S(1)}, u32[]{:S(2)}, u32[]{:S(2)}) %collective-permute-start.2) | collective-permute-done | bytes 262176 | tf_op jit(solution)/shard_map/ppermute | solution.py:583
  23.8 8.4 %substeps.1 = (f32[3,24,8,128]{3,2,1,0:T(8,128)S(1)}, f32[6,24,8,128]{3,2,1,0:T(8,128)S(1)}, f32[24,8,128]{2,1,0:T(8,128)S(1)}, f32[256,128]{1,0:T(8,128)}) custom-call(f32[512,128]{1,0:T(8,128)S(1)} %bitcast.5, f32[512,128]{1,0:T(8,128)S(1)} %collective-permute-done.2.swapped, f32[3,24,8,128]{3,2,1,0:T(8,128)S(1)} %get-tuple-element.20.vel_in, ...), custom_call_target="tpu_custom_call" | custom-call | tf_op jit(solution)/shard_map/substeps/pallas_call | solution.py:584
  32.2 3.7 %all-to-all-start.1 = ((f32[16,16,128]{2,1,0:T(8,128)}), f32[16,16,128]{2,1,0:T(8,128)S(1)}, u32[]{:S(2)}, u32[]{:S(2)}) async-start(f32[16,16,128]{2,1,0:T(8,128)} %bitcast.2), calls=%async_computation.1 | async-start | bytes 262144 | tf_op jit(solution)/shard_map/all_to_all | solution.py:607
  35.9 2.1 %last_updates.1 = (f32[3,8,32,32]{3,2,1,0:T(8,128)}, f32[6,8,32,32]{3,2,1,0:T(8,128)}) custom-call(f32[3,24,8,128]{3,2,1,0:T(8,128)S(1)} %get-tuple-element.23.vel_in, f32[6,24,8,128]{3,2,1,0:T(8,128)S(1)} %get-tuple-element.24.stress_in, f32[5,24,8,128]{3,2,1,0:T(8,128)S(1)} %get-tuple-element.22.mats, f32[24,8,128]{2,1,0:T(8,128)S(1)} %get-tuple-element.25.loads), custom_call_target="tpu_custom_call" | custom-call | tf_op jit(solution)/shard_map/last_updates/pallas_call | solution.py:610
  38.0 5.8 %all-to-all-done.1 = f32[16,16,128]{2,1,0:T(8,128)S(1)} async-done(((f32[16,16,128]{2,1,0:T(8,128)}), f32[16,16,128]{2,1,0:T(8,128)S(1)}, u32[]{:S(2)}, u32[]{:S(2)}) %all-to-all-start.1) | async-done | bytes 131104 | tf_op jit(solution)/shard_map/all_to_all | solution.py:607
  43.9 0.9 %ocean_strips.1 = f32[4,2,32,128]{3,2,1,0:T(8,128)} custom-call(f32[256,128]{1,0:T(8,128)S(1)} %bitcast.6), custom_call_target="tpu_custom_call" | custom-call | tf_op jit(solution)/shard_map/ocean_strips/pallas_call | solution.py:620
Async XLA Ops:
  3.2 10.1 %collective-permute-start.1 = (f32[81,8,128]{2,1,0:T(8,128)S(1)}, f32[81,8,128]{2,1,0:T(8,128)S(1)}, u32[]{:S(2)}, u32[]{:S(2)}) collective-permute-start(f32[81,8,128]{2,1,0:T(8,128)S(1)} %get-tuple-element.17.own), channel_id=1, source_target_pairs={{1,2},{3,4},{5,6},{7,8},{9,10},{11,12},{13,14},{2,1},{4,3},{6,5},{... | collective-permute-start | bytes 995336 | tf_op jit(solution)/shard_map/ppermute | solution.py:562
  3.9 9.4 %collective-permute-start = (f32[81,8,128]{2,1,0:T(8,128)S(1)}, f32[81,8,128]{2,1,0:T(8,128)S(1)}, u32[]{:S(2)}, u32[]{:S(2)}) collective-permute-start(f32[81,8,128]{2,1,0:T(8,128)S(1)} %get-tuple-element.17.own), channel_id=1, source_target_pairs={{0,1},{1,0},{2,3},{3,2},{4,5},{5,4},{6,7},{7,6},{8,9},{9,8},{10,11... | collective-permute-start | bytes 995336 | tf_op jit(solution)/shard_map/ppermute | solution.py:571
  8.3 5.0 %copy-start = (f32[3,8]{1,0:T(4,128)S(1)}, f32[3,8]{1,0:T(4,128)}, u32[]{:S(2)}) copy-start(f32[3,8]{1,0:T(4,128)} %table.1) | copy-start | bytes 292
  8.3 14.0 %all-to-all-start = ((f32[8,64,128]{2,1,0:T(8,128)}), f32[8,64,128]{2,1,0:T(8,128)S(1)}, u32[]{:S(2)}, u32[]{:S(2)}) async-start(f32[8,64,128]{2,1,0:T(8,128)} %bitcast), calls=%async_computation | async-start | bytes 524288 | tf_op jit(solution)/shard_map/all_to_all | solution.py:563
  22.3 1.5 %collective-permute-start.2 = (f32[512,128]{1,0:T(8,128)S(1)}, f32[512,128]{1,0:T(8,128)S(1)}, u32[]{:S(2)}, u32[]{:S(2)}) collective-permute-start(f32[512,128]{1,0:T(8,128)S(1)} %bitcast.4), channel_id=1, source_target_pairs={{0,1},{1,0},{2,3},{3,2},{4,5},{5,4},{6,7},{7,6},{8,9},{9,8},{10,11... | collective-permute-start | bytes 786440 | tf_op jit(solution)/shard_map/ppermute | solution.py:583
  32.2 11.6 %all-to-all-start.1 = ((f32[16,16,128]{2,1,0:T(8,128)}), f32[16,16,128]{2,1,0:T(8,128)S(1)}, u32[]{:S(2)}, u32[]{:S(2)}) async-start(f32[16,16,128]{2,1,0:T(8,128)} %bitcast.2), calls=%async_computation.1 | async-start | bytes 262144 | tf_op jit(solution)/shard_map/all_to_all | solution.py:607

commit v10 on v6

--- a/solution.py
+++ b/solution.py
@@ -72,9 +72,28 @@
     return out
 
 
-def ocean_kernel(plan, ocean, bathy, message, turned, grouped, extra):
-    cells, sub, chunks, n, strips = plan.cells, plan.sub, plan.chunks, plan.n, plan.strips
-    block, sent, rows = plan.block, plan.sent_groups, plan.rows
+def pack_kernel(
+    plan, vel_ref, stress_ref, zones_ref, slip_ref, ocean_ref, bathy_ref, crust, message_out,
+    vel, stress, zones, slip, ocean, bathy, turned, grouped, extra, message, sems,
+):
+    cells, sub, chunks, ny = plan.cells, plan.sub, plan.chunks, plan.ny
+    n, strips, block, sent, rows = plan.n, plan.strips, plan.block, plan.sent_groups, plan.rows
+    pairs = (
+        (ocean_ref, ocean),
+        (bathy_ref, bathy),
+        (vel_ref, vel),
+        (stress_ref, stress),
+        (zones_ref, zones),
+        (slip_ref, slip),
+    )
+    copies = [
+        pltpu.make_async_copy(source, target, sems.at[i])
+        for i, (source, target) in enumerate(pairs)
+    ]
+    for copy in copies:
+        copy.start()
+    copies[0].wait()
+    copies[1].wait()
     border = jnp.zeros((plan.lead, plan.halo_groups, LANES), F32)
     count = plan.nx // chunks
     grouped[:, : plan.halo_groups, :] = border
@@ -125,44 +144,24 @@
                 new = jnp.where((lane >= slot) & (lane < slot + sub), edge, old)
                 new = jnp.where((lane >= slot + sub) & (lane < slot + 2 * sub), floor, new)
                 message[pl.ds(at, pairs, stride=2 * rows), :] = new
-
-
-def crust_kernel(
-    plan, vel_ref, stress_ref, zones_ref, slip_ref, ocean_ref, bathy_ref,
-    crust, ocean, bathy, vel, stress, zones, slip, sems,
-):
-    cells, sub, chunks, ny = plan.cells, plan.sub, plan.chunks, plan.ny
-    pairs = (
-        (vel_ref, vel),
-        (stress_ref, stress),
-        (zones_ref, zones),
-        (slip_ref, slip),
-        (ocean_ref, ocean),
-        (bathy_ref, bathy),
-    )
-    copies = [
-        pltpu.make_async_copy(source, target, sems.at[i])
-        for i, (source, target) in enumerate(pairs)
-    ]
-    for copy in copies:
-        copy.start()
+    message_out[...] = message[...]
 
     def joined(ref, *at):
         parts = [ref[(*at, pl.ds(kc * sub, sub), slice(None))] for kc in range(chunks)]
         return jnp.concatenate(parts, axis=-1) if chunks > 1 else parts[0]
 
-    copies[0].wait()
+    copies[2].wait()
     for f in range(3):
         for x in range(cells):
             crust[f * cells + x] = joined(vel, f, x)
-    copies[1].wait()
+    copies[3].wait()
     for f in range(6):
         for x in range(cells):
             crust[(3 + f) * cells + x] = joined(stress, f, x)
-    copies[2].wait()
+    copies[4].wait()
     for x in range(cells):
         crust[9 * cells + x] = (joined(zones, x) + 1).astype(F32)
-    copies[3].wait()
+    copies[5].wait()
     fault_chunk = (plan.depth // 2) // sub
     pieces = [
         slip[...] if kc == fault_chunk else jnp.zeros((cells, ny), F32) for kc in range(chunks)
@@ -171,8 +170,6 @@
     if sub > cells:
         fault = jnp.concatenate([fault, jnp.zeros((sub - cells, plan.lanes), F32)], axis=0)
     crust[10 * cells] = fault
-    copies[4].wait()
-    copies[5].wait()
 
 
 class Shifts:
@@ -510,30 +507,29 @@
     def pinned(array):
         return pltpu.with_memory_space_constraint(array, pltpu.HBM)
 
+    def near(array):
+        return pltpu.with_memory_space_constraint(array, pltpu.VMEM) if plan.unrolled else array
+
     mates = [(i, i ^ 1) for i in range(n)]
     others = [(i, i + 1) for i in range(1, n - 1, 2)]
     others += [(target, source) for source, target in others]
-    crust, ocean_near, bathy_near = call(
-        crust_kernel,
-        "crust_planes",
-        (shape(10 * cells + 1, sub, lanes), like(ocean), like(bathy)),
+    crust, message = call(
+        pack_kernel,
+        "pack",
+        (shape(10 * cells + 1, sub, lanes), shape(n * plan.rows, LANES)),
         [hbm] * 6,
-        [held(velocity), held(stress), held(zones), held(slip), pltpu.SemaphoreType.DMA((6,))],
-    )(*(pinned(a) for a in (velocity, stress, zones, slip, ocean, bathy)))
-    other = lax.ppermute(crust, "map", others)
-    message = call(
-        ocean_kernel,
-        "ocean_rows",
-        shape(n * plan.rows, LANES),
-        [vmem] * 2,
-        [
+        [held(a) for a in (velocity, stress, zones, slip, ocean, bathy)]
+        + [
             pltpu.VMEM((plan.strips, plan.nx, LANES), F32),
             pltpu.VMEM(
                 (plan.lead, plan.nx // plan.chunks + 2 * plan.halo_groups, LANES), F32
             ),
             pltpu.VMEM((n * plan.strips, LANES), F32),
+            pltpu.VMEM((n * plan.rows, LANES), F32),
+            pltpu.SemaphoreType.DMA((6,)),
         ],
-    )(ocean_near, bathy_near)
+    )(*(pinned(a) for a in (velocity, stress, zones, slip, ocean, bathy)))
+    other = lax.ppermute(crust, "map", others)
     arrived = lax.all_to_all(
         message.reshape(n // 2, 2 * plan.rows, LANES),
         "map",
@@ -550,7 +546,7 @@
         [smem] + [vmem] * 3,
         [],
         cost_estimate=pl.CostEstimate(
-            flops=10**12, bytes_accessed=2 * 10**9, transcendentals=0
+            flops=10**11, bytes_accessed=200 * 10**6, transcendentals=0
         ),
     )(materials, crust, mate, other)
     arrived, vel = lax.optimization_barrier((arrived, vel))
@@ -573,7 +569,7 @@
             pltpu.VMEM((plan.depth, lanes), F32),
         ],
         input_output_aliases={2: 0, 3: 1},
-    )(arrived, swapped, vel, strs, mats)
+    )(*(near(a) for a in (arrived, swapped, vel, strs, mats)))
     returned = lax.all_to_all(
         back.reshape(n, plan.back_rows, LANES), "map", split_axis=0, concat_axis=0, tiled=True
     ).reshape(n * plan.back_rows, LANES)

time: 41.9 us -> 40.2 us (0.959)
  Pallas kernels: 11.4 us -> 10.2 us
  waiting for transfers between devices: 15.7 us -> 15.2 us
    pallas_call x1, Pallas kernels: 4.44 us -> 3.49 us  [on_device(): call(middle_kernel, 'substeps', (shape(3, width, sub, lanes), shape(6, wi...]
    pallas_call x2 -> x1, Pallas kernels: 2.85 us -> 2.6 us  [on_device(): call(pack_kernel, 'pack', (shape(10 * cells + 1, sub, lanes), shape(n * p...]
  transfers between devices with their start and end apart: 5 -> 5, of which waited for: 3 -> 3; matrix products, arithmetic and copies ran while one was open for 0% -> 0% of each run, Pallas kernels for 10% -> 8%
where the time goes in v10:
time: 40.2 us; the launch traced here: 39.9 us
  waiting for transfers between devices  15.2 us (38%)
  starting transfers between devices  13.7 us (34%)
  Pallas kernels  10.2 us (25%)
  between operations  0.69 us (2%)
    all_to_all x1, waiting for transfers between devices, on_device(): lax.all_to_all(message.reshape(n // 2, 2 * plan.rows, LANES), 'map', spli...  7.86 us
    all_to_all x1, waiting for transfers between devices, on_device(): lax.all_to_all(back.reshape(n, plan.back_rows, LANES), 'map', split_axis=...  5.83 us
    all_to_all x1, starting transfers between devices, on_device(): lax.all_to_all(message.reshape(n // 2, 2 * plan.rows, LANES), 'map', spli...  5.01 us
    ppermute x1, starting transfers between devices, on_device(): mate = lax.ppermute(crust, 'map', mates)  4.35 us
    all_to_all x1, starting transfers between devices, on_device(): lax.all_to_all(back.reshape(n, plan.back_rows, LANES), 'map', split_axis=...  3.69 us
    pallas_call x1, Pallas kernels, on_device(): call(middle_kernel, 'substeps', (shape(3, width, sub, lanes), shape(6, wi...  3.49 us
    pallas_call x1, Pallas kernels, on_device(): call(pack_kernel, 'pack', (shape(10 * cells + 1, sub, lanes), shape(n * p...  2.6 us
    pallas_call x1, Pallas kernels, on_device(): call(end_kernel, 'last_updates', (shape(*velocity.shape), shape(*stress.s...  2.1 us
  transfers between devices with their start and end apart: 5, of which 3 were waited for; matrix products, arithmetic and copies ran while one was open for 0% of the time, Pallas kernels for 8%

profile of v10, /device:TPU:0, one launch (start us, length us, event | category | flops | bytes accessed | tf_op | source)
XLA Modules:
  0.0 39.9 jit_solution(6401485050883026810)
XLA Ops:
  0.6 2.6 %pack.1 = (f32[81,8,128]{2,1,0:T(8,128)S(1)}, f32[512,128]{1,0:T(8,128)}) custom-call(f32[3,8,32,32]{3,2,1,0:T(8,128)} %vel_ref.1, f32[6,8,32,32]{3,2,1,0:T(8,128)} %stress_ref.1, s32[8,32,32]{2,1,0:T(8,128)} %zones_ref.1, f32[8,32]{1,0:T(8,128)} %slip_ref.1, f32[4,2,32,128]{3,2,1,0:T(8,128)} %ocean_ref.1, s32[2,128]{1,0:T(2,128)} %bathy_ref.1), custom_call_target="tpu_custom_call" | custom-call | tf_op jit(solution)/shard_map/pack/pallas_call | solution.py:516
  3.2 0.7 %collective-permute-start.1 = (f32[81,8,128]{2,1,0:T(8,128)S(1)}, f32[81,8,128]{2,1,0:T(8,128)S(1)}, u32[]{:S(2)}, u32[]{:S(2)}) collective-permute-start(f32[81,8,128]{2,1,0:T(8,128)S(1)} %get-tuple-element.17.own), channel_id=1, source_target_pairs={{1,2},{3,4},{5,6},{7,8},{9,10},{11,12},{13,14},{2,1},{4,3},{6,5},{... | collective-permute-start | bytes 995336 | tf_op jit(solution)/shard_map/ppermute | solution.py:532
  3.9 4.3 %collective-permute-start = (f32[81,8,128]{2,1,0:T(8,128)S(1)}, f32[81,8,128]{2,1,0:T(8,128)S(1)}, u32[]{:S(2)}, u32[]{:S(2)}) collective-permute-start(f32[81,8,128]{2,1,0:T(8,128)S(1)} %get-tuple-element.17.own), channel_id=1, source_target_pairs={{0,1},{1,0},{2,3},{3,2},{4,5},{5,4},{6,7},{7,6},{8,9},{9,8},{10,11... | collective-permute-start | bytes 995336 | tf_op jit(solution)/shard_map/ppermute | solution.py:541
  8.3 0.0 copy-start
  8.3 5.0 %all-to-all-start = ((f32[8,64,128]{2,1,0:T(8,128)}), f32[8,64,128]{2,1,0:T(8,128)S(1)}, u32[]{:S(2)}, u32[]{:S(2)}) async-start(f32[8,64,128]{2,1,0:T(8,128)} %bitcast), calls=%async_computation | async-start | bytes 524288 | tf_op jit(solution)/shard_map/all_to_all | solution.py:533
  13.3 0.0 collective-permute-done.1.other
  13.3 0.0 collective-permute-done.mate
  13.3 0.0 copy-done
  13.3 1.1 %first_velocity.1 = (f32[3,24,8,128]{3,2,1,0:T(8,128)S(1)}, f32[6,24,8,128]{3,2,1,0:T(8,128)S(1)}, f32[5,24,8,128]{3,2,1,0:T(8,128)S(1)}) custom-call(f32[3,8]{1,0:T(4,128)S(1)} %copy-done, f32[81,8,128]{2,1,0:T(8,128)S(1)} %get-tuple-element.17.own, f32[81,8,128]{2,1,0:T(8,128)S(1)} %collective-permute-done.mate, f32[81,8,128]{2,1,0:T(8,128)S(1)} %collective-permute-done.1.other), custom_call_target="tpu_custom_call" | custom-call | flops 99999997952 | bytes 200000000 | tf_op jit(solution)/shard_map/first_velocity/pallas_call | solution.py:542
  14.4 7.9 %all-to-all-done = f32[8,64,128]{2,1,0:T(8,128)S(1)} async-done(((f32[8,64,128]{2,1,0:T(8,128)}), f32[8,64,128]{2,1,0:T(8,128)S(1)}, u32[]{:S(2)}, u32[]{:S(2)}) %all-to-all-start) | async-done | bytes 262176 | tf_op jit(solution)/shard_map/all_to_all | solution.py:533
  22.3 0.0 collective-permute-start.2
  22.3 1.5 %collective-permute-done.2.swapped = f32[512,128]{1,0:T(8,128)S(1)} collective-permute-done((f32[512,128]{1,0:T(8,128)S(1)}, f32[512,128]{1,0:T(8,128)S(1)}, u32[]{:S(2)}, u32[]{:S(2)}) %collective-permute-start.2) | collective-permute-done | bytes 262176 | tf_op jit(solution)/shard_map/ppermute | solution.py:553
  23.8 3.5 %substeps.1 = (f32[3,24,8,128]{3,2,1,0:T(8,128)S(1)}, f32[6,24,8,128]{3,2,1,0:T(8,128)S(1)}, f32[24,8,128]{2,1,0:T(8,128)S(1)}, f32[256,128]{1,0:T(8,128)}) custom-call(f32[512,128]{1,0:T(8,128)S(1)} %bitcast.5, f32[512,128]{1,0:T(8,128)S(1)} %collective-permute-done.2.swapped, ...), custom_call_target="tpu_custom_call", output_to_operand_aliasing={{0}: (2, {}), {1}: (3, {})} | custom-call | tf_op jit(solution)/shard_map/substeps/pallas_call | solution.py:554
  27.3 3.7 %all-to-all-start.1 = ((f32[16,16,128]{2,1,0:T(8,128)}), f32[16,16,128]{2,1,0:T(8,128)S(1)}, u32[]{:S(2)}, u32[]{:S(2)}) async-start(f32[16,16,128]{2,1,0:T(8,128)} %bitcast.2), calls=%async_computation.1 | async-start | bytes 262144 | tf_op jit(solution)/shard_map/all_to_all | solution.py:573
  31.0 2.1 %last_updates.1 = (f32[3,8,32,32]{3,2,1,0:T(8,128)}, f32[6,8,32,32]{3,2,1,0:T(8,128)}) custom-call(f32[3,24,8,128]{3,2,1,0:T(8,128)S(1)} %get-tuple-element.23.vel_in, f32[6,24,8,128]{3,2,1,0:T(8,128)S(1)} %get-tuple-element.24.stress_in, f32[5,24,8,128]{3,2,1,0:T(8,128)S(1)} %get-tuple-element.22.mats, f32[24,8,128]{2,1,0:T(8,128)S(1)} %get-tuple-element.25.loads), custom_call_target="tpu_custom_call" | custom-call | tf_op jit(solution)/shard_map/last_updates/pallas_call | solution.py:576
  33.1 5.8 %all-to-all-done.1 = f32[16,16,128]{2,1,0:T(8,128)S(1)} async-done(((f32[16,16,128]{2,1,0:T(8,128)}), f32[16,16,128]{2,1,0:T(8,128)S(1)}, u32[]{:S(2)}, u32[]{:S(2)}) %all-to-all-start.1) | async-done | bytes 131104 | tf_op jit(solution)/shard_map/all_to_all | solution.py:573
  38.9 0.9 %ocean_strips.1 = f32[4,2,32,128]{3,2,1,0:T(8,128)} custom-call(f32[256,128]{1,0:T(8,128)S(1)} %bitcast.6), custom_call_target="tpu_custom_call" | custom-call | tf_op jit(solution)/shard_map/ocean_strips/pallas_call | solution.py:586
Async XLA Ops:
  3.2 10.1 %collective-permute-start.1 = (f32[81,8,128]{2,1,0:T(8,128)S(1)}, f32[81,8,128]{2,1,0:T(8,128)S(1)}, u32[]{:S(2)}, u32[]{:S(2)}) collective-permute-start(f32[81,8,128]{2,1,0:T(8,128)S(1)} %get-tuple-element.17.own), channel_id=1, source_target_pairs={{1,2},{3,4},{5,6},{7,8},{9,10},{11,12},{13,14},{2,1},{4,3},{6,5},{... | collective-permute-start | bytes 995336 | tf_op jit(solution)/shard_map/ppermute | solution.py:532
  3.9 9.4 %collective-permute-start = (f32[81,8,128]{2,1,0:T(8,128)S(1)}, f32[81,8,128]{2,1,0:T(8,128)S(1)}, u32[]{:S(2)}, u32[]{:S(2)}) collective-permute-start(f32[81,8,128]{2,1,0:T(8,128)S(1)} %get-tuple-element.17.own), channel_id=1, source_target_pairs={{0,1},{1,0},{2,3},{3,2},{4,5},{5,4},{6,7},{7,6},{8,9},{9,8},{10,11... | collective-permute-start | bytes 995336 | tf_op jit(solution)/shard_map/ppermute | solution.py:541
  8.3 5.0 %copy-start = (f32[3,8]{1,0:T(4,128)S(1)}, f32[3,8]{1,0:T(4,128)}, u32[]{:S(2)}) copy-start(f32[3,8]{1,0:T(4,128)} %table.1) | copy-start | bytes 292
  8.3 14.0 %all-to-all-start = ((f32[8,64,128]{2,1,0:T(8,128)}), f32[8,64,128]{2,1,0:T(8,128)S(1)}, u32[]{:S(2)}, u32[]{:S(2)}) async-start(f32[8,64,128]{2,1,0:T(8,128)} %bitcast), calls=%async_computation | async-start | bytes 524288 | tf_op jit(solution)/shard_map/all_to_all | solution.py:533
  22.3 1.5 %collective-permute-start.2 = (f32[512,128]{1,0:T(8,128)S(1)}, f32[512,128]{1,0:T(8,128)S(1)}, u32[]{:S(2)}, u32[]{:S(2)}) collective-permute-start(f32[512,128]{1,0:T(8,128)S(1)} %bitcast.4), channel_id=1, source_target_pairs={{0,1},{1,0},{2,3},{3,2},{4,5},{5,4},{6,7},{7,6},{8,9},{9,8},{10,11... | collective-permute-start | bytes 786440 | tf_op jit(solution)/shard_map/ppermute | solution.py:553
  27.3 11.6 %all-to-all-start.1 = ((f32[16,16,128]{2,1,0:T(8,128)}), f32[16,16,128]{2,1,0:T(8,128)S(1)}, u32[]{:S(2)}, u32[]{:S(2)}) async-start(f32[16,16,128]{2,1,0:T(8,128)} %bitcast.2), calls=%async_computation.1 | async-start | bytes 262144 | tf_op jit(solution)/shard_map/all_to_all | solution.py:573

commit v11 on v6

--- a/solution.py
+++ b/solution.py
@@ -129,7 +129,7 @@
 
 def crust_kernel(
     plan, vel_ref, stress_ref, zones_ref, slip_ref, ocean_ref, bathy_ref,
-    crust, ocean, bathy, vel, stress, zones, slip, sems,
+    crust, border, ocean, bathy, vel, stress, zones, slip, sems,
 ):
     cells, sub, chunks, ny = plan.cells, plan.sub, plan.chunks, plan.ny
     pairs = (
@@ -171,6 +171,14 @@
     if sub > cells:
         fault = jnp.concatenate([fault, jnp.zeros((sub - cells, plan.lanes), F32)], axis=0)
     crust[10 * cells] = fault
+    odd = odd_device()
+    near = cells - 1
+    for f in range(10):
+        for i in range(near):
+            border[f * near + i] = crust[f * cells + i + odd]
+    for i, f in enumerate((SXX, SXY, SXZ)):
+        border[10 * near + i] = crust[(3 + f) * cells + near * (1 - odd)]
+    border[10 * near + 3] = fault
     copies[4].wait()
     copies[5].wait()
 
@@ -253,30 +261,36 @@
     )
 
 
-def begin_kernel(plan, table, own, mate, other, vel, stress, mats):
+def begin_kernel(plan, table, own, mate, border, vel, stress, mats):
     cells, sub = plan.cells, plan.sub
+    near = cells - 1
     sh = Shifts(plan)
     odd = odd_device()
-    starts = (HALO, (HALO + cells) * (1 - odd), (HALO + cells) * odd)
-    for start, ref in zip(starts, (own, mate, other)):
-        def bring(x, start=start, ref=ref):
-            j = start + x
-            for f in range(3):
-                vel[f, j] = ref[f * cells + x]
-            for f in range(6):
-                stress[f, j] = ref[(3 + f) * cells + x]
-            zone = ref[9 * cells + x]
-            values = [jnp.zeros_like(zone) for _ in range(3)]
-            for z in range(ZONES):
-                here = zone == float(z + 1)
-                values = [jnp.where(here, table[c, z], values[c]) for c in range(3)]
-            for c in range(3):
-                mats[c, j] = values[c] * HALF
-            slip = jnp.broadcast_to(ref[10 * cells, pl.ds(x, 1), :], (sub, plan.lanes))
-            mats[FAULT, j] = jnp.where(sh.row == (plan.depth // 2) % sub, DT * slip, 0.0)
-            mats[FLOOR, j] = sh.seafloor(ref[VZ * cells + x])
-
-        plan.planes(0, cells, bring)
+
+    def bring(x, ref, count, start, first):
+        j = start + x
+        for f in range(3):
+            vel[f, j] = ref[f * count + x]
+        for f in range(6):
+            stress[f, j] = ref[(3 + f) * count + x]
+        zone = ref[9 * count + x]
+        values = [jnp.zeros_like(zone) for _ in range(3)]
+        for z in range(ZONES):
+            here = zone == float(z + 1)
+            values = [jnp.where(here, table[c, z], values[c]) for c in range(3)]
+        for c in range(3):
+            mats[c, j] = values[c] * HALF
+        slips = ref[ref.shape[0] - 1, pl.ds(first + x, 1), :]
+        slip = jnp.broadcast_to(slips, (sub, plan.lanes))
+        mats[FAULT, j] = jnp.where(sh.row == (plan.depth // 2) % sub, DT * slip, 0.0)
+        mats[FLOOR, j] = sh.seafloor(ref[VZ * count + x])
+
+    plan.planes(0, cells, lambda x: bring(x, own, cells, HALO, 0))
+    plan.planes(0, cells, lambda x: bring(x, mate, cells, (HALO + cells) * (1 - odd), 0))
+    low = 1 + (HALO + cells - 1) * odd
+    plan.planes(0, near, lambda x: bring(x, border, near, low, 1 - odd))
+    for i, f in enumerate((SXX, SXY, SXZ)):
+        stress[f, (plan.width - 1) * odd] = border[10 * near + i]
 
     def move(j):
         b = mats[BUOY, j]
@@ -510,17 +524,25 @@
     def pinned(array):
         return pltpu.with_memory_space_constraint(array, pltpu.HBM)
 
+    def near(array):
+        return pltpu.with_memory_space_constraint(array, pltpu.VMEM) if plan.unrolled else array
+
     mates = [(i, i ^ 1) for i in range(n)]
     others = [(i, i + 1) for i in range(1, n - 1, 2)]
     others += [(target, source) for source, target in others]
-    crust, ocean_near, bathy_near = call(
+    crust, border, ocean_near, bathy_near = call(
         crust_kernel,
         "crust_planes",
-        (shape(10 * cells + 1, sub, lanes), like(ocean), like(bathy)),
+        (
+            shape(10 * cells + 1, sub, lanes),
+            shape(10 * cells - 6, sub, lanes),
+            like(ocean),
+            like(bathy),
+        ),
         [hbm] * 6,
-        [held(velocity), held(stress), held(zones), held(slip), pltpu.SemaphoreType.DMA((6,))],
+        [held(a) for a in (velocity, stress, zones, slip)] + [pltpu.SemaphoreType.DMA((6,))],
     )(*(pinned(a) for a in (velocity, stress, zones, slip, ocean, bathy)))
-    other = lax.ppermute(crust, "map", others)
+    other = lax.ppermute(border, "map", others)
     message = call(
         ocean_kernel,
         "ocean_rows",
@@ -534,6 +556,7 @@
             pltpu.VMEM((n * plan.strips, LANES), F32),
         ],
     )(ocean_near, bathy_near)
+    message, crust = lax.optimization_barrier((message, crust))
     arrived = lax.all_to_all(
         message.reshape(n // 2, 2 * plan.rows, LANES),
         "map",
@@ -550,7 +573,7 @@
         [smem] + [vmem] * 3,
         [],
         cost_estimate=pl.CostEstimate(
-            flops=10**12, bytes_accessed=2 * 10**9, transcendentals=0
+            flops=10**11, bytes_accessed=200 * 10**6, transcendentals=0
         ),
     )(materials, crust, mate, other)
     arrived, vel = lax.optimization_barrier((arrived, vel))
@@ -573,7 +596,7 @@
             pltpu.VMEM((plan.depth, lanes), F32),
         ],
         input_output_aliases={2: 0, 3: 1},
-    )(arrived, swapped, vel, strs, mats)
+    )(*(near(a) for a in (arrived, swapped, vel, strs, mats)))
     returned = lax.all_to_all(
         back.reshape(n, plan.back_rows, LANES), "map", split_axis=0, concat_axis=0, tiled=True
     ).reshape(n * plan.back_rows, LANES)

time: 41.9 us -> 40.4 us (0.964)
  Pallas kernels: 11.4 us -> 10.5 us
    ppermute x1, starting transfers between devices: 4.35 us -> 0.45 us  [on_device(): mate = lax.ppermute(crust, 'map', mates)]
    all_to_all x1, starting transfers between devices: 5.01 us -> 8.69 us  [on_device(): lax.all_to_all(message.reshape(n // 2, 2 * plan.rows, LANES), 'map', spli...]
    pallas_call x1, Pallas kernels: 4.44 us -> 3.49 us  [on_device(): call(middle_kernel, 'substeps', (shape(3, width, sub, lanes), shape(6, wi...]
  transfers between devices with their start and end apart: 5 -> 5, of which waited for: 3 -> 3; matrix products, arithmetic and copies ran while one was open for 0% -> 0% of each run, Pallas kernels for 10% -> 8%
where the time goes in v11:
time: 40.4 us; the launch traced here: 40 us
  waiting for transfers between devices  15.4 us (38%)
  starting transfers between devices  13.5 us (33%)
  Pallas kernels  10.5 us (26%)
  between operations  0.69 us (2%)
    all_to_all x1, starting transfers between devices, on_device(): lax.all_to_all(message.reshape(n // 2, 2 * plan.rows, LANES), 'map', spli...  8.69 us
    all_to_all x1, waiting for transfers between devices, on_device(): lax.all_to_all(message.reshape(n // 2, 2 * plan.rows, LANES), 'map', spli...  8 us
    all_to_all x1, waiting for transfers between devices, on_device(): lax.all_to_all(back.reshape(n, plan.back_rows, LANES), 'map', split_axis=...  5.83 us
    all_to_all x1, starting transfers between devices, on_device(): lax.all_to_all(back.reshape(n, plan.back_rows, LANES), 'map', split_axis=...  3.69 us
    pallas_call x1, Pallas kernels, on_device(): call(middle_kernel, 'substeps', (shape(3, width, sub, lanes), shape(6, wi...  3.49 us
    pallas_call x1, Pallas kernels, on_device(): call(end_kernel, 'last_updates', (shape(*velocity.shape), shape(*stress.s...  2.1 us
    pallas_call x1, Pallas kernels, on_device(): call(crust_kernel, 'crust_planes', (shape(10 * cells + 1, sub, lanes), sh...  1.7 us
    ppermute x1, waiting for transfers between devices, on_device(): swapped = lax.ppermute(arrived, 'map', mates)  1.53 us
  transfers between devices with their start and end apart: 5, of which 3 were waited for; matrix products, arithmetic and copies ran while one was open for 0% of the time, Pallas kernels for 8%

profile of v11, /device:TPU:0, one launch (start us, length us, event | category | flops | bytes accessed | tf_op | source)
XLA Modules:
  0.0 40.0 jit_solution(9334299638796652278)
XLA Ops:
  0.6 1.7 %crust_planes.1 = (f32[81,8,128]{2,1,0:T(8,128)S(1)}, f32[74,8,128]{2,1,0:T(8,128)S(1)}, f32[4,2,32,128]{3,2,1,0:T(8,128)S(1)}, s32[2,128]{1,0:T(2,128)S(1)}) custom-call(f32[3,8,32,32]{3,2,1,0:T(8,128)} %vel_ref.1, f32[6,8,32,32]{3,2,1,0:T(8,128)} %stress_ref.1, s32[8,32,32]{2,1,0:T(8,128)} %zones_ref.1, f32[8,32]{1,0:T(8,128)} %slip_ref.1, ...), custom_call_target="tpu_custom_call" | custom-call | tf_op jit(solution)/shard_map/crust_planes/pallas_call | solution.py:533
  2.3 1.2 %ocean_rows.1 = f32[512,128]{1,0:T(8,128)} custom-call(f32[4,2,32,128]{3,2,1,0:T(8,128)S(1)} %get-tuple-element.20.ocean, s32[2,128]{1,0:T(2,128)S(1)} %get-tuple-element.21.bathy), custom_call_target="tpu_custom_call" | custom-call | tf_op jit(solution)/shard_map/ocean_rows/pallas_call | solution.py:546
  3.5 0.5 %collective-permute-start = (f32[81,8,128]{2,1,0:T(8,128)S(1)}, f32[81,8,128]{2,1,0:T(8,128)S(1)}, u32[]{:S(2)}, u32[]{:S(2)}) collective-permute-start(f32[81,8,128]{2,1,0:T(8,128)S(1)} %get-tuple-element.24.own), channel_id=1, source_target_pairs={{0,1},{1,0},{2,3},{3,2},{4,5},{5,4},{6,7},{7,6},{8,9},{9,8},{10,11... | collective-permute-start | bytes 995336 | tf_op jit(solution)/shard_map/ppermute | solution.py:568
  3.9 0.7 %collective-permute-start.1 = (f32[74,8,128]{2,1,0:T(8,128)S(1)}, f32[74,8,128]{2,1,0:T(8,128)S(1)}, u32[]{:S(2)}, u32[]{:S(2)}) collective-permute-start(f32[74,8,128]{2,1,0:T(8,128)S(1)} %get-tuple-element.25), channel_id=1, source_target_pairs={{1,2},{3,4},{5,6},{7,8},{9,10},{11,12},{13,14},{2,1},{4,3},{6,5},{... | collective-permute-start | bytes 909320 | tf_op jit(solution)/shard_map/ppermute | solution.py:545
  4.6 0.0 copy-start
  4.6 8.7 %all-to-all-start = ((f32[8,64,128]{2,1,0:T(8,128)}), f32[8,64,128]{2,1,0:T(8,128)S(1)}, u32[]{:S(2)}, u32[]{:S(2)}) async-start(f32[8,64,128]{2,1,0:T(8,128)} %bitcast), calls=%async_computation | async-start | bytes 524288 | tf_op jit(solution)/shard_map/all_to_all | solution.py:560
  13.3 0.0 collective-permute-done.1.border
  13.3 0.0 collective-permute-done.mate
  13.3 0.0 copy-done
  13.3 1.1 %first_velocity.1 = (f32[3,24,8,128]{3,2,1,0:T(8,128)S(1)}, f32[6,24,8,128]{3,2,1,0:T(8,128)S(1)}, f32[5,24,8,128]{3,2,1,0:T(8,128)S(1)}) custom-call(f32[3,8]{1,0:T(4,128)S(1)} %copy-done, f32[81,8,128]{2,1,0:T(8,128)S(1)} %get-tuple-element.24.own, f32[81,8,128]{2,1,0:T(8,128)S(1)} %collective-permute-done.mate, ...), custom_call_target="tpu_custom_call" | custom-call | flops 99999997952 | bytes 200000000 | tf_op jit(solution)/shard_map/first_velocity/pallas_call | solution.py:569
  14.4 8.0 %all-to-all-done = f32[8,64,128]{2,1,0:T(8,128)S(1)} async-done(((f32[8,64,128]{2,1,0:T(8,128)}), f32[8,64,128]{2,1,0:T(8,128)S(1)}, u32[]{:S(2)}, u32[]{:S(2)}) %all-to-all-start) | async-done | bytes 262176 | tf_op jit(solution)/shard_map/all_to_all | solution.py:560
  22.4 0.0 collective-permute-start.2
  22.4 1.5 %collective-permute-done.2.swapped = f32[512,128]{1,0:T(8,128)S(1)} collective-permute-done((f32[512,128]{1,0:T(8,128)S(1)}, f32[512,128]{1,0:T(8,128)S(1)}, u32[]{:S(2)}, u32[]{:S(2)}) %collective-permute-start.2) | collective-permute-done | bytes 262176 | tf_op jit(solution)/shard_map/ppermute | solution.py:580
  24.0 3.5 %substeps.1 = (f32[3,24,8,128]{3,2,1,0:T(8,128)S(1)}, f32[6,24,8,128]{3,2,1,0:T(8,128)S(1)}, f32[24,8,128]{2,1,0:T(8,128)S(1)}, f32[256,128]{1,0:T(8,128)}) custom-call(f32[512,128]{1,0:T(8,128)S(1)} %bitcast.5, f32[512,128]{1,0:T(8,128)S(1)} %collective-permute-done.2.swapped, ...), custom_call_target="tpu_custom_call", output_to_operand_aliasing={{0}: (2, {}), {1}: (3, {})} | custom-call | tf_op jit(solution)/shard_map/substeps/pallas_call | solution.py:581
  27.5 3.7 %all-to-all-start.1 = ((f32[16,16,128]{2,1,0:T(8,128)}), f32[16,16,128]{2,1,0:T(8,128)S(1)}, u32[]{:S(2)}, u32[]{:S(2)}) async-start(f32[16,16,128]{2,1,0:T(8,128)} %bitcast.2), calls=%async_computation.1 | async-start | bytes 262144 | tf_op jit(solution)/shard_map/all_to_all | solution.py:600
  31.2 2.1 %last_updates.1 = (f32[3,8,32,32]{3,2,1,0:T(8,128)}, f32[6,8,32,32]{3,2,1,0:T(8,128)}) custom-call(f32[3,24,8,128]{3,2,1,0:T(8,128)S(1)} %get-tuple-element.31.vel_in, f32[6,24,8,128]{3,2,1,0:T(8,128)S(1)} %get-tuple-element.32.stress_in, f32[5,24,8,128]{3,2,1,0:T(8,128)S(1)} %get-tuple-element.30.mats, f32[24,8,128]{2,1,0:T(8,128)S(1)} %get-tuple-element.33.loads), custom_call_target="tpu_custom_call" | custom-call | tf_op jit(solution)/shard_map/last_updates/pallas_call | solution.py:603
  33.3 5.8 %all-to-all-done.1 = f32[16,16,128]{2,1,0:T(8,128)S(1)} async-done(((f32[16,16,128]{2,1,0:T(8,128)}), f32[16,16,128]{2,1,0:T(8,128)S(1)}, u32[]{:S(2)}, u32[]{:S(2)}) %all-to-all-start.1) | async-done | bytes 131104 | tf_op jit(solution)/shard_map/all_to_all | solution.py:600
  39.1 0.9 %ocean_strips.1 = f32[4,2,32,128]{3,2,1,0:T(8,128)} custom-call(f32[256,128]{1,0:T(8,128)S(1)} %bitcast.6), custom_call_target="tpu_custom_call" | custom-call | tf_op jit(solution)/shard_map/ocean_strips/pallas_call | solution.py:613
Async XLA Ops:
  3.5 9.8 %collective-permute-start = (f32[81,8,128]{2,1,0:T(8,128)S(1)}, f32[81,8,128]{2,1,0:T(8,128)S(1)}, u32[]{:S(2)}, u32[]{:S(2)}) collective-permute-start(f32[81,8,128]{2,1,0:T(8,128)S(1)} %get-tuple-element.24.own), channel_id=1, source_target_pairs={{0,1},{1,0},{2,3},{3,2},{4,5},{5,4},{6,7},{7,6},{8,9},{9,8},{10,11... | collective-permute-start | bytes 995336 | tf_op jit(solution)/shard_map/ppermute | solution.py:568
  3.9 9.4 %collective-permute-start.1 = (f32[74,8,128]{2,1,0:T(8,128)S(1)}, f32[74,8,128]{2,1,0:T(8,128)S(1)}, u32[]{:S(2)}, u32[]{:S(2)}) collective-permute-start(f32[74,8,128]{2,1,0:T(8,128)S(1)} %get-tuple-element.25), channel_id=1, source_target_pairs={{1,2},{3,4},{5,6},{7,8},{9,10},{11,12},{13,14},{2,1},{4,3},{6,5},{... | collective-permute-start | bytes 909320 | tf_op jit(solution)/shard_map/ppermute | solution.py:545
  4.6 8.7 %copy-start = (f32[3,8]{1,0:T(4,128)S(1)}, f32[3,8]{1,0:T(4,128)}, u32[]{:S(2)}) copy-start(f32[3,8]{1,0:T(4,128)} %table.1) | copy-start | bytes 292
  4.6 17.8 %all-to-all-start = ((f32[8,64,128]{2,1,0:T(8,128)}), f32[8,64,128]{2,1,0:T(8,128)S(1)}, u32[]{:S(2)}, u32[]{:S(2)}) async-start(f32[8,64,128]{2,1,0:T(8,128)} %bitcast), calls=%async_computation | async-start | bytes 524288 | tf_op jit(solution)/shard_map/all_to_all | solution.py:560
  22.4 1.5 %collective-permute-start.2 = (f32[512,128]{1,0:T(8,128)S(1)}, f32[512,128]{1,0:T(8,128)S(1)}, u32[]{:S(2)}, u32[]{:S(2)}) collective-permute-start(f32[512,128]{1,0:T(8,128)S(1)} %bitcast.4), channel_id=1, source_target_pairs={{0,1},{1,0},{2,3},{3,2},{4,5},{5,4},{6,7},{7,6},{8,9},{9,8},{10,11... | collective-permute-start | bytes 786440 | tf_op jit(solution)/shard_map/ppermute | solution.py:580
  27.5 11.6 %all-to-all-start.1 = ((f32[16,16,128]{2,1,0:T(8,128)}), f32[16,16,128]{2,1,0:T(8,128)S(1)}, u32[]{:S(2)}, u32[]{:S(2)}) async-start(f32[16,16,128]{2,1,0:T(8,128)} %bitcast.2), calls=%async_computation.1 | async-start | bytes 262144 | tf_op jit(solution)/shard_map/all_to_all | solution.py:600

commit v12 on v10

--- a/solution.py
+++ b/solution.py
@@ -73,7 +73,7 @@
 
 
 def pack_kernel(
-    plan, vel_ref, stress_ref, zones_ref, slip_ref, ocean_ref, bathy_ref, crust, message_out,
+    plan, vel_ref, stress_ref, zones_ref, slip_ref, ocean_ref, bathy_ref, crust, border, message_out,
     vel, stress, zones, slip, ocean, bathy, turned, grouped, extra, message, sems,
 ):
     cells, sub, chunks, ny = plan.cells, plan.sub, plan.chunks, plan.ny
@@ -94,10 +94,10 @@
         copy.start()
     copies[0].wait()
     copies[1].wait()
-    border = jnp.zeros((plan.lead, plan.halo_groups, LANES), F32)
+    outside = jnp.zeros((plan.lead, plan.halo_groups, LANES), F32)
     count = plan.nx // chunks
-    grouped[:, : plan.halo_groups, :] = border
-    grouped[:, plan.halo_groups + count :, :] = border
+    grouped[:, : plan.halo_groups, :] = outside
+    grouped[:, plan.halo_groups + count :, :] = outside
     for yl in range(strips):
         stacked = jnp.concatenate(
             [ocean[f, yl, kc * sub : (kc + 1) * sub, :] for kc in range(chunks) for f in range(4)],
@@ -170,6 +170,14 @@
     if sub > cells:
         fault = jnp.concatenate([fault, jnp.zeros((sub - cells, plan.lanes), F32)], axis=0)
     crust[10 * cells] = fault
+    odd = odd_device()
+    near = cells - 1
+    for f in range(10):
+        for i in range(near):
+            border[f * near + i] = crust[f * cells + i + odd]
+    for i, f in enumerate((SXX, SXY, SXZ)):
+        border[10 * near + i] = crust[(3 + f) * cells + near * (1 - odd)]
+    border[10 * near + 3] = fault
 
 
 class Shifts:
@@ -250,53 +258,127 @@
     )
 
 
-def begin_kernel(plan, table, own, mate, other, vel, stress, mats):
-    cells, sub = plan.cells, plan.sub
+def bring(plan, sh, table, state, ref, count, x, column, first):
+    vel, stress, mats = state
+    for f in range(3):
+        vel[f, column] = ref[f * count + x]
+    for f in range(6):
+        stress[f, column] = ref[(3 + f) * count + x]
+    zone = ref[9 * count + x]
+    values = [jnp.zeros_like(zone) for _ in range(3)]
+    for z in range(ZONES):
+        here = zone == float(z + 1)
+        values = [jnp.where(here, table[c, z], values[c]) for c in range(3)]
+    for c in range(3):
+        mats[c, column] = values[c] * HALF
+    slip = ref[ref.shape[0] - 1, pl.ds(first + x, 1), :]
+    slip = jnp.broadcast_to(slip, zone.shape)
+    mats[FAULT, column] = jnp.where(sh.row == (plan.depth // 2) % plan.sub, DT * slip, 0.0)
+    mats[FLOOR, column] = sh.seafloor(ref[VZ * count + x])
+
+
+def begin_kernel(plan, table, own, mate, vel, stress, mats):
+    cells = plan.cells
     sh = Shifts(plan)
     odd = odd_device()
-    starts = (HALO, (HALO + cells) * (1 - odd), (HALO + cells) * odd)
-    for start, ref in zip(starts, (own, mate, other)):
-        def bring(x, start=start, ref=ref):
-            j = start + x
-            for f in range(3):
-                vel[f, j] = ref[f * cells + x]
-            for f in range(6):
-                stress[f, j] = ref[(3 + f) * cells + x]
-            zone = ref[9 * cells + x]
-            values = [jnp.zeros_like(zone) for _ in range(3)]
-            for z in range(ZONES):
-                here = zone == float(z + 1)
-                values = [jnp.where(here, table[c, z], values[c]) for c in range(3)]
-            for c in range(3):
-                mats[c, j] = values[c] * HALF
-            slip = jnp.broadcast_to(ref[10 * cells, pl.ds(x, 1), :], (sub, plan.lanes))
-            mats[FAULT, j] = jnp.where(sh.row == (plan.depth // 2) % sub, DT * slip, 0.0)
-            mats[FLOOR, j] = sh.seafloor(ref[VZ * cells + x])
-
-        plan.planes(0, cells, bring)
+    state = (vel, stress, mats)
+    starts = (HALO + cells * odd, HALO + cells * (1 - odd))
+    for start, ref in zip(starts, (own, mate)):
+        plan.planes(
+            0,
+            cells,
+            lambda x, start=start, ref=ref: bring(
+                plan, sh, table, state, ref, cells, x, start + x, 0
+            ),
+        )
 
     def move(j):
         b = mats[BUOY, j]
         for f, a in enumerate(acceleration(sh, stress, j)):
             vel[f, j] = vel[f, j] + b * a
 
-    plan.planes(1, plan.width - 1, move)
-
-
-def middle_kernel(
-    plan, arrived, swapped, vel_in, stress_in, mats, vel, stress, loads, message,
-    oc, water, bottom, gather, depths,
+    plan.planes(HALO + 1, HALO + 2 * cells - 1, move)
+
+
+class Updates:
+    def __init__(self, plan, sh, vel, stress, mats, oc, water, bottom, loads):
+        self.plan, self.sh = plan, sh
+        self.vel, self.stress, self.mats = vel, stress, mats
+        self.oc, self.water, self.bottom, self.loads = oc, water, bottom, loads
+
+    def flow_x(self, j):
+        oc = self.oc
+        oc[1, j + 1] = self.water[j + 1] * (oc[1, j + 1] - HALF * (oc[0, j + 2] - oc[0, j]))
+
+    def flow(self, j):
+        oc, sh = self.oc, self.sh
+        p = oc[0, j + 1]
+        wet = self.water[j + 1]
+        oc[2, j + 1] = wet * (oc[2, j + 1] - HALF * sh.dy(p))
+        rise = sh.below(p) + self.bottom[j + 1] * p - sh.above(p, -p)
+        oc[3, j + 1] = wet * (oc[3, j + 1] - (HALF * rise + (DT * GRAV) * p))
+
+    def press(self, j, start):
+        oc, sh = self.oc, self.sh
+        w = oc[3, j + 1]
+        floor = self.mats[FLOOR, j] if start else sh.seafloor(self.vel[VZ, j])
+        rise = sh.below(w) + self.bottom[j + 1] * floor - sh.above(w, w)
+        total = oc[1, j + 2] - oc[1, j] + sh.dy(oc[2, j + 1]) + rise
+        oc[0, j + 1] = self.water[j + 1] * (oc[0, j + 1] - (HALF * KBULK) * total)
+
+    def load(self, j):
+        sh, plan = self.sh, self.plan
+        column = jnp.sum(self.bottom[j + 1] * self.oc[0, j + 1], axis=0, keepdims=True)
+        column = jnp.broadcast_to(sh.over_chunks(column), (plan.sub, plan.lanes))
+        return jnp.where(sh.top, column, 0.0)
+
+    def keep(self, j):
+        self.loads[j] = self.load(j)
+
+    def add_load(self, j):
+        self.vel[VZ, j] = self.vel[VZ, j] + self.mats[BUOY, j] * self.load(j)
+
+    def move(self, j):
+        vel = self.vel
+        ax, ay, az = acceleration(self.sh, self.stress, j)
+        b = self.mats[BUOY, j]
+        vel[VX, j] = vel[VX, j] + b * ax
+        vel[VY, j] = vel[VY, j] + b * ay
+        vel[VZ, j] = vel[VZ, j] + b * (az + self.load(j))
+
+    def strain(self, j):
+        for f, value in enumerate(strained(self.sh, self.vel, self.stress, self.mats, j)):
+            self.stress[f, j] = value
+
+    def run(self, spans, moved):
+        planes = self.plan.planes
+        for t in range(STEPS):
+            planes(*spans(t, 0), self.flow_x)
+            planes(*spans(t, 1), self.flow)
+            planes(*spans(t, 1), lambda j, t=t: self.press(j, t == 0))
+            if t == STEPS - 1:
+                planes(*spans(t, 1), self.keep)
+            elif t == 0 and moved:
+                planes(*spans(t, 1), self.add_load)
+            else:
+                planes(*spans(t, 1), self.move)
+            if t < STEPS - 2:
+                planes(*spans(t, 2), self.strain)
+
+
+def inner_kernel(
+    plan, arrived, swapped, mats, vel_in, stress_in, vel, stress, oc, water, bottom, loads,
+    gather, depths,
 ):
     sub, chunks, n, strips = plan.sub, plan.chunks, plan.n, plan.strips
-    width, sent = plan.width, plan.sent_groups
+    cells, sent = plan.cells, plan.sent_groups
     sh = Shifts(plan)
     odd = odd_device()
-
     half = n // 2
-    mate = 1 - odd
+    columns = 2 * cells + 2 * HALO
 
     def turn(owner, group):
-        for core, ref in ((odd, arrived), (mate, swapped)):
+        for core, ref in ((odd, arrived), (1 - odd, swapped)):
             for kc in range(chunks):
                 for yl in range(strips):
                     at = owner * plan.rows + (kc * strips + yl) * sent + group
@@ -306,35 +388,28 @@
                     ]
         return gather[...].T
 
-    def spread(turned, group):
-        for i in range(chunks):
-            for f in range(4):
-                at = (i * 4 + f) * sub
-                oc[f, 1 + group * chunks + i] = turned[at : at + sub]
-
-    ends = []
-    for group in range(sent):
-        turned = turn(odd, group)
-        spread(turned, group + plan.halo_groups * odd)
-        if group == 0:
-            ends.append((turned[2 * sub : 3 * sub], turned[3 * sub : 4 * sub]))
-        if group == sent - 1:
-            ends.append((turned[LANES - 2 * sub : LANES - sub], turned[LANES - sub :]))
-    for group in range(plan.halo_groups):
-        spread(turn(mate, group + plan.own_groups * odd), group + sent * mate)
-    turned = turn(mate, plan.own_groups - odd)
-    is_odd = odd == 1
-    oc[0, (width + 1) * odd] = jnp.where(is_odd, ends[1][0], ends[0][0])
-    oc[0, (width + 1) * mate] = jnp.where(
-        is_odd, turned[LANES - 4 * sub : LANES - 3 * sub], turned[:sub]
-    )
-    deep = jnp.where(is_odd, ends[1][1], ends[0][1])
-    for kc in range(chunks):
-        mine = (sh.lane >= kc * plan.ny) & (sh.lane < (kc + 1) * plan.ny)
-        depths[kc * sub : (kc + 1) * sub, :] = sh.over_chunks(jnp.where(mine, deep, 0.0))
-
-    def mask(j):
-        low = jnp.broadcast_to(depths[pl.ds(j, 1), :], (sub, plan.lanes))
+    deeps = []
+    for owner in range(2):
+        for group in range(sent):
+            turned = turn(owner, group)
+            for i in range(chunks):
+                for f in range(4):
+                    at = (i * 4 + f) * sub
+                    column = 1 + owner * (cells + HALO) + group * chunks + i
+                    oc[f, column] = turned[at : at + sub]
+            if owner == 0 and group == 0:
+                oc[0, 0] = turned[2 * sub : 3 * sub]
+                deeps.append(turned[3 * sub : 4 * sub])
+            if owner == 1 and group == sent - 1:
+                oc[0, columns + 1] = turned[LANES - 2 * sub : LANES - sub]
+                deeps.append(turned[LANES - sub :])
+    for i, deep in enumerate(deeps):
+        for kc in range(chunks):
+            mine = (sh.lane >= kc * plan.ny) & (sh.lane < (kc + 1) * plan.ny)
+            depths[i, kc * sub : (kc + 1) * sub, :] = sh.over_chunks(jnp.where(mine, deep, 0.0))
+
+    def mask(owner, j):
+        low = jnp.broadcast_to(depths[owner, pl.ds(j - owner * cells, 1), :], (sub, plan.lanes))
         wet = jnp.where(sh.depth < low, 1.0, 0.0).astype(F32)
         water[j] = wet
         bottom[j] = jnp.where(sh.depth == low - 1.0, 1.0, 0.0).astype(F32)
@@ -347,90 +422,84 @@
         oc[2, j] = oc[2, j] * water[j]
         oc[3, j] = oc[3, j] * water[j]
 
-    plan.planes(0, width + 2, mask)
-    plan.planes(1, width + 1, mask_x)
-    plan.planes(2, width, mask_yw)
-
-    for t in range(STEPS):
-        first, last = 2 * t, width - 2 * t
-        before = t == 0
-
-        def flow_x(j):
-            oc[1, j + 1] = water[j + 1] * (oc[1, j + 1] - HALF * (oc[0, j + 2] - oc[0, j]))
-
-        def flow(j):
-            p = oc[0, j + 1]
-            wet = water[j + 1]
-            oc[2, j + 1] = wet * (oc[2, j + 1] - HALF * sh.dy(p))
-            rise = sh.below(p) + bottom[j + 1] * p - sh.above(p, -p)
-            oc[3, j + 1] = wet * (oc[3, j + 1] - (HALF * rise + (DT * GRAV) * p))
-
-        def press(j):
-            w = oc[3, j + 1]
-            floor = mats[FLOOR, j] if before else sh.seafloor(vel[VZ, j])
-            rise = sh.below(w) + bottom[j + 1] * floor - sh.above(w, w)
-            total = oc[1, j + 2] - oc[1, j] + sh.dy(oc[2, j + 1]) + rise
-            oc[0, j + 1] = water[j + 1] * (oc[0, j + 1] - (HALF * KBULK) * total)
-
-        def load(j):
-            column = jnp.sum(bottom[j + 1] * oc[0, j + 1], axis=0, keepdims=True)
-            column = jnp.broadcast_to(sh.over_chunks(column), (sub, plan.lanes))
-            return jnp.where(sh.top, column, 0.0)
-
-        plan.planes(first, last, flow_x)
-        plan.planes(first + 1, last - 1, flow)
-        plan.planes(first + 1, last - 1, press)
-        if before:
-            def add_load(j):
-                for f in (VX, VY):
-                    vel[f, j] = vel_in[f, j]
-                vel[VZ, j] = vel_in[VZ, j] + mats[BUOY, j] * load(j)
-
-            plan.planes(first + 1, last - 1, add_load)
-        elif t < STEPS - 1:
-            def move(j):
-                ax, ay, az = acceleration(sh, stress, j)
-                b = mats[BUOY, j]
-                vel[VX, j] = vel[VX, j] + b * ax
-                vel[VY, j] = vel[VY, j] + b * ay
-                vel[VZ, j] = vel[VZ, j] + b * (az + load(j))
-
-            plan.planes(first + 1, last - 1, move)
-        else:
-            def keep(j):
-                loads[j] = load(j)
-
-            plan.planes(first + 1, last - 1, keep)
-        if t < STEPS - 2:
-            def strain(j):
-                source = stress_in if before else stress
-                for f, value in enumerate(strained(sh, vel, source, mats, j)):
-                    stress[f, j] = value
-
-            plan.planes(first + 2, last - 2, strain)
-
-    for group in range(plan.own_groups):
-        stacked = jnp.concatenate(
-            [
-                oc[f, 1 + HALO + group * chunks + i]
-                for i in range(chunks)
-                for f in range(4)
-            ],
-            axis=0,
+    plan.planes(0, plan.width + 2, lambda j: mask(0, j))
+    plan.planes(plan.width + 2, columns + 2, lambda j: mask(1, j))
+    plan.planes(1, columns + 1, mask_x)
+    plan.planes(2, columns, mask_yw)
+
+    def bring_in(j):
+        for f in range(3):
+            vel[f, j] = vel_in[f, j]
+        for f in range(6):
+            stress[f, j] = stress_in[f, j]
+
+    if not plan.unrolled:
+        plan.planes(HALO, HALO + 2 * cells, bring_in)
+    updates = Updates(plan, sh, vel, stress, mats, oc, water, bottom, loads)
+    updates.run(lambda t, inset: (HALO + 2 * t + inset, HALO + 2 * cells - 2 * t - inset), True)
+
+
+def outer_kernel(
+    plan, table, border, water, bottom, vel_in, stress_in, mats_in, oc_in, loads_in,
+    vel, stress, mats, oc, loads, message, gather,
+):
+    sub, chunks, n, strips, cells = plan.sub, plan.chunks, plan.n, plan.strips, plan.cells
+    near = cells - 1
+    sh = Shifts(plan)
+    odd = odd_device()
+    if not plan.unrolled:
+        for here, there in (
+            (vel, vel_in), (stress, stress_in), (mats, mats_in), (oc, oc_in), (loads, loads_in)
+        ):
+            here[...] = there[...]
+    updates = Updates(plan, sh, vel, stress, mats, oc, water, bottom, loads)
+
+    def side(core):
+        low, far = ((1, 0), (HALO + 2 * cells, 2 * HALO + 2 * cells - 1))[core]
+        state = (vel, stress, mats)
+        plan.planes(
+            0,
+            near,
+            lambda x: bring(plan, sh, table, state, border, near, x, low + x, 1 - core),
         )
-        gather[...] = stacked.T
-        for kc in range(chunks):
-            for yl in range(strips):
-                at = group * plan.lead + kc * strips + yl
-                message[pl.ds(at, n, stride=plan.back_rows), :] = gather[
-                    pl.ds(kc * plan.ny + yl, n, stride=strips), :
-                ]
-
-
-def end_kernel(plan, vel_in, stress_in, mats, loads, vel_out, stress_out, vel, stress):
+        for i, f in enumerate((SXX, SXY, SXZ)):
+            stress[f, far] = border[10 * near + i]
+
+        def spans(t, inset):
+            if core == 0:
+                return 2 * t + inset, 2 * t + inset + HALO
+            last = 2 * HALO + 2 * cells - 2 * t - inset
+            return last - HALO, last
+
+        updates.run(spans, False)
+        for group in range(plan.own_groups):
+            stacked = jnp.concatenate(
+                [
+                    oc[f, 1 + HALO + core * cells + group * chunks + i]
+                    for i in range(chunks)
+                    for f in range(4)
+                ],
+                axis=0,
+            )
+            gather[...] = stacked.T
+            for kc in range(chunks):
+                for yl in range(strips):
+                    at = group * plan.lead + kc * strips + yl
+                    message[pl.ds(at, n, stride=plan.back_rows), :] = gather[
+                        pl.ds(kc * plan.ny + yl, n, stride=strips), :
+                    ]
+
+    for core in range(2):
+        pl.when(odd == core)(functools.partial(side, core))
+
+
+def end_kernel(plan, vel_all, stress_all, mats_all, loads_all, vel_out, stress_out, vel, stress):
     cells, sub, chunks, ny = plan.cells, plan.sub, plan.chunks, plan.ny
     sh = Shifts(plan)
     first, last = 2 * (STEPS - 1), plan.width - 2 * (STEPS - 1)
+    window = pl.ds(cells * odd_device(), plan.width)
+    vel_in, stress_in = vel_all.at[:, window], stress_all.at[:, window]
+    mats, loads = mats_all.at[:, window], loads_all.at[window]
 
     def put(out, f, x, plane):
         for kc in range(chunks):
@@ -513,10 +582,14 @@
     mates = [(i, i ^ 1) for i in range(n)]
     others = [(i, i + 1) for i in range(1, n - 1, 2)]
     others += [(target, source) for source, target in others]
-    crust, message = call(
+    crust, border, message = call(
         pack_kernel,
         "pack",
-        (shape(10 * cells + 1, sub, lanes), shape(n * plan.rows, LANES)),
+        (
+            shape(10 * cells + 1, sub, lanes),
+            shape(10 * cells - 6, sub, lanes),
+            shape(n * plan.rows, LANES),
+        ),
         [hbm] * 6,
         [held(a) for a in (velocity, stress, zones, slip, ocean, bathy)]
         + [
@@ -529,7 +602,6 @@
             pltpu.SemaphoreType.DMA((6,)),
         ],
     )(*(pinned(a) for a in (velocity, stress, zones, slip, ocean, bathy)))
-    other = lax.ppermute(crust, "map", others)
     arrived = lax.all_to_all(
         message.reshape(n // 2, 2 * plan.rows, LANES),
         "map",
@@ -538,38 +610,46 @@
         axis_index_groups=[list(range(core, n, 2)) for core in range(2)],
         tiled=True,
     ).reshape(n * plan.rows, LANES)
+    other = lax.ppermute(border, "map", others)
     mate = lax.ppermute(crust, "map", mates)
+    columns = 2 * cells + 2 * HALO
     vel, strs, mats = call(
         begin_kernel,
         "first_velocity",
-        (shape(3, width, sub, lanes), shape(6, width, sub, lanes), shape(5, width, sub, lanes)),
-        [smem] + [vmem] * 3,
+        (shape(3, columns, sub, lanes), shape(6, columns, sub, lanes), shape(5, columns, sub, lanes)),
+        [smem] + [vmem] * 2,
         [],
-        cost_estimate=pl.CostEstimate(
-            flops=10**11, bytes_accessed=200 * 10**6, transcendentals=0
-        ),
-    )(materials, crust, mate, other)
+    )(materials, crust, mate)
     arrived, vel = lax.optimization_barrier((arrived, vel))
     swapped = lax.ppermute(arrived, "map", mates)
-    vel, strs, loads, back = call(
-        middle_kernel,
-        "substeps",
-        (
-            shape(3, width, sub, lanes),
-            shape(6, width, sub, lanes),
-            shape(width, sub, lanes),
-            shape(n * plan.back_rows, LANES),
-        ),
+    planes_of = {
+        "vel": shape(3, columns, sub, lanes),
+        "stress": shape(6, columns, sub, lanes),
+        "mats": shape(5, columns, sub, lanes),
+        "oc": shape(4, columns + 2, sub, lanes),
+        "mask": shape(columns + 2, sub, lanes),
+        "loads": shape(columns, sub, lanes),
+    }
+    vel, strs, oc, water, bottom, loads = call(
+        inner_kernel,
+        "inner_substeps",
+        tuple(planes_of[k] for k in ("vel", "stress", "oc", "mask", "mask", "loads")),
         [vmem] * 5,
         [
-            pltpu.VMEM((4, width + 2, sub, lanes), F32),
-            pltpu.VMEM((width + 2, sub, lanes), F32),
-            pltpu.VMEM((width + 2, sub, lanes), F32),
             pltpu.VMEM((lanes, LANES), F32),
-            pltpu.VMEM((plan.depth, lanes), F32),
+            pltpu.VMEM((2, plan.depth, lanes), F32),
         ],
-        input_output_aliases={2: 0, 3: 1},
-    )(*(near(a) for a in (arrived, swapped, vel, strs, mats)))
+        input_output_aliases={3: 0, 4: 1},
+    )(*(near(a) for a in (arrived, swapped, mats, vel, strs)))
+    vel, strs, mats, oc, loads, back = call(
+        outer_kernel,
+        "outer_substeps",
+        tuple(planes_of[k] for k in ("vel", "stress", "mats", "oc", "loads"))
+        + (shape(n * plan.back_rows, LANES),),
+        [smem] + [vmem] * 8,
+        [pltpu.VMEM((lanes, LANES), F32)],
+        input_output_aliases={4: 0, 5: 1, 6: 2, 7: 3, 8: 4},
+    )(materials, *(near(a) for a in (other, water, bottom, vel, strs, mats, oc, loads)))
     returned = lax.all_to_all(
         back.reshape(n, plan.back_rows, LANES), "map", split_axis=0, concat_axis=0, tiled=True
     ).reshape(n * plan.back_rows, LANES)

time: 40.2 us -> 39.4 us (0.980)
  starting transfers between devices: 13.7 us -> 12.1 us
  Pallas kernels: 10.2 us -> 11.6 us
  waiting for transfers between devices: 15.2 us -> 14.7 us
    ppermute x1, starting transfers between devices: 4.35 us -> 0.07 us  [on_device(): mate = lax.ppermute(crust, 'map', mates)]
    all_to_all x1, starting transfers between devices: 5.01 us -> 7.26 us  [on_device(): lax.all_to_all(message.reshape(n // 2, 2 * plan.rows, LANES), 'map', spli...]
    all_to_all x1, waiting for transfers between devices: 7.86 us -> 6.4 us  [on_device(): lax.all_to_all(message.reshape(n // 2, 2 * plan.rows, LANES), 'map', spli...]
    pallas_call x3 -> x4, Pallas kernels: 7.19 us -> 8.56 us  [the longest x1 3.02 us: on_device(): call(outer_kernel, 'outer_substeps', tuple((planes_of[k] for k in ('vel',...]
    ppermute x1, waiting for transfers between devices: 0.01 us -> 0.93 us  [on_device(): mate = lax.ppermute(crust, 'map', mates)]
  transfers between devices with their start and end apart: 5 -> 5, of which waited for: 3 -> 4; matrix products, arithmetic and copies ran while one was open for 0% -> 0% of each run, Pallas kernels for 8% -> 13%
where the time goes in v12:
time: 39.4 us; the launch traced here: 39.1 us
  waiting for transfers between devices  14.7 us (37%)
  starting transfers between devices  12.1 us (31%)
  Pallas kernels  11.6 us (29%)
  between operations  0.68 us (2%)
    all_to_all x1, starting transfers between devices, on_device(): lax.all_to_all(message.reshape(n // 2, 2 * plan.rows, LANES), 'map', spli...  7.26 us
    all_to_all x1, waiting for transfers between devices, on_device(): lax.all_to_all(message.reshape(n // 2, 2 * plan.rows, LANES), 'map', spli...  6.4 us
    all_to_all x1, waiting for transfers between devices, on_device(): lax.all_to_all(back.reshape(n, plan.back_rows, LANES), 'map', split_axis=...  5.82 us
    all_to_all x1, starting transfers between devices, on_device(): lax.all_to_all(back.reshape(n, plan.back_rows, LANES), 'map', split_axis=...  4.09 us
    pallas_call x1, Pallas kernels, on_device(): call(outer_kernel, 'outer_substeps', tuple((planes_of[k] for k in ('vel',...  3.02 us
    pallas_call x1, Pallas kernels, on_device(): call(pack_kernel, 'pack', (shape(10 * cells + 1, sub, lanes), shape(10 *...  2.6 us
    pallas_call x1, Pallas kernels, on_device(): call(end_kernel, 'last_updates', (shape(*velocity.shape), shape(*stress.s...  2.11 us
    pallas_call x1, Pallas kernels, on_device(): call(inner_kernel, 'inner_substeps', tuple((planes_of[k] for k in ('vel',...  2.03 us
  transfers between devices with their start and end apart: 5, of which 4 were waited for; matrix products, arithmetic and copies ran while one was open for 0% of the time, Pallas kernels for 13%

profile of v12, /device:TPU:0, one launch (start us, length us, event | category | flops | bytes accessed | tf_op | source)
XLA Modules:
  0.0 39.1 jit_solution(17676200458103685094)
XLA Ops:
  0.6 2.6 %pack.1 = (f32[81,8,128]{2,1,0:T(8,128)S(1)}, f32[74,8,128]{2,1,0:T(8,128)S(1)}, f32[512,128]{1,0:T(8,128)}) custom-call(f32[3,8,32,32]{3,2,1,0:T(8,128)} %vel_ref.1, f32[6,8,32,32]{3,2,1,0:T(8,128)} %stress_ref.1, s32[8,32,32]{2,1,0:T(8,128)} %zones_ref.1, f32[8,32]{1,0:T(8,128)} %slip_ref.1, f32[4,2,32,128]{3,2,1,0:T(8,128)} %ocean_ref.1, s32[2,128]{1,0:T(2,128)} %bathy_ref.1), custom_call_target="tpu_custom_call" | custom-call | tf_op jit(solution)/shard_map/pack/pallas_call | solution.py:585
  3.2 7.3 %all-to-all-start = ((f32[8,64,128]{2,1,0:T(8,128)}), f32[8,64,128]{2,1,0:T(8,128)S(1)}, u32[]{:S(2)}, u32[]{:S(2)}) async-start(f32[8,64,128]{2,1,0:T(8,128)} %bitcast), calls=%async_computation | async-start | bytes 524288 | tf_op jit(solution)/shard_map/all_to_all | solution.py:605
  10.5 0.0 copy-start
  10.5 0.1 collective-permute-start.1
  10.6 0.7 %collective-permute-start = (f32[74,8,128]{2,1,0:T(8,128)S(1)}, f32[74,8,128]{2,1,0:T(8,128)S(1)}, u32[]{:S(2)}, u32[]{:S(2)}) collective-permute-start(f32[74,8,128]{2,1,0:T(8,128)S(1)} %get-tuple-element.24), channel_id=1, source_target_pairs={{1,2},{3,4},{5,6},{7,8},{9,10},{11,12},{13,14},{2,1},{4,3},{6,5},{... | collective-permute-start | bytes 909320 | tf_op jit(solution)/shard_map/ppermute | solution.py:613
  11.3 0.9 %collective-permute-done.1.mate = f32[81,8,128]{2,1,0:T(8,128)S(1)} collective-permute-done((f32[81,8,128]{2,1,0:T(8,128)S(1)}, f32[81,8,128]{2,1,0:T(8,128)S(1)}, u32[]{:S(2)}, u32[]{:S(2)}) %collective-permute-start.1) | collective-permute-done | bytes 331808 | tf_op jit(solution)/shard_map/ppermute | solution.py:614
  12.2 0.0 copy-done
  12.2 0.9 %first_velocity.1 = (f32[3,32,8,128]{3,2,1,0:T(8,128)S(1)}, f32[6,32,8,128]{3,2,1,0:T(8,128)S(1)}, f32[5,32,8,128]{3,2,1,0:T(8,128)S(1)}) custom-call(f32[3,8]{1,0:T(4,128)S(1)} %copy-done, f32[81,8,128]{2,1,0:T(8,128)S(1)} %get-tuple-element.26.own, f32[81,8,128]{2,1,0:T(8,128)S(1)} %collective-permute-done.1.mate), custom_call_target="tpu_custom_call" | custom-call | tf_op jit(solution)/shard_map/first_velocity/pallas_call | solution.py:616
  13.1 6.4 %all-to-all-done = f32[8,64,128]{2,1,0:T(8,128)S(1)} async-done(((f32[8,64,128]{2,1,0:T(8,128)}), f32[8,64,128]{2,1,0:T(8,128)S(1)}, u32[]{:S(2)}, u32[]{:S(2)}) %all-to-all-start) | async-done | bytes 262176 | tf_op jit(solution)/shard_map/all_to_all | solution.py:605
  19.5 0.0 collective-permute-start.2
  19.5 1.5 %collective-permute-done.2.swapped = f32[512,128]{1,0:T(8,128)S(1)} collective-permute-done((f32[512,128]{1,0:T(8,128)S(1)}, f32[512,128]{1,0:T(8,128)S(1)}, u32[]{:S(2)}, u32[]{:S(2)}) %collective-permute-start.2) | collective-permute-done | bytes 262176 | tf_op jit(solution)/shard_map/ppermute | solution.py:624
  21.1 2.0 %inner_substeps.1 = (f32[3,32,8,128]{3,2,1,0:T(8,128)S(1)}, f32[6,32,8,128]{3,2,1,0:T(8,128)S(1)}, f32[4,34,8,128]{3,2,1,0:T(8,128)S(1)}, f32[34,8,128]{2,1,0:T(...) custom-call(f32[512,128]{1,0:T(8,128)S(1)} %bitcast.5, ...), custom_call_target="tpu_custom_call", output_to_operand_aliasing={{0}: (3, {}), {1}: (4, {})} | custom-call | tf_op jit(solution)/shard_map/inner_substeps/pallas_call | solution.py:633
  23.1 0.0 collective-permute-done.border
  23.1 3.0 %outer_substeps.1 = (f32[3,32,8,128]{3,2,1,0:T(8,128)S(1)}, f32[6,32,8,128]{3,2,1,0:T(8,128)S(1)}, f32[5,32,8,128]{3,2,1,0:T(8,128)S(1)}, f32[4,34,8,128]{3,2,1,...) custom-call(f32[3,8]{1,0:T(4,128)S(1)} %copy-done, ...), custom_call_target="tpu_custom_call", output_to_operand_aliasing={{0}: (4, {}), {1}: (5, {}), {2}: (6, {}), {3}: (7, {}), {4}... | custom-call | tf_op jit(solution)/shard_map/outer_substeps/pallas_call | solution.py:644
  26.1 4.1 %all-to-all-start.1 = ((f32[16,16,128]{2,1,0:T(8,128)}), f32[16,16,128]{2,1,0:T(8,128)S(1)}, u32[]{:S(2)}, u32[]{:S(2)}) async-start(f32[16,16,128]{2,1,0:T(8,128)} %bitcast.2), calls=%async_computation.1 | async-start | bytes 262144 | tf_op jit(solution)/shard_map/all_to_all | solution.py:653
  30.2 2.1 %last_updates.1 = (f32[3,8,32,32]{3,2,1,0:T(8,128)}, f32[6,8,32,32]{3,2,1,0:T(8,128)}) custom-call(f32[3,32,8,128]{3,2,1,0:T(8,128)S(1)} %get-tuple-element.38.vel_all, f32[6,32,8,128]{3,2,1,0:T(8,128)S(1)} %get-tuple-element.39.stress_all, f32[5,32,8,128]{3,2,1,0:T(8,128)S(1)} %get-tuple-element.40.mats_all, f32[32,8,128]{2,1,0:T(8,128)S(1)} %get-tuple-element.41.loads_all), custom_call_target="tpu_custom_call" | custom-call | tf_op jit(solution)/shard_map/last_updates/pallas_call | solution.py:656
  32.3 5.8 %all-to-all-done.1 = f32[16,16,128]{2,1,0:T(8,128)S(1)} async-done(((f32[16,16,128]{2,1,0:T(8,128)}), f32[16,16,128]{2,1,0:T(8,128)S(1)}, u32[]{:S(2)}, u32[]{:S(2)}) %all-to-all-start.1) | async-done | bytes 131104 | tf_op jit(solution)/shard_map/all_to_all | solution.py:653
  38.1 0.9 %ocean_strips.1 = f32[4,2,32,128]{3,2,1,0:T(8,128)} custom-call(f32[256,128]{1,0:T(8,128)S(1)} %bitcast.6), custom_call_target="tpu_custom_call" | custom-call | tf_op jit(solution)/shard_map/ocean_strips/pallas_call | solution.py:666
Async XLA Ops:
  3.2 16.3 %all-to-all-start = ((f32[8,64,128]{2,1,0:T(8,128)}), f32[8,64,128]{2,1,0:T(8,128)S(1)}, u32[]{:S(2)}, u32[]{:S(2)}) async-start(f32[8,64,128]{2,1,0:T(8,128)} %bitcast), calls=%async_computation | async-start | bytes 524288 | tf_op jit(solution)/shard_map/all_to_all | solution.py:605
  10.5 1.7 %copy-start = (f32[3,8]{1,0:T(4,128)S(1)}, f32[3,8]{1,0:T(4,128)}, u32[]{:S(2)}) copy-start(f32[3,8]{1,0:T(4,128)} %table.3) | copy-start | bytes 292
  10.5 1.7 %collective-permute-start.1 = (f32[81,8,128]{2,1,0:T(8,128)S(1)}, f32[81,8,128]{2,1,0:T(8,128)S(1)}, u32[]{:S(2)}, u32[]{:S(2)}) collective-permute-start(f32[81,8,128]{2,1,0:T(8,128)S(1)} %get-tuple-element.26.own), channel_id=1, source_target_pairs={{0,1},{1,0},{2,3},{3,2},{4,5},{5,4},{6,7},{7,6},{8,9},{9,8},{10,11... | collective-permute-start | bytes 995336 | tf_op jit(solution)/shard_map/ppermute | solution.py:614
  10.6 12.5 %collective-permute-start = (f32[74,8,128]{2,1,0:T(8,128)S(1)}, f32[74,8,128]{2,1,0:T(8,128)S(1)}, u32[]{:S(2)}, u32[]{:S(2)}) collective-permute-start(f32[74,8,128]{2,1,0:T(8,128)S(1)} %get-tuple-element.24), channel_id=1, source_target_pairs={{1,2},{3,4},{5,6},{7,8},{9,10},{11,12},{13,14},{2,1},{4,3},{6,5},{... | collective-permute-start | bytes 909320 | tf_op jit(solution)/shard_map/ppermute | solution.py:613
  19.5 1.5 %collective-permute-start.2 = (f32[512,128]{1,0:T(8,128)S(1)}, f32[512,128]{1,0:T(8,128)S(1)}, u32[]{:S(2)}, u32[]{:S(2)}) collective-permute-start(f32[512,128]{1,0:T(8,128)S(1)} %bitcast.4), channel_id=1, source_target_pairs={{0,1},{1,0},{2,3},{3,2},{4,5},{5,4},{6,7},{7,6},{8,9},{9,8},{10,11... | collective-permute-start | bytes 786440 | tf_op jit(solution)/shard_map/ppermute | solution.py:624
  26.1 12.0 %all-to-all-start.1 = ((f32[16,16,128]{2,1,0:T(8,128)}), f32[16,16,128]{2,1,0:T(8,128)S(1)}, u32[]{:S(2)}, u32[]{:S(2)}) async-start(f32[16,16,128]{2,1,0:T(8,128)} %bitcast.2), calls=%async_computation.1 | async-start | bytes 262144 | tf_op jit(solution)/shard_map/all_to_all | solution.py:653

commit v13 on v12

--- a/solution.py
+++ b/solution.py
@@ -43,16 +43,19 @@
         self.unrolled = self.sub * self.lanes <= 1024
         assert devices % 2 == 0 and cells == HALO and self.block * self.chunks == LANES
 
-    def planes(self, start, stop, body):
+    def planes(self, start, stop, body, batch=1):
         if self.unrolled:
-            for j in range(start, stop):
-                body(j)
+            for j in range(start, stop, batch):
+                body(j, min(batch, stop - j))
         else:
             def run(j, carry):
-                body(j)
+                body(j, 1)
                 return carry
 
             lax.fori_loop(start, stop, run, 0)
+
+
+BATCH = 8
 
 
 def odd_device():
@@ -197,84 +200,105 @@
             lax.div(self.lane, plan.ny) * plan.sub + self.row
         ).astype(F32)
 
+    def by_lane(self, f, shift):
+        return pltpu.roll(f, shift % self.plan.lanes, f.ndim - 1)
+
+    def by_row(self, f, shift):
+        return pltpu.roll(f, shift % self.plan.sub, f.ndim - 2)
+
     def dy(self, f):
-        lanes = self.plan.lanes
-        return pltpu.roll(f, lanes - 1, 1) * self.not_high_y - pltpu.roll(f, 1, 1) * self.not_low_y
+        return self.by_lane(f, -1) * self.not_high_y - self.by_lane(f, 1) * self.not_low_y
 
     def below(self, f):
         plan = self.plan
-        moved = pltpu.roll(f, plan.sub - 1, 0)
+        moved = self.by_row(f, -1)
         if plan.chunks > 1:
-            moved = jnp.where(self.last_row, pltpu.roll(moved, plan.lanes - plan.ny, 1), moved)
+            moved = jnp.where(self.last_row, self.by_lane(moved, -plan.ny), moved)
         return jnp.where(self.floor_cell, 0.0, moved)
 
     def above(self, f, top):
         plan = self.plan
-        moved = pltpu.roll(f, 1, 0)
+        moved = self.by_row(f, 1)
         if plan.chunks > 1:
-            moved = jnp.where(self.first_row, pltpu.roll(moved, plan.ny, 1), moved)
+            moved = jnp.where(self.first_row, self.by_lane(moved, plan.ny), moved)
         return jnp.where(self.top, top, moved)
 
     def seafloor(self, vz):
-        row = self.over_chunks(jnp.where(self.top, vz, 0.0)[0:1])
-        return jnp.broadcast_to(row, vz.shape)
+        row = self.over_chunks(jnp.where(self.top, vz, 0.0))
+        return jnp.broadcast_to(row[..., 0:1, :], vz.shape)
+
+    def on_top(self, f):
+        shift = self.plan.sub // 2
+        while shift:
+            f = f + self.by_row(f, shift)
+            shift //= 2
+        return jnp.where(self.top, self.over_chunks(f), 0.0)
 
     def over_chunks(self, f):
         shift = self.plan.ny
         while shift < self.plan.lanes:
-            f = f + pltpu.roll(f, shift, 1)
+            f = f + self.by_lane(f, shift)
             shift *= 2
         return f
 
 
-def acceleration(sh, stress, j):
-    sxy, sxz = stress[SXY, j], stress[SXZ, j]
-    syz, szz = stress[SYZ, j], stress[SZZ, j]
-    ax = stress[SXX, j + 1] - stress[SXX, j - 1] + sh.dy(sxy) + sh.below(sxz) - sh.above(sxz, 0.0)
-    ay = stress[SXY, j + 1] - stress[SXY, j - 1] + sh.dy(stress[SYY, j])
+def acceleration(sh, stress, j, count):
+    at, before, after = (pl.ds(j + k, count) for k in (0, -1, 1))
+    sxy, sxz = stress[SXY, at], stress[SXZ, at]
+    ax = stress[SXX, after] - stress[SXX, before] + sh.dy(sxy) + sh.below(sxz) - sh.above(sxz, 0.0)
+    syz = stress[SYZ, at]
+    ay = stress[SXY, after] - stress[SXY, before] + sh.dy(stress[SYY, at])
     ay = ay + sh.below(syz) - sh.above(syz, 0.0)
-    az = stress[SXZ, j + 1] - stress[SXZ, j - 1] + sh.dy(syz) + sh.below(szz) - sh.above(szz, 0.0)
+    szz = stress[SZZ, at]
+    az = stress[SXZ, after] - stress[SXZ, before] + sh.dy(syz) + sh.below(szz) - sh.above(szz, 0.0)
     return ax, ay, az
 
 
-def strained(sh, vel, stress, mats, j):
-    vx, vy, vz = vel[VX, j], vel[VY, j], vel[VZ, j]
-    exx = vel[VX, j + 1] - vel[VX, j - 1]
+def strained(sh, vel, stress, mats, j, count):
+    at, before, after = (pl.ds(j + k, count) for k in (0, -1, 1))
+    vx, vy, vz = vel[VX, at], vel[VY, at], vel[VZ, at]
+    exx = vel[VX, after] - vel[VX, before]
     eyy = sh.dy(vy)
     ezz = sh.below(vz) - sh.above(vz, vz)
-    mu = mats[SHEAR, j]
+    mu = mats[SHEAR, at]
     mu2 = mu + mu
-    common = mats[LAMB, j] * (exx + eyy + ezz)
-    exy = sh.dy(vx) + vel[VY, j + 1] - vel[VY, j - 1]
-    exz = sh.below(vx) - sh.above(vx, vx) + vel[VZ, j + 1] - vel[VZ, j - 1]
+    common = mats[LAMB, at] * (exx + eyy + ezz)
+    yield SXX, stress[SXX, at] + (common + mu2 * exx)
+    yield SYY, stress[SYY, at] + (common + mu2 * eyy)
+    yield SZZ, stress[SZZ, at] + (common + mu2 * ezz)
+    exy = sh.dy(vx) + vel[VY, after] - vel[VY, before]
+    yield SXY, stress[SXY, at] + mu * exy
+    exz = sh.below(vx) - sh.above(vx, vx) + vel[VZ, after] - vel[VZ, before]
+    yield SXZ, stress[SXZ, at] + (mu * exz + mats[FAULT, at])
     eyz = sh.below(vy) - sh.above(vy, vy) + sh.dy(vz)
-    return (
-        stress[SXX, j] + (common + mu2 * exx),
-        stress[SYY, j] + (common + mu2 * eyy),
-        stress[SZZ, j] + (common + mu2 * ezz),
-        stress[SXY, j] + mu * exy,
-        stress[SXZ, j] + (mu * exz + mats[FAULT, j]),
-        stress[SYZ, j] + mu * eyz,
-    )
-
-
-def bring(plan, sh, table, state, ref, count, x, column, first):
+    yield SYZ, stress[SYZ, at] + mu * eyz
+
+
+def bring(plan, sh, table, state, ref, fields, x, count, column, first):
     vel, stress, mats = state
+    to = pl.ds(column, count)
+
+    def read(f):
+        return ref[pl.ds(f * fields + x, count)]
+
     for f in range(3):
-        vel[f, column] = ref[f * count + x]
+        vel[f, to] = read(f)
     for f in range(6):
-        stress[f, column] = ref[(3 + f) * count + x]
-    zone = ref[9 * count + x]
+        stress[f, to] = read(3 + f)
+    zone = read(9)
     values = [jnp.zeros_like(zone) for _ in range(3)]
     for z in range(ZONES):
         here = zone == float(z + 1)
         values = [jnp.where(here, table[c, z], values[c]) for c in range(3)]
     for c in range(3):
-        mats[c, column] = values[c] * HALF
-    slip = ref[ref.shape[0] - 1, pl.ds(first + x, 1), :]
-    slip = jnp.broadcast_to(slip, zone.shape)
-    mats[FAULT, column] = jnp.where(sh.row == (plan.depth // 2) % plan.sub, DT * slip, 0.0)
-    mats[FLOOR, column] = sh.seafloor(ref[VZ * count + x])
+        mats[c, to] = values[c] * HALF
+    mats[FLOOR, to] = sh.seafloor(read(VZ))
+    for i in range(count):
+        slip = ref[ref.shape[0] - 1, pl.ds(first + x + i, 1), :]
+        slip = jnp.broadcast_to(slip, (plan.sub, plan.lanes))
+        mats[FAULT, column + i] = jnp.where(
+            sh.row == (plan.depth // 2) % plan.sub, DT * slip, 0.0
+        )
 
 
 def begin_kernel(plan, table, own, mate, vel, stress, mats):
@@ -287,17 +311,19 @@
         plan.planes(
             0,
             cells,
-            lambda x, start=start, ref=ref: bring(
-                plan, sh, table, state, ref, cells, x, start + x, 0
+            lambda x, count, start=start, ref=ref: bring(
+                plan, sh, table, state, ref, cells, x, count, start + x, 0
             ),
+            BATCH,
         )
 
-    def move(j):
-        b = mats[BUOY, j]
-        for f, a in enumerate(acceleration(sh, stress, j)):
-            vel[f, j] = vel[f, j] + b * a
-
-    plan.planes(HALO + 1, HALO + 2 * cells - 1, move)
+    def move(j, count):
+        at = pl.ds(j, count)
+        b = mats[BUOY, at]
+        for f, a in enumerate(acceleration(sh, stress, j, count)):
+            vel[f, at] = vel[f, at] + b * a
+
+    plan.planes(HALO + 1, HALO + 2 * cells - 1, move, BATCH)
 
 
 class Updates:
@@ -306,64 +332,70 @@
         self.vel, self.stress, self.mats = vel, stress, mats
         self.oc, self.water, self.bottom, self.loads = oc, water, bottom, loads
 
-    def flow_x(self, j):
+    def flow_x(self, j, count):
         oc = self.oc
-        oc[1, j + 1] = self.water[j + 1] * (oc[1, j + 1] - HALF * (oc[0, j + 2] - oc[0, j]))
-
-    def flow(self, j):
+        before, at, after = (pl.ds(j + k, count) for k in range(3))
+        oc[1, at] = self.water[at] * (oc[1, at] - HALF * (oc[0, after] - oc[0, before]))
+
+    def flow(self, j, count):
         oc, sh = self.oc, self.sh
-        p = oc[0, j + 1]
-        wet = self.water[j + 1]
-        oc[2, j + 1] = wet * (oc[2, j + 1] - HALF * sh.dy(p))
-        rise = sh.below(p) + self.bottom[j + 1] * p - sh.above(p, -p)
-        oc[3, j + 1] = wet * (oc[3, j + 1] - (HALF * rise + (DT * GRAV) * p))
-
-    def press(self, j, start):
+        at = pl.ds(j + 1, count)
+        p = oc[0, at]
+        wet = self.water[at]
+        rise = sh.below(p) + self.bottom[at] * p - sh.above(p, -p)
+        oc[3, at] = wet * (oc[3, at] - (HALF * rise + (DT * GRAV) * p))
+        oc[2, at] = wet * (oc[2, at] - HALF * sh.dy(p))
+
+    def press(self, j, count, start):
         oc, sh = self.oc, self.sh
-        w = oc[3, j + 1]
-        floor = self.mats[FLOOR, j] if start else sh.seafloor(self.vel[VZ, j])
-        rise = sh.below(w) + self.bottom[j + 1] * floor - sh.above(w, w)
-        total = oc[1, j + 2] - oc[1, j] + sh.dy(oc[2, j + 1]) + rise
-        oc[0, j + 1] = self.water[j + 1] * (oc[0, j + 1] - (HALF * KBULK) * total)
-
-    def load(self, j):
-        sh, plan = self.sh, self.plan
-        column = jnp.sum(self.bottom[j + 1] * self.oc[0, j + 1], axis=0, keepdims=True)
-        column = jnp.broadcast_to(sh.over_chunks(column), (plan.sub, plan.lanes))
-        return jnp.where(sh.top, column, 0.0)
-
-    def keep(self, j):
-        self.loads[j] = self.load(j)
-
-    def add_load(self, j):
-        self.vel[VZ, j] = self.vel[VZ, j] + self.mats[BUOY, j] * self.load(j)
-
-    def move(self, j):
+        before, at, after = (pl.ds(j + k, count) for k in range(3))
+        crust = pl.ds(j, count)
+        w = oc[3, at]
+        floor = self.mats[FLOOR, crust] if start else sh.seafloor(self.vel[VZ, crust])
+        rise = sh.below(w) + self.bottom[at] * floor - sh.above(w, w)
+        total = oc[1, after] - oc[1, before] + sh.dy(oc[2, at]) + rise
+        oc[0, at] = self.water[at] * (oc[0, at] - (HALF * KBULK) * total)
+
+    def load(self, j, count):
+        at = pl.ds(j + 1, count)
+        return self.sh.on_top(self.bottom[at] * self.oc[0, at])
+
+    def keep(self, j, count):
+        self.loads[pl.ds(j, count)] = self.load(j, count)
+
+    def add_load(self, j, count):
+        at = pl.ds(j, count)
+        self.vel[VZ, at] = self.vel[VZ, at] + self.mats[BUOY, at] * self.load(j, count)
+
+    def move(self, j, count):
         vel = self.vel
-        ax, ay, az = acceleration(self.sh, self.stress, j)
-        b = self.mats[BUOY, j]
-        vel[VX, j] = vel[VX, j] + b * ax
-        vel[VY, j] = vel[VY, j] + b * ay
-        vel[VZ, j] = vel[VZ, j] + b * (az + self.load(j))
-
-    def strain(self, j):
-        for f, value in enumerate(strained(self.sh, self.vel, self.stress, self.mats, j)):
-            self.stress[f, j] = value
+        at = pl.ds(j, count)
+        ax, ay, az = acceleration(self.sh, self.stress, j, count)
+        b = self.mats[BUOY, at]
+        vel[VX, at] = vel[VX, at] + b * ax
+        vel[VY, at] = vel[VY, at] + b * ay
+        vel[VZ, at] = vel[VZ, at] + b * (az + self.load(j, count))
+
+    def strain(self, j, count):
+        for f, value in strained(self.sh, self.vel, self.stress, self.mats, j, count):
+            self.stress[f, pl.ds(j, count)] = value
 
     def run(self, spans, moved):
-        planes = self.plan.planes
         for t in range(STEPS):
-            planes(*spans(t, 0), self.flow_x)
-            planes(*spans(t, 1), self.flow)
-            planes(*spans(t, 1), lambda j, t=t: self.press(j, t == 0))
+            def planes(inset, update, t=t):
+                self.plan.planes(*spans(t, inset), update, BATCH)
+
+            planes(0, self.flow_x)
+            planes(1, self.flow)
+            planes(1, functools.partial(self.press, start=t == 0))
             if t == STEPS - 1:
-                planes(*spans(t, 1), self.keep)
+                planes(1, self.keep)
             elif t == 0 and moved:
-                planes(*spans(t, 1), self.add_load)
+                planes(1, self.add_load)
             else:
-                planes(*spans(t, 1), self.move)
+                planes(1, self.move)
             if t < STEPS - 2:
-                planes(*spans(t, 2), self.strain)
+                planes(2, self.strain)
 
 
 def inner_kernel(
@@ -408,26 +440,26 @@
             mine = (sh.lane >= kc * plan.ny) & (sh.lane < (kc + 1) * plan.ny)
             depths[i, kc * sub : (kc + 1) * sub, :] = sh.over_chunks(jnp.where(mine, deep, 0.0))
 
-    def mask(owner, j):
+    def mask(owner, j, _):
         low = jnp.broadcast_to(depths[owner, pl.ds(j - owner * cells, 1), :], (sub, plan.lanes))
         wet = jnp.where(sh.depth < low, 1.0, 0.0).astype(F32)
         water[j] = wet
         bottom[j] = jnp.where(sh.depth == low - 1.0, 1.0, 0.0).astype(F32)
         oc[0, j] = oc[0, j] * wet
 
-    def mask_x(j):
+    def mask_x(j, _):
         oc[1, j] = oc[1, j] * water[j]
 
-    def mask_yw(j):
+    def mask_yw(j, _):
         oc[2, j] = oc[2, j] * water[j]
         oc[3, j] = oc[3, j] * water[j]
 
-    plan.planes(0, plan.width + 2, lambda j: mask(0, j))
-    plan.planes(plan.width + 2, columns + 2, lambda j: mask(1, j))
+    plan.planes(0, plan.width + 2, lambda j, _: mask(0, j, _))
+    plan.planes(plan.width + 2, columns + 2, lambda j, _: mask(1, j, _))
     plan.planes(1, columns + 1, mask_x)
     plan.planes(2, columns, mask_yw)
 
-    def bring_in(j):
+    def bring_in(j, _):
         for f in range(3):
             vel[f, j] = vel_in[f, j]
         for f in range(6):
@@ -460,7 +492,10 @@
         plan.planes(
             0,
             near,
-            lambda x: bring(plan, sh, table, state, border, near, x, low + x, 1 - core),
+            lambda x, count: bring(
+                plan, sh, table, state, border, near, x, count, low + x, 1 - core
+            ),
+            BATCH,
         )
         for i, f in enumerate((SXX, SXY, SXZ)):
             stress[f, far] = border[10 * near + i]
@@ -501,29 +536,32 @@
     vel_in, stress_in = vel_all.at[:, window], stress_all.at[:, window]
     mats, loads = mats_all.at[:, window], loads_all.at[window]
 
-    def put(out, f, x, plane):
+    def put(out, f, x, count, planes):
         for kc in range(chunks):
-            out[f, x, kc * sub : (kc + 1) * sub, :] = plane[:, kc * ny : (kc + 1) * ny]
-
-    def strain(j):
-        for f, value in enumerate(strained(sh, vel_in, stress_in, mats, j)):
-            stress[f, j] = value
-
-    def move(j):
-        ax, ay, az = acceleration(sh, stress, j)
-        b = mats[BUOY, j]
-        for f, a in enumerate((ax, ay, az + loads[j])):
-            vel[f, j] = vel_in[f, j] + b * a
-
-    def finish(x):
+            out[f, pl.ds(x, count), kc * sub : (kc + 1) * sub, :] = planes[
+                :, :, kc * ny : (kc + 1) * ny
+            ]
+
+    def strain(j, count):
+        for f, value in strained(sh, vel_in, stress_in, mats, j, count):
+            stress[f, pl.ds(j, count)] = value
+
+    def move(j, count):
+        at = pl.ds(j, count)
+        ax, ay, az = acceleration(sh, stress, j, count)
+        b = mats[BUOY, at]
+        for f, a in enumerate((ax, ay, az + loads[at])):
+            vel[f, at] = vel_in[f, at] + b * a
+
+    def finish(x, count):
         for f in range(3):
-            put(vel_out, f, x, vel[f, x + HALO])
-        for f, value in enumerate(strained(sh, vel, stress, mats, x + HALO)):
-            put(stress_out, f, x, value)
-
-    plan.planes(first, last, strain)
-    plan.planes(first + 1, last - 1, move)
-    plan.planes(0, cells, finish)
+            put(vel_out, f, x, count, vel[f, pl.ds(x + HALO, count)])
+        for f, value in strained(sh, vel, stress, mats, x + HALO, count):
+            put(stress_out, f, x, count, value)
+
+    plan.planes(first, last, strain, BATCH)
+    plan.planes(first + 1, last - 1, move, BATCH)
+    plan.planes(0, cells, finish, BATCH)
 
 
 def unpack_kernel(plan, arrived, ocean, turned):

time: 39.4 us -> 39.4 us (level)
  transfers between devices with their start and end apart: 5 -> 5, of which waited for: 4 -> 4; matrix products, arithmetic and copies ran while one was open for 0% -> 0% of each run, Pallas kernels for 13% -> 12%
where the time goes in v13:
time: 39.4 us; the launch traced here: 39 us
  waiting for transfers between devices  15 us (38%)
  starting transfers between devices  12.1 us (31%)
  Pallas kernels  11.3 us (29%)
  between operations  0.68 us (2%)
    all_to_all x1, starting transfers between devices, on_device(): lax.all_to_all(message.reshape(n // 2, 2 * plan.rows, LANES), 'map', spli...  7.26 us
    all_to_all x1, waiting for transfers between devices, on_device(): lax.all_to_all(message.reshape(n // 2, 2 * plan.rows, LANES), 'map', spli...  6.41 us
    all_to_all x1, waiting for transfers between devices, on_device(): lax.all_to_all(back.reshape(n, plan.back_rows, LANES), 'map', split_axis=...  6.08 us
    all_to_all x1, starting transfers between devices, on_device(): lax.all_to_all(back.reshape(n, plan.back_rows, LANES), 'map', split_axis=...  4.08 us
    pallas_call x1, Pallas kernels, on_device(): call(outer_kernel, 'outer_substeps', tuple((planes_of[k] for k in ('vel',...  2.99 us
    pallas_call x1, Pallas kernels, on_device(): call(pack_kernel, 'pack', (shape(10 * cells + 1, sub, lanes), shape(10 *...  2.6 us
    pallas_call x1, Pallas kernels, on_device(): call(inner_kernel, 'inner_substeps', tuple((planes_of[k] for k in ('vel',...  2.02 us
    pallas_call x1, Pallas kernels, on_device(): call(end_kernel, 'last_updates', (shape(*velocity.shape), shape(*stress.s...  1.85 us
  transfers between devices with their start and end apart: 5, of which 4 were waited for; matrix products, arithmetic and copies ran while one was open for 0% of the time, Pallas kernels for 12%

profile of v13, /device:TPU:0, one launch (start us, length us, event | category | flops | bytes accessed | tf_op | source)
XLA Modules:
  0.0 39.0 jit_solution(15816904989215716301)
XLA Ops:
  0.6 2.6 %pack.1 = (f32[81,8,128]{2,1,0:T(8,128)S(1)}, f32[74,8,128]{2,1,0:T(8,128)S(1)}, f32[512,128]{1,0:T(8,128)}) custom-call(f32[3,8,32,32]{3,2,1,0:T(8,128)} %vel_ref.1, f32[6,8,32,32]{3,2,1,0:T(8,128)} %stress_ref.1, s32[8,32,32]{2,1,0:T(8,128)} %zones_ref.1, f32[8,32]{1,0:T(8,128)} %slip_ref.1, f32[4,2,32,128]{3,2,1,0:T(8,128)} %ocean_ref.1, s32[2,128]{1,0:T(2,128)} %bathy_ref.1), custom_call_target="tpu_custom_call" | custom-call | tf_op jit(solution)/shard_map/pack/pallas_call | solution.py:623
  3.2 7.3 %all-to-all-start = ((f32[8,64,128]{2,1,0:T(8,128)}), f32[8,64,128]{2,1,0:T(8,128)S(1)}, u32[]{:S(2)}, u32[]{:S(2)}) async-start(f32[8,64,128]{2,1,0:T(8,128)} %bitcast), calls=%async_computation | async-start | bytes 524288 | tf_op jit(solution)/shard_map/all_to_all | solution.py:643
  10.5 0.0 copy-start
  10.5 0.1 collective-permute-start.1
  10.6 0.7 %collective-permute-start = (f32[74,8,128]{2,1,0:T(8,128)S(1)}, f32[74,8,128]{2,1,0:T(8,128)S(1)}, u32[]{:S(2)}, u32[]{:S(2)}) collective-permute-start(f32[74,8,128]{2,1,0:T(8,128)S(1)} %get-tuple-element.24), channel_id=1, source_target_pairs={{1,2},{3,4},{5,6},{7,8},{9,10},{11,12},{13,14},{2,1},{4,3},{6,5},{... | collective-permute-start | bytes 909320 | tf_op jit(solution)/shard_map/ppermute | solution.py:651
  11.3 0.9 %collective-permute-done.1.mate = f32[81,8,128]{2,1,0:T(8,128)S(1)} collective-permute-done((f32[81,8,128]{2,1,0:T(8,128)S(1)}, f32[81,8,128]{2,1,0:T(8,128)S(1)}, u32[]{:S(2)}, u32[]{:S(2)}) %collective-permute-start.1) | collective-permute-done | bytes 331808 | tf_op jit(solution)/shard_map/ppermute | solution.py:652
  12.2 0.0 copy-done
  12.2 0.9 %first_velocity.1 = (f32[3,32,8,128]{3,2,1,0:T(8,128)S(1)}, f32[6,32,8,128]{3,2,1,0:T(8,128)S(1)}, f32[5,32,8,128]{3,2,1,0:T(8,128)S(1)}) custom-call(f32[3,8]{1,0:T(4,128)S(1)} %copy-done, f32[81,8,128]{2,1,0:T(8,128)S(1)} %get-tuple-element.26.own, f32[81,8,128]{2,1,0:T(8,128)S(1)} %collective-permute-done.1.mate), custom_call_target="tpu_custom_call" | custom-call | tf_op jit(solution)/shard_map/first_velocity/pallas_call | solution.py:654
  13.1 6.4 %all-to-all-done = f32[8,64,128]{2,1,0:T(8,128)S(1)} async-done(((f32[8,64,128]{2,1,0:T(8,128)}), f32[8,64,128]{2,1,0:T(8,128)S(1)}, u32[]{:S(2)}, u32[]{:S(2)}) %all-to-all-start) | async-done | bytes 262176 | tf_op jit(solution)/shard_map/all_to_all | solution.py:643
  19.5 0.0 collective-permute-start.2
  19.5 1.5 %collective-permute-done.2.swapped = f32[512,128]{1,0:T(8,128)S(1)} collective-permute-done((f32[512,128]{1,0:T(8,128)S(1)}, f32[512,128]{1,0:T(8,128)S(1)}, u32[]{:S(2)}, u32[]{:S(2)}) %collective-permute-start.2) | collective-permute-done | bytes 262176 | tf_op jit(solution)/shard_map/ppermute | solution.py:662
  21.1 2.0 %inner_substeps.1 = (f32[3,32,8,128]{3,2,1,0:T(8,128)S(1)}, f32[6,32,8,128]{3,2,1,0:T(8,128)S(1)}, f32[4,34,8,128]{3,2,1,0:T(8,128)S(1)}, f32[34,8,128]{2,1,0:T(...) custom-call(f32[512,128]{1,0:T(8,128)S(1)} %bitcast.5, ...), custom_call_target="tpu_custom_call", output_to_operand_aliasing={{0}: (3, {}), {1}: (4, {})} | custom-call | tf_op jit(solution)/shard_map/inner_substeps/pallas_call | solution.py:671
  23.1 0.0 collective-permute-done.border
  23.1 3.0 %outer_substeps.1 = (f32[3,32,8,128]{3,2,1,0:T(8,128)S(1)}, f32[6,32,8,128]{3,2,1,0:T(8,128)S(1)}, f32[5,32,8,128]{3,2,1,0:T(8,128)S(1)}, f32[4,34,8,128]{3,2,1,...) custom-call(f32[3,8]{1,0:T(4,128)S(1)} %copy-done, ...), custom_call_target="tpu_custom_call", output_to_operand_aliasing={{0}: (4, {}), {1}: (5, {}), {2}: (6, {}), {3}: (7, {}), {4}... | custom-call | tf_op jit(solution)/shard_map/outer_substeps/pallas_call | solution.py:682
  26.1 4.1 %all-to-all-start.1 = ((f32[16,16,128]{2,1,0:T(8,128)}), f32[16,16,128]{2,1,0:T(8,128)S(1)}, u32[]{:S(2)}, u32[]{:S(2)}) async-start(f32[16,16,128]{2,1,0:T(8,128)} %bitcast.2), calls=%async_computation.1 | async-start | bytes 262144 | tf_op jit(solution)/shard_map/all_to_all | solution.py:691
  30.2 1.9 %last_updates.1 = (f32[3,8,32,32]{3,2,1,0:T(8,128)}, f32[6,8,32,32]{3,2,1,0:T(8,128)}) custom-call(f32[3,32,8,128]{3,2,1,0:T(8,128)S(1)} %get-tuple-element.38.vel_all, f32[6,32,8,128]{3,2,1,0:T(8,128)S(1)} %get-tuple-element.39.stress_all, f32[5,32,8,128]{3,2,1,0:T(8,128)S(1)} %get-tuple-element.40.mats_all, f32[32,8,128]{2,1,0:T(8,128)S(1)} %get-tuple-element.41.loads_all), custom_call_target="tpu_custom_call" | custom-call | tf_op jit(solution)/shard_map/last_updates/pallas_call | solution.py:694
  32.0 6.1 %all-to-all-done.1 = f32[16,16,128]{2,1,0:T(8,128)S(1)} async-done(((f32[16,16,128]{2,1,0:T(8,128)}), f32[16,16,128]{2,1,0:T(8,128)S(1)}, u32[]{:S(2)}, u32[]{:S(2)}) %all-to-all-start.1) | async-done | bytes 131104 | tf_op jit(solution)/shard_map/all_to_all | solution.py:691
  38.1 0.9 %ocean_strips.1 = f32[4,2,32,128]{3,2,1,0:T(8,128)} custom-call(f32[256,128]{1,0:T(8,128)S(1)} %bitcast.6), custom_call_target="tpu_custom_call" | custom-call | tf_op jit(solution)/shard_map/ocean_strips/pallas_call | solution.py:704
Async XLA Ops:
  3.2 16.3 %all-to-all-start = ((f32[8,64,128]{2,1,0:T(8,128)}), f32[8,64,128]{2,1,0:T(8,128)S(1)}, u32[]{:S(2)}, u32[]{:S(2)}) async-start(f32[8,64,128]{2,1,0:T(8,128)} %bitcast), calls=%async_computation | async-start | bytes 524288 | tf_op jit(solution)/shard_map/all_to_all | solution.py:643
  10.5 1.7 %copy-start = (f32[3,8]{1,0:T(4,128)S(1)}, f32[3,8]{1,0:T(4,128)}, u32[]{:S(2)}) copy-start(f32[3,8]{1,0:T(4,128)} %table.3) | copy-start | bytes 292
  10.5 1.7 %collective-permute-start.1 = (f32[81,8,128]{2,1,0:T(8,128)S(1)}, f32[81,8,128]{2,1,0:T(8,128)S(1)}, u32[]{:S(2)}, u32[]{:S(2)}) collective-permute-start(f32[81,8,128]{2,1,0:T(8,128)S(1)} %get-tuple-element.26.own), channel_id=1, source_target_pairs={{0,1},{1,0},{2,3},{3,2},{4,5},{5,4},{6,7},{7,6},{8,9},{9,8},{10,11... | collective-permute-start | bytes 995336 | tf_op jit(solution)/shard_map/ppermute | solution.py:652
  10.6 12.5 %collective-permute-start = (f32[74,8,128]{2,1,0:T(8,128)S(1)}, f32[74,8,128]{2,1,0:T(8,128)S(1)}, u32[]{:S(2)}, u32[]{:S(2)}) collective-permute-start(f32[74,8,128]{2,1,0:T(8,128)S(1)} %get-tuple-element.24), channel_id=1, source_target_pairs={{1,2},{3,4},{5,6},{7,8},{9,10},{11,12},{13,14},{2,1},{4,3},{6,5},{... | collective-permute-start | bytes 909320 | tf_op jit(solution)/shard_map/ppermute | solution.py:651
  19.5 1.5 %collective-permute-start.2 = (f32[512,128]{1,0:T(8,128)S(1)}, f32[512,128]{1,0:T(8,128)S(1)}, u32[]{:S(2)}, u32[]{:S(2)}) collective-permute-start(f32[512,128]{1,0:T(8,128)S(1)} %bitcast.4), channel_id=1, source_target_pairs={{0,1},{1,0},{2,3},{3,2},{4,5},{5,4},{6,7},{7,6},{8,9},{9,8},{10,11... | collective-permute-start | bytes 786440 | tf_op jit(solution)/shard_map/ppermute | solution.py:662
  26.1 12.0 %all-to-all-start.1 = ((f32[16,16,128]{2,1,0:T(8,128)}), f32[16,16,128]{2,1,0:T(8,128)S(1)}, u32[]{:S(2)}, u32[]{:S(2)}) async-start(f32[16,16,128]{2,1,0:T(8,128)} %bitcast.2), calls=%async_computation.1 | async-start | bytes 262144 | tf_op jit(solution)/shard_map/all_to_all | solution.py:691

commit v14 on v13

--- a/solution.py
+++ b/solution.py
@@ -75,11 +75,11 @@
     return out
 
 
-def pack_kernel(
-    plan, vel_ref, stress_ref, zones_ref, slip_ref, ocean_ref, bathy_ref, crust, border, message_out,
-    vel, stress, zones, slip, ocean, bathy, turned, grouped, extra, message, sems,
+def ocean_kernel(
+    plan, vel_ref, stress_ref, zones_ref, slip_ref, ocean_ref, bathy_ref,
+    message_out, vel, stress, zones, slip, ocean, bathy, turned, grouped, extra, message, sems,
 ):
-    cells, sub, chunks, ny = plan.cells, plan.sub, plan.chunks, plan.ny
+    cells, sub, chunks = plan.cells, plan.sub, plan.chunks
     n, strips, block, sent, rows = plan.n, plan.strips, plan.block, plan.sent_groups, plan.rows
     pairs = (
         (ocean_ref, ocean),
@@ -148,23 +148,25 @@
                 new = jnp.where((lane >= slot + sub) & (lane < slot + 2 * sub), floor, new)
                 message[pl.ds(at, pairs, stride=2 * rows), :] = new
     message_out[...] = message[...]
+    for copy in copies[2:]:
+        copy.wait()
+
+
+def crust_kernel(plan, vel, stress, zones, slip, crust, border):
+    cells, sub, chunks, ny = plan.cells, plan.sub, plan.chunks, plan.ny
 
     def joined(ref, *at):
         parts = [ref[(*at, pl.ds(kc * sub, sub), slice(None))] for kc in range(chunks)]
         return jnp.concatenate(parts, axis=-1) if chunks > 1 else parts[0]
 
-    copies[2].wait()
     for f in range(3):
         for x in range(cells):
             crust[f * cells + x] = joined(vel, f, x)
-    copies[3].wait()
     for f in range(6):
         for x in range(cells):
             crust[(3 + f) * cells + x] = joined(stress, f, x)
-    copies[4].wait()
     for x in range(cells):
         crust[9 * cells + x] = (joined(zones, x) + 1).astype(F32)
-    copies[5].wait()
     fault_chunk = (plan.depth // 2) // sub
     pieces = [
         slip[...] if kc == fault_chunk else jnp.zeros((cells, ny), F32) for kc in range(chunks)
@@ -274,7 +276,7 @@
     yield SYZ, stress[SYZ, at] + mu * eyz
 
 
-def bring(plan, sh, table, state, ref, fields, x, count, column, first):
+def bring(plan, sh, material, state, ref, fields, x, count, column, first):
     vel, stress, mats = state
     to = pl.ds(column, count)
 
@@ -289,7 +291,7 @@
     values = [jnp.zeros_like(zone) for _ in range(3)]
     for z in range(ZONES):
         here = zone == float(z + 1)
-        values = [jnp.where(here, table[c, z], values[c]) for c in range(3)]
+        values = [jnp.where(here, material(c, z), values[c]) for c in range(3)]
     for c in range(3):
         mats[c, to] = values[c] * HALF
     mats[FLOOR, to] = sh.seafloor(read(VZ))
@@ -301,7 +303,7 @@
         )
 
 
-def begin_kernel(plan, table, own, mate, vel, stress, mats):
+def begin_kernel(plan, table, own, mate, vel, stress, mats, rows):
     cells = plan.cells
     sh = Shifts(plan)
     odd = odd_device()
@@ -312,7 +314,7 @@
             0,
             cells,
             lambda x, count, start=start, ref=ref: bring(
-                plan, sh, table, state, ref, cells, x, count, start + x, 0
+                plan, sh, lambda c, z: table[c, z], state, ref, cells, x, count, start + x, 0
             ),
             BATCH,
         )
@@ -324,6 +326,10 @@
             vel[f, at] = vel[f, at] + b * a
 
     plan.planes(HALO + 1, HALO + 2 * cells - 1, move, BATCH)
+    for c in range(3):
+        for z in range(ZONES):
+            at = c * ZONES + z
+            rows[at : at + 1, :] = jnp.full((1, plan.lanes), table[c, z], F32)
 
 
 class Updates:
@@ -380,7 +386,7 @@
         for f, value in strained(self.sh, self.vel, self.stress, self.mats, j, count):
             self.stress[f, pl.ds(j, count)] = value
 
-    def run(self, spans, moved):
+    def run(self, spans, moved, send=None):
         for t in range(STEPS):
             def planes(inset, update, t=t):
                 self.plan.planes(*spans(t, inset), update, BATCH)
@@ -389,6 +395,8 @@
             planes(1, self.flow)
             planes(1, functools.partial(self.press, start=t == 0))
             if t == STEPS - 1:
+                if send is not None:
+                    send()
                 planes(1, self.keep)
             elif t == 0 and moved:
                 planes(1, self.add_load)
@@ -472,8 +480,8 @@
 
 
 def outer_kernel(
-    plan, table, border, water, bottom, vel_in, stress_in, mats_in, oc_in, loads_in,
-    vel, stress, mats, oc, loads, message, gather,
+    plan, materials, border, water, bottom, vel_in, stress_in, mats_in, oc_in, loads_in,
+    vel, stress, mats, oc, loads, message, gather, rows, sem,
 ):
     sub, chunks, n, strips, cells = plan.sub, plan.chunks, plan.n, plan.strips, plan.cells
     near = cells - 1
@@ -486,6 +494,10 @@
             here[...] = there[...]
     updates = Updates(plan, sh, vel, stress, mats, oc, water, bottom, loads)
 
+    def material(c, z):
+        row = materials[pl.ds(c * ZONES + z, 1), :]
+        return jnp.broadcast_to(row, (sub, plan.lanes))
+
     def side(core):
         low, far = ((1, 0), (HALO + 2 * cells, 2 * HALO + 2 * cells - 1))[core]
         state = (vel, stress, mats)
@@ -493,7 +505,7 @@
             0,
             near,
             lambda x, count: bring(
-                plan, sh, table, state, border, near, x, count, low + x, 1 - core
+                plan, sh, material, state, border, near, x, count, low + x, 1 - core
             ),
             BATCH,
         )
@@ -506,23 +518,29 @@
             last = 2 * HALO + 2 * cells - 2 * t - inset
             return last - HALO, last
 
-        updates.run(spans, False)
-        for group in range(plan.own_groups):
-            stacked = jnp.concatenate(
-                [
-                    oc[f, 1 + HALO + core * cells + group * chunks + i]
-                    for i in range(chunks)
-                    for f in range(4)
-                ],
-                axis=0,
-            )
-            gather[...] = stacked.T
-            for kc in range(chunks):
-                for yl in range(strips):
-                    at = group * plan.lead + kc * strips + yl
-                    message[pl.ds(at, n, stride=plan.back_rows), :] = gather[
-                        pl.ds(kc * plan.ny + yl, n, stride=strips), :
-                    ]
+        copy = pltpu.make_async_copy(rows, message, sem)
+
+        def send():
+            for group in range(plan.own_groups):
+                stacked = jnp.concatenate(
+                    [
+                        oc[f, 1 + HALO + core * cells + group * chunks + i]
+                        for i in range(chunks)
+                        for f in range(4)
+                    ],
+                    axis=0,
+                )
+                gather[group] = stacked.T
+                for kc in range(chunks):
+                    for yl in range(strips):
+                        at = group * plan.lead + kc * strips + yl
+                        rows[pl.ds(at, n, stride=plan.back_rows), :] = gather[
+                            group, pl.ds(kc * plan.ny + yl, n, stride=strips), :
+                        ]
+            copy.start()
+
+        updates.run(spans, False, send)
+        copy.wait()
 
     for core in range(2):
         pl.when(odd == core)(functools.partial(side, core))
@@ -564,23 +582,30 @@
     plan.planes(0, cells, finish, BATCH)
 
 
-def unpack_kernel(plan, arrived, ocean, turned):
+def unpack_kernel(plan, arrived, ocean, turned, strips, sems):
     sub, chunks = plan.sub, plan.chunks
     block = 4 * sub
+    copies = [
+        pltpu.make_async_copy(strips.at[yl], ocean.at[:, yl], sems.at[yl])
+        for yl in range(plan.strips)
+    ]
     for yl in range(plan.strips):
         by_chunk = [
             arrived[pl.ds(kc * plan.strips + yl, plan.nx // chunks, stride=plan.lead), :]
             for kc in range(chunks)
         ]
         for i in range(chunks):
-            turned[pl.ds(i, plan.nx // chunks, stride=chunks), :] = place(
+            turned[yl, pl.ds(i, plan.nx // chunks, stride=chunks), :] = place(
                 by_chunk, [i] * chunks, block
             )
-        whole = turned[...].T
+        whole = turned[yl].T
         for kc in range(chunks):
             for f in range(4):
                 at = (kc * 4 + f) * sub
-                ocean[f, yl, kc * sub : (kc + 1) * sub, :] = whole[at : at + sub]
+                strips[yl, f, kc * sub : (kc + 1) * sub, :] = whole[at : at + sub]
+        copies[yl].start()
+    for copy in copies:
+        copy.wait()
 
 
 def on_device(plan, velocity, stress, ocean, zones, materials, slip, bathy):
@@ -598,13 +623,13 @@
     def held(array):
         return pltpu.VMEM(array.shape, array.dtype)
 
-    def call(kernel, name, out, ins, scratch, room=16, **rest):
+    def call(kernel, name, out, ins, scratch, room=16, outs=None, **rest):
         room = room if plan.unrolled else 56
         return pl.pallas_call(
             functools.partial(kernel, plan),
             out_shape=out,
             in_specs=ins,
-            out_specs=jax.tree.map(lambda _: vmem, out),
+            out_specs=jax.tree.map(lambda _: vmem, out) if outs is None else outs,
             scratch_shapes=scratch,
             compiler_params=pltpu.CompilerParams(vmem_limit_bytes=room * 1024 * 1024),
             name=name,
@@ -620,17 +645,15 @@
     mates = [(i, i ^ 1) for i in range(n)]
     others = [(i, i + 1) for i in range(1, n - 1, 2)]
     others += [(target, source) for source, target in others]
-    crust, border, message = call(
-        pack_kernel,
-        "pack",
-        (
-            shape(10 * cells + 1, sub, lanes),
-            shape(10 * cells - 6, sub, lanes),
-            shape(n * plan.rows, LANES),
-        ),
+    crust_args = (velocity, stress, zones, slip)
+    message, *near_args = call(
+        ocean_kernel,
+        "ocean_rows",
+        (shape(n * plan.rows, LANES), *(like(a) for a in crust_args)),
         [hbm] * 6,
-        [held(a) for a in (velocity, stress, zones, slip, ocean, bathy)]
-        + [
+        [
+            held(ocean),
+            held(bathy),
             pltpu.VMEM((plan.strips, plan.nx, LANES), F32),
             pltpu.VMEM(
                 (plan.lead, plan.nx // plan.chunks + 2 * plan.halo_groups, LANES), F32
@@ -639,7 +662,7 @@
             pltpu.VMEM((n * plan.rows, LANES), F32),
             pltpu.SemaphoreType.DMA((6,)),
         ],
-    )(*(pinned(a) for a in (velocity, stress, zones, slip, ocean, bathy)))
+    )(*(pinned(a) for a in (*crust_args, ocean, bathy)))
     arrived = lax.all_to_all(
         message.reshape(n // 2, 2 * plan.rows, LANES),
         "map",
@@ -648,13 +671,25 @@
         axis_index_groups=[list(range(core, n, 2)) for core in range(2)],
         tiled=True,
     ).reshape(n * plan.rows, LANES)
+    crust, border = call(
+        crust_kernel,
+        "crust_planes",
+        (shape(10 * cells + 1, sub, lanes), shape(10 * cells - 6, sub, lanes)),
+        [vmem] * 4,
+        [],
+    )(*near_args)
     other = lax.ppermute(border, "map", others)
     mate = lax.ppermute(crust, "map", mates)
     columns = 2 * cells + 2 * HALO
-    vel, strs, mats = call(
+    vel, strs, mats, material_rows = call(
         begin_kernel,
         "first_velocity",
-        (shape(3, columns, sub, lanes), shape(6, columns, sub, lanes), shape(5, columns, sub, lanes)),
+        (
+            shape(3, columns, sub, lanes),
+            shape(6, columns, sub, lanes),
+            shape(5, columns, sub, lanes),
+            shape(3 * ZONES, lanes),
+        ),
         [smem] + [vmem] * 2,
         [],
     )(materials, crust, mate)
@@ -684,10 +719,15 @@
         "outer_substeps",
         tuple(planes_of[k] for k in ("vel", "stress", "mats", "oc", "loads"))
         + (shape(n * plan.back_rows, LANES),),
-        [smem] + [vmem] * 8,
-        [pltpu.VMEM((lanes, LANES), F32)],
+        [vmem] * 9,
+        [
+            pltpu.VMEM((plan.own_groups, lanes, LANES), F32),
+            pltpu.VMEM((n * plan.back_rows, LANES), F32),
+            pltpu.SemaphoreType.DMA,
+        ],
+        outs=(vmem,) * 5 + (hbm,),
         input_output_aliases={4: 0, 5: 1, 6: 2, 7: 3, 8: 4},
-    )(materials, *(near(a) for a in (other, water, bottom, vel, strs, mats, oc, loads)))
+    )(*(near(a) for a in (material_rows, other, water, bottom, vel, strs, mats, oc, loads)))
     returned = lax.all_to_all(
         back.reshape(n, plan.back_rows, LANES), "map", split_axis=0, concat_axis=0, tiled=True
     ).reshape(n * plan.back_rows, LANES)
@@ -706,7 +746,12 @@
         "ocean_strips",
         shape(*ocean.shape),
         [vmem],
-        [pltpu.VMEM((plan.nx, LANES), F32)],
+        [
+            pltpu.VMEM((plan.strips, plan.nx, LANES), F32),
+            pltpu.VMEM((plan.strips, 4, plan.depth, plan.nx), F32),
+            pltpu.SemaphoreType.DMA((plan.strips,)),
+        ],
+        outs=hbm,
     )(returned)
     return new_velocity, new_stress, new_ocean
 

time: 39.4 us -> 38.7 us (0.982)
  Pallas kernels: 11.3 us -> 10.5 us
  starting transfers between devices: 12.1 us -> 12.5 us
  waiting for transfers between devices: 15 us -> 14.6 us
    pallas_call x1, Pallas kernels: 2.99 us -> 2.35 us  [on_device(): call(outer_kernel, 'outer_substeps', tuple((planes_of[k] for k in ('vel',...]
    all_to_all x1, starting transfers between devices: 4.08 us -> 4.48 us  [on_device(): lax.all_to_all(back.reshape(n, plan.back_rows, LANES), 'map', split_axis=...]
    pallas_call x1 -> x2, Pallas kernels: 2.6 us -> 2.47 us  [the longest x1 2.14 us: on_device(): call(ocean_kernel, 'ocean_rows', (shape(n * plan.rows, LANES), *(like(a)...]
  transfers between devices with their start and end apart: 5 -> 5, of which waited for: 4 -> 4; matrix products, arithmetic and copies ran while one was open for 0% -> 0% of each run, Pallas kernels for 12% -> 13%
where the time goes in v14:
time: 38.7 us; the launch traced here: 38.3 us
  waiting for transfers between devices  14.6 us (38%)
  starting transfers between devices  12.5 us (32%)
  Pallas kernels  10.5 us (27%)
  between operations  0.69 us (2%)
    all_to_all x1, starting transfers between devices, on_device(): lax.all_to_all(message.reshape(n // 2, 2 * plan.rows, LANES), 'map', spli...  7.26 us
    all_to_all x1, waiting for transfers between devices, on_device(): lax.all_to_all(back.reshape(n, plan.back_rows, LANES), 'map', split_axis=...  6.08 us
    all_to_all x1, waiting for transfers between devices, on_device(): lax.all_to_all(message.reshape(n // 2, 2 * plan.rows, LANES), 'map', spli...  6.07 us
    all_to_all x1, starting transfers between devices, on_device(): lax.all_to_all(back.reshape(n, plan.back_rows, LANES), 'map', split_axis=...  4.48 us
    pallas_call x1, Pallas kernels, on_device(): call(outer_kernel, 'outer_substeps', tuple((planes_of[k] for k in ('vel',...  2.35 us
    pallas_call x1, Pallas kernels, on_device(): call(ocean_kernel, 'ocean_rows', (shape(n * plan.rows, LANES), *(like(a)...  2.14 us
    pallas_call x1, Pallas kernels, on_device(): call(inner_kernel, 'inner_substeps', tuple((planes_of[k] for k in ('vel',...  2.02 us
    pallas_call x1, Pallas kernels, on_device(): call(end_kernel, 'last_updates', (shape(*velocity.shape), shape(*stress.s...  1.85 us
  transfers between devices with their start and end apart: 5, of which 4 were waited for; matrix products, arithmetic and copies ran while one was open for 0% of the time, Pallas kernels for 13%

profile of v14, /device:TPU:0, one launch (start us, length us, event | category | flops | bytes accessed | tf_op | source)
XLA Modules:
  0.0 38.3 jit_solution(16868011574181521288)
XLA Ops:
  0.6 2.1 %ocean_rows.1 = (f32[512,128]{1,0:T(8,128)}, f32[3,8,32,32]{3,2,1,0:T(8,128)S(1)}, f32[6,8,32,32]{3,2,1,0:T(8,128)S(1)}, s32[8,32,32]{2,1,0:T(8,128)S(1)}, f32[8,32]{1,0:T(8,128)S(1)}) custom-call(f32[3,8,32,32]{3,2,1,0:T(8,128)} %vel_ref.1, f32[6,8,32,32]{3,2,1,0:T(8,128)} %stress_ref.1, s32[8,32,32]{2,1,0:T(8,128)} %zones_ref.1, f32[8,32]{1,0:T(8,128)} %slip_ref.1, ...), custom_call_target="tpu_custom_call" | custom-call | tf_op jit(solution)/shard_map/ocean_rows/pallas_call | solution.py:649
  2.8 7.3 %all-to-all-start = ((f32[8,64,128]{2,1,0:T(8,128)}), f32[8,64,128]{2,1,0:T(8,128)S(1)}, u32[]{:S(2)}, u32[]{:S(2)}) async-start(f32[8,64,128]{2,1,0:T(8,128)} %bitcast), calls=%async_computation | async-start | bytes 524288 | tf_op jit(solution)/shard_map/all_to_all | solution.py:666
  10.0 0.3 crust_planes.1
  10.4 0.0 copy-start
  10.4 0.1 collective-permute-start
  10.5 0.7 %collective-permute-start.1 = (f32[74,8,128]{2,1,0:T(8,128)S(1)}, f32[74,8,128]{2,1,0:T(8,128)S(1)}, u32[]{:S(2)}, u32[]{:S(2)}) collective-permute-start(f32[74,8,128]{2,1,0:T(8,128)S(1)} %get-tuple-element.35), channel_id=1, source_target_pairs={{1,2},{3,4},{5,6},{7,8},{9,10},{11,12},{13,14},{2,1},{4,3},{6,5},{... | collective-permute-start | bytes 909320 | tf_op jit(solution)/shard_map/ppermute | solution.py:681
  11.2 0.9 %collective-permute-done.mate = f32[81,8,128]{2,1,0:T(8,128)S(1)} collective-permute-done((f32[81,8,128]{2,1,0:T(8,128)S(1)}, f32[81,8,128]{2,1,0:T(8,128)S(1)}, u32[]{:S(2)}, u32[]{:S(2)}) %collective-permute-start) | collective-permute-done | bytes 331808 | tf_op jit(solution)/shard_map/ppermute | solution.py:682
  12.1 0.0 copy-done
  12.1 0.9 %first_velocity.1 = (f32[3,32,8,128]{3,2,1,0:T(8,128)S(1)}, f32[6,32,8,128]{3,2,1,0:T(8,128)S(1)}, f32[5,32,8,128]{3,2,1,0:T(8,128)S(1)}, f32[24,128]{1,0:T(8,128)S(1)}) custom-call(f32[3,8]{1,0:T(4,128)S(1)} %copy-done, f32[81,8,128]{2,1,0:T(8,128)S(1)} %get-tuple-element.33.own, f32[81,8,128]{2,1,0:T(8,128)S(1)} %collective-permute-done.mate), custom_call_target="tpu_custom_call" | custom-call | tf_op jit(solution)/shard_map/first_velocity/pallas_call | solution.py:684
  13.0 6.1 %all-to-all-done = f32[8,64,128]{2,1,0:T(8,128)S(1)} async-done(((f32[8,64,128]{2,1,0:T(8,128)}), f32[8,64,128]{2,1,0:T(8,128)S(1)}, u32[]{:S(2)}, u32[]{:S(2)}) %all-to-all-start) | async-done | bytes 262176 | tf_op jit(solution)/shard_map/all_to_all | solution.py:666
  19.1 0.0 collective-permute-start.2
  19.1 1.5 %collective-permute-done.2.swapped = f32[512,128]{1,0:T(8,128)S(1)} collective-permute-done((f32[512,128]{1,0:T(8,128)S(1)}, f32[512,128]{1,0:T(8,128)S(1)}, u32[]{:S(2)}, u32[]{:S(2)}) %collective-permute-start.2) | collective-permute-done | bytes 262176 | tf_op jit(solution)/shard_map/ppermute | solution.py:697
  20.6 2.0 %inner_substeps.1 = (f32[3,32,8,128]{3,2,1,0:T(8,128)S(1)}, f32[6,32,8,128]{3,2,1,0:T(8,128)S(1)}, f32[4,34,8,128]{3,2,1,0:T(8,128)S(1)}, f32[34,8,128]{2,1,0:T(...) custom-call(f32[512,128]{1,0:T(8,128)S(1)} %bitcast.5, ...), custom_call_target="tpu_custom_call", output_to_operand_aliasing={{0}: (3, {}), {1}: (4, {})} | custom-call | tf_op jit(solution)/shard_map/inner_substeps/pallas_call | solution.py:706
  22.6 0.0 collective-permute-done.1.border
  22.6 2.3 %outer_substeps.1 = (f32[3,32,8,128]{3,2,1,0:T(8,128)S(1)}, f32[6,32,8,128]{3,2,1,0:T(8,128)S(1)}, f32[5,32,8,128]{3,2,1,0:T(8,128)S(1)}, f32[4,34,8,128]{3,2,1,...) custom-call(f32[24,128]{1,0:T(8,128)S(1)} %get-tuple-element.34.mate, ...), custom_call_target="tpu_custom_call", output_to_operand_aliasing={{0}: (4, {}), {1}: (5, {}), {2}: (6, {}), {3}: (7, {}), {4}... | custom-call | tf_op jit(solution)/shard_map/outer_substeps/pallas_call | solution.py:717
  25.0 4.5 %all-to-all-start.1 = ((f32[16,16,128]{2,1,0:T(8,128)}), f32[16,16,128]{2,1,0:T(8,128)S(1)}, u32[]{:S(2)}, u32[]{:S(2)}) async-start(f32[16,16,128]{2,1,0:T(8,128)} %bitcast.2), calls=%async_computation.1 | async-start | bytes 262144 | tf_op jit(solution)/shard_map/all_to_all | solution.py:731
  29.5 1.9 %last_updates.1 = (f32[3,8,32,32]{3,2,1,0:T(8,128)}, f32[6,8,32,32]{3,2,1,0:T(8,128)}) custom-call(f32[3,32,8,128]{3,2,1,0:T(8,128)S(1)} %get-tuple-element.48.vel_all, f32[6,32,8,128]{3,2,1,0:T(8,128)S(1)} %get-tuple-element.49.stress_all, f32[5,32,8,128]{3,2,1,0:T(8,128)S(1)} %get-tuple-element.50.mats_all, f32[32,8,128]{2,1,0:T(8,128)S(1)} %get-tuple-element.51.loads_all), custom_call_target="tpu_custom_call" | custom-call | tf_op jit(solution)/shard_map/last_updates/pallas_call | solution.py:734
  31.3 6.1 %all-to-all-done.1 = f32[16,16,128]{2,1,0:T(8,128)S(1)} async-done(((f32[16,16,128]{2,1,0:T(8,128)}), f32[16,16,128]{2,1,0:T(8,128)S(1)}, u32[]{:S(2)}, u32[]{:S(2)}) %all-to-all-start.1) | async-done | bytes 131104 | tf_op jit(solution)/shard_map/all_to_all | solution.py:731
  37.4 0.9 %ocean_strips.1 = f32[4,2,32,128]{3,2,1,0:T(8,128)} custom-call(f32[256,128]{1,0:T(8,128)S(1)} %bitcast.6), custom_call_target="tpu_custom_call" | custom-call | tf_op jit(solution)/shard_map/ocean_strips/pallas_call | solution.py:744
Async XLA Ops:
  2.8 16.3 %all-to-all-start = ((f32[8,64,128]{2,1,0:T(8,128)}), f32[8,64,128]{2,1,0:T(8,128)S(1)}, u32[]{:S(2)}, u32[]{:S(2)}) async-start(f32[8,64,128]{2,1,0:T(8,128)} %bitcast), calls=%async_computation | async-start | bytes 524288 | tf_op jit(solution)/shard_map/all_to_all | solution.py:666
  10.4 1.7 %copy-start = (f32[3,8]{1,0:T(4,128)S(1)}, f32[3,8]{1,0:T(4,128)}, u32[]{:S(2)}) copy-start(f32[3,8]{1,0:T(4,128)} %table.1) | copy-start | bytes 292
  10.4 1.7 %collective-permute-start = (f32[81,8,128]{2,1,0:T(8,128)S(1)}, f32[81,8,128]{2,1,0:T(8,128)S(1)}, u32[]{:S(2)}, u32[]{:S(2)}) collective-permute-start(f32[81,8,128]{2,1,0:T(8,128)S(1)} %get-tuple-element.33.own), channel_id=1, source_target_pairs={{0,1},{1,0},{2,3},{3,2},{4,5},{5,4},{6,7},{7,6},{8,9},{9,8},{10,11... | collective-permute-start | bytes 995336 | tf_op jit(solution)/shard_map/ppermute | solution.py:682
  10.5 12.2 %collective-permute-start.1 = (f32[74,8,128]{2,1,0:T(8,128)S(1)}, f32[74,8,128]{2,1,0:T(8,128)S(1)}, u32[]{:S(2)}, u32[]{:S(2)}) collective-permute-start(f32[74,8,128]{2,1,0:T(8,128)S(1)} %get-tuple-element.35), channel_id=1, source_target_pairs={{1,2},{3,4},{5,6},{7,8},{9,10},{11,12},{13,14},{2,1},{4,3},{6,5},{... | collective-permute-start | bytes 909320 | tf_op jit(solution)/shard_map/ppermute | solution.py:681
  19.1 1.5 %collective-permute-start.2 = (f32[512,128]{1,0:T(8,128)S(1)}, f32[512,128]{1,0:T(8,128)S(1)}, u32[]{:S(2)}, u32[]{:S(2)}) collective-permute-start(f32[512,128]{1,0:T(8,128)S(1)} %bitcast.4), channel_id=1, source_target_pairs={{0,1},{1,0},{2,3},{3,2},{4,5},{5,4},{6,7},{7,6},{8,9},{9,8},{10,11... | collective-permute-start | bytes 786440 | tf_op jit(solution)/shard_map/ppermute | solution.py:697
  25.0 12.4 %all-to-all-start.1 = ((f32[16,16,128]{2,1,0:T(8,128)}), f32[16,16,128]{2,1,0:T(8,128)S(1)}, u32[]{:S(2)}, u32[]{:S(2)}) async-start(f32[16,16,128]{2,1,0:T(8,128)} %bitcast.2), calls=%async_computation.1 | async-start | bytes 262144 | tf_op jit(solution)/shard_map/all_to_all | solution.py:731

commit v15 on v14

--- a/solution.py
+++ b/solution.py
@@ -97,10 +97,11 @@
         copy.start()
     copies[0].wait()
     copies[1].wait()
-    outside = jnp.zeros((plan.lead, plan.halo_groups, LANES), F32)
     count = plan.nx // chunks
-    grouped[:, : plan.halo_groups, :] = outside
-    grouped[:, plan.halo_groups + count :, :] = outside
+    lead = plan.lead
+    pad = plan.halo_groups * lead
+    grouped[:pad, :] = jnp.zeros((pad, LANES), F32)
+    grouped[pad + count * lead :, :] = jnp.zeros((pad, LANES), F32)
     for yl in range(strips):
         stacked = jnp.concatenate(
             [ocean[f, yl, kc * sub : (kc + 1) * sub, :] for kc in range(chunks) for f in range(4)],
@@ -109,15 +110,12 @@
         turned[yl] = stacked.T
         by_x = [turned[yl, pl.ds(i, count, stride=chunks), :] for i in range(chunks)]
         for kc in range(chunks):
-            grouped[kc * strips + yl, pl.ds(plan.halo_groups, count), :] = place(
+            grouped[pl.ds(pad + kc * strips + yl, count, stride=lead), :] = place(
                 by_x, [kc] * chunks, block
             )
     for d in range(n):
-        start = d * plan.own_groups + (d % 2) * plan.halo_groups
-        for q in range(plan.lead):
-            message[d * rows + q * sent : d * rows + (q + 1) * sent, :] = grouped[
-                q, start : start + sent, :
-            ]
+        start = (d * plan.own_groups + (d % 2) * plan.halo_groups) * lead
+        message[d * rows : (d + 1) * rows, :] = grouped[start : start + rows, :]
     depths = bathy[...].astype(F32)
     wide = lax.broadcasted_iota(jnp.int32, depths.shape, 1)
     for d in range(n):
@@ -140,7 +138,7 @@
                 column = jnp.concatenate([blank, column], axis=0)
             deep = extra[pl.ds(odd * strips + yl, pairs, stride=2 * strips), :]
             for kc in range(chunks):
-                at = odd * rows + (kc * strips + yl) * sent + group
+                at = odd * rows + group * lead + kc * strips + yl
                 old = message[pl.ds(at, pairs, stride=2 * rows), :]
                 edge = pltpu.roll(column, (slot - kc * block) % LANES, 1)
                 floor = pltpu.roll(deep, (slot + sub - kc * sub) % LANES, 1)
@@ -421,7 +419,7 @@
         for core, ref in ((odd, arrived), (1 - odd, swapped)):
             for kc in range(chunks):
                 for yl in range(strips):
-                    at = owner * plan.rows + (kc * strips + yl) * sent + group
+                    at = owner * plan.rows + group * plan.lead + kc * strips + yl
                     to = kc * plan.ny + core * strips + yl
                     gather[pl.ds(to, half, stride=2 * strips), :] = ref[
                         pl.ds(at, half, stride=2 * plan.rows), :
@@ -656,7 +654,7 @@
             held(bathy),
             pltpu.VMEM((plan.strips, plan.nx, LANES), F32),
             pltpu.VMEM(
-                (plan.lead, plan.nx // plan.chunks + 2 * plan.halo_groups, LANES), F32
+                ((plan.nx // plan.chunks + 2 * plan.halo_groups) * plan.lead, LANES), F32
             ),
             pltpu.VMEM((n * plan.strips, LANES), F32),
             pltpu.VMEM((n * plan.rows, LANES), F32),
@@ -679,6 +677,8 @@
         [],
     )(*near_args)
     other = lax.ppermute(border, "map", others)
+    arrived, crust = lax.optimization_barrier((arrived, crust))
+    swapped = lax.ppermute(arrived, "map", mates)
     mate = lax.ppermute(crust, "map", mates)
     columns = 2 * cells + 2 * HALO
     vel, strs, mats, material_rows = call(
@@ -693,8 +693,6 @@
         [smem] + [vmem] * 2,
         [],
     )(materials, crust, mate)
-    arrived, vel = lax.optimization_barrier((arrived, vel))
-    swapped = lax.ppermute(arrived, "map", mates)
     planes_of = {
         "vel": shape(3, columns, sub, lanes),
         "stress": shape(6, columns, sub, lanes),

time: 38.7 us -> 44.8 us (1.16)
  starting transfers between devices: 12.5 us -> 18.4 us
    all_to_all x1, starting transfers between devices: 4.48 us -> 7.48 us  [on_device(): lax.all_to_all(back.reshape(n, plan.back_rows, LANES), 'map', split_axis=...]
    ppermute x1, starting transfers between devices: 0.01 us -> 2.82 us  [on_device(): swapped = lax.ppermute(arrived, 'map', mates)]
    all_to_all x1, waiting for transfers between devices: 6.07 us -> 8.59 us  [on_device(): lax.all_to_all(message.reshape(n // 2, 2 * plan.rows, LANES), 'map', spli...]
    ppermute x1, waiting for transfers between devices: 1.53 us -> 0.25 us  [on_device(): swapped = lax.ppermute(arrived, 'map', mates)]
    ppermute x1, waiting for transfers between devices: 0.93 us -> 0.01 us  [on_device(): mate = lax.ppermute(crust, 'map', mates)]
  transfers between devices with their start and end apart: 5 -> 5, of which waited for: 4 -> 3; matrix products, arithmetic and copies ran while one was open for 0% -> 0% of each run, Pallas kernels for 13% -> 11%
where the time goes in v15:
time: 44.8 us; the launch traced here: 44.5 us
  starting transfers between devices  18.4 us (41%)
  waiting for transfers between devices  14.9 us (33%)
  Pallas kernels  10.5 us (23%)
  between operations  0.68 us (2%)
    all_to_all x1, waiting for transfers between devices, on_device(): lax.all_to_all(message.reshape(n // 2, 2 * plan.rows, LANES), 'map', spli...  8.59 us
    all_to_all x1, starting transfers between devices, on_device(): lax.all_to_all(back.reshape(n, plan.back_rows, LANES), 'map', split_axis=...  7.48 us
    all_to_all x1, starting transfers between devices, on_device(): lax.all_to_all(message.reshape(n // 2, 2 * plan.rows, LANES), 'map', spli...  7.26 us
    all_to_all x1, waiting for transfers between devices, on_device(): lax.all_to_all(back.reshape(n, plan.back_rows, LANES), 'map', split_axis=...  6.08 us
    ppermute x1, starting transfers between devices, on_device(): swapped = lax.ppermute(arrived, 'map', mates)  2.82 us
    pallas_call x1, Pallas kernels, on_device(): call(outer_kernel, 'outer_substeps', tuple((planes_of[k] for k in ('vel',...  2.35 us
    pallas_call x1, Pallas kernels, on_device(): call(ocean_kernel, 'ocean_rows', (shape(n * plan.rows, LANES), *(like(a)...  2.1 us
    pallas_call x1, Pallas kernels, on_device(): call(inner_kernel, 'inner_substeps', tuple((planes_of[k] for k in ('vel',...  2.02 us
  transfers between devices with their start and end apart: 5, of which 3 were waited for; matrix products, arithmetic and copies ran while one was open for 0% of the time, Pallas kernels for 11%

profile of v15, /device:TPU:0, one launch (start us, length us, event | category | flops | bytes accessed | tf_op | source)
XLA Modules:
  0.0 44.5 jit_solution(15403827016691309425)
XLA Ops:
  0.6 2.1 %ocean_rows.1 = (f32[512,128]{1,0:T(8,128)}, f32[3,8,32,32]{3,2,1,0:T(8,128)S(1)}, f32[6,8,32,32]{3,2,1,0:T(8,128)S(1)}, s32[8,32,32]{2,1,0:T(8,128)S(1)}, f32[8,32]{1,0:T(8,128)S(1)}) custom-call(f32[3,8,32,32]{3,2,1,0:T(8,128)} %vel_ref.1, f32[6,8,32,32]{3,2,1,0:T(8,128)} %stress_ref.1, s32[8,32,32]{2,1,0:T(8,128)} %zones_ref.1, f32[8,32]{1,0:T(8,128)} %slip_ref.1, ...), custom_call_target="tpu_custom_call" | custom-call | tf_op jit(solution)/shard_map/ocean_rows/pallas_call | solution.py:647
  2.7 7.3 %all-to-all-start = ((f32[8,64,128]{2,1,0:T(8,128)}), f32[8,64,128]{2,1,0:T(8,128)S(1)}, u32[]{:S(2)}, u32[]{:S(2)}) async-start(f32[8,64,128]{2,1,0:T(8,128)} %bitcast), calls=%async_computation | async-start | bytes 524288 | tf_op jit(solution)/shard_map/all_to_all | solution.py:664
  10.0 0.3 crust_planes.1
  10.3 8.6 %all-to-all-done = f32[8,64,128]{2,1,0:T(8,128)S(1)} async-done(((f32[8,64,128]{2,1,0:T(8,128)}), f32[8,64,128]{2,1,0:T(8,128)S(1)}, u32[]{:S(2)}, u32[]{:S(2)}) %all-to-all-start) | async-done | bytes 262176 | tf_op jit(solution)/shard_map/all_to_all | solution.py:664
  18.9 0.0 copy-start
  18.9 0.0 collective-permute-start
  18.9 0.8 %collective-permute-start.1 = (f32[74,8,128]{2,1,0:T(8,128)S(1)}, f32[74,8,128]{2,1,0:T(8,128)S(1)}, u32[]{:S(2)}, u32[]{:S(2)}) collective-permute-start(f32[74,8,128]{2,1,0:T(8,128)S(1)} %get-tuple-element.37), channel_id=1, source_target_pairs={{1,2},{3,4},{5,6},{7,8},{9,10},{11,12},{13,14},{2,1},{4,3},{6,5},{... | collective-permute-start | bytes 909320 | tf_op jit(solution)/shard_map/ppermute | solution.py:679
  19.7 2.8 %collective-permute-start.2 = (f32[512,128]{1,0:T(8,128)S(1)}, f32[512,128]{1,0:T(8,128)S(1)}, u32[]{:S(2)}, u32[]{:S(2)}) collective-permute-start(f32[512,128]{1,0:T(8,128)S(1)} %bitcast.4), channel_id=1, source_target_pairs={{0,1},{1,0},{2,3},{3,2},{4,5},{5,4},{6,7},{7,6},{8,9},{9,8},{10,11... | collective-permute-start | bytes 786440 | tf_op jit(solution)/shard_map/ppermute | solution.py:681
  22.6 0.0 collective-permute-done.mate
  22.6 0.0 copy-done
  22.6 0.9 %first_velocity.1 = (f32[3,32,8,128]{3,2,1,0:T(8,128)S(1)}, f32[6,32,8,128]{3,2,1,0:T(8,128)S(1)}, f32[5,32,8,128]{3,2,1,0:T(8,128)S(1)}, f32[24,128]{1,0:T(8,128)S(1)}) custom-call(f32[3,8]{1,0:T(4,128)S(1)} %copy-done, f32[81,8,128]{2,1,0:T(8,128)S(1)} %get-tuple-element.35.own, f32[81,8,128]{2,1,0:T(8,128)S(1)} %collective-permute-done.mate), custom_call_target="tpu_custom_call" | custom-call | tf_op jit(solution)/shard_map/first_velocity/pallas_call | solution.py:684
  23.5 0.3 collective-permute-done.2.swapped
  23.7 2.0 %inner_substeps.1 = (f32[3,32,8,128]{3,2,1,0:T(8,128)S(1)}, f32[6,32,8,128]{3,2,1,0:T(8,128)S(1)}, f32[4,34,8,128]{3,2,1,0:T(8,128)S(1)}, f32[34,8,128]{2,1,0:T(...) custom-call(f32[512,128]{1,0:T(8,128)S(1)} %bitcast.5, ...), custom_call_target="tpu_custom_call", output_to_operand_aliasing={{0}: (3, {}), {1}: (4, {})} | custom-call | tf_op jit(solution)/shard_map/inner_substeps/pallas_call | solution.py:704
  25.7 0.0 collective-permute-done.1.border
  25.7 2.4 %outer_substeps.1 = (f32[3,32,8,128]{3,2,1,0:T(8,128)S(1)}, f32[6,32,8,128]{3,2,1,0:T(8,128)S(1)}, f32[5,32,8,128]{3,2,1,0:T(8,128)S(1)}, f32[4,34,8,128]{3,2,1,...) custom-call(f32[24,128]{1,0:T(8,128)S(1)} %get-tuple-element.36.mate, ...), custom_call_target="tpu_custom_call", output_to_operand_aliasing={{0}: (4, {}), {1}: (5, {}), {2}: (6, {}), {3}: (7, {}), {4}... | custom-call | tf_op jit(solution)/shard_map/outer_substeps/pallas_call | solution.py:715
  28.1 7.5 %all-to-all-start.1 = ((f32[16,16,128]{2,1,0:T(8,128)}), f32[16,16,128]{2,1,0:T(8,128)S(1)}, u32[]{:S(2)}, u32[]{:S(2)}) async-start(f32[16,16,128]{2,1,0:T(8,128)} %bitcast.2), calls=%async_computation.1 | async-start | bytes 262144 | tf_op jit(solution)/shard_map/all_to_all | solution.py:729
  35.6 1.9 %last_updates.1 = (f32[3,8,32,32]{3,2,1,0:T(8,128)}, f32[6,8,32,32]{3,2,1,0:T(8,128)}) custom-call(f32[3,32,8,128]{3,2,1,0:T(8,128)S(1)} %get-tuple-element.48.vel_all, f32[6,32,8,128]{3,2,1,0:T(8,128)S(1)} %get-tuple-element.49.stress_all, f32[5,32,8,128]{3,2,1,0:T(8,128)S(1)} %get-tuple-element.50.mats_all, f32[32,8,128]{2,1,0:T(8,128)S(1)} %get-tuple-element.51.loads_all), custom_call_target="tpu_custom_call" | custom-call | tf_op jit(solution)/shard_map/last_updates/pallas_call | solution.py:732
  37.5 6.1 %all-to-all-done.1 = f32[16,16,128]{2,1,0:T(8,128)S(1)} async-done(((f32[16,16,128]{2,1,0:T(8,128)}), f32[16,16,128]{2,1,0:T(8,128)S(1)}, u32[]{:S(2)}, u32[]{:S(2)}) %all-to-all-start.1) | async-done | bytes 131104 | tf_op jit(solution)/shard_map/all_to_all | solution.py:729
  43.5 0.9 %ocean_strips.1 = f32[4,2,32,128]{3,2,1,0:T(8,128)} custom-call(f32[256,128]{1,0:T(8,128)S(1)} %bitcast.6), custom_call_target="tpu_custom_call" | custom-call | tf_op jit(solution)/shard_map/ocean_strips/pallas_call | solution.py:742
Async XLA Ops:
  2.7 16.2 %all-to-all-start = ((f32[8,64,128]{2,1,0:T(8,128)}), f32[8,64,128]{2,1,0:T(8,128)S(1)}, u32[]{:S(2)}, u32[]{:S(2)}) async-start(f32[8,64,128]{2,1,0:T(8,128)} %bitcast), calls=%async_computation | async-start | bytes 524288 | tf_op jit(solution)/shard_map/all_to_all | solution.py:664
  18.9 3.6 %copy-start = (f32[3,8]{1,0:T(4,128)S(1)}, f32[3,8]{1,0:T(4,128)}, u32[]{:S(2)}) copy-start(f32[3,8]{1,0:T(4,128)} %table.1) | copy-start | bytes 292
  18.9 3.6 %collective-permute-start = (f32[81,8,128]{2,1,0:T(8,128)S(1)}, f32[81,8,128]{2,1,0:T(8,128)S(1)}, u32[]{:S(2)}, u32[]{:S(2)}) collective-permute-start(f32[81,8,128]{2,1,0:T(8,128)S(1)} %get-tuple-element.35.own), channel_id=1, source_target_pairs={{0,1},{1,0},{2,3},{3,2},{4,5},{5,4},{6,7},{7,6},{8,9},{9,8},{10,11... | collective-permute-start | bytes 995336 | tf_op jit(solution)/shard_map/ppermute | solution.py:682
  18.9 6.8 %collective-permute-start.1 = (f32[74,8,128]{2,1,0:T(8,128)S(1)}, f32[74,8,128]{2,1,0:T(8,128)S(1)}, u32[]{:S(2)}, u32[]{:S(2)}) collective-permute-start(f32[74,8,128]{2,1,0:T(8,128)S(1)} %get-tuple-element.37), channel_id=1, source_target_pairs={{1,2},{3,4},{5,6},{7,8},{9,10},{11,12},{13,14},{2,1},{4,3},{6,5},{... | collective-permute-start | bytes 909320 | tf_op jit(solution)/shard_map/ppermute | solution.py:679
  19.7 4.0 %collective-permute-start.2 = (f32[512,128]{1,0:T(8,128)S(1)}, f32[512,128]{1,0:T(8,128)S(1)}, u32[]{:S(2)}, u32[]{:S(2)}) collective-permute-start(f32[512,128]{1,0:T(8,128)S(1)} %bitcast.4), channel_id=1, source_target_pairs={{0,1},{1,0},{2,3},{3,2},{4,5},{5,4},{6,7},{7,6},{8,9},{9,8},{10,11... | collective-permute-start | bytes 786440 | tf_op jit(solution)/shard_map/ppermute | solution.py:681
  28.1 15.4 %all-to-all-start.1 = ((f32[16,16,128]{2,1,0:T(8,128)}), f32[16,16,128]{2,1,0:T(8,128)S(1)}, u32[]{:S(2)}, u32[]{:S(2)}) async-start(f32[16,16,128]{2,1,0:T(8,128)} %bitcast.2), calls=%async_computation.1 | async-start | bytes 262144 | tf_op jit(solution)/shard_map/all_to_all | solution.py:729

commit v16 on v15

--- a/solution.py
+++ b/solution.py
@@ -350,15 +350,26 @@
         oc[3, at] = wet * (oc[3, at] - (HALF * rise + (DT * GRAV) * p))
         oc[2, at] = wet * (oc[2, at] - HALF * sh.dy(p))
 
-    def press(self, j, count, start):
+    def press(self, j, count, floor):
         oc, sh = self.oc, self.sh
         before, at, after = (pl.ds(j + k, count) for k in range(3))
-        crust = pl.ds(j, count)
         w = oc[3, at]
-        floor = self.mats[FLOOR, crust] if start else sh.seafloor(self.vel[VZ, crust])
-        rise = sh.below(w) + self.bottom[at] * floor - sh.above(w, w)
+        rise = sh.below(w) - sh.above(w, w)
+        if floor is not None:
+            rise = rise + self.bottom[at] * floor(pl.ds(j, count))
         total = oc[1, after] - oc[1, before] + sh.dy(oc[2, at]) + rise
         oc[0, at] = self.water[at] * (oc[0, at] - (HALF * KBULK) * total)
+
+    def add_floor(self, j, count):
+        at = pl.ds(j + 1, count)
+        floor = self.first_floor(pl.ds(j, count))
+        self.oc[0, at] = self.oc[0, at] - (HALF * KBULK) * (self.bottom[at] * floor)
+
+    def first_floor(self, at):
+        return self.mats[FLOOR, at]
+
+    def floor(self, at):
+        return self.sh.seafloor(self.vel[VZ, at])
 
     def load(self, j, count):
         at = pl.ds(j + 1, count)
@@ -384,19 +395,32 @@
         for f, value in strained(self.sh, self.vel, self.stress, self.mats, j, count):
             self.stress[f, pl.ds(j, count)] = value
 
-    def run(self, spans, moved, send=None):
+    def run(self, spans, inner, send=None):
         for t in range(STEPS):
             def planes(inset, update, t=t):
                 self.plan.planes(*spans(t, inset), update, BATCH)
 
-            planes(0, self.flow_x)
-            planes(1, self.flow)
-            planes(1, functools.partial(self.press, start=t == 0))
+            if t:
+                planes(0, self.flow_x)
+                planes(1, self.flow)
+                planes(1, functools.partial(self.press, floor=self.floor))
+            elif inner:
+                columns = self.vel.shape[1]
+                first, last = spans(0, 1)
+                self.plan.planes(0, columns, self.flow_x, BATCH)
+                self.plan.planes(1, columns - 1, self.flow, BATCH)
+                planes(1, functools.partial(self.press, floor=self.first_floor))
+                self.plan.planes(1, first, functools.partial(self.press, floor=None), BATCH)
+                self.plan.planes(
+                    last, columns - 1, functools.partial(self.press, floor=None), BATCH
+                )
+            else:
+                planes(1, self.add_floor)
             if t == STEPS - 1:
                 if send is not None:
                     send()
                 planes(1, self.keep)
-            elif t == 0 and moved:
+            elif t == 0 and inner:
                 planes(1, self.add_load)
             else:
                 planes(1, self.move)
@@ -677,8 +701,6 @@
         [],
     )(*near_args)
     other = lax.ppermute(border, "map", others)
-    arrived, crust = lax.optimization_barrier((arrived, crust))
-    swapped = lax.ppermute(arrived, "map", mates)
     mate = lax.ppermute(crust, "map", mates)
     columns = 2 * cells + 2 * HALO
     vel, strs, mats, material_rows = call(
@@ -693,6 +715,8 @@
         [smem] + [vmem] * 2,
         [],
     )(materials, crust, mate)
+    arrived, vel = lax.optimization_barrier((arrived, vel))
+    swapped = lax.ppermute(arrived, "map", mates)
     planes_of = {
         "vel": shape(3, columns, sub, lanes),
         "stress": shape(6, columns, sub, lanes),

time: 44.8 us -> 38.6 us (0.86)
  starting transfers between devices: 18.4 us -> 12.4 us
    all_to_all x1, starting transfers between devices: 7.48 us -> 4.33 us  [on_device(): lax.all_to_all(back.reshape(n, plan.back_rows, LANES), 'map', split_axis=...]
    ppermute x1, starting transfers between devices: 2.82 us -> 0.01 us  [on_device(): swapped = lax.ppermute(arrived, 'map', mates)]
    all_to_all x1, waiting for transfers between devices: 8.59 us -> 6.07 us  [on_device(): lax.all_to_all(message.reshape(n // 2, 2 * plan.rows, LANES), 'map', spli...]
    ppermute x1, waiting for transfers between devices: 0.25 us -> 1.53 us  [on_device(): swapped = lax.ppermute(arrived, 'map', mates)]
    ppermute x1, waiting for transfers between devices: 0.01 us -> 0.93 us  [on_device(): mate = lax.ppermute(crust, 'map', mates)]
  transfers between devices with their start and end apart: 5 -> 5, of which waited for: 3 -> 4; matrix products, arithmetic and copies ran while one was open for 0% -> 0% of each run, Pallas kernels for 11% -> 14%
where the time goes in v16:
time: 38.6 us; the launch traced here: 38.3 us
  waiting for transfers between devices  14.6 us (38%)
  starting transfers between devices  12.4 us (32%)
  Pallas kernels  10.6 us (27%)
  between operations  0.69 us (2%)
    all_to_all x1, starting transfers between devices, on_device(): lax.all_to_all(message.reshape(n // 2, 2 * plan.rows, LANES), 'map', spli...  7.26 us
    all_to_all x1, waiting for transfers between devices, on_device(): lax.all_to_all(back.reshape(n, plan.back_rows, LANES), 'map', split_axis=...  6.08 us
    all_to_all x1, waiting for transfers between devices, on_device(): lax.all_to_all(message.reshape(n // 2, 2 * plan.rows, LANES), 'map', spli...  6.07 us
    all_to_all x1, starting transfers between devices, on_device(): lax.all_to_all(back.reshape(n, plan.back_rows, LANES), 'map', split_axis=...  4.33 us
    pallas_call x1, Pallas kernels, on_device(): call(outer_kernel, 'outer_substeps', tuple((planes_of[k] for k in ('vel',...  2.31 us
    pallas_call x1, Pallas kernels, on_device(): call(inner_kernel, 'inner_substeps', tuple((planes_of[k] for k in ('vel',...  2.18 us
    pallas_call x1, Pallas kernels, on_device(): call(ocean_kernel, 'ocean_rows', (shape(n * plan.rows, LANES), *(like(a)...  2.1 us
    pallas_call x1, Pallas kernels, on_device(): call(end_kernel, 'last_updates', (shape(*velocity.shape), shape(*stress.s...  1.85 us
  transfers between devices with their start and end apart: 5, of which 4 were waited for; matrix products, arithmetic and copies ran while one was open for 0% of the time, Pallas kernels for 14%

profile of v16, /device:TPU:0, one launch (start us, length us, event | category | flops | bytes accessed | tf_op | source)
XLA Modules:
  0.0 38.3 jit_solution(1773692019538620479)
XLA Ops:
  0.6 2.1 %ocean_rows.1 = (f32[512,128]{1,0:T(8,128)}, f32[3,8,32,32]{3,2,1,0:T(8,128)S(1)}, f32[6,8,32,32]{3,2,1,0:T(8,128)S(1)}, s32[8,32,32]{2,1,0:T(8,128)S(1)}, f32[8,32]{1,0:T(8,128)S(1)}) custom-call(f32[3,8,32,32]{3,2,1,0:T(8,128)} %vel_ref.1, f32[6,8,32,32]{3,2,1,0:T(8,128)} %stress_ref.1, s32[8,32,32]{2,1,0:T(8,128)} %zones_ref.1, f32[8,32]{1,0:T(8,128)} %slip_ref.1, ...), custom_call_target="tpu_custom_call" | custom-call | tf_op jit(solution)/shard_map/ocean_rows/pallas_call | solution.py:671
  2.7 7.3 %all-to-all-start = ((f32[8,64,128]{2,1,0:T(8,128)}), f32[8,64,128]{2,1,0:T(8,128)S(1)}, u32[]{:S(2)}, u32[]{:S(2)}) async-start(f32[8,64,128]{2,1,0:T(8,128)} %bitcast), calls=%async_computation | async-start | bytes 524288 | tf_op jit(solution)/shard_map/all_to_all | solution.py:688
  10.0 0.3 crust_planes.1
  10.3 0.0 copy-start
  10.3 0.1 collective-permute-start
  10.4 0.7 %collective-permute-start.1 = (f32[74,8,128]{2,1,0:T(8,128)S(1)}, f32[74,8,128]{2,1,0:T(8,128)S(1)}, u32[]{:S(2)}, u32[]{:S(2)}) collective-permute-start(f32[74,8,128]{2,1,0:T(8,128)S(1)} %get-tuple-element.35), channel_id=1, source_target_pairs={{1,2},{3,4},{5,6},{7,8},{9,10},{11,12},{13,14},{2,1},{4,3},{6,5},{... | collective-permute-start | bytes 909320 | tf_op jit(solution)/shard_map/ppermute | solution.py:703
  11.1 0.9 %collective-permute-done.mate = f32[81,8,128]{2,1,0:T(8,128)S(1)} collective-permute-done((f32[81,8,128]{2,1,0:T(8,128)S(1)}, f32[81,8,128]{2,1,0:T(8,128)S(1)}, u32[]{:S(2)}, u32[]{:S(2)}) %collective-permute-start) | collective-permute-done | bytes 331808 | tf_op jit(solution)/shard_map/ppermute | solution.py:704
  12.0 0.0 copy-done
  12.1 0.9 %first_velocity.1 = (f32[3,32,8,128]{3,2,1,0:T(8,128)S(1)}, f32[6,32,8,128]{3,2,1,0:T(8,128)S(1)}, f32[5,32,8,128]{3,2,1,0:T(8,128)S(1)}, f32[24,128]{1,0:T(8,128)S(1)}) custom-call(f32[3,8]{1,0:T(4,128)S(1)} %copy-done, f32[81,8,128]{2,1,0:T(8,128)S(1)} %get-tuple-element.33.own, f32[81,8,128]{2,1,0:T(8,128)S(1)} %collective-permute-done.mate), custom_call_target="tpu_custom_call" | custom-call | tf_op jit(solution)/shard_map/first_velocity/pallas_call | solution.py:706
  13.0 6.1 %all-to-all-done = f32[8,64,128]{2,1,0:T(8,128)S(1)} async-done(((f32[8,64,128]{2,1,0:T(8,128)}), f32[8,64,128]{2,1,0:T(8,128)S(1)}, u32[]{:S(2)}, u32[]{:S(2)}) %all-to-all-start) | async-done | bytes 262176 | tf_op jit(solution)/shard_map/all_to_all | solution.py:688
  19.0 0.0 collective-permute-start.2
  19.0 1.5 %collective-permute-done.2.swapped = f32[512,128]{1,0:T(8,128)S(1)} collective-permute-done((f32[512,128]{1,0:T(8,128)S(1)}, f32[512,128]{1,0:T(8,128)S(1)}, u32[]{:S(2)}, u32[]{:S(2)}) %collective-permute-start.2) | collective-permute-done | bytes 262176 | tf_op jit(solution)/shard_map/ppermute | solution.py:719
  20.6 2.2 %inner_substeps.1 = (f32[3,32,8,128]{3,2,1,0:T(8,128)S(1)}, f32[6,32,8,128]{3,2,1,0:T(8,128)S(1)}, f32[4,34,8,128]{3,2,1,0:T(8,128)S(1)}, f32[34,8,128]{2,1,0:T(...) custom-call(f32[512,128]{1,0:T(8,128)S(1)} %bitcast.5, ...), custom_call_target="tpu_custom_call", output_to_operand_aliasing={{0}: (3, {}), {1}: (4, {})} | custom-call | tf_op jit(solution)/shard_map/inner_substeps/pallas_call | solution.py:728
  22.8 0.0 collective-permute-done.1.border
  22.8 2.3 %outer_substeps.1 = (f32[3,32,8,128]{3,2,1,0:T(8,128)S(1)}, f32[6,32,8,128]{3,2,1,0:T(8,128)S(1)}, f32[5,32,8,128]{3,2,1,0:T(8,128)S(1)}, f32[4,34,8,128]{3,2,1,...) custom-call(f32[24,128]{1,0:T(8,128)S(1)} %get-tuple-element.34.mate, ...), custom_call_target="tpu_custom_call", output_to_operand_aliasing={{0}: (4, {}), {1}: (5, {}), {2}: (6, {}), {3}: (7, {}), {4}... | custom-call | tf_op jit(solution)/shard_map/outer_substeps/pallas_call | solution.py:739
  25.1 4.3 %all-to-all-start.1 = ((f32[16,16,128]{2,1,0:T(8,128)}), f32[16,16,128]{2,1,0:T(8,128)S(1)}, u32[]{:S(2)}, u32[]{:S(2)}) async-start(f32[16,16,128]{2,1,0:T(8,128)} %bitcast.2), calls=%async_computation.1 | async-start | bytes 262144 | tf_op jit(solution)/shard_map/all_to_all | solution.py:753
  29.4 1.9 %last_updates.1 = (f32[3,8,32,32]{3,2,1,0:T(8,128)}, f32[6,8,32,32]{3,2,1,0:T(8,128)}) custom-call(f32[3,32,8,128]{3,2,1,0:T(8,128)S(1)} %get-tuple-element.48.vel_all, f32[6,32,8,128]{3,2,1,0:T(8,128)S(1)} %get-tuple-element.49.stress_all, f32[5,32,8,128]{3,2,1,0:T(8,128)S(1)} %get-tuple-element.50.mats_all, f32[32,8,128]{2,1,0:T(8,128)S(1)} %get-tuple-element.51.loads_all), custom_call_target="tpu_custom_call" | custom-call | tf_op jit(solution)/shard_map/last_updates/pallas_call | solution.py:756
  31.3 6.1 %all-to-all-done.1 = f32[16,16,128]{2,1,0:T(8,128)S(1)} async-done(((f32[16,16,128]{2,1,0:T(8,128)}), f32[16,16,128]{2,1,0:T(8,128)S(1)}, u32[]{:S(2)}, u32[]{:S(2)}) %all-to-all-start.1) | async-done | bytes 131104 | tf_op jit(solution)/shard_map/all_to_all | solution.py:753
  37.4 0.9 %ocean_strips.1 = f32[4,2,32,128]{3,2,1,0:T(8,128)} custom-call(f32[256,128]{1,0:T(8,128)S(1)} %bitcast.6), custom_call_target="tpu_custom_call" | custom-call | tf_op jit(solution)/shard_map/ocean_strips/pallas_call | solution.py:766
Async XLA Ops:
  2.7 16.3 %all-to-all-start = ((f32[8,64,128]{2,1,0:T(8,128)}), f32[8,64,128]{2,1,0:T(8,128)S(1)}, u32[]{:S(2)}, u32[]{:S(2)}) async-start(f32[8,64,128]{2,1,0:T(8,128)} %bitcast), calls=%async_computation | async-start | bytes 524288 | tf_op jit(solution)/shard_map/all_to_all | solution.py:688
  10.3 1.7 %copy-start = (f32[3,8]{1,0:T(4,128)S(1)}, f32[3,8]{1,0:T(4,128)}, u32[]{:S(2)}) copy-start(f32[3,8]{1,0:T(4,128)} %table.1) | copy-start | bytes 292
  10.3 1.7 %collective-permute-start = (f32[81,8,128]{2,1,0:T(8,128)S(1)}, f32[81,8,128]{2,1,0:T(8,128)S(1)}, u32[]{:S(2)}, u32[]{:S(2)}) collective-permute-start(f32[81,8,128]{2,1,0:T(8,128)S(1)} %get-tuple-element.33.own), channel_id=1, source_target_pairs={{0,1},{1,0},{2,3},{3,2},{4,5},{5,4},{6,7},{7,6},{8,9},{9,8},{10,11... | collective-permute-start | bytes 995336 | tf_op jit(solution)/shard_map/ppermute | solution.py:704
  10.4 12.3 %collective-permute-start.1 = (f32[74,8,128]{2,1,0:T(8,128)S(1)}, f32[74,8,128]{2,1,0:T(8,128)S(1)}, u32[]{:S(2)}, u32[]{:S(2)}) collective-permute-start(f32[74,8,128]{2,1,0:T(8,128)S(1)} %get-tuple-element.35), channel_id=1, source_target_pairs={{1,2},{3,4},{5,6},{7,8},{9,10},{11,12},{13,14},{2,1},{4,3},{6,5},{... | collective-permute-start | bytes 909320 | tf_op jit(solution)/shard_map/ppermute | solution.py:703
  19.0 1.5 %collective-permute-start.2 = (f32[512,128]{1,0:T(8,128)S(1)}, f32[512,128]{1,0:T(8,128)S(1)}, u32[]{:S(2)}, u32[]{:S(2)}) collective-permute-start(f32[512,128]{1,0:T(8,128)S(1)} %bitcast.4), channel_id=1, source_target_pairs={{0,1},{1,0},{2,3},{3,2},{4,5},{5,4},{6,7},{7,6},{8,9},{9,8},{10,11... | collective-permute-start | bytes 786440 | tf_op jit(solution)/shard_map/ppermute | solution.py:719
  25.1 12.3 %all-to-all-start.1 = ((f32[16,16,128]{2,1,0:T(8,128)}), f32[16,16,128]{2,1,0:T(8,128)S(1)}, u32[]{:S(2)}, u32[]{:S(2)}) async-start(f32[16,16,128]{2,1,0:T(8,128)} %bitcast.2), calls=%async_computation.1 | async-start | bytes 262144 | tf_op jit(solution)/shard_map/all_to_all | solution.py:753

commit v17 on v16

--- a/solution.py
+++ b/solution.py
@@ -56,6 +56,11 @@
 
 
 BATCH = 8
+SLOTS = 16
+
+
+def slot_rows(plan):
+    return BATCH * 2 * (plan.sub + 2)
 
 
 def odd_device():
@@ -184,8 +189,10 @@
 
 
 class Shifts:
-    def __init__(self, plan):
+    def __init__(self, plan, memory=None):
         self.plan = plan
+        self.memory = memory if plan.unrolled else None
+        self.slot = 0
         shape = (plan.sub, plan.lanes)
         self.row = lax.broadcasted_iota(jnp.int32, shape, 0)
         self.lane = lax.broadcasted_iota(jnp.int32, shape, 1)
@@ -223,16 +230,74 @@
             moved = jnp.where(self.first_row, self.by_lane(moved, plan.ny), moved)
         return jnp.where(self.top, top, moved)
 
+    def block(self):
+        start = self.slot * slot_rows(self.plan)
+        self.slot = (self.slot + 1) % SLOTS
+        return start
+
+    def dz(self, f, top):
+        if self.memory is None or f.ndim == 2:
+            return self.below(f) - self.above(f, top * f if top else 0.0)
+        plan, memory = self.plan, self.memory
+        count, sub = f.shape[:2]
+        start, size = self.block(), 2 * (sub + 2)
+        for i in range(count):
+            memory[pl.ds(start + i * size + 2, sub, stride=2), :] = f[i]
+        lane = lax.broadcasted_iota(jnp.int32, (count, plan.lanes), 1)
+        first = memory[pl.ds(start + 2, count, stride=size), :]
+        last = memory[pl.ds(start + 2 * sub, count, stride=size), :]
+        after = jnp.where(lane < plan.lanes - plan.ny, self.by_lane(first, -plan.ny), 0.0)
+        before = jnp.where(lane >= plan.ny, self.by_lane(last, plan.ny), top * first)
+        memory[pl.ds(start, count, stride=size), :] = before
+        memory[pl.ds(start + 2 * (sub + 1), count, stride=size), :] = after
+        return jnp.stack(
+            [
+                memory[pl.ds(start + i * size + 4, sub, stride=2), :]
+                - memory[pl.ds(start + i * size, sub, stride=2), :]
+                for i in range(count)
+            ]
+        )
+
+    def spread_rows(self, start, rows):
+        plan, memory = self.plan, self.memory
+        count = rows.shape[0]
+        memory[pl.ds(start, count), :] = rows
+        return jnp.stack(
+            [
+                jnp.broadcast_to(memory[pl.ds(start + i, 1), :], (plan.sub, plan.lanes))
+                for i in range(count)
+            ]
+        )
+
     def seafloor(self, vz):
-        row = self.over_chunks(jnp.where(self.top, vz, 0.0))
-        return jnp.broadcast_to(row[..., 0:1, :], vz.shape)
+        if self.memory is None or vz.ndim == 2:
+            row = self.over_chunks(jnp.where(self.top, vz, 0.0))
+            return jnp.broadcast_to(row[..., 0:1, :], vz.shape)
+        memory, start = self.memory, self.block()
+        count, sub, lanes = vz.shape
+        for i in range(count):
+            memory[pl.ds(start + i * sub, sub), :] = vz[i]
+        rows = memory[pl.ds(start, count, stride=sub), :]
+        lane = lax.broadcasted_iota(jnp.int32, rows.shape, 1)
+        rows = self.over_chunks(jnp.where(lane < self.plan.ny, rows, 0.0))
+        return self.spread_rows(start + BATCH * sub, rows)
 
     def on_top(self, f):
-        shift = self.plan.sub // 2
-        while shift:
-            f = f + self.by_row(f, shift)
-            shift //= 2
-        return jnp.where(self.top, self.over_chunks(f), 0.0)
+        if self.memory is None or f.ndim == 2:
+            shift = self.plan.sub // 2
+            while shift:
+                f = f + self.by_row(f, shift)
+                shift //= 2
+            return jnp.where(self.top, self.over_chunks(f), 0.0)
+        memory, start = self.memory, self.block()
+        count, sub, lanes = f.shape
+        for i in range(count):
+            memory[pl.ds(start + i * sub, sub), :] = f[i]
+        rows = memory[pl.ds(start, count, stride=sub), :]
+        for k in range(1, sub):
+            rows = rows + memory[pl.ds(start + k, count, stride=sub), :]
+        rows = self.spread_rows(start + BATCH * sub, self.over_chunks(rows))
+        return jnp.where(self.top, rows, 0.0)
 
     def over_chunks(self, f):
         shift = self.plan.ny
@@ -245,12 +310,12 @@
 def acceleration(sh, stress, j, count):
     at, before, after = (pl.ds(j + k, count) for k in (0, -1, 1))
     sxy, sxz = stress[SXY, at], stress[SXZ, at]
-    ax = stress[SXX, after] - stress[SXX, before] + sh.dy(sxy) + sh.below(sxz) - sh.above(sxz, 0.0)
+    ax = stress[SXX, after] - stress[SXX, before] + sh.dy(sxy) + sh.dz(sxz, 0.0)
     syz = stress[SYZ, at]
     ay = stress[SXY, after] - stress[SXY, before] + sh.dy(stress[SYY, at])
-    ay = ay + sh.below(syz) - sh.above(syz, 0.0)
+    ay = ay + sh.dz(syz, 0.0)
     szz = stress[SZZ, at]
-    az = stress[SXZ, after] - stress[SXZ, before] + sh.dy(syz) + sh.below(szz) - sh.above(szz, 0.0)
+    az = stress[SXZ, after] - stress[SXZ, before] + sh.dy(syz) + sh.dz(szz, 0.0)
     return ax, ay, az
 
 
@@ -259,7 +324,7 @@
     vx, vy, vz = vel[VX, at], vel[VY, at], vel[VZ, at]
     exx = vel[VX, after] - vel[VX, before]
     eyy = sh.dy(vy)
-    ezz = sh.below(vz) - sh.above(vz, vz)
+    ezz = sh.dz(vz, 1.0)
     mu = mats[SHEAR, at]
     mu2 = mu + mu
     common = mats[LAMB, at] * (exx + eyy + ezz)
@@ -268,9 +333,9 @@
     yield SZZ, stress[SZZ, at] + (common + mu2 * ezz)
     exy = sh.dy(vx) + vel[VY, after] - vel[VY, before]
     yield SXY, stress[SXY, at] + mu * exy
-    exz = sh.below(vx) - sh.above(vx, vx) + vel[VZ, after] - vel[VZ, before]
+    exz = sh.dz(vx, 1.0) + vel[VZ, after] - vel[VZ, before]
     yield SXZ, stress[SXZ, at] + (mu * exz + mats[FAULT, at])
-    eyz = sh.below(vy) - sh.above(vy, vy) + sh.dy(vz)
+    eyz = sh.dz(vy, 1.0) + sh.dy(vz)
     yield SYZ, stress[SYZ, at] + mu * eyz
 
 
@@ -346,7 +411,7 @@
         at = pl.ds(j + 1, count)
         p = oc[0, at]
         wet = self.water[at]
-        rise = sh.below(p) + self.bottom[at] * p - sh.above(p, -p)
+        rise = sh.dz(p, -1.0) + self.bottom[at] * p
         oc[3, at] = wet * (oc[3, at] - (HALF * rise + (DT * GRAV) * p))
         oc[2, at] = wet * (oc[2, at] - HALF * sh.dy(p))
 
@@ -354,7 +419,7 @@
         oc, sh = self.oc, self.sh
         before, at, after = (pl.ds(j + k, count) for k in range(3))
         w = oc[3, at]
-        rise = sh.below(w) - sh.above(w, w)
+        rise = sh.dz(w, 1.0)
         if floor is not None:
             rise = rise + self.bottom[at] * floor(pl.ds(j, count))
         total = oc[1, after] - oc[1, before] + sh.dy(oc[2, at]) + rise
@@ -430,11 +495,11 @@
 
 def inner_kernel(
     plan, arrived, swapped, mats, vel_in, stress_in, vel, stress, oc, water, bottom, loads,
-    gather, depths,
+    gather, depths, memory,
 ):
     sub, chunks, n, strips = plan.sub, plan.chunks, plan.n, plan.strips
     cells, sent = plan.cells, plan.sent_groups
-    sh = Shifts(plan)
+    sh = Shifts(plan, memory)
     odd = odd_device()
     half = n // 2
     columns = 2 * cells + 2 * HALO
@@ -503,11 +568,11 @@
 
 def outer_kernel(
     plan, materials, border, water, bottom, vel_in, stress_in, mats_in, oc_in, loads_in,
-    vel, stress, mats, oc, loads, message, gather, rows, sem,
+    vel, stress, mats, oc, loads, message, gather, rows, memory, sem,
 ):
     sub, chunks, n, strips, cells = plan.sub, plan.chunks, plan.n, plan.strips, plan.cells
     near = cells - 1
-    sh = Shifts(plan)
+    sh = Shifts(plan, memory)
     odd = odd_device()
     if not plan.unrolled:
         for here, there in (
@@ -733,6 +798,7 @@
         [
             pltpu.VMEM((lanes, LANES), F32),
             pltpu.VMEM((2, plan.depth, lanes), F32),
+            pltpu.VMEM((SLOTS * slot_rows(plan), lanes), F32),
         ],
         input_output_aliases={3: 0, 4: 1},
     )(*(near(a) for a in (arrived, swapped, mats, vel, strs)))
@@ -745,6 +811,7 @@
         [
             pltpu.VMEM((plan.own_groups, lanes, LANES), F32),
             pltpu.VMEM((n * plan.back_rows, LANES), F32),
+            pltpu.VMEM((SLOTS * slot_rows(plan), lanes), F32),
             pltpu.SemaphoreType.DMA,
         ],
         outs=(vmem,) * 5 + (hbm,),

time: 38.6 us -> 38.5 us (level)
  Pallas kernels: 10.6 us -> 10.2 us
  transfers between devices with their start and end apart: 5 -> 5, of which waited for: 4 -> 4; matrix products, arithmetic and copies ran while one was open for 0% -> 0% of each run, Pallas kernels for 14% -> 13%
where the time goes in v17:
time: 38.5 us; the launch traced here: 38.1 us
  waiting for transfers between devices  14.6 us (38%)
  starting transfers between devices  12.5 us (32%)
  Pallas kernels  10.2 us (26%)
  between operations  0.69 us (2%)
    all_to_all x1, starting transfers between devices, on_device(): lax.all_to_all(message.reshape(n // 2, 2 * plan.rows, LANES), 'map', spli...  7.26 us
    all_to_all x1, waiting for transfers between devices, on_device(): lax.all_to_all(message.reshape(n // 2, 2 * plan.rows, LANES), 'map', spli...  6.08 us
    all_to_all x1, waiting for transfers between devices, on_device(): lax.all_to_all(back.reshape(n, plan.back_rows, LANES), 'map', split_axis=...  6.08 us
    all_to_all x1, starting transfers between devices, on_device(): lax.all_to_all(back.reshape(n, plan.back_rows, LANES), 'map', split_axis=...  4.53 us
    pallas_call x1, Pallas kernels, on_device(): call(outer_kernel, 'outer_substeps', tuple((planes_of[k] for k in ('vel',...  2.14 us
    pallas_call x1, Pallas kernels, on_device(): call(ocean_kernel, 'ocean_rows', (shape(n * plan.rows, LANES), *(like(a)...  2.1 us
    pallas_call x1, Pallas kernels, on_device(): call(inner_kernel, 'inner_substeps', tuple((planes_of[k] for k in ('vel',...  1.99 us
    pallas_call x1, Pallas kernels, on_device(): call(end_kernel, 'last_updates', (shape(*velocity.shape), shape(*stress.s...  1.85 us
  transfers between devices with their start and end apart: 5, of which 4 were waited for; matrix products, arithmetic and copies ran while one was open for 0% of the time, Pallas kernels for 13%

profile of v17, /device:TPU:0, one launch (start us, length us, event | category | flops | bytes accessed | tf_op | source)
XLA Modules:
  0.0 38.1 jit_solution(17565486471124985834)
XLA Ops:
  0.6 2.1 %ocean_rows.1 = (f32[512,128]{1,0:T(8,128)}, f32[3,8,32,32]{3,2,1,0:T(8,128)S(1)}, f32[6,8,32,32]{3,2,1,0:T(8,128)S(1)}, s32[8,32,32]{2,1,0:T(8,128)S(1)}, f32[8,32]{1,0:T(8,128)S(1)}) custom-call(f32[3,8,32,32]{3,2,1,0:T(8,128)} %vel_ref.1, f32[6,8,32,32]{3,2,1,0:T(8,128)} %stress_ref.1, s32[8,32,32]{2,1,0:T(8,128)} %zones_ref.1, f32[8,32]{1,0:T(8,128)} %slip_ref.1, ...), custom_call_target="tpu_custom_call" | custom-call | tf_op jit(solution)/shard_map/ocean_rows/pallas_call | solution.py:736
  2.7 7.3 %all-to-all-start = ((f32[8,64,128]{2,1,0:T(8,128)}), f32[8,64,128]{2,1,0:T(8,128)S(1)}, u32[]{:S(2)}, u32[]{:S(2)}) async-start(f32[8,64,128]{2,1,0:T(8,128)} %bitcast), calls=%async_computation | async-start | bytes 524288 | tf_op jit(solution)/shard_map/all_to_all | solution.py:753
  10.0 0.3 crust_planes.1
  10.3 0.0 copy-start
  10.3 0.1 collective-permute-start
  10.4 0.7 %collective-permute-start.1 = (f32[74,8,128]{2,1,0:T(8,128)S(1)}, f32[74,8,128]{2,1,0:T(8,128)S(1)}, u32[]{:S(2)}, u32[]{:S(2)}) collective-permute-start(f32[74,8,128]{2,1,0:T(8,128)S(1)} %get-tuple-element.35), channel_id=1, source_target_pairs={{1,2},{3,4},{5,6},{7,8},{9,10},{11,12},{13,14},{2,1},{4,3},{6,5},{... | collective-permute-start | bytes 909320 | tf_op jit(solution)/shard_map/ppermute | solution.py:768
  11.1 0.9 %collective-permute-done.mate = f32[81,8,128]{2,1,0:T(8,128)S(1)} collective-permute-done((f32[81,8,128]{2,1,0:T(8,128)S(1)}, f32[81,8,128]{2,1,0:T(8,128)S(1)}, u32[]{:S(2)}, u32[]{:S(2)}) %collective-permute-start) | collective-permute-done | bytes 331808 | tf_op jit(solution)/shard_map/ppermute | solution.py:769
  12.0 0.0 copy-done
  12.1 0.9 %first_velocity.1 = (f32[3,32,8,128]{3,2,1,0:T(8,128)S(1)}, f32[6,32,8,128]{3,2,1,0:T(8,128)S(1)}, f32[5,32,8,128]{3,2,1,0:T(8,128)S(1)}, f32[24,128]{1,0:T(8,128)S(1)}) custom-call(f32[3,8]{1,0:T(4,128)S(1)} %copy-done, f32[81,8,128]{2,1,0:T(8,128)S(1)} %get-tuple-element.33.own, f32[81,8,128]{2,1,0:T(8,128)S(1)} %collective-permute-done.mate), custom_call_target="tpu_custom_call" | custom-call | tf_op jit(solution)/shard_map/first_velocity/pallas_call | solution.py:771
  12.9 6.1 %all-to-all-done = f32[8,64,128]{2,1,0:T(8,128)S(1)} async-done(((f32[8,64,128]{2,1,0:T(8,128)}), f32[8,64,128]{2,1,0:T(8,128)S(1)}, u32[]{:S(2)}, u32[]{:S(2)}) %all-to-all-start) | async-done | bytes 262176 | tf_op jit(solution)/shard_map/all_to_all | solution.py:753
  19.0 0.0 collective-permute-start.2
  19.0 1.5 %collective-permute-done.2.swapped = f32[512,128]{1,0:T(8,128)S(1)} collective-permute-done((f32[512,128]{1,0:T(8,128)S(1)}, f32[512,128]{1,0:T(8,128)S(1)}, u32[]{:S(2)}, u32[]{:S(2)}) %collective-permute-start.2) | collective-permute-done | bytes 262176 | tf_op jit(solution)/shard_map/ppermute | solution.py:784
  20.6 2.0 %inner_substeps.1 = (f32[3,32,8,128]{3,2,1,0:T(8,128)S(1)}, f32[6,32,8,128]{3,2,1,0:T(8,128)S(1)}, f32[4,34,8,128]{3,2,1,0:T(8,128)S(1)}, f32[34,8,128]{2,1,0:T(...) custom-call(f32[512,128]{1,0:T(8,128)S(1)} %bitcast.5, ...), custom_call_target="tpu_custom_call", output_to_operand_aliasing={{0}: (3, {}), {1}: (4, {})} | custom-call | tf_op jit(solution)/shard_map/inner_substeps/pallas_call | solution.py:793
  22.6 0.0 collective-permute-done.1.border
  22.6 2.1 %outer_substeps.1 = (f32[3,32,8,128]{3,2,1,0:T(8,128)S(1)}, f32[6,32,8,128]{3,2,1,0:T(8,128)S(1)}, f32[5,32,8,128]{3,2,1,0:T(8,128)S(1)}, f32[4,34,8,128]{3,2,1,...) custom-call(f32[24,128]{1,0:T(8,128)S(1)} %get-tuple-element.34.mate, ...), custom_call_target="tpu_custom_call", output_to_operand_aliasing={{0}: (4, {}), {1}: (5, {}), {2}: (6, {}), {3}: (7, {}), {4}... | custom-call | tf_op jit(solution)/shard_map/outer_substeps/pallas_call | solution.py:805
  24.7 4.5 %all-to-all-start.1 = ((f32[16,16,128]{2,1,0:T(8,128)}), f32[16,16,128]{2,1,0:T(8,128)S(1)}, u32[]{:S(2)}, u32[]{:S(2)}) async-start(f32[16,16,128]{2,1,0:T(8,128)} %bitcast.2), calls=%async_computation.1 | async-start | bytes 262144 | tf_op jit(solution)/shard_map/all_to_all | solution.py:820
  29.2 1.9 %last_updates.1 = (f32[3,8,32,32]{3,2,1,0:T(8,128)}, f32[6,8,32,32]{3,2,1,0:T(8,128)}) custom-call(f32[3,32,8,128]{3,2,1,0:T(8,128)S(1)} %get-tuple-element.48.vel_all, f32[6,32,8,128]{3,2,1,0:T(8,128)S(1)} %get-tuple-element.49.stress_all, f32[5,32,8,128]{3,2,1,0:T(8,128)S(1)} %get-tuple-element.50.mats_all, f32[32,8,128]{2,1,0:T(8,128)S(1)} %get-tuple-element.51.loads_all), custom_call_target="tpu_custom_call" | custom-call | tf_op jit(solution)/shard_map/last_updates/pallas_call | solution.py:823
  31.1 6.1 %all-to-all-done.1 = f32[16,16,128]{2,1,0:T(8,128)S(1)} async-done(((f32[16,16,128]{2,1,0:T(8,128)}), f32[16,16,128]{2,1,0:T(8,128)S(1)}, u32[]{:S(2)}, u32[]{:S(2)}) %all-to-all-start.1) | async-done | bytes 131104 | tf_op jit(solution)/shard_map/all_to_all | solution.py:820
  37.2 0.9 %ocean_strips.1 = f32[4,2,32,128]{3,2,1,0:T(8,128)} custom-call(f32[256,128]{1,0:T(8,128)S(1)} %bitcast.6), custom_call_target="tpu_custom_call" | custom-call | tf_op jit(solution)/shard_map/ocean_strips/pallas_call | solution.py:833
Async XLA Ops:
  2.7 16.3 %all-to-all-start = ((f32[8,64,128]{2,1,0:T(8,128)}), f32[8,64,128]{2,1,0:T(8,128)S(1)}, u32[]{:S(2)}, u32[]{:S(2)}) async-start(f32[8,64,128]{2,1,0:T(8,128)} %bitcast), calls=%async_computation | async-start | bytes 524288 | tf_op jit(solution)/shard_map/all_to_all | solution.py:753
  10.3 1.7 %copy-start = (f32[3,8]{1,0:T(4,128)S(1)}, f32[3,8]{1,0:T(4,128)}, u32[]{:S(2)}) copy-start(f32[3,8]{1,0:T(4,128)} %table.1) | copy-start | bytes 292
  10.3 1.7 %collective-permute-start = (f32[81,8,128]{2,1,0:T(8,128)S(1)}, f32[81,8,128]{2,1,0:T(8,128)S(1)}, u32[]{:S(2)}, u32[]{:S(2)}) collective-permute-start(f32[81,8,128]{2,1,0:T(8,128)S(1)} %get-tuple-element.33.own), channel_id=1, source_target_pairs={{0,1},{1,0},{2,3},{3,2},{4,5},{5,4},{6,7},{7,6},{8,9},{9,8},{10,11... | collective-permute-start | bytes 995336 | tf_op jit(solution)/shard_map/ppermute | solution.py:769
  10.4 12.1 %collective-permute-start.1 = (f32[74,8,128]{2,1,0:T(8,128)S(1)}, f32[74,8,128]{2,1,0:T(8,128)S(1)}, u32[]{:S(2)}, u32[]{:S(2)}) collective-permute-start(f32[74,8,128]{2,1,0:T(8,128)S(1)} %get-tuple-element.35), channel_id=1, source_target_pairs={{1,2},{3,4},{5,6},{7,8},{9,10},{11,12},{13,14},{2,1},{4,3},{6,5},{... | collective-permute-start | bytes 909320 | tf_op jit(solution)/shard_map/ppermute | solution.py:768
  19.0 1.5 %collective-permute-start.2 = (f32[512,128]{1,0:T(8,128)S(1)}, f32[512,128]{1,0:T(8,128)S(1)}, u32[]{:S(2)}, u32[]{:S(2)}) collective-permute-start(f32[512,128]{1,0:T(8,128)S(1)} %bitcast.4), channel_id=1, source_target_pairs={{0,1},{1,0},{2,3},{3,2},{4,5},{5,4},{6,7},{7,6},{8,9},{9,8},{10,11... | collective-permute-start | bytes 786440 | tf_op jit(solution)/shard_map/ppermute | solution.py:784
  24.7 12.5 %all-to-all-start.1 = ((f32[16,16,128]{2,1,0:T(8,128)}), f32[16,16,128]{2,1,0:T(8,128)S(1)}, u32[]{:S(2)}, u32[]{:S(2)}) async-start(f32[16,16,128]{2,1,0:T(8,128)} %bitcast.2), calls=%async_computation.1 | async-start | bytes 262144 | tf_op jit(solution)/shard_map/all_to_all | solution.py:820

commit v18 on v17

--- a/solution.py
+++ b/solution.py
@@ -150,9 +150,11 @@
                 new = jnp.where((lane >= slot) & (lane < slot + sub), edge, old)
                 new = jnp.where((lane >= slot + sub) & (lane < slot + 2 * sub), floor, new)
                 message[pl.ds(at, pairs, stride=2 * rows), :] = new
-    message_out[...] = message[...]
+    out = pltpu.make_async_copy(message, message_out, sems.at[6])
+    out.start()
     for copy in copies[2:]:
         copy.wait()
+    out.wait()
 
 
 def crust_kernel(plan, vel, stress, zones, slip, crust, border):
@@ -461,36 +463,33 @@
             self.stress[f, pl.ds(j, count)] = value
 
     def run(self, spans, inner, send=None):
-        for t in range(STEPS):
-            def planes(inset, update, t=t):
-                self.plan.planes(*spans(t, inset), update, BATCH)
-
-            if t:
-                planes(0, self.flow_x)
-                planes(1, self.flow)
-                planes(1, functools.partial(self.press, floor=self.floor))
-            elif inner:
-                columns = self.vel.shape[1]
-                first, last = spans(0, 1)
-                self.plan.planes(0, columns, self.flow_x, BATCH)
-                self.plan.planes(1, columns - 1, self.flow, BATCH)
-                planes(1, functools.partial(self.press, floor=self.first_floor))
-                self.plan.planes(1, first, functools.partial(self.press, floor=None), BATCH)
-                self.plan.planes(
-                    last, columns - 1, functools.partial(self.press, floor=None), BATCH
-                )
-            else:
-                planes(1, self.add_floor)
-            if t == STEPS - 1:
-                if send is not None:
-                    send()
-                planes(1, self.keep)
-            elif t == 0 and inner:
-                planes(1, self.add_load)
-            else:
-                planes(1, self.move)
+        def planes(t, inset, update):
+            self.plan.planes(*spans(t, inset), update, BATCH)
+
+        def flows(t):
+            planes(t, 0, self.flow_x)
+            planes(t, 1, self.flow)
+
+        if inner:
+            columns = self.vel.shape[1]
+            first, last = spans(0, 1)
+            self.plan.planes(0, columns, self.flow_x, BATCH)
+            self.plan.planes(1, columns - 1, self.flow, BATCH)
+            planes(0, 1, functools.partial(self.press, floor=self.first_floor))
+            later = functools.partial(self.press, floor=None)
+            self.plan.planes(1, first, later, BATCH)
+            self.plan.planes(last, columns - 1, later, BATCH)
+        else:
+            planes(0, 1, self.add_floor)
+        for t in range(STEPS - 1):
+            flows(t + 1)
+            planes(t, 1, self.add_load if inner and t == 0 else self.move)
             if t < STEPS - 2:
-                planes(2, self.strain)
+                planes(t, 2, self.strain)
+            planes(t + 1, 1, functools.partial(self.press, floor=self.floor))
+        if send is not None:
+            send()
+        planes(STEPS - 1, 1, self.keep)
 
 
 def inner_kernel(
@@ -747,8 +746,9 @@
             ),
             pltpu.VMEM((n * plan.strips, LANES), F32),
             pltpu.VMEM((n * plan.rows, LANES), F32),
-            pltpu.SemaphoreType.DMA((6,)),
+            pltpu.SemaphoreType.DMA((7,)),
         ],
+        outs=(hbm,) + (vmem,) * 4,
     )(*(pinned(a) for a in (*crust_args, ocean, bathy)))
     arrived = lax.all_to_all(
         message.reshape(n // 2, 2 * plan.rows, LANES),

time: 38.5 us -> 38.5 us (level)
  no operation moved by 1% of the time
where the time goes in v18:
time: 38.5 us; the launch traced here: 38.1 us
  waiting for transfers between devices  14.6 us (38%)
  starting transfers between devices  12.6 us (33%)
  Pallas kernels  10.2 us (26%)
  between operations  0.69 us (2%)
    all_to_all x1, starting transfers between devices, on_device(): lax.all_to_all(message.reshape(n // 2, 2 * plan.rows, LANES), 'map', spli...  7.26 us
    all_to_all x1, waiting for transfers between devices, on_device(): lax.all_to_all(message.reshape(n // 2, 2 * plan.rows, LANES), 'map', spli...  6.08 us
    all_to_all x1, waiting for transfers between devices, on_device(): lax.all_to_all(back.reshape(n, plan.back_rows, LANES), 'map', split_axis=...  6.08 us
    all_to_all x1, starting transfers between devices, on_device(): lax.all_to_all(back.reshape(n, plan.back_rows, LANES), 'map', split_axis=...  4.54 us
    pallas_call x1, Pallas kernels, on_device(): call(outer_kernel, 'outer_substeps', tuple((planes_of[k] for k in ('vel',...  2.14 us
    pallas_call x1, Pallas kernels, on_device(): call(ocean_kernel, 'ocean_rows', (shape(n * plan.rows, LANES), *(like(a)...  2.09 us
    pallas_call x1, Pallas kernels, on_device(): call(inner_kernel, 'inner_substeps', tuple((planes_of[k] for k in ('vel',...  1.97 us
    pallas_call x1, Pallas kernels, on_device(): call(end_kernel, 'last_updates', (shape(*velocity.shape), shape(*stress.s...  1.85 us
  transfers between devices with their start and end apart: 5, of which 4 were waited for; matrix products, arithmetic and copies ran while one was open for 0% of the time, Pallas kernels for 13%

profile of v18, /device:TPU:0, one launch (start us, length us, event | category | flops | bytes accessed | tf_op | source)
XLA Modules:
  0.0 38.1 jit_solution(11290440492477431920)
XLA Ops:
  0.6 2.1 %ocean_rows.1 = (f32[512,128]{1,0:T(8,128)}, f32[3,8,32,32]{3,2,1,0:T(8,128)S(1)}, f32[6,8,32,32]{3,2,1,0:T(8,128)S(1)}, s32[8,32,32]{2,1,0:T(8,128)S(1)}, f32[8,32]{1,0:T(8,128)S(1)}) custom-call(f32[3,8,32,32]{3,2,1,0:T(8,128)} %vel_ref.1, f32[6,8,32,32]{3,2,1,0:T(8,128)} %stress_ref.1, s32[8,32,32]{2,1,0:T(8,128)} %zones_ref.1, f32[8,32]{1,0:T(8,128)} %slip_ref.1, ...), custom_call_target="tpu_custom_call" | custom-call | tf_op jit(solution)/shard_map/ocean_rows/pallas_call | solution.py:735
  2.7 7.3 %all-to-all-start = ((f32[8,64,128]{2,1,0:T(8,128)}), f32[8,64,128]{2,1,0:T(8,128)S(1)}, u32[]{:S(2)}, u32[]{:S(2)}) async-start(f32[8,64,128]{2,1,0:T(8,128)} %bitcast), calls=%async_computation | async-start | bytes 524288 | tf_op jit(solution)/shard_map/all_to_all | solution.py:753
  10.0 0.3 crust_planes.1
  10.3 0.0 copy-start
  10.3 0.1 collective-permute-start
  10.4 0.7 %collective-permute-start.1 = (f32[74,8,128]{2,1,0:T(8,128)S(1)}, f32[74,8,128]{2,1,0:T(8,128)S(1)}, u32[]{:S(2)}, u32[]{:S(2)}) collective-permute-start(f32[74,8,128]{2,1,0:T(8,128)S(1)} %get-tuple-element.35), channel_id=1, source_target_pairs={{1,2},{3,4},{5,6},{7,8},{9,10},{11,12},{13,14},{2,1},{4,3},{6,5},{... | collective-permute-start | bytes 909320 | tf_op jit(solution)/shard_map/ppermute | solution.py:768
  11.1 0.9 %collective-permute-done.mate = f32[81,8,128]{2,1,0:T(8,128)S(1)} collective-permute-done((f32[81,8,128]{2,1,0:T(8,128)S(1)}, f32[81,8,128]{2,1,0:T(8,128)S(1)}, u32[]{:S(2)}, u32[]{:S(2)}) %collective-permute-start) | collective-permute-done | bytes 331808 | tf_op jit(solution)/shard_map/ppermute | solution.py:769
  12.0 0.0 copy-done
  12.0 0.9 %first_velocity.1 = (f32[3,32,8,128]{3,2,1,0:T(8,128)S(1)}, f32[6,32,8,128]{3,2,1,0:T(8,128)S(1)}, f32[5,32,8,128]{3,2,1,0:T(8,128)S(1)}, f32[24,128]{1,0:T(8,128)S(1)}) custom-call(f32[3,8]{1,0:T(4,128)S(1)} %copy-done, f32[81,8,128]{2,1,0:T(8,128)S(1)} %get-tuple-element.33.own, f32[81,8,128]{2,1,0:T(8,128)S(1)} %collective-permute-done.mate), custom_call_target="tpu_custom_call" | custom-call | tf_op jit(solution)/shard_map/first_velocity/pallas_call | solution.py:771
  12.9 6.1 %all-to-all-done = f32[8,64,128]{2,1,0:T(8,128)S(1)} async-done(((f32[8,64,128]{2,1,0:T(8,128)}), f32[8,64,128]{2,1,0:T(8,128)S(1)}, u32[]{:S(2)}, u32[]{:S(2)}) %all-to-all-start) | async-done | bytes 262176 | tf_op jit(solution)/shard_map/all_to_all | solution.py:753
  19.0 0.0 collective-permute-start.2
  19.0 1.5 %collective-permute-done.2.swapped = f32[512,128]{1,0:T(8,128)S(1)} collective-permute-done((f32[512,128]{1,0:T(8,128)S(1)}, f32[512,128]{1,0:T(8,128)S(1)}, u32[]{:S(2)}, u32[]{:S(2)}) %collective-permute-start.2) | collective-permute-done | bytes 262176 | tf_op jit(solution)/shard_map/ppermute | solution.py:784
  20.6 2.0 %inner_substeps.1 = (f32[3,32,8,128]{3,2,1,0:T(8,128)S(1)}, f32[6,32,8,128]{3,2,1,0:T(8,128)S(1)}, f32[4,34,8,128]{3,2,1,0:T(8,128)S(1)}, f32[34,8,128]{2,1,0:T(...) custom-call(f32[512,128]{1,0:T(8,128)S(1)} %bitcast.5, ...), custom_call_target="tpu_custom_call", output_to_operand_aliasing={{0}: (3, {}), {1}: (4, {})} | custom-call | tf_op jit(solution)/shard_map/inner_substeps/pallas_call | solution.py:793
  22.5 0.0 collective-permute-done.1.border
  22.5 2.1 %outer_substeps.1 = (f32[3,32,8,128]{3,2,1,0:T(8,128)S(1)}, f32[6,32,8,128]{3,2,1,0:T(8,128)S(1)}, f32[5,32,8,128]{3,2,1,0:T(8,128)S(1)}, f32[4,34,8,128]{3,2,1,...) custom-call(f32[24,128]{1,0:T(8,128)S(1)} %get-tuple-element.34.mate, ...), custom_call_target="tpu_custom_call", output_to_operand_aliasing={{0}: (4, {}), {1}: (5, {}), {2}: (6, {}), {3}: (7, {}), {4}... | custom-call | tf_op jit(solution)/shard_map/outer_substeps/pallas_call | solution.py:805
  24.7 4.5 %all-to-all-start.1 = ((f32[16,16,128]{2,1,0:T(8,128)}), f32[16,16,128]{2,1,0:T(8,128)S(1)}, u32[]{:S(2)}, u32[]{:S(2)}) async-start(f32[16,16,128]{2,1,0:T(8,128)} %bitcast.2), calls=%async_computation.1 | async-start | bytes 262144 | tf_op jit(solution)/shard_map/all_to_all | solution.py:820
  29.2 1.9 %last_updates.1 = (f32[3,8,32,32]{3,2,1,0:T(8,128)}, f32[6,8,32,32]{3,2,1,0:T(8,128)}) custom-call(f32[3,32,8,128]{3,2,1,0:T(8,128)S(1)} %get-tuple-element.48.vel_all, f32[6,32,8,128]{3,2,1,0:T(8,128)S(1)} %get-tuple-element.49.stress_all, f32[5,32,8,128]{3,2,1,0:T(8,128)S(1)} %get-tuple-element.50.mats_all, f32[32,8,128]{2,1,0:T(8,128)S(1)} %get-tuple-element.51.loads_all), custom_call_target="tpu_custom_call" | custom-call | tf_op jit(solution)/shard_map/last_updates/pallas_call | solution.py:823
  31.1 6.1 %all-to-all-done.1 = f32[16,16,128]{2,1,0:T(8,128)S(1)} async-done(((f32[16,16,128]{2,1,0:T(8,128)}), f32[16,16,128]{2,1,0:T(8,128)S(1)}, u32[]{:S(2)}, u32[]{:S(2)}) %all-to-all-start.1) | async-done | bytes 131104 | tf_op jit(solution)/shard_map/all_to_all | solution.py:820
  37.2 0.9 %ocean_strips.1 = f32[4,2,32,128]{3,2,1,0:T(8,128)} custom-call(f32[256,128]{1,0:T(8,128)S(1)} %bitcast.6), custom_call_target="tpu_custom_call" | custom-call | tf_op jit(solution)/shard_map/ocean_strips/pallas_call | solution.py:833
Async XLA Ops:
  2.7 16.3 %all-to-all-start = ((f32[8,64,128]{2,1,0:T(8,128)}), f32[8,64,128]{2,1,0:T(8,128)S(1)}, u32[]{:S(2)}, u32[]{:S(2)}) async-start(f32[8,64,128]{2,1,0:T(8,128)} %bitcast), calls=%async_computation | async-start | bytes 524288 | tf_op jit(solution)/shard_map/all_to_all | solution.py:753
  10.3 1.7 %copy-start = (f32[3,8]{1,0:T(4,128)S(1)}, f32[3,8]{1,0:T(4,128)}, u32[]{:S(2)}) copy-start(f32[3,8]{1,0:T(4,128)} %table.1) | copy-start | bytes 292
  10.3 1.7 %collective-permute-start = (f32[81,8,128]{2,1,0:T(8,128)S(1)}, f32[81,8,128]{2,1,0:T(8,128)S(1)}, u32[]{:S(2)}, u32[]{:S(2)}) collective-permute-start(f32[81,8,128]{2,1,0:T(8,128)S(1)} %get-tuple-element.33.own), channel_id=1, source_target_pairs={{0,1},{1,0},{2,3},{3,2},{4,5},{5,4},{6,7},{7,6},{8,9},{9,8},{10,11... | collective-permute-start | bytes 995336 | tf_op jit(solution)/shard_map/ppermute | solution.py:769
  10.4 12.1 %collective-permute-start.1 = (f32[74,8,128]{2,1,0:T(8,128)S(1)}, f32[74,8,128]{2,1,0:T(8,128)S(1)}, u32[]{:S(2)}, u32[]{:S(2)}) collective-permute-start(f32[74,8,128]{2,1,0:T(8,128)S(1)} %get-tuple-element.35), channel_id=1, source_target_pairs={{1,2},{3,4},{5,6},{7,8},{9,10},{11,12},{13,14},{2,1},{4,3},{6,5},{... | collective-permute-start | bytes 909320 | tf_op jit(solution)/shard_map/ppermute | solution.py:768
  19.0 1.5 %collective-permute-start.2 = (f32[512,128]{1,0:T(8,128)S(1)}, f32[512,128]{1,0:T(8,128)S(1)}, u32[]{:S(2)}, u32[]{:S(2)}) collective-permute-start(f32[512,128]{1,0:T(8,128)S(1)} %bitcast.4), channel_id=1, source_target_pairs={{0,1},{1,0},{2,3},{3,2},{4,5},{5,4},{6,7},{7,6},{8,9},{9,8},{10,11... | collective-permute-start | bytes 786440 | tf_op jit(solution)/shard_map/ppermute | solution.py:784
  24.7 12.5 %all-to-all-start.1 = ((f32[16,16,128]{2,1,0:T(8,128)}), f32[16,16,128]{2,1,0:T(8,128)S(1)}, u32[]{:S(2)}, u32[]{:S(2)}) async-start(f32[16,16,128]{2,1,0:T(8,128)} %bitcast.2), calls=%async_computation.1 | async-start | bytes 262144 | tf_op jit(solution)/shard_map/all_to_all | solution.py:820

commit v19 on v18

--- a/solution.py
+++ b/solution.py
@@ -462,33 +462,25 @@
         for f, value in strained(self.sh, self.vel, self.stress, self.mats, j, count):
             self.stress[f, pl.ds(j, count)] = value
 
-    def run(self, spans, inner, send=None):
+    def run(self, spans):
         def planes(t, inset, update):
             self.plan.planes(*spans(t, inset), update, BATCH)
 
-        def flows(t):
-            planes(t, 0, self.flow_x)
-            planes(t, 1, self.flow)
-
-        if inner:
-            columns = self.vel.shape[1]
-            first, last = spans(0, 1)
-            self.plan.planes(0, columns, self.flow_x, BATCH)
-            self.plan.planes(1, columns - 1, self.flow, BATCH)
-            planes(0, 1, functools.partial(self.press, floor=self.first_floor))
-            later = functools.partial(self.press, floor=None)
-            self.plan.planes(1, first, later, BATCH)
-            self.plan.planes(last, columns - 1, later, BATCH)
-        else:
-            planes(0, 1, self.add_floor)
+        columns = self.vel.shape[1]
+        first, last = spans(0, 1)
+        self.plan.planes(0, columns, self.flow_x, BATCH)
+        self.plan.planes(1, columns - 1, self.flow, BATCH)
+        planes(0, 1, functools.partial(self.press, floor=self.first_floor))
+        later = functools.partial(self.press, floor=None)
+        self.plan.planes(1, first, later, BATCH)
+        self.plan.planes(last, columns - 1, later, BATCH)
         for t in range(STEPS - 1):
-            flows(t + 1)
-            planes(t, 1, self.add_load if inner and t == 0 else self.move)
+            planes(t + 1, 0, self.flow_x)
+            planes(t + 1, 1, self.flow)
+            planes(t, 1, self.add_load if t == 0 else self.move)
             if t < STEPS - 2:
                 planes(t, 2, self.strain)
             planes(t + 1, 1, functools.partial(self.press, floor=self.floor))
-        if send is not None:
-            send()
         planes(STEPS - 1, 1, self.keep)
 
 
@@ -562,7 +554,7 @@
     if not plan.unrolled:
         plan.planes(HALO, HALO + 2 * cells, bring_in)
     updates = Updates(plan, sh, vel, stress, mats, oc, water, bottom, loads)
-    updates.run(lambda t, inset: (HALO + 2 * t + inset, HALO + 2 * cells - 2 * t - inset), True)
+    updates.run(lambda t, inset: (HALO + 2 * t + inset, HALO + 2 * cells - 2 * t - inset))
 
 
 def outer_kernel(
@@ -584,52 +576,61 @@
         row = materials[pl.ds(c * ZONES + z, 1), :]
         return jnp.broadcast_to(row, (sub, plan.lanes))
 
-    def side(core):
-        low, far = ((1, 0), (HALO + 2 * cells, 2 * HALO + 2 * cells - 1))[core]
-        state = (vel, stress, mats)
-        plan.planes(
-            0,
-            near,
-            lambda x, count: bring(
-                plan, sh, material, state, border, near, x, count, low + x, 1 - core
-            ),
-            BATCH,
+    low = 1 + (HALO + 2 * cells - 1) * odd
+    far = (2 * HALO + 2 * cells - 1) * odd
+
+    def planes(t, inset, update):
+        start = odd * (HALO + 2 * cells) + (1 - 2 * odd) * (2 * t + inset)
+        if plan.unrolled:
+            update(start, HALO)
+        else:
+            lax.fori_loop(0, HALO, lambda j, _: [update(start + j, 1), 0][1], 0)
+
+    plan.planes(
+        0,
+        near,
+        lambda x, count: bring(
+            plan, sh, material, (vel, stress, mats), border, near, x, count, low + x, 1 - odd
+        ),
+        BATCH,
+    )
+    for i, f in enumerate((SXX, SXY, SXZ)):
+        stress[f, far] = border[10 * near + i]
+    planes(0, 1, updates.add_floor)
+
+    def substep(t, carry):
+        planes(t, 1, updates.move)
+
+        @pl.when(t < STEPS - 2)
+        def _():
+            planes(t, 2, updates.strain)
+
+        planes(t + 1, 0, updates.flow_x)
+        planes(t + 1, 1, updates.flow)
+        planes(t + 1, 1, functools.partial(updates.press, floor=updates.floor))
+        return carry
+
+    lax.fori_loop(0, STEPS - 1, substep, 0)
+    for group in range(plan.own_groups):
+        stacked = jnp.concatenate(
+            [
+                oc[f, 1 + HALO + odd * cells + group * chunks + i]
+                for i in range(chunks)
+                for f in range(4)
+            ],
+            axis=0,
         )
-        for i, f in enumerate((SXX, SXY, SXZ)):
-            stress[f, far] = border[10 * near + i]
-
-        def spans(t, inset):
-            if core == 0:
-                return 2 * t + inset, 2 * t + inset + HALO
-            last = 2 * HALO + 2 * cells - 2 * t - inset
-            return last - HALO, last
-
-        copy = pltpu.make_async_copy(rows, message, sem)
-
-        def send():
-            for group in range(plan.own_groups):
-                stacked = jnp.concatenate(
-                    [
-                        oc[f, 1 + HALO + core * cells + group * chunks + i]
-                        for i in range(chunks)
-                        for f in range(4)
-                    ],
-                    axis=0,
-                )
-                gather[group] = stacked.T
-                for kc in range(chunks):
-                    for yl in range(strips):
-                        at = group * plan.lead + kc * strips + yl
-                        rows[pl.ds(at, n, stride=plan.back_rows), :] = gather[
-                            group, pl.ds(kc * plan.ny + yl, n, stride=strips), :
-                        ]
-            copy.start()
-
-        updates.run(spans, False, send)
-        copy.wait()
-
-    for core in range(2):
-        pl.when(odd == core)(functools.partial(side, core))
+        gather[group] = stacked.T
+        for kc in range(chunks):
+            for yl in range(strips):
+                at = group * plan.lead + kc * strips + yl
+                rows[pl.ds(at, n, stride=plan.back_rows), :] = gather[
+                    group, pl.ds(kc * plan.ny + yl, n, stride=strips), :
+                ]
+    copy = pltpu.make_async_copy(rows, message, sem)
+    copy.start()
+    planes(STEPS - 1, 1, updates.keep)
+    copy.wait()
 
 
 def end_kernel(plan, vel_all, stress_all, mats_all, loads_all, vel_out, stress_out, vel, stress):

time: 38.5 us -> 38.9 us (1.010)
  Pallas kernels: 10.2 us -> 10.6 us
    pallas_call x1, Pallas kernels: 2.14 us -> 2.57 us  [on_device(): call(outer_kernel, 'outer_substeps', tuple((planes_of[k] for k in ('vel',...]
where the time goes in v19:
time: 38.9 us; the launch traced here: 38.5 us
  waiting for transfers between devices  14.6 us (38%)
  starting transfers between devices  12.6 us (32%)
  Pallas kernels  10.6 us (27%)
  between operations  0.69 us (2%)
    all_to_all x1, starting transfers between devices, on_device(): lax.all_to_all(message.reshape(n // 2, 2 * plan.rows, LANES), 'map', spli...  7.26 us
    all_to_all x1, waiting for transfers between devices, on_device(): lax.all_to_all(message.reshape(n // 2, 2 * plan.rows, LANES), 'map', spli...  6.08 us
    all_to_all x1, waiting for transfers between devices, on_device(): lax.all_to_all(back.reshape(n, plan.back_rows, LANES), 'map', split_axis=...  6.08 us
    all_to_all x1, starting transfers between devices, on_device(): lax.all_to_all(back.reshape(n, plan.back_rows, LANES), 'map', split_axis=...  4.55 us
    pallas_call x1, Pallas kernels, on_device(): call(outer_kernel, 'outer_substeps', tuple((planes_of[k] for k in ('vel',...  2.57 us
    pallas_call x1, Pallas kernels, on_device(): call(ocean_kernel, 'ocean_rows', (shape(n * plan.rows, LANES), *(like(a)...  2.09 us
    pallas_call x1, Pallas kernels, on_device(): call(inner_kernel, 'inner_substeps', tuple((planes_of[k] for k in ('vel',...  1.97 us
    pallas_call x1, Pallas kernels, on_device(): call(end_kernel, 'last_updates', (shape(*velocity.shape), shape(*stress.s...  1.85 us
  transfers between devices with their start and end apart: 5, of which 4 were waited for; matrix products, arithmetic and copies ran while one was open for 0% of the time, Pallas kernels for 13%

profile of v19, /device:TPU:0, one launch (start us, length us, event | category | flops | bytes accessed | tf_op | source)
XLA Modules:
  0.0 38.5 jit_solution(9261215173308988902)
XLA Ops:
  0.6 2.1 %ocean_rows.1 = (f32[512,128]{1,0:T(8,128)}, f32[3,8,32,32]{3,2,1,0:T(8,128)S(1)}, f32[6,8,32,32]{3,2,1,0:T(8,128)S(1)}, s32[8,32,32]{2,1,0:T(8,128)S(1)}, f32[8,32]{1,0:T(8,128)S(1)}) custom-call(f32[3,8,32,32]{3,2,1,0:T(8,128)} %vel_ref.1, f32[6,8,32,32]{3,2,1,0:T(8,128)} %stress_ref.1, s32[8,32,32]{2,1,0:T(8,128)} %zones_ref.1, f32[8,32]{1,0:T(8,128)} %slip_ref.1, ...), custom_call_target="tpu_custom_call" | custom-call | tf_op jit(solution)/shard_map/ocean_rows/pallas_call | solution.py:736
  2.7 7.3 %all-to-all-start = ((f32[8,64,128]{2,1,0:T(8,128)}), f32[8,64,128]{2,1,0:T(8,128)S(1)}, u32[]{:S(2)}, u32[]{:S(2)}) async-start(f32[8,64,128]{2,1,0:T(8,128)} %bitcast), calls=%async_computation | async-start | bytes 524288 | tf_op jit(solution)/shard_map/all_to_all | solution.py:754
  10.0 0.3 crust_planes.1
  10.3 0.0 copy-start
  10.3 0.1 collective-permute-start
  10.4 0.7 %collective-permute-start.1 = (f32[74,8,128]{2,1,0:T(8,128)S(1)}, f32[74,8,128]{2,1,0:T(8,128)S(1)}, u32[]{:S(2)}, u32[]{:S(2)}) collective-permute-start(f32[74,8,128]{2,1,0:T(8,128)S(1)} %get-tuple-element.35), channel_id=1, source_target_pairs={{1,2},{3,4},{5,6},{7,8},{9,10},{11,12},{13,14},{2,1},{4,3},{6,5},{... | collective-permute-start | bytes 909320 | tf_op jit(solution)/shard_map/ppermute | solution.py:769
  11.1 0.9 %collective-permute-done.mate = f32[81,8,128]{2,1,0:T(8,128)S(1)} collective-permute-done((f32[81,8,128]{2,1,0:T(8,128)S(1)}, f32[81,8,128]{2,1,0:T(8,128)S(1)}, u32[]{:S(2)}, u32[]{:S(2)}) %collective-permute-start) | collective-permute-done | bytes 331808 | tf_op jit(solution)/shard_map/ppermute | solution.py:770
  12.0 0.0 copy-done
  12.0 0.9 %first_velocity.1 = (f32[3,32,8,128]{3,2,1,0:T(8,128)S(1)}, f32[6,32,8,128]{3,2,1,0:T(8,128)S(1)}, f32[5,32,8,128]{3,2,1,0:T(8,128)S(1)}, f32[24,128]{1,0:T(8,128)S(1)}) custom-call(f32[3,8]{1,0:T(4,128)S(1)} %copy-done, f32[81,8,128]{2,1,0:T(8,128)S(1)} %get-tuple-element.33.own, f32[81,8,128]{2,1,0:T(8,128)S(1)} %collective-permute-done.mate), custom_call_target="tpu_custom_call" | custom-call | tf_op jit(solution)/shard_map/first_velocity/pallas_call | solution.py:772
  12.9 6.1 %all-to-all-done = f32[8,64,128]{2,1,0:T(8,128)S(1)} async-done(((f32[8,64,128]{2,1,0:T(8,128)}), f32[8,64,128]{2,1,0:T(8,128)S(1)}, u32[]{:S(2)}, u32[]{:S(2)}) %all-to-all-start) | async-done | bytes 262176 | tf_op jit(solution)/shard_map/all_to_all | solution.py:754
  19.0 0.0 collective-permute-start.2
  19.0 1.5 %collective-permute-done.2.swapped = f32[512,128]{1,0:T(8,128)S(1)} collective-permute-done((f32[512,128]{1,0:T(8,128)S(1)}, f32[512,128]{1,0:T(8,128)S(1)}, u32[]{:S(2)}, u32[]{:S(2)}) %collective-permute-start.2) | collective-permute-done | bytes 262176 | tf_op jit(solution)/shard_map/ppermute | solution.py:785
  20.6 2.0 %inner_substeps.1 = (f32[3,32,8,128]{3,2,1,0:T(8,128)S(1)}, f32[6,32,8,128]{3,2,1,0:T(8,128)S(1)}, f32[4,34,8,128]{3,2,1,0:T(8,128)S(1)}, f32[34,8,128]{2,1,0:T(...) custom-call(f32[512,128]{1,0:T(8,128)S(1)} %bitcast.5, ...), custom_call_target="tpu_custom_call", output_to_operand_aliasing={{0}: (3, {}), {1}: (4, {})} | custom-call | tf_op jit(solution)/shard_map/inner_substeps/pallas_call | solution.py:794
  22.5 0.0 collective-permute-done.1.border
  22.5 2.6 %outer_substeps.1 = (f32[3,32,8,128]{3,2,1,0:T(8,128)S(1)}, f32[6,32,8,128]{3,2,1,0:T(8,128)S(1)}, f32[5,32,8,128]{3,2,1,0:T(8,128)S(1)}, f32[4,34,8,128]{3,2,1,...) custom-call(f32[24,128]{1,0:T(8,128)S(1)} %get-tuple-element.34.mate, ...), custom_call_target="tpu_custom_call", output_to_operand_aliasing={{0}: (4, {}), {1}: (5, {}), {2}: (6, {}), {3}: (7, {}), {4}... | custom-call | tf_op jit(solution)/shard_map/outer_substeps/pallas_call | solution.py:806
  25.1 4.6 %all-to-all-start.1 = ((f32[16,16,128]{2,1,0:T(8,128)}), f32[16,16,128]{2,1,0:T(8,128)S(1)}, u32[]{:S(2)}, u32[]{:S(2)}) async-start(f32[16,16,128]{2,1,0:T(8,128)} %bitcast.2), calls=%async_computation.1 | async-start | bytes 262144 | tf_op jit(solution)/shard_map/all_to_all | solution.py:821
  29.7 1.9 %last_updates.1 = (f32[3,8,32,32]{3,2,1,0:T(8,128)}, f32[6,8,32,32]{3,2,1,0:T(8,128)}) custom-call(f32[3,32,8,128]{3,2,1,0:T(8,128)S(1)} %get-tuple-element.48.vel_all, f32[6,32,8,128]{3,2,1,0:T(8,128)S(1)} %get-tuple-element.49.stress_all, f32[5,32,8,128]{3,2,1,0:T(8,128)S(1)} %get-tuple-element.50.mats_all, f32[32,8,128]{2,1,0:T(8,128)S(1)} %get-tuple-element.51.loads_all), custom_call_target="tpu_custom_call" | custom-call | tf_op jit(solution)/shard_map/last_updates/pallas_call | solution.py:824
  31.5 6.1 %all-to-all-done.1 = f32[16,16,128]{2,1,0:T(8,128)S(1)} async-done(((f32[16,16,128]{2,1,0:T(8,128)}), f32[16,16,128]{2,1,0:T(8,128)S(1)}, u32[]{:S(2)}, u32[]{:S(2)}) %all-to-all-start.1) | async-done | bytes 131104 | tf_op jit(solution)/shard_map/all_to_all | solution.py:821
  37.6 0.9 %ocean_strips.1 = f32[4,2,32,128]{3,2,1,0:T(8,128)} custom-call(f32[256,128]{1,0:T(8,128)S(1)} %bitcast.6), custom_call_target="tpu_custom_call" | custom-call | tf_op jit(solution)/shard_map/ocean_strips/pallas_call | solution.py:834
Async XLA Ops:
  2.7 16.3 %all-to-all-start = ((f32[8,64,128]{2,1,0:T(8,128)}), f32[8,64,128]{2,1,0:T(8,128)S(1)}, u32[]{:S(2)}, u32[]{:S(2)}) async-start(f32[8,64,128]{2,1,0:T(8,128)} %bitcast), calls=%async_computation | async-start | bytes 524288 | tf_op jit(solution)/shard_map/all_to_all | solution.py:754
  10.3 1.7 %copy-start = (f32[3,8]{1,0:T(4,128)S(1)}, f32[3,8]{1,0:T(4,128)}, u32[]{:S(2)}) copy-start(f32[3,8]{1,0:T(4,128)} %table.1) | copy-start | bytes 292
  10.3 1.7 %collective-permute-start = (f32[81,8,128]{2,1,0:T(8,128)S(1)}, f32[81,8,128]{2,1,0:T(8,128)S(1)}, u32[]{:S(2)}, u32[]{:S(2)}) collective-permute-start(f32[81,8,128]{2,1,0:T(8,128)S(1)} %get-tuple-element.33.own), channel_id=1, source_target_pairs={{0,1},{1,0},{2,3},{3,2},{4,5},{5,4},{6,7},{7,6},{8,9},{9,8},{10,11... | collective-permute-start | bytes 995336 | tf_op jit(solution)/shard_map/ppermute | solution.py:770
  10.4 12.1 %collective-permute-start.1 = (f32[74,8,128]{2,1,0:T(8,128)S(1)}, f32[74,8,128]{2,1,0:T(8,128)S(1)}, u32[]{:S(2)}, u32[]{:S(2)}) collective-permute-start(f32[74,8,128]{2,1,0:T(8,128)S(1)} %get-tuple-element.35), channel_id=1, source_target_pairs={{1,2},{3,4},{5,6},{7,8},{9,10},{11,12},{13,14},{2,1},{4,3},{6,5},{... | collective-permute-start | bytes 909320 | tf_op jit(solution)/shard_map/ppermute | solution.py:769
  19.0 1.5 %collective-permute-start.2 = (f32[512,128]{1,0:T(8,128)S(1)}, f32[512,128]{1,0:T(8,128)S(1)}, u32[]{:S(2)}, u32[]{:S(2)}) collective-permute-start(f32[512,128]{1,0:T(8,128)S(1)} %bitcast.4), channel_id=1, source_target_pairs={{0,1},{1,0},{2,3},{3,2},{4,5},{5,4},{6,7},{7,6},{8,9},{9,8},{10,11... | collective-permute-start | bytes 786440 | tf_op jit(solution)/shard_map/ppermute | solution.py:785
  25.1 12.5 %all-to-all-start.1 = ((f32[16,16,128]{2,1,0:T(8,128)}), f32[16,16,128]{2,1,0:T(8,128)S(1)}, u32[]{:S(2)}, u32[]{:S(2)}) async-start(f32[16,16,128]{2,1,0:T(8,128)} %bitcast.2), calls=%async_computation.1 | async-start | bytes 262144 | tf_op jit(solution)/shard_map/all_to_all | solution.py:821

commit v20 on v18

--- a/solution.py
+++ b/solution.py
@@ -80,11 +80,12 @@
     return out
 
 
-def ocean_kernel(
+def pack_kernel(
     plan, vel_ref, stress_ref, zones_ref, slip_ref, ocean_ref, bathy_ref,
-    message_out, vel, stress, zones, slip, ocean, bathy, turned, grouped, extra, message, sems,
+    message_out, crust, border,
+    vel, stress, zones, slip, ocean, bathy, turned, grouped, extra, message, sems,
 ):
-    cells, sub, chunks = plan.cells, plan.sub, plan.chunks
+    cells, sub, chunks, ny = plan.cells, plan.sub, plan.chunks, plan.ny
     n, strips, block, sent, rows = plan.n, plan.strips, plan.block, plan.sent_groups, plan.rows
     pairs = (
         (ocean_ref, ocean),
@@ -100,8 +101,15 @@
     ]
     for copy in copies:
         copy.start()
+    copies[1].wait()
+    depths = bathy[...].astype(F32)
+    wide = lax.broadcasted_iota(jnp.int32, depths.shape, 1)
+    for d in range(n):
+        first = d * cells - HALO - 1
+        moved = pltpu.roll(depths, -first % plan.nx, 1)
+        moved = jnp.where((wide + first >= 0) & (wide + first < plan.nx), moved, 0.0)
+        extra[d * strips : (d + 1) * strips, :] = moved[:, :LANES]
     copies[0].wait()
-    copies[1].wait()
     count = plan.nx // chunks
     lead = plan.lead
     pad = plan.halo_groups * lead
@@ -121,13 +129,6 @@
     for d in range(n):
         start = (d * plan.own_groups + (d % 2) * plan.halo_groups) * lead
         message[d * rows : (d + 1) * rows, :] = grouped[start : start + rows, :]
-    depths = bathy[...].astype(F32)
-    wide = lax.broadcasted_iota(jnp.int32, depths.shape, 1)
-    for d in range(n):
-        first = d * cells - HALO - 1
-        moved = pltpu.roll(depths, -first % plan.nx, 1)
-        moved = jnp.where((wide + first >= 0) & (wide + first < plan.nx), moved, 0.0)
-        extra[d * strips : (d + 1) * strips, :] = moved[:, :LANES]
     pairs = n // 2
     lane = lax.broadcasted_iota(jnp.int32, (pairs, LANES), 1)
     blank = jnp.zeros((1, LANES), F32)
@@ -152,13 +153,9 @@
                 message[pl.ds(at, pairs, stride=2 * rows), :] = new
     out = pltpu.make_async_copy(message, message_out, sems.at[6])
     out.start()
+
     for copy in copies[2:]:
         copy.wait()
-    out.wait()
-
-
-def crust_kernel(plan, vel, stress, zones, slip, crust, border):
-    cells, sub, chunks, ny = plan.cells, plan.sub, plan.chunks, plan.ny
 
     def joined(ref, *at):
         parts = [ref[(*at, pl.ds(kc * sub, sub), slice(None))] for kc in range(chunks)]
@@ -188,6 +185,7 @@
     for i, f in enumerate((SXX, SXY, SXZ)):
         border[10 * near + i] = crust[(3 + f) * cells + near * (1 - odd)]
     border[10 * near + 3] = fault
+    out.wait()
 
 
 class Shifts:
@@ -731,15 +729,17 @@
     mates = [(i, i ^ 1) for i in range(n)]
     others = [(i, i + 1) for i in range(1, n - 1, 2)]
     others += [(target, source) for source, target in others]
-    crust_args = (velocity, stress, zones, slip)
-    message, *near_args = call(
-        ocean_kernel,
-        "ocean_rows",
-        (shape(n * plan.rows, LANES), *(like(a) for a in crust_args)),
+    message, crust, border = call(
+        pack_kernel,
+        "pack",
+        (
+            shape(n * plan.rows, LANES),
+            shape(10 * cells + 1, sub, lanes),
+            shape(10 * cells - 6, sub, lanes),
+        ),
         [hbm] * 6,
-        [
-            held(ocean),
-            held(bathy),
+        [held(a) for a in (velocity, stress, zones, slip, ocean, bathy)]
+        + [
             pltpu.VMEM((plan.strips, plan.nx, LANES), F32),
             pltpu.VMEM(
                 ((plan.nx // plan.chunks + 2 * plan.halo_groups) * plan.lead, LANES), F32
@@ -748,8 +748,8 @@
             pltpu.VMEM((n * plan.rows, LANES), F32),
             pltpu.SemaphoreType.DMA((7,)),
         ],
-        outs=(hbm,) + (vmem,) * 4,
-    )(*(pinned(a) for a in (*crust_args, ocean, bathy)))
+        outs=(hbm, vmem, vmem),
+    )(*(pinned(a) for a in (velocity, stress, zones, slip, ocean, bathy)))
     arrived = lax.all_to_all(
         message.reshape(n // 2, 2 * plan.rows, LANES),
         "map",
@@ -758,13 +758,6 @@
         axis_index_groups=[list(range(core, n, 2)) for core in range(2)],
         tiled=True,
     ).reshape(n * plan.rows, LANES)
-    crust, border = call(
-        crust_kernel,
-        "crust_planes",
-        (shape(10 * cells + 1, sub, lanes), shape(10 * cells - 6, sub, lanes)),
-        [vmem] * 4,
-        [],
-    )(*near_args)
     other = lax.ppermute(border, "map", others)
     mate = lax.ppermute(crust, "map", mates)
     columns = 2 * cells + 2 * HALO

time: 38.5 us -> 38 us (0.987)
  starting transfers between devices: 12.6 us -> 12.2 us
  waiting for transfers between devices: 14.6 us -> 15 us
    pallas_call x2 -> x1, Pallas kernels: 2.41 us -> 2.07 us  [on_device(): call(pack_kernel, 'pack', (shape(n * plan.rows, LANES), shape(10 * cells...]
  transfers between devices with their start and end apart: 5 -> 5, of which waited for: 4 -> 4; matrix products, arithmetic and copies ran while one was open for 0% -> 0% of each run, Pallas kernels for 13% -> 12%
where the time goes in v20:
time: 38 us; the launch traced here: 37.7 us
  waiting for transfers between devices  15 us (39%)
  starting transfers between devices  12.2 us (32%)
  Pallas kernels  9.84 us (26%)
  between operations  0.69 us (2%)
    all_to_all x1, starting transfers between devices, on_device(): lax.all_to_all(message.reshape(n // 2, 2 * plan.rows, LANES), 'map', spli...  7.26 us
    all_to_all x1, waiting for transfers between devices, on_device(): lax.all_to_all(message.reshape(n // 2, 2 * plan.rows, LANES), 'map', spli...  6.42 us
    all_to_all x1, waiting for transfers between devices, on_device(): lax.all_to_all(back.reshape(n, plan.back_rows, LANES), 'map', split_axis=...  6.08 us
    all_to_all x1, starting transfers between devices, on_device(): lax.all_to_all(back.reshape(n, plan.back_rows, LANES), 'map', split_axis=...  4.17 us
    pallas_call x1, Pallas kernels, on_device(): call(outer_kernel, 'outer_substeps', tuple((planes_of[k] for k in ('vel',...  2.14 us
    pallas_call x1, Pallas kernels, on_device(): call(pack_kernel, 'pack', (shape(n * plan.rows, LANES), shape(10 * cells...  2.07 us
    pallas_call x1, Pallas kernels, on_device(): call(inner_kernel, 'inner_substeps', tuple((planes_of[k] for k in ('vel',...  1.95 us
    pallas_call x1, Pallas kernels, on_device(): call(end_kernel, 'last_updates', (shape(*velocity.shape), shape(*stress.s...  1.85 us
  transfers between devices with their start and end apart: 5, of which 4 were waited for; matrix products, arithmetic and copies ran while one was open for 0% of the time, Pallas kernels for 12%

profile of v20, /device:TPU:0, one launch (start us, length us, event | category | flops | bytes accessed | tf_op | source)
XLA Modules:
  0.0 37.7 jit_solution(17577407765274748429)
XLA Ops:
  0.6 2.1 %pack.1 = (f32[512,128]{1,0:T(8,128)}, f32[81,8,128]{2,1,0:T(8,128)S(1)}, f32[74,8,128]{2,1,0:T(8,128)S(1)}) custom-call(f32[3,8,32,32]{3,2,1,0:T(8,128)} %vel_ref.1, f32[6,8,32,32]{3,2,1,0:T(8,128)} %stress_ref.1, s32[8,32,32]{2,1,0:T(8,128)} %zones_ref.1, f32[8,32]{1,0:T(8,128)} %slip_ref.1, f32[4,2,32,128]{3,2,1,0:T(8,128)} %ocean_ref.1, s32[2,128]{1,0:T(2,128)} %bathy_ref.1), custom_call_target="tpu_custom_call" | custom-call | tf_op jit(solution)/shard_map/pack/pallas_call | solution.py:732
  2.7 7.3 %all-to-all-start = ((f32[8,64,128]{2,1,0:T(8,128)}), f32[8,64,128]{2,1,0:T(8,128)S(1)}, u32[]{:S(2)}, u32[]{:S(2)}) async-start(f32[8,64,128]{2,1,0:T(8,128)} %bitcast), calls=%async_computation | async-start | bytes 524288 | tf_op jit(solution)/shard_map/all_to_all | solution.py:753
  10.0 0.0 copy-start
  10.0 0.1 collective-permute-start
  10.1 0.7 %collective-permute-start.1 = (f32[74,8,128]{2,1,0:T(8,128)S(1)}, f32[74,8,128]{2,1,0:T(8,128)S(1)}, u32[]{:S(2)}, u32[]{:S(2)}) collective-permute-start(f32[74,8,128]{2,1,0:T(8,128)S(1)} %get-tuple-element.27), channel_id=1, source_target_pairs={{1,2},{3,4},{5,6},{7,8},{9,10},{11,12},{13,14},{2,1},{4,3},{6,5},{... | collective-permute-start | bytes 909320 | tf_op jit(solution)/shard_map/ppermute | solution.py:761
  10.8 0.9 %collective-permute-done.mate = f32[81,8,128]{2,1,0:T(8,128)S(1)} collective-permute-done((f32[81,8,128]{2,1,0:T(8,128)S(1)}, f32[81,8,128]{2,1,0:T(8,128)S(1)}, u32[]{:S(2)}, u32[]{:S(2)}) %collective-permute-start) | collective-permute-done | bytes 331808 | tf_op jit(solution)/shard_map/ppermute | solution.py:762
  11.7 0.0 copy-done
  11.7 0.9 %first_velocity.1 = (f32[3,32,8,128]{3,2,1,0:T(8,128)S(1)}, f32[6,32,8,128]{3,2,1,0:T(8,128)S(1)}, f32[5,32,8,128]{3,2,1,0:T(8,128)S(1)}, f32[24,128]{1,0:T(8,128)S(1)}) custom-call(f32[3,8]{1,0:T(4,128)S(1)} %copy-done, f32[81,8,128]{2,1,0:T(8,128)S(1)} %get-tuple-element.25.own, f32[81,8,128]{2,1,0:T(8,128)S(1)} %collective-permute-done.mate), custom_call_target="tpu_custom_call" | custom-call | tf_op jit(solution)/shard_map/first_velocity/pallas_call | solution.py:764
  12.6 6.4 %all-to-all-done = f32[8,64,128]{2,1,0:T(8,128)S(1)} async-done(((f32[8,64,128]{2,1,0:T(8,128)}), f32[8,64,128]{2,1,0:T(8,128)S(1)}, u32[]{:S(2)}, u32[]{:S(2)}) %all-to-all-start) | async-done | bytes 262176 | tf_op jit(solution)/shard_map/all_to_all | solution.py:753
  19.0 0.0 collective-permute-start.2
  19.0 1.5 %collective-permute-done.2.swapped = f32[512,128]{1,0:T(8,128)S(1)} collective-permute-done((f32[512,128]{1,0:T(8,128)S(1)}, f32[512,128]{1,0:T(8,128)S(1)}, u32[]{:S(2)}, u32[]{:S(2)}) %collective-permute-start.2) | collective-permute-done | bytes 262176 | tf_op jit(solution)/shard_map/ppermute | solution.py:777
  20.5 1.9 %inner_substeps.1 = (f32[3,32,8,128]{3,2,1,0:T(8,128)S(1)}, f32[6,32,8,128]{3,2,1,0:T(8,128)S(1)}, f32[4,34,8,128]{3,2,1,0:T(8,128)S(1)}, f32[34,8,128]{2,1,0:T(...) custom-call(f32[512,128]{1,0:T(8,128)S(1)} %bitcast.5, ...), custom_call_target="tpu_custom_call", output_to_operand_aliasing={{0}: (3, {}), {1}: (4, {})} | custom-call | tf_op jit(solution)/shard_map/inner_substeps/pallas_call | solution.py:786
  22.5 0.0 collective-permute-done.1.border
  22.5 2.1 %outer_substeps.1 = (f32[3,32,8,128]{3,2,1,0:T(8,128)S(1)}, f32[6,32,8,128]{3,2,1,0:T(8,128)S(1)}, f32[5,32,8,128]{3,2,1,0:T(8,128)S(1)}, f32[4,34,8,128]{3,2,1,...) custom-call(f32[24,128]{1,0:T(8,128)S(1)} %get-tuple-element.26.mate, ...), custom_call_target="tpu_custom_call", output_to_operand_aliasing={{0}: (4, {}), {1}: (5, {}), {2}: (6, {}), {3}: (7, {}), {4}... | custom-call | tf_op jit(solution)/shard_map/outer_substeps/pallas_call | solution.py:798
  24.6 4.2 %all-to-all-start.1 = ((f32[16,16,128]{2,1,0:T(8,128)}), f32[16,16,128]{2,1,0:T(8,128)S(1)}, u32[]{:S(2)}, u32[]{:S(2)}) async-start(f32[16,16,128]{2,1,0:T(8,128)} %bitcast.2), calls=%async_computation.1 | async-start | bytes 262144 | tf_op jit(solution)/shard_map/all_to_all | solution.py:813
  28.8 1.9 %last_updates.1 = (f32[3,8,32,32]{3,2,1,0:T(8,128)}, f32[6,8,32,32]{3,2,1,0:T(8,128)}) custom-call(f32[3,32,8,128]{3,2,1,0:T(8,128)S(1)} %get-tuple-element.40.vel_all, f32[6,32,8,128]{3,2,1,0:T(8,128)S(1)} %get-tuple-element.41.stress_all, f32[5,32,8,128]{3,2,1,0:T(8,128)S(1)} %get-tuple-element.42.mats_all, f32[32,8,128]{2,1,0:T(8,128)S(1)} %get-tuple-element.43.loads_all), custom_call_target="tpu_custom_call" | custom-call | tf_op jit(solution)/shard_map/last_updates/pallas_call | solution.py:816
  30.7 6.1 %all-to-all-done.1 = f32[16,16,128]{2,1,0:T(8,128)S(1)} async-done(((f32[16,16,128]{2,1,0:T(8,128)}), f32[16,16,128]{2,1,0:T(8,128)S(1)}, u32[]{:S(2)}, u32[]{:S(2)}) %all-to-all-start.1) | async-done | bytes 131104 | tf_op jit(solution)/shard_map/all_to_all | solution.py:813
  36.8 0.9 %ocean_strips.1 = f32[4,2,32,128]{3,2,1,0:T(8,128)} custom-call(f32[256,128]{1,0:T(8,128)S(1)} %bitcast.6), custom_call_target="tpu_custom_call" | custom-call | tf_op jit(solution)/shard_map/ocean_strips/pallas_call | solution.py:826
Async XLA Ops:
  2.7 16.3 %all-to-all-start = ((f32[8,64,128]{2,1,0:T(8,128)}), f32[8,64,128]{2,1,0:T(8,128)S(1)}, u32[]{:S(2)}, u32[]{:S(2)}) async-start(f32[8,64,128]{2,1,0:T(8,128)} %bitcast), calls=%async_computation | async-start | bytes 524288 | tf_op jit(solution)/shard_map/all_to_all | solution.py:753
  10.0 1.7 %copy-start = (f32[3,8]{1,0:T(4,128)S(1)}, f32[3,8]{1,0:T(4,128)}, u32[]{:S(2)}) copy-start(f32[3,8]{1,0:T(4,128)} %table.1) | copy-start | bytes 292
  10.0 1.7 %collective-permute-start = (f32[81,8,128]{2,1,0:T(8,128)S(1)}, f32[81,8,128]{2,1,0:T(8,128)S(1)}, u32[]{:S(2)}, u32[]{:S(2)}) collective-permute-start(f32[81,8,128]{2,1,0:T(8,128)S(1)} %get-tuple-element.25.own), channel_id=1, source_target_pairs={{0,1},{1,0},{2,3},{3,2},{4,5},{5,4},{6,7},{7,6},{8,9},{9,8},{10,11... | collective-permute-start | bytes 995336 | tf_op jit(solution)/shard_map/ppermute | solution.py:762
  10.1 12.4 %collective-permute-start.1 = (f32[74,8,128]{2,1,0:T(8,128)S(1)}, f32[74,8,128]{2,1,0:T(8,128)S(1)}, u32[]{:S(2)}, u32[]{:S(2)}) collective-permute-start(f32[74,8,128]{2,1,0:T(8,128)S(1)} %get-tuple-element.27), channel_id=1, source_target_pairs={{1,2},{3,4},{5,6},{7,8},{9,10},{11,12},{13,14},{2,1},{4,3},{6,5},{... | collective-permute-start | bytes 909320 | tf_op jit(solution)/shard_map/ppermute | solution.py:761
  19.0 1.5 %collective-permute-start.2 = (f32[512,128]{1,0:T(8,128)S(1)}, f32[512,128]{1,0:T(8,128)S(1)}, u32[]{:S(2)}, u32[]{:S(2)}) collective-permute-start(f32[512,128]{1,0:T(8,128)S(1)} %bitcast.4), channel_id=1, source_target_pairs={{0,1},{1,0},{2,3},{3,2},{4,5},{5,4},{6,7},{7,6},{8,9},{9,8},{10,11... | collective-permute-start | bytes 786440 | tf_op jit(solution)/shard_map/ppermute | solution.py:777
  24.6 12.1 %all-to-all-start.1 = ((f32[16,16,128]{2,1,0:T(8,128)}), f32[16,16,128]{2,1,0:T(8,128)S(1)}, u32[]{:S(2)}, u32[]{:S(2)}) async-start(f32[16,16,128]{2,1,0:T(8,128)} %bitcast.2), calls=%async_computation.1 | async-start | bytes 262144 | tf_op jit(solution)/shard_map/all_to_all | solution.py:813

commit v21 on v20

--- a/solution.py
+++ b/solution.py
@@ -55,7 +55,7 @@
             lax.fori_loop(start, stop, run, 0)
 
 
-BATCH = 8
+BATCH = 4
 SLOTS = 16
 
 

time: 38 us -> 38.1 us (level)
  transfers between devices with their start and end apart: 5 -> 5, of which waited for: 4 -> 4; matrix products, arithmetic and copies ran while one was open for 0% -> 0% of each run, Pallas kernels for 12% -> 13%
where the time goes in v21:
time: 38.1 us; the launch traced here: 37.7 us
  waiting for transfers between devices  14.9 us (39%)
  starting transfers between devices  12.1 us (32%)
  Pallas kernels  10.1 us (27%)
  between operations  0.69 us (2%)
    all_to_all x1, starting transfers between devices, on_device(): lax.all_to_all(message.reshape(n // 2, 2 * plan.rows, LANES), 'map', spli...  7.26 us
    all_to_all x1, waiting for transfers between devices, on_device(): lax.all_to_all(message.reshape(n // 2, 2 * plan.rows, LANES), 'map', spli...  6.42 us
    all_to_all x1, waiting for transfers between devices, on_device(): lax.all_to_all(back.reshape(n, plan.back_rows, LANES), 'map', split_axis=...  5.96 us
    all_to_all x1, starting transfers between devices, on_device(): lax.all_to_all(back.reshape(n, plan.back_rows, LANES), 'map', split_axis=...  4.05 us
    pallas_call x1, Pallas kernels, on_device(): call(outer_kernel, 'outer_substeps', tuple((planes_of[k] for k in ('vel',...  2.13 us
    pallas_call x1, Pallas kernels, on_device(): call(inner_kernel, 'inner_substeps', tuple((planes_of[k] for k in ('vel',...  2.11 us
    pallas_call x1, Pallas kernels, on_device(): call(pack_kernel, 'pack', (shape(n * plan.rows, LANES), shape(10 * cells...  2.07 us
    pallas_call x1, Pallas kernels, on_device(): call(end_kernel, 'last_updates', (shape(*velocity.shape), shape(*stress.s...  1.97 us
  transfers between devices with their start and end apart: 5, of which 4 were waited for; matrix products, arithmetic and copies ran while one was open for 0% of the time, Pallas kernels for 13%

profile of v21, /device:TPU:0, one launch (start us, length us, event | category | flops | bytes accessed | tf_op | source)
XLA Modules:
  0.0 37.7 jit_solution(2339252584490977096)
XLA Ops:
  0.6 2.1 %pack.1 = (f32[512,128]{1,0:T(8,128)}, f32[81,8,128]{2,1,0:T(8,128)S(1)}, f32[74,8,128]{2,1,0:T(8,128)S(1)}) custom-call(f32[3,8,32,32]{3,2,1,0:T(8,128)} %vel_ref.1, f32[6,8,32,32]{3,2,1,0:T(8,128)} %stress_ref.1, s32[8,32,32]{2,1,0:T(8,128)} %zones_ref.1, f32[8,32]{1,0:T(8,128)} %slip_ref.1, f32[4,2,32,128]{3,2,1,0:T(8,128)} %ocean_ref.1, s32[2,128]{1,0:T(2,128)} %bathy_ref.1), custom_call_target="tpu_custom_call" | custom-call | tf_op jit(solution)/shard_map/pack/pallas_call | solution.py:732
  2.7 7.3 %all-to-all-start = ((f32[8,64,128]{2,1,0:T(8,128)}), f32[8,64,128]{2,1,0:T(8,128)S(1)}, u32[]{:S(2)}, u32[]{:S(2)}) async-start(f32[8,64,128]{2,1,0:T(8,128)} %bitcast), calls=%async_computation | async-start | bytes 524288 | tf_op jit(solution)/shard_map/all_to_all | solution.py:753
  10.0 0.0 copy-start
  10.0 0.1 collective-permute-start
  10.1 0.7 %collective-permute-start.1 = (f32[74,8,128]{2,1,0:T(8,128)S(1)}, f32[74,8,128]{2,1,0:T(8,128)S(1)}, u32[]{:S(2)}, u32[]{:S(2)}) collective-permute-start(f32[74,8,128]{2,1,0:T(8,128)S(1)} %get-tuple-element.27), channel_id=1, source_target_pairs={{1,2},{3,4},{5,6},{7,8},{9,10},{11,12},{13,14},{2,1},{4,3},{6,5},{... | collective-permute-start | bytes 909320 | tf_op jit(solution)/shard_map/ppermute | solution.py:761
  10.8 0.9 %collective-permute-done.mate = f32[81,8,128]{2,1,0:T(8,128)S(1)} collective-permute-done((f32[81,8,128]{2,1,0:T(8,128)S(1)}, f32[81,8,128]{2,1,0:T(8,128)S(1)}, u32[]{:S(2)}, u32[]{:S(2)}) %collective-permute-start) | collective-permute-done | bytes 331808 | tf_op jit(solution)/shard_map/ppermute | solution.py:762
  11.7 0.0 copy-done
  11.7 0.9 %first_velocity.1 = (f32[3,32,8,128]{3,2,1,0:T(8,128)S(1)}, f32[6,32,8,128]{3,2,1,0:T(8,128)S(1)}, f32[5,32,8,128]{3,2,1,0:T(8,128)S(1)}, f32[24,128]{1,0:T(8,128)S(1)}) custom-call(f32[3,8]{1,0:T(4,128)S(1)} %copy-done, f32[81,8,128]{2,1,0:T(8,128)S(1)} %get-tuple-element.25.own, f32[81,8,128]{2,1,0:T(8,128)S(1)} %collective-permute-done.mate), custom_call_target="tpu_custom_call" | custom-call | tf_op jit(solution)/shard_map/first_velocity/pallas_call | solution.py:764
  12.6 6.4 %all-to-all-done = f32[8,64,128]{2,1,0:T(8,128)S(1)} async-done(((f32[8,64,128]{2,1,0:T(8,128)}), f32[8,64,128]{2,1,0:T(8,128)S(1)}, u32[]{:S(2)}, u32[]{:S(2)}) %all-to-all-start) | async-done | bytes 262176 | tf_op jit(solution)/shard_map/all_to_all | solution.py:753
  19.0 0.0 collective-permute-start.2
  19.0 1.5 %collective-permute-done.2.swapped = f32[512,128]{1,0:T(8,128)S(1)} collective-permute-done((f32[512,128]{1,0:T(8,128)S(1)}, f32[512,128]{1,0:T(8,128)S(1)}, u32[]{:S(2)}, u32[]{:S(2)}) %collective-permute-start.2) | collective-permute-done | bytes 262176 | tf_op jit(solution)/shard_map/ppermute | solution.py:777
  20.5 2.1 %inner_substeps.1 = (f32[3,32,8,128]{3,2,1,0:T(8,128)S(1)}, f32[6,32,8,128]{3,2,1,0:T(8,128)S(1)}, f32[4,34,8,128]{3,2,1,0:T(8,128)S(1)}, f32[34,8,128]{2,1,0:T(...) custom-call(f32[512,128]{1,0:T(8,128)S(1)} %bitcast.5, ...), custom_call_target="tpu_custom_call", output_to_operand_aliasing={{0}: (3, {}), {1}: (4, {})} | custom-call | tf_op jit(solution)/shard_map/inner_substeps/pallas_call | solution.py:786
  22.7 0.0 collective-permute-done.1.border
  22.7 2.1 %outer_substeps.1 = (f32[3,32,8,128]{3,2,1,0:T(8,128)S(1)}, f32[6,32,8,128]{3,2,1,0:T(8,128)S(1)}, f32[5,32,8,128]{3,2,1,0:T(8,128)S(1)}, f32[4,34,8,128]{3,2,1,...) custom-call(f32[24,128]{1,0:T(8,128)S(1)} %get-tuple-element.26.mate, ...), custom_call_target="tpu_custom_call", output_to_operand_aliasing={{0}: (4, {}), {1}: (5, {}), {2}: (6, {}), {3}: (7, {}), {4}... | custom-call | tf_op jit(solution)/shard_map/outer_substeps/pallas_call | solution.py:798
  24.8 4.0 %all-to-all-start.1 = ((f32[16,16,128]{2,1,0:T(8,128)}), f32[16,16,128]{2,1,0:T(8,128)S(1)}, u32[]{:S(2)}, u32[]{:S(2)}) async-start(f32[16,16,128]{2,1,0:T(8,128)} %bitcast.2), calls=%async_computation.1 | async-start | bytes 262144 | tf_op jit(solution)/shard_map/all_to_all | solution.py:813
  28.8 2.0 %last_updates.1 = (f32[3,8,32,32]{3,2,1,0:T(8,128)}, f32[6,8,32,32]{3,2,1,0:T(8,128)}) custom-call(f32[3,32,8,128]{3,2,1,0:T(8,128)S(1)} %get-tuple-element.40.vel_all, f32[6,32,8,128]{3,2,1,0:T(8,128)S(1)} %get-tuple-element.41.stress_all, f32[5,32,8,128]{3,2,1,0:T(8,128)S(1)} %get-tuple-element.42.mats_all, f32[32,8,128]{2,1,0:T(8,128)S(1)} %get-tuple-element.43.loads_all), custom_call_target="tpu_custom_call" | custom-call | tf_op jit(solution)/shard_map/last_updates/pallas_call | solution.py:816
  30.8 6.0 %all-to-all-done.1 = f32[16,16,128]{2,1,0:T(8,128)S(1)} async-done(((f32[16,16,128]{2,1,0:T(8,128)}), f32[16,16,128]{2,1,0:T(8,128)S(1)}, u32[]{:S(2)}, u32[]{:S(2)}) %all-to-all-start.1) | async-done | bytes 131104 | tf_op jit(solution)/shard_map/all_to_all | solution.py:813
  36.8 0.9 %ocean_strips.1 = f32[4,2,32,128]{3,2,1,0:T(8,128)} custom-call(f32[256,128]{1,0:T(8,128)S(1)} %bitcast.6), custom_call_target="tpu_custom_call" | custom-call | tf_op jit(solution)/shard_map/ocean_strips/pallas_call | solution.py:826
Async XLA Ops:
  2.7 16.3 %all-to-all-start = ((f32[8,64,128]{2,1,0:T(8,128)}), f32[8,64,128]{2,1,0:T(8,128)S(1)}, u32[]{:S(2)}, u32[]{:S(2)}) async-start(f32[8,64,128]{2,1,0:T(8,128)} %bitcast), calls=%async_computation | async-start | bytes 524288 | tf_op jit(solution)/shard_map/all_to_all | solution.py:753
  10.0 1.7 %copy-start = (f32[3,8]{1,0:T(4,128)S(1)}, f32[3,8]{1,0:T(4,128)}, u32[]{:S(2)}) copy-start(f32[3,8]{1,0:T(4,128)} %table.1) | copy-start | bytes 292
  10.0 1.7 %collective-permute-start = (f32[81,8,128]{2,1,0:T(8,128)S(1)}, f32[81,8,128]{2,1,0:T(8,128)S(1)}, u32[]{:S(2)}, u32[]{:S(2)}) collective-permute-start(f32[81,8,128]{2,1,0:T(8,128)S(1)} %get-tuple-element.25.own), channel_id=1, source_target_pairs={{0,1},{1,0},{2,3},{3,2},{4,5},{5,4},{6,7},{7,6},{8,9},{9,8},{10,11... | collective-permute-start | bytes 995336 | tf_op jit(solution)/shard_map/ppermute | solution.py:762
  10.1 12.6 %collective-permute-start.1 = (f32[74,8,128]{2,1,0:T(8,128)S(1)}, f32[74,8,128]{2,1,0:T(8,128)S(1)}, u32[]{:S(2)}, u32[]{:S(2)}) collective-permute-start(f32[74,8,128]{2,1,0:T(8,128)S(1)} %get-tuple-element.27), channel_id=1, source_target_pairs={{1,2},{3,4},{5,6},{7,8},{9,10},{11,12},{13,14},{2,1},{4,3},{6,5},{... | collective-permute-start | bytes 909320 | tf_op jit(solution)/shard_map/ppermute | solution.py:761
  19.0 1.5 %collective-permute-start.2 = (f32[512,128]{1,0:T(8,128)S(1)}, f32[512,128]{1,0:T(8,128)S(1)}, u32[]{:S(2)}, u32[]{:S(2)}) collective-permute-start(f32[512,128]{1,0:T(8,128)S(1)} %bitcast.4), channel_id=1, source_target_pairs={{0,1},{1,0},{2,3},{3,2},{4,5},{5,4},{6,7},{7,6},{8,9},{9,8},{10,11... | collective-permute-start | bytes 786440 | tf_op jit(solution)/shard_map/ppermute | solution.py:777
  24.8 12.0 %all-to-all-start.1 = ((f32[16,16,128]{2,1,0:T(8,128)}), f32[16,16,128]{2,1,0:T(8,128)S(1)}, u32[]{:S(2)}, u32[]{:S(2)}) async-start(f32[16,16,128]{2,1,0:T(8,128)} %bitcast.2), calls=%async_computation.1 | async-start | bytes 262144 | tf_op jit(solution)/shard_map/all_to_all | solution.py:813

commit v22 on v20

--- a/solution.py
+++ b/solution.py
@@ -565,7 +565,7 @@
 
 def outer_kernel(
     plan, materials, border, water, bottom, vel_in, stress_in, mats_in, oc_in, loads_in,
-    vel, stress, mats, oc, loads, message, gather, rows, memory, sem,
+    vel, stress, mats, oc, loads, rows, gather, memory,
 ):
     sub, chunks, n, strips, cells = plan.sub, plan.chunks, plan.n, plan.strips, plan.cells
     near = cells - 1
@@ -601,8 +601,6 @@
                 return 2 * t + inset, 2 * t + inset + HALO
             last = 2 * HALO + 2 * cells - 2 * t - inset
             return last - HALO, last
-
-        copy = pltpu.make_async_copy(rows, message, sem)
 
         def send():
             for group in range(plan.own_groups):
@@ -621,10 +619,8 @@
                         rows[pl.ds(at, n, stride=plan.back_rows), :] = gather[
                             group, pl.ds(kc * plan.ny + yl, n, stride=strips), :
                         ]
-            copy.start()
 
         updates.run(spans, False, send)
-        copy.wait()
 
     for core in range(2):
         pl.when(odd == core)(functools.partial(side, core))
@@ -700,6 +696,9 @@
 
     def shape(*dims):
         return jax.ShapeDtypeStruct(dims, F32)
+
+    def in_vmem(*dims):
+        return pltpu.VMEM(dims, F32) if plan.unrolled else shape(*dims)
 
     def like(array):
         return jax.ShapeDtypeStruct(array.shape, array.dtype)
@@ -799,15 +798,13 @@
         outer_kernel,
         "outer_substeps",
         tuple(planes_of[k] for k in ("vel", "stress", "mats", "oc", "loads"))
-        + (shape(n * plan.back_rows, LANES),),
+        + (in_vmem(n * plan.back_rows, LANES),),
         [vmem] * 9,
         [
             pltpu.VMEM((plan.own_groups, lanes, LANES), F32),
-            pltpu.VMEM((n * plan.back_rows, LANES), F32),
             pltpu.VMEM((SLOTS * slot_rows(plan), lanes), F32),
-            pltpu.SemaphoreType.DMA,
         ],
-        outs=(vmem,) * 5 + (hbm,),
+        outs=(vmem,) * 6,
         input_output_aliases={4: 0, 5: 1, 6: 2, 7: 3, 8: 4},
     )(*(near(a) for a in (material_rows, other, water, bottom, vel, strs, mats, oc, loads)))
     returned = lax.all_to_all(

time: 38 us -> 38 us (level)
  no operation moved by 1% of the time
where the time goes in v22:
time: 38 us; the launch traced here: 37.7 us
  waiting for transfers between devices  15 us (39%)
  starting transfers between devices  12.2 us (32%)
  Pallas kernels  9.83 us (26%)
  between operations  0.68 us (2%)
    all_to_all x1, starting transfers between devices, on_device(): lax.all_to_all(message.reshape(n // 2, 2 * plan.rows, LANES), 'map', spli...  7.26 us
    all_to_all x1, waiting for transfers between devices, on_device(): lax.all_to_all(message.reshape(n // 2, 2 * plan.rows, LANES), 'map', spli...  6.42 us
    all_to_all x1, waiting for transfers between devices, on_device(): lax.all_to_all(back.reshape(n, plan.back_rows, LANES), 'map', split_axis=...  6.08 us
    all_to_all x1, starting transfers between devices, on_device(): lax.all_to_all(back.reshape(n, plan.back_rows, LANES), 'map', split_axis=...  4.16 us
    pallas_call x1, Pallas kernels, on_device(): call(outer_kernel, 'outer_substeps', tuple((planes_of[k] for k in ('vel',...  2.13 us
    pallas_call x1, Pallas kernels, on_device(): call(pack_kernel, 'pack', (shape(n * plan.rows, LANES), shape(10 * cells...  2.07 us
    pallas_call x1, Pallas kernels, on_device(): call(inner_kernel, 'inner_substeps', tuple((planes_of[k] for k in ('vel',...  1.95 us
    pallas_call x1, Pallas kernels, on_device(): call(end_kernel, 'last_updates', (shape(*velocity.shape), shape(*stress.s...  1.85 us
  transfers between devices with their start and end apart: 5, of which 4 were waited for; matrix products, arithmetic and copies ran while one was open for 0% of the time, Pallas kernels for 12%

profile of v22, /device:TPU:0, one launch (start us, length us, event | category | flops | bytes accessed | tf_op | source)
XLA Modules:
  0.0 37.7 jit_solution(7316619468908986690)
XLA Ops:
  0.6 2.1 %pack.1 = (f32[512,128]{1,0:T(8,128)}, f32[81,8,128]{2,1,0:T(8,128)S(1)}, f32[74,8,128]{2,1,0:T(8,128)S(1)}) custom-call(f32[3,8,32,32]{3,2,1,0:T(8,128)} %vel_ref.1, f32[6,8,32,32]{3,2,1,0:T(8,128)} %stress_ref.1, s32[8,32,32]{2,1,0:T(8,128)} %zones_ref.1, f32[8,32]{1,0:T(8,128)} %slip_ref.1, f32[4,2,32,128]{3,2,1,0:T(8,128)} %ocean_ref.1, s32[2,128]{1,0:T(2,128)} %bathy_ref.1), custom_call_target="tpu_custom_call" | custom-call | tf_op jit(solution)/shard_map/pack/pallas_call | solution.py:731
  2.7 7.3 %all-to-all-start = ((f32[8,64,128]{2,1,0:T(8,128)}), f32[8,64,128]{2,1,0:T(8,128)S(1)}, u32[]{:S(2)}, u32[]{:S(2)}) async-start(f32[8,64,128]{2,1,0:T(8,128)} %bitcast), calls=%async_computation | async-start | bytes 524288 | tf_op jit(solution)/shard_map/all_to_all | solution.py:752
  10.0 0.0 copy-start
  10.0 0.1 collective-permute-start
  10.1 0.7 %collective-permute-start.1 = (f32[74,8,128]{2,1,0:T(8,128)S(1)}, f32[74,8,128]{2,1,0:T(8,128)S(1)}, u32[]{:S(2)}, u32[]{:S(2)}) collective-permute-start(f32[74,8,128]{2,1,0:T(8,128)S(1)} %get-tuple-element.27), channel_id=1, source_target_pairs={{1,2},{3,4},{5,6},{7,8},{9,10},{11,12},{13,14},{2,1},{4,3},{6,5},{... | collective-permute-start | bytes 909320 | tf_op jit(solution)/shard_map/ppermute | solution.py:760
  10.8 0.9 %collective-permute-done.mate = f32[81,8,128]{2,1,0:T(8,128)S(1)} collective-permute-done((f32[81,8,128]{2,1,0:T(8,128)S(1)}, f32[81,8,128]{2,1,0:T(8,128)S(1)}, u32[]{:S(2)}, u32[]{:S(2)}) %collective-permute-start) | collective-permute-done | bytes 331808 | tf_op jit(solution)/shard_map/ppermute | solution.py:761
  11.7 0.0 copy-done
  11.7 0.9 %first_velocity.1 = (f32[3,32,8,128]{3,2,1,0:T(8,128)S(1)}, f32[6,32,8,128]{3,2,1,0:T(8,128)S(1)}, f32[5,32,8,128]{3,2,1,0:T(8,128)S(1)}, f32[24,128]{1,0:T(8,128)S(1)}) custom-call(f32[3,8]{1,0:T(4,128)S(1)} %copy-done, f32[81,8,128]{2,1,0:T(8,128)S(1)} %get-tuple-element.25.own, f32[81,8,128]{2,1,0:T(8,128)S(1)} %collective-permute-done.mate), custom_call_target="tpu_custom_call" | custom-call | tf_op jit(solution)/shard_map/first_velocity/pallas_call | solution.py:763
  12.6 6.4 %all-to-all-done = f32[8,64,128]{2,1,0:T(8,128)S(1)} async-done(((f32[8,64,128]{2,1,0:T(8,128)}), f32[8,64,128]{2,1,0:T(8,128)S(1)}, u32[]{:S(2)}, u32[]{:S(2)}) %all-to-all-start) | async-done | bytes 262176 | tf_op jit(solution)/shard_map/all_to_all | solution.py:752
  19.0 0.0 collective-permute-start.2
  19.0 1.5 %collective-permute-done.2.swapped = f32[512,128]{1,0:T(8,128)S(1)} collective-permute-done((f32[512,128]{1,0:T(8,128)S(1)}, f32[512,128]{1,0:T(8,128)S(1)}, u32[]{:S(2)}, u32[]{:S(2)}) %collective-permute-start.2) | collective-permute-done | bytes 262176 | tf_op jit(solution)/shard_map/ppermute | solution.py:776
  20.5 1.9 %inner_substeps.1 = (f32[3,32,8,128]{3,2,1,0:T(8,128)S(1)}, f32[6,32,8,128]{3,2,1,0:T(8,128)S(1)}, f32[4,34,8,128]{3,2,1,0:T(8,128)S(1)}, f32[34,8,128]{2,1,0:T(...) custom-call(f32[512,128]{1,0:T(8,128)S(1)} %bitcast.5, ...), custom_call_target="tpu_custom_call", output_to_operand_aliasing={{0}: (3, {}), {1}: (4, {})} | custom-call | tf_op jit(solution)/shard_map/inner_substeps/pallas_call | solution.py:785
  22.5 0.0 collective-permute-done.1.border
  22.5 2.1 %outer_substeps.1 = (f32[3,32,8,128]{3,2,1,0:T(8,128)S(1)}, f32[6,32,8,128]{3,2,1,0:T(8,128)S(1)}, f32[5,32,8,128]{3,2,1,0:T(8,128)S(1)}, f32[4,34,8,128]{3,2,1,...) custom-call(f32[24,128]{1,0:T(8,128)S(1)} %get-tuple-element.26.mate, ...), custom_call_target="tpu_custom_call", output_to_operand_aliasing={{0}: (4, {}), {1}: (5, {}), {2}: (6, {}), {3}: (7, {}), {4}... | custom-call | tf_op jit(solution)/shard_map/outer_substeps/pallas_call | solution.py:797
  24.6 4.2 %all-to-all-start.1 = ((f32[16,16,128]{2,1,0:T(8,128)}), f32[16,16,128]{2,1,0:T(8,128)S(1)}, u32[]{:S(2)}, u32[]{:S(2)}) async-start(f32[16,16,128]{2,1,0:T(8,128)} %bitcast.2), calls=%async_computation.1 | async-start | bytes 262144 | tf_op jit(solution)/shard_map/all_to_all | solution.py:810
  28.8 1.9 %last_updates.1 = (f32[3,8,32,32]{3,2,1,0:T(8,128)}, f32[6,8,32,32]{3,2,1,0:T(8,128)}) custom-call(f32[3,32,8,128]{3,2,1,0:T(8,128)S(1)} %get-tuple-element.40.vel_all, f32[6,32,8,128]{3,2,1,0:T(8,128)S(1)} %get-tuple-element.41.stress_all, f32[5,32,8,128]{3,2,1,0:T(8,128)S(1)} %get-tuple-element.42.mats_all, f32[32,8,128]{2,1,0:T(8,128)S(1)} %get-tuple-element.43.loads_all), custom_call_target="tpu_custom_call" | custom-call | tf_op jit(solution)/shard_map/last_updates/pallas_call | solution.py:813
  30.6 6.1 %all-to-all-done.1 = f32[16,16,128]{2,1,0:T(8,128)S(1)} async-done(((f32[16,16,128]{2,1,0:T(8,128)}), f32[16,16,128]{2,1,0:T(8,128)S(1)}, u32[]{:S(2)}, u32[]{:S(2)}) %all-to-all-start.1) | async-done | bytes 131104 | tf_op jit(solution)/shard_map/all_to_all | solution.py:810
  36.7 0.9 %ocean_strips.1 = f32[4,2,32,128]{3,2,1,0:T(8,128)} custom-call(f32[256,128]{1,0:T(8,128)S(1)} %bitcast.6), custom_call_target="tpu_custom_call" | custom-call | tf_op jit(solution)/shard_map/ocean_strips/pallas_call | solution.py:823
Async XLA Ops:
  2.7 16.3 %all-to-all-start = ((f32[8,64,128]{2,1,0:T(8,128)}), f32[8,64,128]{2,1,0:T(8,128)S(1)}, u32[]{:S(2)}, u32[]{:S(2)}) async-start(f32[8,64,128]{2,1,0:T(8,128)} %bitcast), calls=%async_computation | async-start | bytes 524288 | tf_op jit(solution)/shard_map/all_to_all | solution.py:752
  10.0 1.7 %copy-start = (f32[3,8]{1,0:T(4,128)S(1)}, f32[3,8]{1,0:T(4,128)}, u32[]{:S(2)}) copy-start(f32[3,8]{1,0:T(4,128)} %table.1) | copy-start | bytes 292
  10.0 1.7 %collective-permute-start = (f32[81,8,128]{2,1,0:T(8,128)S(1)}, f32[81,8,128]{2,1,0:T(8,128)S(1)}, u32[]{:S(2)}, u32[]{:S(2)}) collective-permute-start(f32[81,8,128]{2,1,0:T(8,128)S(1)} %get-tuple-element.25.own), channel_id=1, source_target_pairs={{0,1},{1,0},{2,3},{3,2},{4,5},{5,4},{6,7},{7,6},{8,9},{9,8},{10,11... | collective-permute-start | bytes 995336 | tf_op jit(solution)/shard_map/ppermute | solution.py:761
  10.1 12.4 %collective-permute-start.1 = (f32[74,8,128]{2,1,0:T(8,128)S(1)}, f32[74,8,128]{2,1,0:T(8,128)S(1)}, u32[]{:S(2)}, u32[]{:S(2)}) collective-permute-start(f32[74,8,128]{2,1,0:T(8,128)S(1)} %get-tuple-element.27), channel_id=1, source_target_pairs={{1,2},{3,4},{5,6},{7,8},{9,10},{11,12},{13,14},{2,1},{4,3},{6,5},{... | collective-permute-start | bytes 909320 | tf_op jit(solution)/shard_map/ppermute | solution.py:760
  19.0 1.5 %collective-permute-start.2 = (f32[512,128]{1,0:T(8,128)S(1)}, f32[512,128]{1,0:T(8,128)S(1)}, u32[]{:S(2)}, u32[]{:S(2)}) collective-permute-start(f32[512,128]{1,0:T(8,128)S(1)} %bitcast.4), channel_id=1, source_target_pairs={{0,1},{1,0},{2,3},{3,2},{4,5},{5,4},{6,7},{7,6},{8,9},{9,8},{10,11... | collective-permute-start | bytes 786440 | tf_op jit(solution)/shard_map/ppermute | solution.py:776
  24.6 12.1 %all-to-all-start.1 = ((f32[16,16,128]{2,1,0:T(8,128)}), f32[16,16,128]{2,1,0:T(8,128)S(1)}, u32[]{:S(2)}, u32[]{:S(2)}) async-start(f32[16,16,128]{2,1,0:T(8,128)} %bitcast.2), calls=%async_computation.1 | async-start | bytes 262144 | tf_op jit(solution)/shard_map/all_to_all | solution.py:810

commit v23 on v22

--- a/solution.py
+++ b/solution.py
@@ -396,10 +396,10 @@
 
 
 class Updates:
-    def __init__(self, plan, sh, vel, stress, mats, oc, water, bottom, loads):
+    def __init__(self, plan, sh, vel, stress, mats, oc, water, bottom):
         self.plan, self.sh = plan, sh
         self.vel, self.stress, self.mats = vel, stress, mats
-        self.oc, self.water, self.bottom, self.loads = oc, water, bottom, loads
+        self.oc, self.water, self.bottom = oc, water, bottom
 
     def flow_x(self, j, count):
         oc = self.oc
@@ -439,9 +439,6 @@
     def load(self, j, count):
         at = pl.ds(j + 1, count)
         return self.sh.on_top(self.bottom[at] * self.oc[0, at])
-
-    def keep(self, j, count):
-        self.loads[pl.ds(j, count)] = self.load(j, count)
 
     def add_load(self, j, count):
         at = pl.ds(j, count)
@@ -487,11 +484,10 @@
             planes(t + 1, 1, functools.partial(self.press, floor=self.floor))
         if send is not None:
             send()
-        planes(STEPS - 1, 1, self.keep)
 
 
 def inner_kernel(
-    plan, arrived, swapped, mats, vel_in, stress_in, vel, stress, oc, water, bottom, loads,
+    plan, arrived, swapped, mats, vel_in, stress_in, vel, stress, oc, water, bottom,
     gather, depths, memory,
 ):
     sub, chunks, n, strips = plan.sub, plan.chunks, plan.n, plan.strips
@@ -559,13 +555,13 @@
 
     if not plan.unrolled:
         plan.planes(HALO, HALO + 2 * cells, bring_in)
-    updates = Updates(plan, sh, vel, stress, mats, oc, water, bottom, loads)
+    updates = Updates(plan, sh, vel, stress, mats, oc, water, bottom)
     updates.run(lambda t, inset: (HALO + 2 * t + inset, HALO + 2 * cells - 2 * t - inset), True)
 
 
 def outer_kernel(
-    plan, materials, border, water, bottom, vel_in, stress_in, mats_in, oc_in, loads_in,
-    vel, stress, mats, oc, loads, rows, gather, memory,
+    plan, materials, border, water, bottom, vel_in, stress_in, mats_in, oc_in,
+    vel, stress, mats, oc, rows, gather, memory,
 ):
     sub, chunks, n, strips, cells = plan.sub, plan.chunks, plan.n, plan.strips, plan.cells
     near = cells - 1
@@ -573,10 +569,10 @@
     odd = odd_device()
     if not plan.unrolled:
         for here, there in (
-            (vel, vel_in), (stress, stress_in), (mats, mats_in), (oc, oc_in), (loads, loads_in)
+            (vel, vel_in), (stress, stress_in), (mats, mats_in), (oc, oc_in)
         ):
             here[...] = there[...]
-    updates = Updates(plan, sh, vel, stress, mats, oc, water, bottom, loads)
+    updates = Updates(plan, sh, vel, stress, mats, oc, water, bottom)
 
     def material(c, z):
         row = materials[pl.ds(c * ZONES + z, 1), :]
@@ -626,13 +622,17 @@
         pl.when(odd == core)(functools.partial(side, core))
 
 
-def end_kernel(plan, vel_all, stress_all, mats_all, loads_all, vel_out, stress_out, vel, stress):
+def end_kernel(
+    plan, vel_all, stress_all, mats_all, oc_all, bottom_all, vel_out, stress_out, vel, stress
+):
     cells, sub, chunks, ny = plan.cells, plan.sub, plan.chunks, plan.ny
     sh = Shifts(plan)
     first, last = 2 * (STEPS - 1), plan.width - 2 * (STEPS - 1)
     window = pl.ds(cells * odd_device(), plan.width)
     vel_in, stress_in = vel_all.at[:, window], stress_all.at[:, window]
-    mats, loads = mats_all.at[:, window], loads_all.at[window]
+    mats = mats_all.at[:, window]
+    window = pl.ds(cells * odd_device(), plan.width + 2)
+    pressure, bottom = oc_all.at[0, window], bottom_all.at[window]
 
     def put(out, f, x, count, planes):
         for kc in range(chunks):
@@ -648,7 +648,9 @@
         at = pl.ds(j, count)
         ax, ay, az = acceleration(sh, stress, j, count)
         b = mats[BUOY, at]
-        for f, a in enumerate((ax, ay, az + loads[at])):
+        wet = pl.ds(j + 1, count)
+        load = sh.on_top(bottom[wet] * pressure[wet])
+        for f, a in enumerate((ax, ay, az + load)):
             vel[f, at] = vel_in[f, at] + b * a
 
     def finish(x, count):
@@ -780,12 +782,11 @@
         "mats": shape(5, columns, sub, lanes),
         "oc": shape(4, columns + 2, sub, lanes),
         "mask": shape(columns + 2, sub, lanes),
-        "loads": shape(columns, sub, lanes),
     }
-    vel, strs, oc, water, bottom, loads = call(
+    vel, strs, oc, water, bottom = call(
         inner_kernel,
         "inner_substeps",
-        tuple(planes_of[k] for k in ("vel", "stress", "oc", "mask", "mask", "loads")),
+        tuple(planes_of[k] for k in ("vel", "stress", "oc", "mask", "mask")),
         [vmem] * 5,
         [
             pltpu.VMEM((lanes, LANES), F32),
@@ -794,19 +795,19 @@
         ],
         input_output_aliases={3: 0, 4: 1},
     )(*(near(a) for a in (arrived, swapped, mats, vel, strs)))
-    vel, strs, mats, oc, loads, back = call(
+    vel, strs, mats, oc, back = call(
         outer_kernel,
         "outer_substeps",
-        tuple(planes_of[k] for k in ("vel", "stress", "mats", "oc", "loads"))
+        tuple(planes_of[k] for k in ("vel", "stress", "mats", "oc"))
         + (in_vmem(n * plan.back_rows, LANES),),
-        [vmem] * 9,
+        [vmem] * 8,
         [
             pltpu.VMEM((plan.own_groups, lanes, LANES), F32),
             pltpu.VMEM((SLOTS * slot_rows(plan), lanes), F32),
         ],
-        outs=(vmem,) * 6,
-        input_output_aliases={4: 0, 5: 1, 6: 2, 7: 3, 8: 4},
-    )(*(near(a) for a in (material_rows, other, water, bottom, vel, strs, mats, oc, loads)))
+        outs=(vmem,) * 5,
+        input_output_aliases={4: 0, 5: 1, 6: 2, 7: 3},
+    )(*(near(a) for a in (material_rows, other, water, bottom, vel, strs, mats, oc)))
     returned = lax.all_to_all(
         back.reshape(n, plan.back_rows, LANES), "map", split_axis=0, concat_axis=0, tiled=True
     ).reshape(n * plan.back_rows, LANES)
@@ -814,12 +815,12 @@
         end_kernel,
         "last_updates",
         (shape(*velocity.shape), shape(*stress.shape)),
-        [vmem] * 4,
+        [vmem] * 5,
         [
             pltpu.VMEM((3, width, sub, lanes), F32),
             pltpu.VMEM((6, width, sub, lanes), F32),
         ],
-    )(vel, strs, mats, loads)
+    )(vel, strs, mats, oc, bottom)
     new_ocean = call(
         unpack_kernel,
         "ocean_strips",

time: 38 us -> 37.9 us (level)
  transfers between devices with their start and end apart: 5 -> 5, of which waited for: 4 -> 4; matrix products, arithmetic and copies ran while one was open for 0% -> 0% of each run, Pallas kernels for 12% -> 13%
where the time goes in v23:
time: 37.9 us; the launch traced here: 37.6 us
  waiting for transfers between devices  14.8 us (39%)
  starting transfers between devices  12.3 us (32%)
  Pallas kernels  9.8 us (26%)
  between operations  0.69 us (2%)
    all_to_all x1, starting transfers between devices, on_device(): lax.all_to_all(message.reshape(n // 2, 2 * plan.rows, LANES), 'map', spli...  7.26 us
    all_to_all x1, waiting for transfers between devices, on_device(): lax.all_to_all(message.reshape(n // 2, 2 * plan.rows, LANES), 'map', spli...  6.42 us
    all_to_all x1, waiting for transfers between devices, on_device(): lax.all_to_all(back.reshape(n, plan.back_rows, LANES), 'map', split_axis=...  5.94 us
    all_to_all x1, starting transfers between devices, on_device(): lax.all_to_all(back.reshape(n, plan.back_rows, LANES), 'map', split_axis=...  4.25 us
    pallas_call x1, Pallas kernels, on_device(): call(pack_kernel, 'pack', (shape(n * plan.rows, LANES), shape(10 * cells...  2.07 us
    pallas_call x1, Pallas kernels, on_device(): call(outer_kernel, 'outer_substeps', tuple((planes_of[k] for k in ('vel',...  2.04 us
    pallas_call x1, Pallas kernels, on_device(): call(end_kernel, 'last_updates', (shape(*velocity.shape), shape(*stress.s...  2 us
    pallas_call x1, Pallas kernels, on_device(): call(inner_kernel, 'inner_substeps', tuple((planes_of[k] for k in ('vel',...  1.87 us
  transfers between devices with their start and end apart: 5, of which 4 were waited for; matrix products, arithmetic and copies ran while one was open for 0% of the time, Pallas kernels for 13%

profile of v23, /device:TPU:0, one launch (start us, length us, event | category | flops | bytes accessed | tf_op | source)
XLA Modules:
  0.0 37.6 jit_solution(6044318818504370769)
XLA Ops:
  0.6 2.1 %pack.1 = (f32[512,128]{1,0:T(8,128)}, f32[81,8,128]{2,1,0:T(8,128)S(1)}, f32[74,8,128]{2,1,0:T(8,128)S(1)}) custom-call(f32[3,8,32,32]{3,2,1,0:T(8,128)} %vel_ref.1, f32[6,8,32,32]{3,2,1,0:T(8,128)} %stress_ref.1, s32[8,32,32]{2,1,0:T(8,128)} %zones_ref.1, f32[8,32]{1,0:T(8,128)} %slip_ref.1, f32[4,2,32,128]{3,2,1,0:T(8,128)} %ocean_ref.1, s32[2,128]{1,0:T(2,128)} %bathy_ref.1), custom_call_target="tpu_custom_call" | custom-call | tf_op jit(solution)/shard_map/pack/pallas_call | solution.py:733
  2.7 7.3 %all-to-all-start = ((f32[8,64,128]{2,1,0:T(8,128)}), f32[8,64,128]{2,1,0:T(8,128)S(1)}, u32[]{:S(2)}, u32[]{:S(2)}) async-start(f32[8,64,128]{2,1,0:T(8,128)} %bitcast), calls=%async_computation | async-start | bytes 524288 | tf_op jit(solution)/shard_map/all_to_all | solution.py:754
  10.0 0.0 copy-start
  10.0 0.1 collective-permute-start
  10.1 0.7 %collective-permute-start.1 = (f32[74,8,128]{2,1,0:T(8,128)S(1)}, f32[74,8,128]{2,1,0:T(8,128)S(1)}, u32[]{:S(2)}, u32[]{:S(2)}) collective-permute-start(f32[74,8,128]{2,1,0:T(8,128)S(1)} %get-tuple-element.26), channel_id=1, source_target_pairs={{1,2},{3,4},{5,6},{7,8},{9,10},{11,12},{13,14},{2,1},{4,3},{6,5},{... | collective-permute-start | bytes 909320 | tf_op jit(solution)/shard_map/ppermute | solution.py:762
  10.8 0.9 %collective-permute-done.mate = f32[81,8,128]{2,1,0:T(8,128)S(1)} collective-permute-done((f32[81,8,128]{2,1,0:T(8,128)S(1)}, f32[81,8,128]{2,1,0:T(8,128)S(1)}, u32[]{:S(2)}, u32[]{:S(2)}) %collective-permute-start) | collective-permute-done | bytes 331808 | tf_op jit(solution)/shard_map/ppermute | solution.py:763
  11.7 0.0 copy-done
  11.7 0.9 %first_velocity.1 = (f32[3,32,8,128]{3,2,1,0:T(8,128)S(1)}, f32[6,32,8,128]{3,2,1,0:T(8,128)S(1)}, f32[5,32,8,128]{3,2,1,0:T(8,128)S(1)}, f32[24,128]{1,0:T(8,128)S(1)}) custom-call(f32[3,8]{1,0:T(4,128)S(1)} %copy-done, f32[81,8,128]{2,1,0:T(8,128)S(1)} %get-tuple-element.24.own, f32[81,8,128]{2,1,0:T(8,128)S(1)} %collective-permute-done.mate), custom_call_target="tpu_custom_call" | custom-call | tf_op jit(solution)/shard_map/first_velocity/pallas_call | solution.py:765
  12.6 6.4 %all-to-all-done = f32[8,64,128]{2,1,0:T(8,128)S(1)} async-done(((f32[8,64,128]{2,1,0:T(8,128)}), f32[8,64,128]{2,1,0:T(8,128)S(1)}, u32[]{:S(2)}, u32[]{:S(2)}) %all-to-all-start) | async-done | bytes 262176 | tf_op jit(solution)/shard_map/all_to_all | solution.py:754
  19.0 0.0 collective-permute-start.2
  19.0 1.5 %collective-permute-done.2.swapped = f32[512,128]{1,0:T(8,128)S(1)} collective-permute-done((f32[512,128]{1,0:T(8,128)S(1)}, f32[512,128]{1,0:T(8,128)S(1)}, u32[]{:S(2)}, u32[]{:S(2)}) %collective-permute-start.2) | collective-permute-done | bytes 262176 | tf_op jit(solution)/shard_map/ppermute | solution.py:778
  20.5 1.9 %inner_substeps.1 = (f32[3,32,8,128]{3,2,1,0:T(8,128)S(1)}, f32[6,32,8,128]{3,2,1,0:T(8,128)S(1)}, f32[4,34,8,128]{3,2,1,0:T(8,128)S(1)}, f32[34,8,128]{2,1,0:T(8,128)S(1)}, f32[34,8,128]{2,1,0:T(8,128)S(1)}) custom-call(f32[512,128]{1,0:T(8,128)S(1)} %bitcast.5, ...), custom_call_target="tpu_custom_call", output_to_operand_aliasing={{0}: (3, {}), {1}: (4, {})} | custom-call | tf_op jit(solution)/shard_map/inner_substeps/pallas_call | solution.py:786
  22.4 0.0 collective-permute-done.1.border
  22.4 2.0 %outer_substeps.1 = (f32[3,32,8,128]{3,2,1,0:T(8,128)S(1)}, f32[6,32,8,128]{3,2,1,0:T(8,128)S(1)}, f32[5,32,8,128]{3,2,1,0:T(8,128)S(1)}, f32[4,34,8,128]{3,2,1,0:T(8,128)S(1)}, f32[256,128]{1,0:T(8,128)}) custom-call(f32[24,128]{1,0:T(8,128)S(1)} %get-tuple-element.25.materials, ...), custom_call_target="tpu_custom_call", output_to_operand_aliasing={{0}: (4, {}), {1}: (5, {}), {2}: (6, {}), {3}: (7, {})} | custom-call | tf_op jit(solution)/shard_map/outer_substeps/pallas_call | solution.py:798
  24.5 4.2 %all-to-all-start.1 = ((f32[16,16,128]{2,1,0:T(8,128)}), f32[16,16,128]{2,1,0:T(8,128)S(1)}, u32[]{:S(2)}, u32[]{:S(2)}) async-start(f32[16,16,128]{2,1,0:T(8,128)} %bitcast.2), calls=%async_computation.1 | async-start | bytes 262144 | tf_op jit(solution)/shard_map/all_to_all | solution.py:811
  28.7 2.0 %last_updates.1 = (f32[3,8,32,32]{3,2,1,0:T(8,128)}, f32[6,8,32,32]{3,2,1,0:T(8,128)}) custom-call(f32[3,32,8,128]{3,2,1,0:T(8,128)S(1)} %get-tuple-element.38.vel_all, f32[6,32,8,128]{3,2,1,0:T(8,128)S(1)} %get-tuple-element.39.stress_all, f32[5,32,8,128]{3,2,1,0:T(8,128)S(1)} %get-tuple-element.40.mats_all, ...), custom_call_target="tpu_custom_call" | custom-call | tf_op jit(solution)/shard_map/last_updates/pallas_call | solution.py:814
  30.7 5.9 %all-to-all-done.1 = f32[16,16,128]{2,1,0:T(8,128)S(1)} async-done(((f32[16,16,128]{2,1,0:T(8,128)}), f32[16,16,128]{2,1,0:T(8,128)S(1)}, u32[]{:S(2)}, u32[]{:S(2)}) %all-to-all-start.1) | async-done | bytes 131104 | tf_op jit(solution)/shard_map/all_to_all | solution.py:811
  36.7 0.9 %ocean_strips.1 = f32[4,2,32,128]{3,2,1,0:T(8,128)} custom-call(f32[256,128]{1,0:T(8,128)S(1)} %bitcast.6), custom_call_target="tpu_custom_call" | custom-call | tf_op jit(solution)/shard_map/ocean_strips/pallas_call | solution.py:824
Async XLA Ops:
  2.7 16.3 %all-to-all-start = ((f32[8,64,128]{2,1,0:T(8,128)}), f32[8,64,128]{2,1,0:T(8,128)S(1)}, u32[]{:S(2)}, u32[]{:S(2)}) async-start(f32[8,64,128]{2,1,0:T(8,128)} %bitcast), calls=%async_computation | async-start | bytes 524288 | tf_op jit(solution)/shard_map/all_to_all | solution.py:754
  10.0 1.7 %copy-start = (f32[3,8]{1,0:T(4,128)S(1)}, f32[3,8]{1,0:T(4,128)}, u32[]{:S(2)}) copy-start(f32[3,8]{1,0:T(4,128)} %table.1) | copy-start | bytes 292
  10.0 1.7 %collective-permute-start = (f32[81,8,128]{2,1,0:T(8,128)S(1)}, f32[81,8,128]{2,1,0:T(8,128)S(1)}, u32[]{:S(2)}, u32[]{:S(2)}) collective-permute-start(f32[81,8,128]{2,1,0:T(8,128)S(1)} %get-tuple-element.24.own), channel_id=1, source_target_pairs={{0,1},{1,0},{2,3},{3,2},{4,5},{5,4},{6,7},{7,6},{8,9},{9,8},{10,11... | collective-permute-start | bytes 995336 | tf_op jit(solution)/shard_map/ppermute | solution.py:763
  10.1 12.4 %collective-permute-start.1 = (f32[74,8,128]{2,1,0:T(8,128)S(1)}, f32[74,8,128]{2,1,0:T(8,128)S(1)}, u32[]{:S(2)}, u32[]{:S(2)}) collective-permute-start(f32[74,8,128]{2,1,0:T(8,128)S(1)} %get-tuple-element.26), channel_id=1, source_target_pairs={{1,2},{3,4},{5,6},{7,8},{9,10},{11,12},{13,14},{2,1},{4,3},{6,5},{... | collective-permute-start | bytes 909320 | tf_op jit(solution)/shard_map/ppermute | solution.py:762
  19.0 1.5 %collective-permute-start.2 = (f32[512,128]{1,0:T(8,128)S(1)}, f32[512,128]{1,0:T(8,128)S(1)}, u32[]{:S(2)}, u32[]{:S(2)}) collective-permute-start(f32[512,128]{1,0:T(8,128)S(1)} %bitcast.4), channel_id=1, source_target_pairs={{0,1},{1,0},{2,3},{3,2},{4,5},{5,4},{6,7},{7,6},{8,9},{9,8},{10,11... | collective-permute-start | bytes 786440 | tf_op jit(solution)/shard_map/ppermute | solution.py:778
  24.5 12.2 %all-to-all-start.1 = ((f32[16,16,128]{2,1,0:T(8,128)}), f32[16,16,128]{2,1,0:T(8,128)S(1)}, u32[]{:S(2)}, u32[]{:S(2)}) async-start(f32[16,16,128]{2,1,0:T(8,128)} %bitcast.2), calls=%async_computation.1 | async-start | bytes 262144 | tf_op jit(solution)/shard_map/all_to_all | solution.py:811

commit v24 on v23

--- a/solution.py
+++ b/solution.py
@@ -126,15 +126,12 @@
             grouped[pl.ds(pad + kc * strips + yl, count, stride=lead), :] = place(
                 by_x, [kc] * chunks, block
             )
-    for d in range(n):
-        start = (d * plan.own_groups + (d % 2) * plan.halo_groups) * lead
-        message[d * rows : (d + 1) * rows, :] = grouped[start : start + rows, :]
     pairs = n // 2
     lane = lax.broadcasted_iota(jnp.int32, (pairs, LANES), 1)
     blank = jnp.zeros((1, LANES), F32)
+    slots = {}
     for odd in range(2):
         slot = (odd * (chunks - 1) * 4 + 2) * sub
-        group = odd * (sent - 1)
         for yl in range(strips):
             if odd:
                 column = turned[yl, pl.ds(2 * cells + HALO, pairs - 1, stride=2 * cells), :]
@@ -144,15 +141,26 @@
                 column = jnp.concatenate([blank, column], axis=0)
             deep = extra[pl.ds(odd * strips + yl, pairs, stride=2 * strips), :]
             for kc in range(chunks):
-                at = odd * rows + group * lead + kc * strips + yl
-                old = message[pl.ds(at, pairs, stride=2 * rows), :]
                 edge = pltpu.roll(column, (slot - kc * block) % LANES, 1)
                 floor = pltpu.roll(deep, (slot + sub - kc * sub) % LANES, 1)
-                new = jnp.where((lane >= slot) & (lane < slot + sub), edge, old)
-                new = jnp.where((lane >= slot + sub) & (lane < slot + 2 * sub), floor, new)
-                message[pl.ds(at, pairs, stride=2 * rows), :] = new
-    out = pltpu.make_async_copy(message, message_out, sems.at[6])
-    out.start()
+                slots[odd, kc, yl] = jnp.where(lane < slot + sub, edge, floor)
+    outs = []
+    for part in range(2):
+        for d in range(part * pairs, (part + 1) * pairs):
+            start = (d * plan.own_groups + (d % 2) * plan.halo_groups) * lead
+            message[d * rows : (d + 1) * rows, :] = grouped[start : start + rows, :]
+        some = pl.ds(part * pairs * rows, pairs * rows)
+        mine = slice(part * pairs // 2, (part + 1) * pairs // 2)
+        for (odd, kc, yl), new in slots.items():
+            slot = (odd * (chunks - 1) * 4 + 2) * sub
+            at = part * pairs * rows + odd * rows + odd * (sent - 1) * lead + kc * strips + yl
+            to = pl.ds(at, pairs // 2, stride=2 * rows)
+            inside = (lane[mine] >= slot) & (lane[mine] < slot + 2 * sub)
+            message[to, :] = jnp.where(inside, new[mine], message[to, :])
+        outs.append(
+            pltpu.make_async_copy(message.at[some], message_out.at[some], sems.at[6 + part])
+        )
+        outs[-1].start()
 
     for copy in copies[2:]:
         copy.wait()
@@ -185,7 +193,8 @@
     for i, f in enumerate((SXX, SXY, SXZ)):
         border[10 * near + i] = crust[(3 + f) * cells + near * (1 - odd)]
     border[10 * near + 3] = fault
-    out.wait()
+    for out in outs:
+        out.wait()
 
 
 class Shifts:
@@ -346,6 +355,7 @@
     def read(f):
         return ref[pl.ds(f * fields + x, count)]
 
+    mats[FLOOR, to] = sh.seafloor(read(VZ))
     for f in range(3):
         vel[f, to] = read(f)
     for f in range(6):
@@ -357,7 +367,6 @@
         values = [jnp.where(here, material(c, z), values[c]) for c in range(3)]
     for c in range(3):
         mats[c, to] = values[c] * HALF
-    mats[FLOOR, to] = sh.seafloor(read(VZ))
     for i in range(count):
         slip = ref[ref.shape[0] - 1, pl.ds(first + x + i, 1), :]
         slip = jnp.broadcast_to(slip, (plan.sub, plan.lanes))
@@ -747,7 +756,7 @@
             ),
             pltpu.VMEM((n * plan.strips, LANES), F32),
             pltpu.VMEM((n * plan.rows, LANES), F32),
-            pltpu.SemaphoreType.DMA((7,)),
+            pltpu.SemaphoreType.DMA((8,)),
         ],
         outs=(hbm, vmem, vmem),
     )(*(pinned(a) for a in (velocity, stress, zones, slip, ocean, bathy)))

time: 37.9 us -> 37.9 us (level)
  no operation moved by 1% of the time
where the time goes in v24:
time: 37.9 us; the launch traced here: 37.6 us
  waiting for transfers between devices  14.8 us (39%)
  starting transfers between devices  12.3 us (32%)
  Pallas kernels  9.77 us (26%)
  between operations  0.69 us (2%)
    all_to_all x1, starting transfers between devices, on_device(): lax.all_to_all(message.reshape(n // 2, 2 * plan.rows, LANES), 'map', spli...  7.26 us
    all_to_all x1, waiting for transfers between devices, on_device(): lax.all_to_all(message.reshape(n // 2, 2 * plan.rows, LANES), 'map', spli...  6.42 us
    all_to_all x1, waiting for transfers between devices, on_device(): lax.all_to_all(back.reshape(n, plan.back_rows, LANES), 'map', split_axis=...  5.94 us
    all_to_all x1, starting transfers between devices, on_device(): lax.all_to_all(back.reshape(n, plan.back_rows, LANES), 'map', split_axis=...  4.25 us
    pallas_call x1, Pallas kernels, on_device(): call(outer_kernel, 'outer_substeps', tuple((planes_of[k] for k in ('vel',...  2.04 us
    pallas_call x1, Pallas kernels, on_device(): call(pack_kernel, 'pack', (shape(n * plan.rows, LANES), shape(10 * cells...  2.04 us
    pallas_call x1, Pallas kernels, on_device(): call(end_kernel, 'last_updates', (shape(*velocity.shape), shape(*stress.s...  2 us
    pallas_call x1, Pallas kernels, on_device(): call(inner_kernel, 'inner_substeps', tuple((planes_of[k] for k in ('vel',...  1.87 us
  transfers between devices with their start and end apart: 5, of which 4 were waited for; matrix products, arithmetic and copies ran while one was open for 0% of the time, Pallas kernels for 13%

profile of v24, /device:TPU:0, one launch (start us, length us, event | category | flops | bytes accessed | tf_op | source)
XLA Modules:
  0.0 37.6 jit_solution(15434191449431054404)
XLA Ops:
  0.6 2.0 %pack.1 = (f32[512,128]{1,0:T(8,128)}, f32[81,8,128]{2,1,0:T(8,128)S(1)}, f32[74,8,128]{2,1,0:T(8,128)S(1)}) custom-call(f32[3,8,32,32]{3,2,1,0:T(8,128)} %vel_ref.1, f32[6,8,32,32]{3,2,1,0:T(8,128)} %stress_ref.1, s32[8,32,32]{2,1,0:T(8,128)} %zones_ref.1, f32[8,32]{1,0:T(8,128)} %slip_ref.1, f32[4,2,32,128]{3,2,1,0:T(8,128)} %ocean_ref.1, s32[2,128]{1,0:T(2,128)} %bathy_ref.1), custom_call_target="tpu_custom_call" | custom-call | tf_op jit(solution)/shard_map/pack/pallas_call | solution.py:742
  2.7 7.3 %all-to-all-start = ((f32[8,64,128]{2,1,0:T(8,128)}), f32[8,64,128]{2,1,0:T(8,128)S(1)}, u32[]{:S(2)}, u32[]{:S(2)}) async-start(f32[8,64,128]{2,1,0:T(8,128)} %bitcast), calls=%async_computation | async-start | bytes 524288 | tf_op jit(solution)/shard_map/all_to_all | solution.py:763
  9.9 0.0 copy-start
  9.9 0.1 collective-permute-start
  10.0 0.7 %collective-permute-start.1 = (f32[74,8,128]{2,1,0:T(8,128)S(1)}, f32[74,8,128]{2,1,0:T(8,128)S(1)}, u32[]{:S(2)}, u32[]{:S(2)}) collective-permute-start(f32[74,8,128]{2,1,0:T(8,128)S(1)} %get-tuple-element.26), channel_id=1, source_target_pairs={{1,2},{3,4},{5,6},{7,8},{9,10},{11,12},{13,14},{2,1},{4,3},{6,5},{... | collective-permute-start | bytes 909320 | tf_op jit(solution)/shard_map/ppermute | solution.py:771
  10.7 0.9 %collective-permute-done.mate = f32[81,8,128]{2,1,0:T(8,128)S(1)} collective-permute-done((f32[81,8,128]{2,1,0:T(8,128)S(1)}, f32[81,8,128]{2,1,0:T(8,128)S(1)}, u32[]{:S(2)}, u32[]{:S(2)}) %collective-permute-start) | collective-permute-done | bytes 331808 | tf_op jit(solution)/shard_map/ppermute | solution.py:772
  11.6 0.0 copy-done
  11.6 0.9 %first_velocity.1 = (f32[3,32,8,128]{3,2,1,0:T(8,128)S(1)}, f32[6,32,8,128]{3,2,1,0:T(8,128)S(1)}, f32[5,32,8,128]{3,2,1,0:T(8,128)S(1)}, f32[24,128]{1,0:T(8,128)S(1)}) custom-call(f32[3,8]{1,0:T(4,128)S(1)} %copy-done, f32[81,8,128]{2,1,0:T(8,128)S(1)} %get-tuple-element.24.own, f32[81,8,128]{2,1,0:T(8,128)S(1)} %collective-permute-done.mate), custom_call_target="tpu_custom_call" | custom-call | tf_op jit(solution)/shard_map/first_velocity/pallas_call | solution.py:774
  12.5 6.4 %all-to-all-done = f32[8,64,128]{2,1,0:T(8,128)S(1)} async-done(((f32[8,64,128]{2,1,0:T(8,128)}), f32[8,64,128]{2,1,0:T(8,128)S(1)}, u32[]{:S(2)}, u32[]{:S(2)}) %all-to-all-start) | async-done | bytes 262176 | tf_op jit(solution)/shard_map/all_to_all | solution.py:763
  19.0 0.0 collective-permute-start.2
  19.0 1.5 %collective-permute-done.2.swapped = f32[512,128]{1,0:T(8,128)S(1)} collective-permute-done((f32[512,128]{1,0:T(8,128)S(1)}, f32[512,128]{1,0:T(8,128)S(1)}, u32[]{:S(2)}, u32[]{:S(2)}) %collective-permute-start.2) | collective-permute-done | bytes 262176 | tf_op jit(solution)/shard_map/ppermute | solution.py:787
  20.5 1.9 %inner_substeps.1 = (f32[3,32,8,128]{3,2,1,0:T(8,128)S(1)}, f32[6,32,8,128]{3,2,1,0:T(8,128)S(1)}, f32[4,34,8,128]{3,2,1,0:T(8,128)S(1)}, f32[34,8,128]{2,1,0:T(8,128)S(1)}, f32[34,8,128]{2,1,0:T(8,128)S(1)}) custom-call(f32[512,128]{1,0:T(8,128)S(1)} %bitcast.5, ...), custom_call_target="tpu_custom_call", output_to_operand_aliasing={{0}: (3, {}), {1}: (4, {})} | custom-call | tf_op jit(solution)/shard_map/inner_substeps/pallas_call | solution.py:795
  22.4 0.0 collective-permute-done.1.border
  22.4 2.0 %outer_substeps.1 = (f32[3,32,8,128]{3,2,1,0:T(8,128)S(1)}, f32[6,32,8,128]{3,2,1,0:T(8,128)S(1)}, f32[5,32,8,128]{3,2,1,0:T(8,128)S(1)}, f32[4,34,8,128]{3,2,1,0:T(8,128)S(1)}, f32[256,128]{1,0:T(8,128)}) custom-call(f32[24,128]{1,0:T(8,128)S(1)} %get-tuple-element.25.materials, ...), custom_call_target="tpu_custom_call", output_to_operand_aliasing={{0}: (4, {}), {1}: (5, {}), {2}: (6, {}), {3}: (7, {})} | custom-call | tf_op jit(solution)/shard_map/outer_substeps/pallas_call | solution.py:807
  24.4 4.2 %all-to-all-start.1 = ((f32[16,16,128]{2,1,0:T(8,128)}), f32[16,16,128]{2,1,0:T(8,128)S(1)}, u32[]{:S(2)}, u32[]{:S(2)}) async-start(f32[16,16,128]{2,1,0:T(8,128)} %bitcast.2), calls=%async_computation.1 | async-start | bytes 262144 | tf_op jit(solution)/shard_map/all_to_all | solution.py:820
  28.7 2.0 %last_updates.1 = (f32[3,8,32,32]{3,2,1,0:T(8,128)}, f32[6,8,32,32]{3,2,1,0:T(8,128)}) custom-call(f32[3,32,8,128]{3,2,1,0:T(8,128)S(1)} %get-tuple-element.38.vel_all, f32[6,32,8,128]{3,2,1,0:T(8,128)S(1)} %get-tuple-element.39.stress_all, f32[5,32,8,128]{3,2,1,0:T(8,128)S(1)} %get-tuple-element.40.mats_all, ...), custom_call_target="tpu_custom_call" | custom-call | tf_op jit(solution)/shard_map/last_updates/pallas_call | solution.py:823
  30.7 5.9 %all-to-all-done.1 = f32[16,16,128]{2,1,0:T(8,128)S(1)} async-done(((f32[16,16,128]{2,1,0:T(8,128)}), f32[16,16,128]{2,1,0:T(8,128)S(1)}, u32[]{:S(2)}, u32[]{:S(2)}) %all-to-all-start.1) | async-done | bytes 131104 | tf_op jit(solution)/shard_map/all_to_all | solution.py:820
  36.6 0.9 %ocean_strips.1 = f32[4,2,32,128]{3,2,1,0:T(8,128)} custom-call(f32[256,128]{1,0:T(8,128)S(1)} %bitcast.6), custom_call_target="tpu_custom_call" | custom-call | tf_op jit(solution)/shard_map/ocean_strips/pallas_call | solution.py:833
Async XLA Ops:
  2.7 16.3 %all-to-all-start = ((f32[8,64,128]{2,1,0:T(8,128)}), f32[8,64,128]{2,1,0:T(8,128)S(1)}, u32[]{:S(2)}, u32[]{:S(2)}) async-start(f32[8,64,128]{2,1,0:T(8,128)} %bitcast), calls=%async_computation | async-start | bytes 524288 | tf_op jit(solution)/shard_map/all_to_all | solution.py:763
  9.9 1.7 %copy-start = (f32[3,8]{1,0:T(4,128)S(1)}, f32[3,8]{1,0:T(4,128)}, u32[]{:S(2)}) copy-start(f32[3,8]{1,0:T(4,128)} %table.1) | copy-start | bytes 292
  9.9 1.7 %collective-permute-start = (f32[81,8,128]{2,1,0:T(8,128)S(1)}, f32[81,8,128]{2,1,0:T(8,128)S(1)}, u32[]{:S(2)}, u32[]{:S(2)}) collective-permute-start(f32[81,8,128]{2,1,0:T(8,128)S(1)} %get-tuple-element.24.own), channel_id=1, source_target_pairs={{0,1},{1,0},{2,3},{3,2},{4,5},{5,4},{6,7},{7,6},{8,9},{9,8},{10,11... | collective-permute-start | bytes 995336 | tf_op jit(solution)/shard_map/ppermute | solution.py:772
  10.0 12.4 %collective-permute-start.1 = (f32[74,8,128]{2,1,0:T(8,128)S(1)}, f32[74,8,128]{2,1,0:T(8,128)S(1)}, u32[]{:S(2)}, u32[]{:S(2)}) collective-permute-start(f32[74,8,128]{2,1,0:T(8,128)S(1)} %get-tuple-element.26), channel_id=1, source_target_pairs={{1,2},{3,4},{5,6},{7,8},{9,10},{11,12},{13,14},{2,1},{4,3},{6,5},{... | collective-permute-start | bytes 909320 | tf_op jit(solution)/shard_map/ppermute | solution.py:771
  19.0 1.5 %collective-permute-start.2 = (f32[512,128]{1,0:T(8,128)S(1)}, f32[512,128]{1,0:T(8,128)S(1)}, u32[]{:S(2)}, u32[]{:S(2)}) collective-permute-start(f32[512,128]{1,0:T(8,128)S(1)} %bitcast.4), channel_id=1, source_target_pairs={{0,1},{1,0},{2,3},{3,2},{4,5},{5,4},{6,7},{7,6},{8,9},{9,8},{10,11... | collective-permute-start | bytes 786440 | tf_op jit(solution)/shard_map/ppermute | solution.py:787
  24.4 12.2 %all-to-all-start.1 = ((f32[16,16,128]{2,1,0:T(8,128)}), f32[16,16,128]{2,1,0:T(8,128)S(1)}, u32[]{:S(2)}, u32[]{:S(2)}) async-start(f32[16,16,128]{2,1,0:T(8,128)} %bitcast.2), calls=%async_computation.1 | async-start | bytes 262144 | tf_op jit(solution)/shard_map/all_to_all | solution.py:820

commit v25 on v23

--- a/solution.py
+++ b/solution.py
@@ -453,6 +453,12 @@
         vel[VY, at] = vel[VY, at] + b * ay
         vel[VZ, at] = vel[VZ, at] + b * (az + self.load(j, count))
 
+    def move_z(self, j, count):
+        at = pl.ds(j, count)
+        _, _, az = acceleration(self.sh, self.stress, j, count)
+        vz = self.vel[VZ, at] + self.mats[BUOY, at] * (az + self.load(j, count))
+        self.vel[VZ, at] = vz
+
     def strain(self, j, count):
         for f, value in strained(self.sh, self.vel, self.stress, self.mats, j, count):
             self.stress[f, pl.ds(j, count)] = value
@@ -478,7 +484,10 @@
             planes(0, 1, self.add_floor)
         for t in range(STEPS - 1):
             flows(t + 1)
-            planes(t, 1, self.add_load if inner and t == 0 else self.move)
+            move = self.add_load if inner and t == 0 else self.move
+            if not inner and t == STEPS - 2:
+                move = self.move_z
+            planes(t, 1, move)
             if t < STEPS - 2:
                 planes(t, 2, self.strain)
             planes(t + 1, 1, functools.partial(self.press, floor=self.floor))
@@ -640,8 +649,19 @@
                 :, :, kc * ny : (kc + 1) * ny
             ]
 
+    def hold(j, count):
+        for f in range(3):
+            vel[f, pl.ds(j, count)] = vel_in[f, pl.ds(j, count)]
+
+    def catch_up(x, count):
+        j = first - 1 + (last - first - 6) * odd_device() + x
+        at = pl.ds(j, count)
+        ax, ay, _ = acceleration(sh, stress_in, j, count)
+        vel[VX, at] = vel[VX, at] + mats[BUOY, at] * ax
+        vel[VY, at] = vel[VY, at] + mats[BUOY, at] * ay
+
     def strain(j, count):
-        for f, value in strained(sh, vel_in, stress_in, mats, j, count):
+        for f, value in strained(sh, vel, stress_in, mats, j, count):
             stress[f, pl.ds(j, count)] = value
 
     def move(j, count):
@@ -651,7 +671,7 @@
         wet = pl.ds(j + 1, count)
         load = sh.on_top(bottom[wet] * pressure[wet])
         for f, a in enumerate((ax, ay, az + load)):
-            vel[f, at] = vel_in[f, at] + b * a
+            vel[f, at] = vel[f, at] + b * a
 
     def finish(x, count):
         for f in range(3):
@@ -659,6 +679,8 @@
         for f, value in strained(sh, vel, stress, mats, x + HALO, count):
             put(stress_out, f, x, count, value)
 
+    plan.planes(first - 1, last + 1, hold, BATCH)
+    plan.planes(0, HALO, catch_up, BATCH)
     plan.planes(first, last, strain, BATCH)
     plan.planes(first + 1, last - 1, move, BATCH)
     plan.planes(0, cells, finish, BATCH)

time: 37.9 us -> 37.9 us (level)
  no operation moved by 1% of the time
where the time goes in v25:
time: 37.9 us; the launch traced here: 37.5 us
  waiting for transfers between devices  14.7 us (39%)
  starting transfers between devices  12.2 us (32%)
  Pallas kernels  9.92 us (26%)
  between operations  0.69 us (2%)
    all_to_all x1, starting transfers between devices, on_device(): lax.all_to_all(message.reshape(n // 2, 2 * plan.rows, LANES), 'map', spli...  7.26 us
    all_to_all x1, waiting for transfers between devices, on_device(): lax.all_to_all(message.reshape(n // 2, 2 * plan.rows, LANES), 'map', spli...  6.42 us
    all_to_all x1, waiting for transfers between devices, on_device(): lax.all_to_all(back.reshape(n, plan.back_rows, LANES), 'map', split_axis=...  5.8 us
    all_to_all x1, starting transfers between devices, on_device(): lax.all_to_all(back.reshape(n, plan.back_rows, LANES), 'map', split_axis=...  4.23 us
    pallas_call x1, Pallas kernels, on_device(): call(end_kernel, 'last_updates', (shape(*velocity.shape), shape(*stress.s...  2.14 us
    pallas_call x1, Pallas kernels, on_device(): call(pack_kernel, 'pack', (shape(n * plan.rows, LANES), shape(10 * cells...  2.07 us
    pallas_call x1, Pallas kernels, on_device(): call(outer_kernel, 'outer_substeps', tuple((planes_of[k] for k in ('vel',...  2.01 us
    pallas_call x1, Pallas kernels, on_device(): call(inner_kernel, 'inner_substeps', tuple((planes_of[k] for k in ('vel',...  1.87 us
  transfers between devices with their start and end apart: 5, of which 4 were waited for; matrix products, arithmetic and copies ran while one was open for 0% of the time, Pallas kernels for 13%

profile of v25, /device:TPU:0, one launch (start us, length us, event | category | flops | bytes accessed | tf_op | source)
XLA Modules:
  0.0 37.5 jit_solution(3566852814888526598)
XLA Ops:
  0.6 2.1 %pack.1 = (f32[512,128]{1,0:T(8,128)}, f32[81,8,128]{2,1,0:T(8,128)S(1)}, f32[74,8,128]{2,1,0:T(8,128)S(1)}) custom-call(f32[3,8,32,32]{3,2,1,0:T(8,128)} %vel_ref.1, f32[6,8,32,32]{3,2,1,0:T(8,128)} %stress_ref.1, s32[8,32,32]{2,1,0:T(8,128)} %zones_ref.1, f32[8,32]{1,0:T(8,128)} %slip_ref.1, f32[4,2,32,128]{3,2,1,0:T(8,128)} %ocean_ref.1, s32[2,128]{1,0:T(2,128)} %bathy_ref.1), custom_call_target="tpu_custom_call" | custom-call | tf_op jit(solution)/shard_map/pack/pallas_call | solution.py:755
  2.7 7.3 %all-to-all-start = ((f32[8,64,128]{2,1,0:T(8,128)}), f32[8,64,128]{2,1,0:T(8,128)S(1)}, u32[]{:S(2)}, u32[]{:S(2)}) async-start(f32[8,64,128]{2,1,0:T(8,128)} %bitcast), calls=%async_computation | async-start | bytes 524288 | tf_op jit(solution)/shard_map/all_to_all | solution.py:776
  10.0 0.0 copy-start
  10.0 0.1 collective-permute-start
  10.1 0.7 %collective-permute-start.1 = (f32[74,8,128]{2,1,0:T(8,128)S(1)}, f32[74,8,128]{2,1,0:T(8,128)S(1)}, u32[]{:S(2)}, u32[]{:S(2)}) collective-permute-start(f32[74,8,128]{2,1,0:T(8,128)S(1)} %get-tuple-element.26), channel_id=1, source_target_pairs={{1,2},{3,4},{5,6},{7,8},{9,10},{11,12},{13,14},{2,1},{4,3},{6,5},{... | collective-permute-start | bytes 909320 | tf_op jit(solution)/shard_map/ppermute | solution.py:784
  10.8 0.9 %collective-permute-done.mate = f32[81,8,128]{2,1,0:T(8,128)S(1)} collective-permute-done((f32[81,8,128]{2,1,0:T(8,128)S(1)}, f32[81,8,128]{2,1,0:T(8,128)S(1)}, u32[]{:S(2)}, u32[]{:S(2)}) %collective-permute-start) | collective-permute-done | bytes 331808 | tf_op jit(solution)/shard_map/ppermute | solution.py:785
  11.7 0.0 copy-done
  11.7 0.9 %first_velocity.1 = (f32[3,32,8,128]{3,2,1,0:T(8,128)S(1)}, f32[6,32,8,128]{3,2,1,0:T(8,128)S(1)}, f32[5,32,8,128]{3,2,1,0:T(8,128)S(1)}, f32[24,128]{1,0:T(8,128)S(1)}) custom-call(f32[3,8]{1,0:T(4,128)S(1)} %copy-done, f32[81,8,128]{2,1,0:T(8,128)S(1)} %get-tuple-element.24.own, f32[81,8,128]{2,1,0:T(8,128)S(1)} %collective-permute-done.mate), custom_call_target="tpu_custom_call" | custom-call | tf_op jit(solution)/shard_map/first_velocity/pallas_call | solution.py:787
  12.6 6.4 %all-to-all-done = f32[8,64,128]{2,1,0:T(8,128)S(1)} async-done(((f32[8,64,128]{2,1,0:T(8,128)}), f32[8,64,128]{2,1,0:T(8,128)S(1)}, u32[]{:S(2)}, u32[]{:S(2)}) %all-to-all-start) | async-done | bytes 262176 | tf_op jit(solution)/shard_map/all_to_all | solution.py:776
  19.0 0.0 collective-permute-start.2
  19.0 1.5 %collective-permute-done.2.swapped = f32[512,128]{1,0:T(8,128)S(1)} collective-permute-done((f32[512,128]{1,0:T(8,128)S(1)}, f32[512,128]{1,0:T(8,128)S(1)}, u32[]{:S(2)}, u32[]{:S(2)}) %collective-permute-start.2) | collective-permute-done | bytes 262176 | tf_op jit(solution)/shard_map/ppermute | solution.py:800
  20.5 1.9 %inner_substeps.1 = (f32[3,32,8,128]{3,2,1,0:T(8,128)S(1)}, f32[6,32,8,128]{3,2,1,0:T(8,128)S(1)}, f32[4,34,8,128]{3,2,1,0:T(8,128)S(1)}, f32[34,8,128]{2,1,0:T(8,128)S(1)}, f32[34,8,128]{2,1,0:T(8,128)S(1)}) custom-call(f32[512,128]{1,0:T(8,128)S(1)} %bitcast.5, ...), custom_call_target="tpu_custom_call", output_to_operand_aliasing={{0}: (3, {}), {1}: (4, {})} | custom-call | tf_op jit(solution)/shard_map/inner_substeps/pallas_call | solution.py:808
  22.4 0.0 collective-permute-done.1.border
  22.4 2.0 %outer_substeps.1 = (f32[3,32,8,128]{3,2,1,0:T(8,128)S(1)}, f32[6,32,8,128]{3,2,1,0:T(8,128)S(1)}, f32[5,32,8,128]{3,2,1,0:T(8,128)S(1)}, f32[4,34,8,128]{3,2,1,0:T(8,128)S(1)}, f32[256,128]{1,0:T(8,128)}) custom-call(f32[24,128]{1,0:T(8,128)S(1)} %get-tuple-element.25.materials, ...), custom_call_target="tpu_custom_call", output_to_operand_aliasing={{0}: (4, {}), {1}: (5, {}), {2}: (6, {}), {3}: (7, {})} | custom-call | tf_op jit(solution)/shard_map/outer_substeps/pallas_call | solution.py:820
  24.4 4.2 %all-to-all-start.1 = ((f32[16,16,128]{2,1,0:T(8,128)}), f32[16,16,128]{2,1,0:T(8,128)S(1)}, u32[]{:S(2)}, u32[]{:S(2)}) async-start(f32[16,16,128]{2,1,0:T(8,128)} %bitcast.2), calls=%async_computation.1 | async-start | bytes 262144 | tf_op jit(solution)/shard_map/all_to_all | solution.py:833
  28.7 2.1 %last_updates.1 = (f32[3,8,32,32]{3,2,1,0:T(8,128)}, f32[6,8,32,32]{3,2,1,0:T(8,128)}) custom-call(f32[3,32,8,128]{3,2,1,0:T(8,128)S(1)} %get-tuple-element.38.vel_all, f32[6,32,8,128]{3,2,1,0:T(8,128)S(1)} %get-tuple-element.39.stress_all, f32[5,32,8,128]{3,2,1,0:T(8,128)S(1)} %get-tuple-element.40.mats_all, ...), custom_call_target="tpu_custom_call" | custom-call | tf_op jit(solution)/shard_map/last_updates/pallas_call | solution.py:836
  30.8 5.8 %all-to-all-done.1 = f32[16,16,128]{2,1,0:T(8,128)S(1)} async-done(((f32[16,16,128]{2,1,0:T(8,128)}), f32[16,16,128]{2,1,0:T(8,128)S(1)}, u32[]{:S(2)}, u32[]{:S(2)}) %all-to-all-start.1) | async-done | bytes 131104 | tf_op jit(solution)/shard_map/all_to_all | solution.py:833
  36.6 0.9 %ocean_strips.1 = f32[4,2,32,128]{3,2,1,0:T(8,128)} custom-call(f32[256,128]{1,0:T(8,128)S(1)} %bitcast.6), custom_call_target="tpu_custom_call" | custom-call | tf_op jit(solution)/shard_map/ocean_strips/pallas_call | solution.py:846
Async XLA Ops:
  2.7 16.3 %all-to-all-start = ((f32[8,64,128]{2,1,0:T(8,128)}), f32[8,64,128]{2,1,0:T(8,128)S(1)}, u32[]{:S(2)}, u32[]{:S(2)}) async-start(f32[8,64,128]{2,1,0:T(8,128)} %bitcast), calls=%async_computation | async-start | bytes 524288 | tf_op jit(solution)/shard_map/all_to_all | solution.py:776
  10.0 1.7 %copy-start = (f32[3,8]{1,0:T(4,128)S(1)}, f32[3,8]{1,0:T(4,128)}, u32[]{:S(2)}) copy-start(f32[3,8]{1,0:T(4,128)} %table.1) | copy-start | bytes 292
  10.0 1.7 %collective-permute-start = (f32[81,8,128]{2,1,0:T(8,128)S(1)}, f32[81,8,128]{2,1,0:T(8,128)S(1)}, u32[]{:S(2)}, u32[]{:S(2)}) collective-permute-start(f32[81,8,128]{2,1,0:T(8,128)S(1)} %get-tuple-element.24.own), channel_id=1, source_target_pairs={{0,1},{1,0},{2,3},{3,2},{4,5},{5,4},{6,7},{7,6},{8,9},{9,8},{10,11... | collective-permute-start | bytes 995336 | tf_op jit(solution)/shard_map/ppermute | solution.py:785
  10.1 12.4 %collective-permute-start.1 = (f32[74,8,128]{2,1,0:T(8,128)S(1)}, f32[74,8,128]{2,1,0:T(8,128)S(1)}, u32[]{:S(2)}, u32[]{:S(2)}) collective-permute-start(f32[74,8,128]{2,1,0:T(8,128)S(1)} %get-tuple-element.26), channel_id=1, source_target_pairs={{1,2},{3,4},{5,6},{7,8},{9,10},{11,12},{13,14},{2,1},{4,3},{6,5},{... | collective-permute-start | bytes 909320 | tf_op jit(solution)/shard_map/ppermute | solution.py:784
  19.0 1.5 %collective-permute-start.2 = (f32[512,128]{1,0:T(8,128)S(1)}, f32[512,128]{1,0:T(8,128)S(1)}, u32[]{:S(2)}, u32[]{:S(2)}) collective-permute-start(f32[512,128]{1,0:T(8,128)S(1)} %bitcast.4), channel_id=1, source_target_pairs={{0,1},{1,0},{2,3},{3,2},{4,5},{5,4},{6,7},{7,6},{8,9},{9,8},{10,11... | collective-permute-start | bytes 786440 | tf_op jit(solution)/shard_map/ppermute | solution.py:800
  24.4 12.2 %all-to-all-start.1 = ((f32[16,16,128]{2,1,0:T(8,128)}), f32[16,16,128]{2,1,0:T(8,128)S(1)}, u32[]{:S(2)}, u32[]{:S(2)}) async-start(f32[16,16,128]{2,1,0:T(8,128)} %bitcast.2), calls=%async_computation.1 | async-start | bytes 262144 | tf_op jit(solution)/shard_map/all_to_all | solution.py:833
